TPU v7x, 32 devices: a whole 2x2x4 slice. The times are simulated.
32 devices in a mesh: dp: 16 (over z, y, x), tensor: 2 (over core).
Axes of the slice: x: 2, y: 2, z: 4, core: 2. Of those that a mesh axis runs over, the one named last changes fastest.
Arguments:
- residual: bfloat16 [4096, 768], P(('dp', 'tensor')), may hold values from -6 to 6
- cotangent: bfloat16 [4096, 768], P(('dp', 'tensor')), may hold values from -6 to 6
- seq_lengths: int32 [16, 4], P('dp'), may hold values from 0 to 256, as said below
- gain_attn: float32 [768], replicated, may hold values from 0.1 to 1.9
- shift_attn: float32 [768], replicated, may hold values from -1.75 to 1.75
- gain_mlp: float32 [768], replicated, may hold values from 0.1 to 1.9
- shift_mlp: float32 [768], replicated, may hold values from -1.75 to 1.75
- w_qkv: bfloat16 [3, 768, 768], P(None, 'dp', 'tensor'), may hold values from -0.3125 to 0.3125
- b_qkv: float32 [3, 768], P(None, 'tensor'), may hold values from -1.75 to 1.75
- w_out: bfloat16 [768, 768], P('tensor', 'dp'), may hold values from -1.25 to 1.25
- b_out: float32 [768], replicated, may hold values from -1.75 to 1.75
- w_up: bfloat16 [768, 3072], P('dp', 'tensor'), may hold values from -0.21875 to 0.21875
- b_up: float32 [3072], P('tensor'), may hold values from -3 to 3
- w_down: bfloat16 [3072, 768], P('tensor', 'dp'), may hold values from -0.15625 to 0.15625
- b_down: float32 [768], replicated, may hold values from -1.75 to 1.75
Outputs:
- result: bfloat16 [4096, 768], P(('dp', 'tensor'))
- grad_residual: float32 [4096, 768], P(('dp', 'tensor'))
- grad_gain_attn: float32 [768], replicated
- grad_shift_attn: float32 [768], replicated
- grad_gain_mlp: float32 [768], replicated
- grad_shift_mlp: float32 [768], replicated
- grad_w_qkv: float32 [3, 768, 768], P(None, 'dp', 'tensor')
- grad_b_qkv: float32 [3, 768], P(None, 'tensor')
- grad_w_out: float32 [768, 768], P('tensor', 'dp')
- grad_b_out: float32 [768], replicated
- grad_w_up: float32 [768, 3072], P('dp', 'tensor')
- grad_b_up: float32 [3072], P('tensor')
- grad_w_down: float32 [3072, 768], P('tensor', 'dp')
- grad_b_down: float32 [768], replicated
Inputs may be any that keep to these rules, and one draw needn't show every extreme that they name: `seq_lengths`: in each group the padded lengths sum to at most 256; the sequence that holds row 127 of a group also holds row 128; in some group a single sequence of exactly 256 rows fills it.
All inputs are finite; a program needn't handle non-finite values.
Results may differ from a plain program's by a relative error of at most 0.012.
The roundings to bfloat16 on the way count: a program that leaves them out, or rounds other values in their place, can miss the bound.
Values may be sent and summed in bfloat16 or wider, within the bound.
No kernel may reach another device: no remote copies, remote signals or barrier semaphores. Data moves between devices by JAX's collectives and lax.ppermute only.
A program may use at most 128 MiB of HBM per device.

v0:
```python
from functools import partial

import jax
import jax.numpy as jnp
from jax import lax
from jax.sharding import PartitionSpec as P

HD = 64
ROT = 16
BLOCK = 128


eps = 1e-05


def layout_rows(lengths, row_count, block_rows):
    row_index = jnp.arange(row_count, dtype=jnp.int32)
    padded = (lengths + block_rows - 1) // block_rows * block_rows
    ends = jnp.cumsum(padded)
    starts = ends - padded
    sequence = jnp.sum((row_index[:, None] >= ends[None, :]).astype(jnp.int32), axis=1)
    starts_all = jnp.concatenate([starts, ends[-1:]])
    lengths_all = jnp.concatenate([lengths, jnp.zeros((1,), jnp.int32)])
    places = jnp.arange(lengths.shape[0] + 1, dtype=jnp.int32)
    picked = sequence[:, None] == places[None, :]
    first_row = jnp.sum(jnp.where(picked, starts_all[None, :], 0), axis=1)
    limit = jnp.sum(jnp.where(picked, lengths_all[None, :], 0), axis=1)
    position = row_index - first_row
    return (sequence, position, position < limit)


def rotate(field, position, rot_dims):
    half = rot_dims // 2
    inverse = 10000.0 ** (-jnp.arange(half, dtype=jnp.float32) * 2.0 / rot_dims)
    angle = position.astype(jnp.float32)[:, None] * inverse[None, :]
    angle = jnp.concatenate([angle, angle], axis=1)
    turned_part = field[..., :rot_dims]
    first_half = turned_part[..., :half]
    second_half = turned_part[..., half:]
    swapped = jnp.concatenate([-second_half, first_half], axis=-1)
    rotated = turned_part * jnp.cos(angle) + swapped * jnp.sin(angle)
    return jnp.concatenate([rotated, field[..., rot_dims:]], axis=-1)


def layer_norm(block_rows, gain, shift):
    centre = jnp.mean(block_rows, axis=-1, keepdims=True)
    spread = jnp.mean((block_rows - centre) ** 2, axis=-1, keepdims=True)
    return (block_rows - centre) * lax.rsqrt(spread + eps) * gain + shift


def both_norms(block_rows, gain_attn, shift_attn, gain_mlp, shift_mlp):
    return (
        layer_norm(block_rows, gain_attn, shift_attn),
        layer_norm(block_rows, gain_mlp, shift_mlp),
    )


def reduce_columns(out_grad, down_grad):
    joined = jnp.concatenate([out_grad, down_grad], axis=0)
    summed = lax.psum_scatter(joined, "dp", scatter_dimension=1, tiled=True)
    split_at = out_grad.shape[0]
    return (summed[:split_at], summed[split_at:])


def per_device(
    residual,
    cotangent,
    seq_lengths,
    gain_attn,
    shift_attn,
    gain_mlp,
    shift_mlp,
    w_qkv,
    b_qkv,
    w_out,
    b_out,
    w_up,
    b_up,
    w_down,
    b_down,
):
    tensor_size = lax.axis_size("tensor")
    own_rows = residual.shape[0]
    slot_count = own_rows * tensor_size
    offset = lax.axis_index("tensor") * own_rows
    sequence, position, live_row = layout_rows(seq_lengths[0], slot_count, BLOCK)
    live_own = lax.dynamic_slice_in_dim(live_row, offset, own_rows, 0)
    residual_f = residual.astype(jnp.float32)
    norm_params = (gain_attn, shift_attn, gain_mlp, shift_mlp)
    (first_own, second_own), norm_back = jax.vjp(both_norms, residual_f, *norm_params)
    first_norm, second_norm = (
        lax.all_gather(first_own.astype(jnp.bfloat16), "tensor", axis=0, tiled=True),
        lax.all_gather(second_own.astype(jnp.bfloat16), "tensor", axis=0, tiled=True),
    )
    full_qkv, full_out, full_up, full_down = (
        lax.all_gather(w_qkv, "dp", axis=1, tiled=True),
        lax.all_gather(w_out, "dp", axis=1, tiled=True),
        lax.all_gather(w_up, "dp", axis=0, tiled=True),
        lax.all_gather(w_down, "dp", axis=1, tiled=True),
    )
    local_width = full_out.shape[0]
    head_count = local_width // HD
    projected = (
        jnp.einsum("sd,cde->cse", first_norm, full_qkv, preferred_element_type=jnp.float32)
        + b_qkv[:, None, :]
    )
    split_heads = projected.reshape(3, slot_count, head_count, HD).transpose(0, 2, 1, 3)
    turned_query, rotate_back = jax.vjp(lambda field: rotate(field, position, ROT), split_heads[0])
    queries = turned_query.astype(jnp.bfloat16)
    key_heads = rotate(split_heads[1], position, ROT).astype(jnp.bfloat16)
    value_heads = split_heads[2].astype(jnp.bfloat16)
    scale = HD ** (-0.5)
    span = min(512, slot_count)
    starts = jnp.arange(slot_count // span, dtype=jnp.int32) * span
    row_index = jnp.arange(slot_count, dtype=jnp.int32)

    def block_logits(start):
        rows_here = start + jnp.arange(span, dtype=jnp.int32)
        allowed = (sequence[:, None] == sequence[None, :]) & (
            row_index[None, :] <= rows_here[:, None]
        )
        allowed = allowed & (live_row[None, :] | (row_index[None, :] == rows_here[:, None]))
        logits = (
            jnp.einsum("hqe,hke->hqk", queries, key_heads, preferred_element_type=jnp.float32)
            * scale
        )
        return jnp.where(allowed[None], logits, -1000000000.0)

    def attend(start):
        logits = block_logits(start)
        largest = jnp.max(logits, axis=-1, keepdims=True)
        weights = jnp.exp(logits - largest)
        total = jnp.sum(weights, axis=-1, keepdims=True)
        normalized = (weights / total).astype(jnp.bfloat16)
        block_out = jnp.einsum(
            "hqk,hke->hqe", normalized, value_heads, preferred_element_type=jnp.float32
        )
        return (block_out.astype(jnp.bfloat16), largest[..., 0] + jnp.log(total[..., 0]))

    attended, log_total = lax.map(attend, starts)
    attended = attended.transpose(1, 0, 2, 3).reshape(head_count, slot_count, HD)
    log_total = log_total.transpose(1, 0, 2).reshape(head_count, slot_count)
    flat_attended = attended.transpose(1, 0, 2).reshape(slot_count, local_width)
    hidden_pre = jnp.dot(second_norm, full_up, preferred_element_type=jnp.float32) + b_up
    gelu_value, gelu_back = jax.vjp(partial(jax.nn.gelu, approximate=False), hidden_pre)
    activated = gelu_value.astype(jnp.bfloat16)
    partial_sum = jnp.dot(flat_attended, full_out, preferred_element_type=jnp.float32) + jnp.dot(
        activated, full_down, preferred_element_type=jnp.float32
    )
    branch = (
        lax.psum_scatter(
            partial_sum.astype(jnp.bfloat16), "tensor", scatter_dimension=0, tiled=True
        ).astype(jnp.float32)
        + b_out
        + b_down
    )
    result = (residual_f + branch).astype(jnp.bfloat16)
    grad_out = cotangent.astype(jnp.float32) * live_own[:, None].astype(jnp.float32)
    grad_branch = grad_out.astype(jnp.bfloat16)
    grad_bias_out = jnp.sum(grad_branch.astype(jnp.float32), axis=0)
    grad_full = lax.all_gather(grad_branch, "tensor", axis=0, tiled=True)
    back_qkv, back_out, back_up, back_down = (
        lax.all_gather(w_qkv, "dp", axis=1, tiled=True),
        lax.all_gather(w_out, "dp", axis=1, tiled=True),
        lax.all_gather(w_up, "dp", axis=0, tiled=True),
        lax.all_gather(w_down, "dp", axis=1, tiled=True),
    )
    grad_w_out = jnp.dot(flat_attended.T, grad_full, preferred_element_type=jnp.float32)
    grad_w_down = jnp.dot(activated.T, grad_full, preferred_element_type=jnp.float32)
    grad_act = jnp.dot(grad_full, back_down.T, preferred_element_type=jnp.float32)
    grad_hidden = gelu_back(grad_act)[0].astype(jnp.bfloat16)
    grad_b_up = jnp.sum(grad_hidden.astype(jnp.float32), axis=0)
    grad_w_up = jnp.dot(second_norm.T, grad_hidden, preferred_element_type=jnp.float32)
    grad_second = jnp.dot(grad_hidden, back_up.T, preferred_element_type=jnp.float32)
    grad_attended = jnp.dot(grad_full, back_out.T, preferred_element_type=jnp.float32).astype(
        jnp.bfloat16
    )
    grad_heads = grad_attended.reshape(slot_count, head_count, HD).transpose(1, 0, 2)

    def attend_back(carry, start):
        grad_keys, grad_values = carry
        logits = block_logits(start)
        probs = jnp.exp(logits - log_total[..., None])
        grad_probs = jnp.einsum(
            "hqe,hke->hqk", grad_heads, value_heads, preferred_element_type=jnp.float32
        )
        row_inner = jnp.sum(probs * grad_probs, axis=-1, keepdims=True)
        grad_logits = (probs * (grad_probs - row_inner)).astype(jnp.bfloat16)
        grad_query = (
            jnp.einsum("hqk,hke->hqe", grad_logits, key_heads, preferred_element_type=jnp.float32)
            * scale
        )
        grad_keys = (
            grad_keys
            + jnp.einsum("hqk,hqe->hke", grad_logits, queries, preferred_element_type=jnp.float32)
            * scale
        )
        grad_values = grad_values + jnp.einsum(
            "hqk,hqe->hke",
            probs.astype(jnp.bfloat16),
            grad_heads,
            preferred_element_type=jnp.float32,
        )
        return ((grad_keys, grad_values), grad_query)

    zero_heads = jnp.zeros((head_count, slot_count, HD), jnp.float32)
    (grad_keys, grad_values), grad_queries = lax.scan(attend_back, (zero_heads, zero_heads), starts)
    grad_queries = grad_queries.transpose(1, 0, 2, 3).reshape(head_count, slot_count, HD)
    stacked = jnp.stack([rotate_back(grad_queries)[0], rotate_back(grad_keys)[0], grad_values])
    grad_projected = (
        stacked.transpose(0, 2, 1, 3).reshape(3, slot_count, local_width).astype(jnp.bfloat16)
    )
    grad_b_qkv = jnp.sum(grad_projected.astype(jnp.float32), axis=1)
    grad_w_qkv = jnp.einsum(
        "sd,cse->dce", first_norm, grad_projected, preferred_element_type=jnp.float32
    )
    grad_first = jnp.einsum(
        "cse,cde->sd", grad_projected, back_qkv, preferred_element_type=jnp.float32
    )
    both_grads = lax.psum_scatter(
        jnp.stack([grad_first, grad_second]).astype(jnp.bfloat16),
        "tensor",
        scatter_dimension=1,
        tiled=True,
    ).astype(jnp.float32)
    norm_grads = norm_back((both_grads[0], both_grads[1]))
    grad_residual = grad_out + norm_grads[0]
    shard_out, shard_down = reduce_columns(grad_w_out, grad_w_down)
    row_joined = jnp.concatenate(
        [grad_w_qkv.reshape(grad_w_qkv.shape[0], 3 * local_width), grad_w_up], axis=1
    )
    row_summed = lax.psum_scatter(row_joined, "dp", scatter_dimension=0, tiled=True)
    owned = row_summed.shape[0]
    shard_qkv = row_summed[:, : 3 * local_width].reshape(owned, 3, local_width).transpose(1, 0, 2)
    shard_up = row_summed[:, 3 * local_width :]
    summed_qkv, summed_up = lax.psum((grad_b_qkv, grad_b_up), "dp")
    shared = lax.psum(
        (grad_bias_out, norm_grads[1], norm_grads[2], norm_grads[3], norm_grads[4]),
        ("dp", "tensor"),
    )
    return (
        result,
        grad_residual,
        shared[1],
        shared[2],
        shared[3],
        shared[4],
        shard_qkv,
        summed_qkv,
        shard_out,
        shared[0],
        shard_up,
        summed_up,
        shard_down,
        shared[0],
    )


def solution(mesh):
    return jax.shard_map(
        per_device,
        mesh=mesh,
        in_specs=(
            P(("dp", "tensor"), None),
            P(("dp", "tensor"), None),
            P("dp", None),
            P(),
            P(),
            P(),
            P(),
            P(None, "dp", "tensor"),
            P(None, "tensor"),
            P("tensor", "dp"),
            P(),
            P("dp", "tensor"),
            P("tensor"),
            P("tensor", "dp"),
            P(),
        ),
        out_specs=(
            P(("dp", "tensor"), None),
            P(("dp", "tensor"), None),
            P(),
            P(),
            P(),
            P(),
            P(None, "dp", "tensor"),
            P(None, "tensor"),
            P("tensor", "dp"),
            P(),
            P("dp", "tensor"),
            P("tensor"),
            P("tensor", "dp"),
            P(),
        ),
        check_vma=False,
    )
```

profile of v0, /device:TPU:0, one launch (start us, length us, event | category | flops | bytes accessed | tf_op | source)
XLA Modules:
  0.0 559.6 jit_solution(17673063773990928029)
XLA Ops:
  7.3 0.7 all-gather.4.cloned.1.call-update
  8.0 0.7 all-gather.6.cloned.1.call-update
  8.8 0.7 all-gather.8.cloned.1.call-update
  9.5 0.7 fusion.64
  10.9 0.7 multiply_subtract_fusion
  11.6 1.0 convert_reduce_fusion.2
  12.7 1.1 fusion.39
  14.4 1.4 pad_add_fusion.2
  16.3 1.6 convert_reduce_fusion.3
  17.9 2.2 all_gather.31
  20.3 2.1 all_gather.25
  22.4 2.2 all_gather.28
  24.6 46.6 %all_gather.27 = bf16[384,768]{0,1:T(8,128)(2,1)S(1)} all-gather(bf16[384,48]{0,1:T(8,128)(2,1)S(1)} %copy-done.15), channel_id=1, replica_groups=mesh['dp'=16,'tensor'=2] {'dp'}, dimensions={1}, use_global_device_ids=true | all-gather | bytes 626688 | tf_op jit(solution)/shard_map/all_gather | solution.py:97
  71.7 2.9 all-gather.4.cloned.1.call-done
  74.6 3.2 fusion.6
  77.7 1.6 copy.59
  79.6 0.9 copy-done.1
  81.8 1.5 multiply_reduce_fusion
  85.2 0.9 copy-done.35
  86.1 1.5 fusion.10
  87.6 51.7 %all-gather.6.cloned.1.call-done = bf16[768,1536]{1,0:T(8,128)(2,1)} async-done(((bf16[48,1536]{1,0:T(8,128)(2,1)}), bf16[768,1536]{1,0:T(8,128)(2,1)}) %all-gather.6.cloned.1.call-update) | async-done | bytes 2359312 | tf_op jit(solution)/shard_map/all_gather | solution.py:98
  139.2 3.8 convolution_add_fusion
  143.0 60.2 %all-gather.8.cloned.1.call-done = bf16[1536,768]{0,1:T(8,128)(2,1)} async-done(((bf16[1536,48]{0,1:T(8,128)(2,1)}), bf16[1536,768]{0,1:T(8,128)(2,1)}) %all-gather.8.cloned.1.call-update) | async-done | bytes 2359312 | tf_op jit(solution)/shard_map/all_gather | solution.py:99
  203.2 7.8 %convert_reduce_fusion = (f32[1536]{0:T(1024)}, bf16[256,1536]{1,0:T(8,128)(2,1)S(1)}, f32[256,1536]{1,0:T(8,128)}) fusion(f32[256,1536]{1,0:T(8,128)} %convolution_add_fusion, bf16[256,768]{1,0:T(8,128)(2,1)S(1)} %all_gather.31, bf16[1536,768]{0,1:T(8,128)(2,1)} %all-gather.8.cloned.1.call-done), kind=kOutput, calls=%fused_computation.5 | convolution fusion | flops 633076224 | bytes 6690816 | tf_op jit(solution)/shard_map/dot_general | solution.py:170
  211.0 0.8 fusion.11
  212.3 0.9 pad_maximum_fusion.2
  213.3 1.5 convolution_convert_fusion.1
  215.6 1.4 copy-done.33
  217.0 0.8 fusion.72
  217.8 1.2 fusion.9
  219.5 0.8 fusion.76
  220.4 2.9 pad_maximum_fusion.1
  223.3 6.6 %copy.74 = f32[1920,768]{0,1:T(8,128)} copy(f32[1920,768]{1,0:T(8,128)} %pad_maximum_fusion.1) | data formatting | bytes 11796480
  229.9 0.9 copy-done.4
  230.8 0.7 fusion.73
  232.1 0.8 fusion.74
  232.9 3.7 pad_maximum_fusion
  237.3 75.7 %all-reduce.9 = (f32[3,384]{1,0:T(4,128)}, f32[1536]{0:T(1024)}) all-reduce(f32[3,384]{1,0:T(4,128)S(1)} %reduce_sum.242, f32[1536]{0:T(1024)S(1)} %copy-done.21), channel_id=1, replica_groups=mesh['dp'=16,'tensor'=2] {'dp'}, use_global_device_ids=true, to_apply=%region_27.28 | all-reduce | flops 2688 | bytes 21504 | tf_op jit(solution)/shard_map/psum | solution.py:236
  313.1 1.1 convert_element_type.123
  314.7 38.5 %all-reduce.8 = (f32[768]{0:T(1024)}, f32[768]{0:T(1024)}, f32[768]{0:T(1024)}, f32[768]{0:T(1024)}, f32[768]{0:T(1024)S(1)}) all-reduce(f32[768]{0:T(1024)S(1)} %get-tuple-element.134, f32[768]{0:T(1024)S(1)} %get-tuple-element.140, f32[768]{0:T(1024)S(1)} %get-tuple-element.133, ...), channel_id=1, replica_groups=mesh['dp'=16,'tensor'=2] {'dp','tensor'}, use_global_device_ids=true, to_apply=%region_18.19 | all-reduce | flops 3840 | bytes 30720 | tf_op jit(solution)/shard_map/psum | solution.py:237
  353.6 2.0 fusion.30
  355.5 27.4 %reduce-scatter.13.cloned.1.call-done = f32[48,1920]{1,0:T(8,128)} async-done(((f32[768,1920]{1,0:T(8,128)}), f32[48,1920]{1,0:T(8,128)}) %reduce-scatter.13.cloned.1.call-update) | async-done | bytes 368656
  382.9 1.5 slice.97
  384.5 1.7 slice.99
  386.2 163.5 %reduce-scatter.11.cloned.1.call-done = f32[48,2688]{1,0:T(8,128)} async-done(((f32[768,2688]{1,0:T(8,128)}), f32[48,2688]{1,0:T(8,128)}) %reduce-scatter.11.cloned.1.call-update) | async-done | bytes 516112 | tf_op jit(solution)/shard_map/reduce_scatter | solution.py:232
  549.6 1.0 slice.96
  550.8 0.7 copy.66
  551.5 0.7 slice.98
  (134 shorter events, 10.5 us)
Async XLA Ops:
  7.2 12.9 %copy-start = (bf16[128,768]{1,0:T(8,128)(2,1)S(1)}, bf16[128,768]{1,0:T(8,128)(2,1)}, u32[]{:S(2)}) copy-start(bf16[128,768]{1,0:T(8,128)(2,1)} %param.15) | copy-start | bytes 589828
  7.2 12.9 %copy-start.13 = (f32[768]{0:T(1024)S(1)}, f32[768]{0:T(1024)}, u32[]{:S(2)}) copy-start(f32[768]{0:T(1024)} %param.20) | copy-start | bytes 9220
  7.2 12.9 %copy-start.12 = (f32[768]{0:T(1024)S(1)}, f32[768]{0:T(1024)}, u32[]{:S(2)}) copy-start(f32[768]{0:T(1024)} %param.18) | copy-start | bytes 9220
  7.2 12.8 %copy-start.25 = (f32[768]{0:T(1024)S(1)}, f32[768]{0:T(1024)}, u32[]{:S(2)}) copy-start(f32[768]{0:T(1024)} %param.21) | copy-start | bytes 9220
  7.2 12.8 %copy-start.24 = (f32[768]{0:T(1024)S(1)}, f32[768]{0:T(1024)}, u32[]{:S(2)}) copy-start(f32[768]{0:T(1024)} %param.19) | copy-start | bytes 9220
  7.2 67.3 %all-gather.4.cloned.1.call-start = ((), (), s32[]{:S(2)}) async-start(), calls=%async_computation.4 | async-start | bytes 1880064 | tf_op jit(solution)/shard_map/all_gather | solution.py:96
  8.0 131.3 %all-gather.6.cloned.1.call-start = ((), (), s32[]{:S(2)}) async-start(), calls=%async_computation.5 | async-start | bytes 2506752 | tf_op jit(solution)/shard_map/all_gather | solution.py:98
  8.7 194.5 %all-gather.8.cloned.1.call-start = ((), (), s32[]{:S(2)}) async-start(), calls=%async_computation.6 | async-start | bytes 2506752 | tf_op jit(solution)/shard_map/all_gather | solution.py:99
  9.5 303.6 %reduce-scatter.9.cloned.1.call-start = ((), (), s32[]{:S(2)}) async-start(), calls=%async_computation.8 | async-start | bytes 1179648 | tf_op jit(solution)/shard_map/reduce_scatter | solution.py:220
  12.7 11.9 %copy-start.15 = (bf16[384,48]{0,1:T(8,128)(2,1)S(1)}, bf16[384,48]{0,1:T(8,128)(2,1)}, u32[]{:S(2)}) copy-start(bf16[384,48]{0,1:T(8,128)(2,1)} %param.24) | copy-start | bytes 110596
  12.7 58.5 %copy-start.19 = (f32[128]{0:T(128)}, f32[128]{0:T(128)S(1)}, u32[]{:S(2)}) copy-start(f32[128]{0:T(128)S(1)} %broadcast_multiply_fusion.1) | copy-start | bytes 1540
  13.8 0.5 copy-start.31
  14.3 56.8 %copy-start.22 = (f32[128]{0:T(128)}, f32[128]{0:T(128)S(1)}, u32[]{:S(2)}) copy-start(f32[128]{0:T(128)S(1)} %fusion.65) | copy-start | bytes 1540
  16.1 55.0 %copy-start.29 = (f32[128]{0:T(128)}, f32[128]{0:T(128)S(1)}, u32[]{:S(2)}) copy-start(f32[128]{0:T(128)S(1)} %dynamic-slice_convert_fusion) | copy-start | bytes 1540
  20.3 54.3 %copy-start.37 = (f32[3,384]{1,0:T(4,128)S(1)}, f32[3,384]{1,0:T(4,128)}, u32[]{:S(2)}) copy-start(f32[3,384]{1,0:T(4,128)} %param.23) | copy-start | bytes 13828
  22.4 52.2 %copy-start.3 = (bf16[256,768]{1,0:T(8,128)(2,1)}, bf16[256,768]{1,0:T(8,128)(2,1)S(1)}, u32[]{:S(2)}) copy-start(bf16[256,768]{1,0:T(8,128)(2,1)S(1)} %all_gather.25) | copy-start | bytes 1179652
  79.4 1.1 copy-start.1
  81.0 2.3 copy-start.16
  81.2 0.6 copy-start.17
  84.6 1.5 copy-start.35
  85.2 54.1 %copy-start.36 = (f32[1536]{0:T(1024)S(1)}, f32[1536]{0:T(1024)}, u32[]{:S(2)}) copy-start(f32[1536]{0:T(1024)} %param.27) | copy-start | bytes 18436
  203.2 7.8 %copy-start.34 = (bf16[768,1536]{1,0:T(8,128)(2,1)S(1)}, bf16[768,1536]{1,0:T(8,128)(2,1)}, u32[]{:S(2)}) copy-start(bf16[768,1536]{1,0:T(8,128)(2,1)} %all-gather.6.cloned.1.call-done) | copy-start | bytes 7077892
  211.0 0.9 copy-start.7
  211.0 1.3 copy-start.11
  213.2 140.3 %reduce-scatter.7.cloned.1.call-start = ((), (), s32[]{:S(2)}) async-start(), calls=%async_computation.7 | async-start | bytes 589824 | tf_op jit(solution)/shard_map/reduce_scatter | solution.py:151
  213.3 1.6 copy-start.5
  213.3 2.0 copy-start.6
  215.3 1.7 copy-start.33
  219.0 164.0 %reduce-scatter.13.cloned.1.call-start = ((), (), s32[]{:S(2)}) async-start(), calls=%async_computation.10 | async-start | bytes 6266880
  229.8 1.0 copy-start.4
  229.9 319.8 %reduce-scatter.11.cloned.1.call-start = ((), (), s32[]{:S(2)}) async-start(), calls=%async_computation.9 | async-start | bytes 8773632 | tf_op jit(solution)/shard_map/reduce_scatter | solution.py:232
  230.8 1.0 copy-start.2
  230.8 1.3 copy-start.8
  236.6 0.7 copy-start.21
  236.7 77.6 %copy-start.14 = (f32[768]{0:T(1024)S(1)}, f32[768]{0:T(1024)}, u32[]{:S(2)}) copy-start(f32[768]{0:T(1024)} %param.20) | copy-start | bytes 9220
  236.7 77.6 %copy-start.20 = (f32[128]{0:T(128)S(1)}, f32[128]{0:T(128)}, u32[]{:S(2)}) copy-start(f32[128]{0:T(128)} %copy-done.19) | copy-start | bytes 1540
  236.7 77.6 %copy-start.23 = (f32[128]{0:T(128)S(1)}, f32[128]{0:T(128)}, u32[]{:S(2)}) copy-start(f32[128]{0:T(128)} %copy-done.22) | copy-start | bytes 1540
  236.7 78.0 %copy-start.18 = (f32[768]{0:T(1024)S(1)}, f32[768]{0:T(1024)}, u32[]{:S(2)}) copy-start(f32[768]{0:T(1024)} %get-tuple-element.157) | copy-start | bytes 9220
  236.7 116.5 %copy-start.32 = (f32[128]{0:T(128)S(1)}, f32[128]{0:T(128)}, u32[]{:S(2)}) copy-start(f32[128]{0:T(128)} %copy-done.31) | copy-start | bytes 1540
  313.0 40.5 %copy-start.9 = (bf16[128,768]{1,0:T(8,128)(2,1)S(1)}, bf16[128,768]{1,0:T(8,128)(2,1)}, u32[]{:S(2)}) copy-start(bf16[128,768]{1,0:T(8,128)(2,1)} %param.16) | copy-start | bytes 589828
  313.0 40.5 %copy-start.26 = (f32[768]{0:T(1024)S(1)}, f32[768]{0:T(1024)}, u32[]{:S(2)}) copy-start(f32[768]{0:T(1024)} %param.29) | copy-start | bytes 9220
  313.0 40.5 %copy-start.27 = (f32[768]{0:T(1024)S(1)}, f32[768]{0:T(1024)}, u32[]{:S(2)}) copy-start(f32[768]{0:T(1024)} %param.25) | copy-start | bytes 9220
  313.0 40.5 %copy-start.30 = (f32[128]{0:T(128)S(1)}, f32[128]{0:T(128)}, u32[]{:S(2)}) copy-start(f32[128]{0:T(128)} %copy-done.29) | copy-start | bytes 1540
  353.2 199.0 %copy-start.28 = (f32[768]{0:T(1024)}, f32[768]{0:T(1024)S(1)}, u32[]{:S(2)}) copy-start(f32[768]{0:T(1024)S(1)} %get-tuple-element.218) | copy-start | bytes 9220
  549.6 1.8 copy-start.10
Sparse Core Ops, SparseCore 0:
  10.8 63.7 all-gather.3
  77.3 61.8 all-gather.5
  142.0 61.0 all-gather.7
  213.4 7.0 reduce-scatter.8
  223.2 8.9 reduce-scatter.6
  237.4 145.5 reduce-scatter.12
  388.6 161.0 reduce-scatter.10
where the time goes:
time: 561 us; the launch traced here: 560 us
  waiting for transfers between devices  308 us (55%)
  blocking collectives  167 us (30%)
  matrix products  26.5 us (5%)
  local copies, waits for them, and re-layouts  22.8 us (4%)
  other arithmetic  20.1 us (4%)
  between operations  14.7 us (3%)
    reduce_scatter x1, waiting for transfers between devices, per_device(): lax.psum_scatter(row_joined, 'dp', scatter_dimension=0, tiled=True)  163 us
    psum x1, blocking collectives, per_device(): summed_qkv, summed_up = lax.psum((grad_b_qkv, grad_b_up), 'dp')  75.7 us
    all_gather x1, waiting for transfers between devices, per_device(): lax.all_gather(w_down, 'dp', axis=1, tiled=True)  60.2 us
    all_gather x1, waiting for transfers between devices, per_device(): lax.all_gather(w_up, 'dp', axis=0, tiled=True)  51.7 us
    all_gather x1, blocking collectives, per_device(): lax.all_gather(w_out, 'dp', axis=1, tiled=True)  46.6 us
    psum x1, blocking collectives, per_device(): lax.psum((grad_bias_out, norm_grads[1], norm_grads[2], norm_grads[3], nor...  38.5 us
    unnamed x8, waiting for transfers between devices  29.5 us
    unnamed x79, local copies, waits for them, and re-layouts  15.2 us
  transfers between devices with their start and end apart: 7, of which 5 were waited for; matrix products, arithmetic and copies ran while one was open for 9% of the time, Pallas kernels for 0%

commit v1 on v0

v1 whole, which is shorter than its diff:
```python
import math
from functools import partial

import jax
import jax.numpy as jnp
from jax import lax
from jax.experimental import pallas as pl
from jax.experimental.pallas import tpu as pltpu
from jax.sharding import PartitionSpec as P

HD = 64
ROT = 16
PLANE = 4
BLK = 2 * HD
NOTES = 16
eps = 1e-05
F32 = jnp.float32
BF16 = jnp.bfloat16


def dot(a, b):
    return jnp.dot(a, b, preferred_element_type=F32)


def dot_nt(a, b):
    return lax.dot_general(a, b, (((1,), (1,)), ((), ())), preferred_element_type=F32)


def dot_tn(a, b):
    return lax.dot_general(a, b, (((0,), (0,)), ((), ())), preferred_element_type=F32)


def xor_sorted(parts, index):
    parts = list(parts)
    bit = 1
    while bit < len(parts):
        swap = (index & bit) != 0
        parts = [jnp.where(swap, parts[j ^ bit], parts[j]) for j in range(len(parts))]
        bit *= 2
    return parts


def tree_sum(parts):
    parts = list(parts)
    while len(parts) > 1:
        parts = [parts[j] + parts[j + 1] for j in range(0, len(parts), 2)]
    return parts[0]


def rotary_tables(rows):
    half = ROT // 2
    inverse = 10000.0 ** (-jnp.arange(half, dtype=F32) * 2.0 / ROT)
    angle = jnp.arange(rows, dtype=F32)[:, None] * inverse[None, :]
    cos, sin = jnp.cos(angle), jnp.sin(angle)
    rest = jnp.ones((rows, HD - ROT), F32)
    none = jnp.zeros((rows, half), F32)
    keep = jnp.concatenate([cos, cos, rest], axis=1)
    low = jnp.concatenate([-sin, none, 0.0 * rest], axis=1)
    high = jnp.concatenate([none, sin, 0.0 * rest], axis=1)
    return tuple(jnp.concatenate([t] * (BLK // HD), axis=1) for t in (keep, low, high))


def rows_kernel(half_ref, length_ref, params_ref, own_ref, peer_ref, x1_ref, x2_ref, xh_ref, g_ref, bo_ref):
    half = half_ref[0]
    own_rows = own_ref.shape[1] // 2
    slots = 2 * own_rows
    params = params_ref[...]
    for k in range(PLANE):
        for which, ref in enumerate((own_ref, peer_ref)):
            part = half if which == 0 else 1 - half
            x = ref[k, :own_rows, :].astype(F32)
            centre = jnp.mean(x, axis=-1, keepdims=True)
            off = x - centre
            spread = jnp.mean(off * off, axis=-1, keepdims=True)
            xh = off * lax.rsqrt(spread + eps)
            at = pl.ds(pl.multiple_of(k * slots + part * own_rows, own_rows), own_rows)
            x1_ref[at, :] = (xh * params[0:1] + params[1:2]).astype(BF16)
            x2_ref[at, :] = (xh * params[2:3] + params[3:4]).astype(BF16)
            xh_ref[at, :] = xh.astype(BF16)
            row = lax.broadcasted_iota(jnp.int32, (own_rows, 1), 0) + part * own_rows
            g = jnp.where(row < length_ref[k], ref[k, own_rows:, :].astype(F32), 0.0)
            g_ref[at, :] = g.astype(BF16)
            if k == 0 and which == 0:
                bo_ref[...] = jnp.sum(g, axis=0, keepdims=True)


def attention_kernel(
    length_ref, x1_ref, g_ref, wa_ref, bias_ref, keep_ref, low_ref, high_ref, att_ref, gp_ref, gw_ref, gb_ref
):
    slots = keep_ref.shape[0]
    keep, low, high = keep_ref[...], low_ref[...], high_ref[...]

    def turn(x, sign):
        return x * keep + sign * (
            pltpu.roll(x, BLK - ROT // 2, 1) * low + pltpu.roll(x, ROT // 2, 1) * high
        )

    lane = lax.broadcasted_iota(jnp.int32, (slots, BLK), 1)
    first = lane < HD
    q_row = lax.broadcasted_iota(jnp.int32, (2 * slots, slots), 0) & (slots - 1)
    k_row = lax.broadcasted_iota(jnp.int32, (2 * slots, slots), 1)

    def stacked(x):
        zero = jnp.zeros_like(x)
        return jnp.concatenate([jnp.where(first, x, zero), jnp.where(first, zero, x)], axis=0)

    def joined(x):
        return jnp.where(first, x[:slots], x[slots:])

    total = jnp.zeros((1, 3 * BLK), F32)
    for k in range(PLANE):
        at = pl.ds(k * slots, slots)
        proj = dot(x1_ref[at, :], wa_ref[:, : 3 * BLK]) + bias_ref[...]
        query = stacked((turn(proj[:, :BLK], 1.0) * HD**-0.5).astype(BF16))
        key = turn(proj[:, BLK : 2 * BLK], 1.0).astype(BF16)
        value = proj[:, 2 * BLK :].astype(BF16)
        ga = stacked(dot(g_ref[at, :], wa_ref[:, 3 * BLK :]).astype(BF16))
        logits = dot_nt(query, key)
        allowed = (k_row <= q_row) & ((k_row < length_ref[k]) | (k_row == q_row))
        logits = jnp.where(allowed, logits, -1000000000.0)
        weights = jnp.exp(logits - jnp.max(logits, axis=-1, keepdims=True))
        probs = weights / jnp.sum(weights, axis=-1, keepdims=True)
        rounded = probs.astype(BF16)
        att_ref[at, :] = joined(dot(rounded, value)).astype(BF16)
        grad_probs = dot_nt(ga, value)
        inner = jnp.sum(probs * grad_probs, axis=-1, keepdims=True)
        grad_logits = (probs * (grad_probs - inner)).astype(BF16)
        grad_query = joined(dot(grad_logits, key)) * HD**-0.5
        grad_key = dot_tn(grad_logits, query)
        grad_value = dot_tn(rounded, ga)
        gp = jnp.concatenate([turn(grad_query, -1.0), turn(grad_key, -1.0), grad_value], axis=1).astype(BF16)
        gp_ref[at, :] = gp
        total = total + jnp.sum(gp.astype(F32), axis=0, keepdims=True)
    gb_ref[...] = total
    gw_ref[:, : 3 * BLK] = dot_tn(x1_ref[...], gp_ref[...]).astype(BF16)
    gw_ref[:, 3 * BLK :] = dot_tn(g_ref[...], att_ref[...]).astype(BF16)


def feed_kernel(
    half_ref, params_ref, x2_ref, xh_ref, g_ref, wf_ref, wa_ref, att_ref, gp_ref, bias_ref, gb_ref, bo_ref,
    keep_ref, send_ref, gw_ref, notes_ref, act_ref, gh_ref, stage_ref
):
    half = half_ref[0]
    own_rows = keep_ref.shape[2]
    slots = 2 * own_rows
    width = bias_ref.shape[1]
    params = params_ref[...]
    gain1, gain2 = params[0:1], params[2:3]
    sums = [jnp.zeros((1, x2_ref.shape[1]), F32) for _ in range(4)]
    gb_up = jnp.zeros((1, width), F32)
    for k in range(PLANE):
        at = pl.ds(k * slots, slots)
        hidden = dot(x2_ref[at, :], wf_ref[:, :width]) + bias_ref[...]
        grad_act = dot(g_ref[at, :], wf_ref[:, width:])
        part = 0.5 + 0.5 * lax.erf(hidden * (0.5**0.5))
        act = (hidden * part).astype(BF16)
        slope = part + hidden * jnp.exp(-0.5 * hidden * hidden) * (2.0 * math.pi) ** -0.5
        gh = (grad_act * slope).astype(BF16)
        act_ref[at, :] = act
        gh_ref[at, :] = gh
        gb_up = gb_up + jnp.sum(gh.astype(F32), axis=0, keepdims=True)
        stage_ref[0] = dot_nt(act, wf_ref[:, width:]) + dot_nt(att_ref[at, :], wa_ref[:, 3 * BLK :])
        g1 = dot_nt(gp_ref[at, :], wa_ref[:, : 3 * BLK])
        g2 = dot_nt(gh, wf_ref[:, :width])
        stage_ref[1] = gain1 * g1 + gain2 * g2
        xh = xh_ref[at, :].astype(F32)
        for j, term in enumerate((g1 * xh, g1, g2 * xh, g2)):
            sums[j] = sums[j] + jnp.sum(term, axis=0, keepdims=True)
        mine = pl.ds(pl.multiple_of(half * own_rows, own_rows), own_rows)
        other = pl.ds(pl.multiple_of((1 - half) * own_rows, own_rows), own_rows)
        for j in range(2):
            keep_ref[j, k] = stage_ref[j, mine, :].astype(BF16)
            send_ref[j, k] = stage_ref[j, other, :].astype(BF16)
    gw_ref[:, :width] = dot_tn(x2_ref[...], gh_ref[...]).astype(BF16)
    gw_ref[:, width:] = dot_tn(g_ref[...], act_ref[...]).astype(BF16)
    notes_ref[...] = jnp.zeros_like(notes_ref)
    notes_ref[0:1, :width] = gb_up
    notes_ref[0:1, width:] = gb_ref[...]
    notes_ref[1:2, :] = bo_ref[...]
    for j in range(4):
        notes_ref[2 + j : 3 + j, :] = sums[j]


def kernel_call(body, out_shapes, in_smem, operands, scratch=(), flops=0):
    vmem = pl.BlockSpec(memory_space=pltpu.VMEM)
    smem = pl.BlockSpec(memory_space=pltpu.SMEM)
    bytes_accessed = sum(
        math.prod(a.shape) * a.dtype.itemsize for a in list(operands) + list(out_shapes)
    )
    return pl.pallas_call(
        body,
        out_shape=out_shapes,
        in_specs=[smem] * in_smem + [vmem] * (len(operands) - in_smem),
        out_specs=[vmem] * len(out_shapes),
        scratch_shapes=list(scratch),
        compiler_params=pltpu.CompilerParams(vmem_limit_bytes=48 * 2**20),
        cost_estimate=pl.CostEstimate(flops=flops, bytes_accessed=bytes_accessed, transcendentals=0),
    )(*operands)


def per_device(
    residual,
    cotangent,
    seq_lengths,
    gain_attn,
    shift_attn,
    gain_mlp,
    shift_mlp,
    w_qkv,
    b_qkv,
    w_out,
    b_out,
    w_up,
    b_up,
    w_down,
    b_down,
):
    places = lax.axis_size("dp")
    levels = places // PLANE
    index = lax.axis_index("dp")
    half = lax.axis_index("tensor")
    plane_at = index % PLANE
    level_at = index // PLANE
    own_rows, model = residual.shape
    slots = 2 * own_rows
    owned = w_up.shape[0]
    width = w_up.shape[1] // PLANE
    head_blocks = w_out.shape[0] // BLK
    direct = levels <= 4
    level_groups = [[lev * PLANE + j for lev in range(levels)] for j in range(PLANE)]

    def to_plane(x, k):
        return lax.ppermute(x, "dp", [(j, j ^ k) for j in range(places)])

    def to_level(x, m):
        return lax.ppermute(x, "dp", [(j, j ^ (m * PLANE)) for j in range(places)])

    def to_peer(x):
        return lax.ppermute(x, "tensor", [(0, 1), (1, 0)])

    def gather_levels(x):
        if direct:
            return xor_sorted([x] + [to_level(x, m) for m in range(1, levels)], level_at)
        every = lax.all_gather(x, "dp", axis=0, axis_index_groups=level_groups)
        return [every[j] for j in range(levels)]

    def scatter_levels(x, notes):
        chunk = model // levels
        if direct:
            def message(m):
                rows = lax.dynamic_slice_in_dim(x, (level_at ^ m) * chunk, chunk, 0)
                return rows if notes is None else jnp.concatenate([rows, notes], axis=0)

            parts = [message(0)] + [to_level(message(m), m) for m in range(1, levels)]
            total = tree_sum([part.astype(F32) for part in parts])
            return total[:chunk], total[chunk:]
        rows = lax.psum_scatter(x, "dp", scatter_dimension=0, tiled=True, axis_index_groups=level_groups)
        if notes is not None:
            every = lax.all_gather(notes, "dp", axis=0, axis_index_groups=level_groups)
            notes = jnp.sum(every.astype(F32), axis=0)
        return rows.astype(F32), notes

    def share(place):
        at = jnp.minimum(place, head_blocks - 1) * BLK
        qkv = lax.dynamic_slice_in_dim(w_qkv, at, BLK, 2)
        out = lax.dynamic_slice_in_dim(w_out, at, BLK, 0).T
        heads = jnp.concatenate([qkv[0], qkv[1], qkv[2], out], axis=1)
        heads = jnp.where(place < head_blocks, heads, jnp.zeros_like(heads))
        up = lax.dynamic_slice_in_dim(w_up, place * width, width, 1)
        down = lax.dynamic_slice_in_dim(w_down, place * width, width, 0).T
        return jnp.concatenate([heads, up, down], axis=1)

    shares = [share(plane_at)] + [to_plane(share(plane_at ^ k), k) for k in range(1, PLANE)]
    shares = jnp.concatenate(xor_sorted(shares, plane_at), axis=0)

    length = jnp.sum(seq_lengths[0])
    lengths_rows = jnp.full((NOTES, model), length.astype(BF16))
    message = jnp.concatenate([residual, cotangent, lengths_rows], axis=0)
    messages = [message] + [to_plane(message, k) for k in range(1, PLANE)]
    lengths = jnp.stack([part[slots, 0] for part in messages]).astype(jnp.int32)
    own = jnp.stack([part[:slots] for part in messages])
    peer = to_peer(own)

    wa = jnp.concatenate(gather_levels(shares[:, : 4 * BLK]), axis=0)
    wf = jnp.concatenate(gather_levels(shares[:, 4 * BLK :]), axis=0)

    half_s = half.astype(jnp.int32).reshape(1)
    params = jnp.stack([gain_attn, shift_attn, gain_mlp, shift_mlp] + [jnp.zeros_like(gain_attn)] * 4)
    rows_all = PLANE * slots
    shape = jax.ShapeDtypeStruct
    x1, x2, xh, g, bo = kernel_call(
        rows_kernel,
        [shape((rows_all, model), BF16)] * 4 + [shape((1, model), F32)],
        2,
        (half_s, lengths, params, own, peer),
        flops=rows_all * model * 20,
    )

    block_at = jnp.minimum(plane_at, head_blocks - 1) * BLK
    bias_heads = lax.dynamic_slice_in_dim(b_qkv, block_at, BLK, 1).reshape(1, 3 * BLK)
    att, gp, gw_heads, gb = kernel_call(
        attention_kernel,
        [
            shape((rows_all, BLK), BF16),
            shape((rows_all, 3 * BLK), BF16),
            shape((model, 4 * BLK), BF16),
            shape((1, 3 * BLK), F32),
        ],
        1,
        (lengths, x1, g, wa, bias_heads) + rotary_tables(slots),
        flops=4 * rows_all * model * 4 * BLK + 12 * rows_all * 2 * slots * BLK,
    )
    grad_heads, _ = scatter_levels(gw_heads, None)

    bias_up = lax.dynamic_slice_in_dim(b_up, plane_at * width, width, 0).reshape(1, width)
    keep, send, gw_feed, notes = kernel_call(
        feed_kernel,
        [
            shape((2, PLANE, own_rows, model), BF16),
            shape((2, PLANE, own_rows, model), BF16),
            shape((model, 2 * width), BF16),
            shape((NOTES, model), F32),
        ],
        1,
        (half_s, params, x2, xh, g, wf, wa, att, gp, bias_up, gb, bo),
        scratch=[
            pltpu.VMEM((rows_all, width), BF16),
            pltpu.VMEM((rows_all, width), BF16),
            pltpu.VMEM((2, slots, model), F32),
        ],
        flops=12 * rows_all * model * width,
    )
    grad_feed, notes = scatter_levels(gw_feed, notes.astype(BF16))

    summed = (keep.astype(F32) + to_peer(send).astype(F32)).astype(BF16)
    parts = [summed[:, 0]] + [to_plane(summed[:, k], k) for k in range(1, PLANE)]
    branch, grad_norm = tree_sum([part.astype(F32) for part in parts])
    residual_f = residual.astype(F32)
    result = (residual_f + (branch + b_out + b_down)).astype(BF16)
    centre = jnp.mean(residual_f, axis=-1, keepdims=True)
    off = residual_f - centre
    scale = lax.rsqrt(jnp.mean(off * off, axis=-1, keepdims=True) + eps)
    xh_own = off * scale
    row = half * own_rows + jnp.arange(own_rows, dtype=jnp.int32)
    grad_out = jnp.where((row < length)[:, None], cotangent.astype(F32), 0.0)
    grad_residual = grad_out + scale * (
        grad_norm
        - jnp.mean(grad_norm, axis=-1, keepdims=True)
        - xh_own * jnp.mean(grad_norm * xh_own, axis=-1, keepdims=True)
    )

    grad_heads = grad_heads.astype(BF16).reshape(PLANE, owned, 4 * BLK)
    grad_feed = grad_feed.astype(BF16).reshape(PLANE, owned, 2 * width)
    notes = notes.astype(BF16)

    def back(place):
        feed = lax.dynamic_index_in_dim(grad_feed, place, 0, keepdims=False)
        heads = lax.dynamic_index_in_dim(grad_heads, place, 0, keepdims=False)
        return jnp.concatenate([feed, notes], axis=0), heads

    feeds, heads = [], []
    for k in range(PLANE):
        feed, head = back(plane_at ^ k)
        feeds.append(feed if k == 0 else to_plane(feed, k))
        heads.append(head if k == 0 else to_plane(head, k))
    common = tree_sum([part[owned + 1 : owned + 6].astype(F32) for part in feeds])
    common = common + to_peer(common)
    feeds = [part.astype(F32) for part in xor_sorted(feeds, plane_at)]
    heads = [part.astype(F32) for part in xor_sorted(heads, plane_at)][:head_blocks]
    grad_up = jnp.concatenate([part[:owned, :width] for part in feeds], axis=1)
    grad_down = jnp.concatenate([part[:owned, width:] for part in feeds], axis=1).T
    grad_qkv = jnp.stack(
        [jnp.concatenate([part[:, c * BLK : (c + 1) * BLK] for part in heads], axis=1) for c in range(3)]
    )
    grad_out_w = jnp.concatenate([part[:, 3 * BLK :] for part in heads], axis=1).T
    grad_b_up = jnp.concatenate([part[owned, :width] for part in feeds])
    grad_b_qkv = jnp.concatenate(
        [part[owned, width:].reshape(3, BLK) for part in feeds[:head_blocks]], axis=1
    )
    return (
        result,
        grad_residual,
        common[1],
        common[2],
        common[3],
        common[4],
        grad_qkv,
        grad_b_qkv,
        grad_out_w,
        common[0],
        grad_up,
        grad_b_up,
        grad_down,
        common[0],
    )


def solution(mesh):
    return jax.shard_map(
        per_device,
        mesh=mesh,
        in_specs=(
            P(("dp", "tensor"), None),
            P(("dp", "tensor"), None),
            P("dp", None),
            P(),
            P(),
            P(),
            P(),
            P(None, "dp", "tensor"),
            P(None, "tensor"),
            P("tensor", "dp"),
            P(),
            P("dp", "tensor"),
            P("tensor"),
            P("tensor", "dp"),
            P(),
        ),
        out_specs=(
            P(("dp", "tensor"), None),
            P(("dp", "tensor"), None),
            P(),
            P(),
            P(),
            P(),
            P(None, "dp", "tensor"),
            P(None, "tensor"),
            P("tensor", "dp"),
            P(),
            P("dp", "tensor"),
            P("tensor"),
            P("tensor", "dp"),
            P(),
        ),
        check_vma=False,
    )
```

time: 561 us -> 180 us (0.32)
  waiting for transfers between devices: 308 us -> 59.5 us
  blocking collectives: 167 us -> 0 us
  starting transfers between devices: 0.46 us -> 58 us
  matrix products: 26.5 us -> 0 us
  Pallas kernels: 0 us -> 22.5 us
  between operations: 14.7 us -> 2.01 us
  local copies, waits for them, and re-layouts: 22.8 us -> 16.6 us
    reduce_scatter x3 -> x0, waiting for transfers between devices: 164 us -> none  [the longest x1 163 us: per_device(): lax.psum_scatter(row_joined, 'dp', scatter_dimension=0, tiled=True)]
    all_gather x3 -> x0, waiting for transfers between devices: 115 us -> none  [the longest x1 60.2 us: per_device(): lax.all_gather(w_down, 'dp', axis=1, tiled=True)]
    psum x2 -> x0, blocking collectives: 114 us -> none  [the longest x1 75.7 us: per_device(): summed_qkv, summed_up = lax.psum((grad_b_qkv, grad_b_up), 'dp')]
    ppermute x0 -> x30, waiting for transfers between devices: none -> 59.5 us  [the longest x12 35.8 us: to_level(): return lax.ppermute(x, 'dp', [(j, j ^ m * PLANE) for j in range(places)])]
    ppermute x0 -> x30, starting transfers between devices: none -> 58 us  [the longest x12 37.8 us: to_level(): return lax.ppermute(x, 'dp', [(j, j ^ m * PLANE) for j in range(places)])]
    all_gather x4 -> x0, blocking collectives: 53 us -> none  [the longest x1 46.6 us: per_device(): lax.all_gather(w_out, 'dp', axis=1, tiled=True)]
    unnamed x8 -> x0, waiting for transfers between devices: 29.5 us -> none
    dot_general x18 -> x0, matrix products: 26.5 us -> none  [the longest x1 7.82 us: per_device(): jnp.dot(grad_full, back_down.T, preferred_element_type=jnp.float32)]
  transfers between devices with their start and end apart: 7 -> 30, of which waited for: 5 -> 15; matrix products, arithmetic and copies ran while one was open for 9% -> 14% of each run, Pallas kernels for 0% -> 6%
where the time goes in v1:
time: 180 us; the launch traced here: 177 us
  waiting for transfers between devices  59.5 us (33%)
  starting transfers between devices  58 us (32%)
  Pallas kernels  22.5 us (12%)
  other arithmetic  18.1 us (10%)
  local copies, waits for them, and re-layouts  16.6 us (9%)
  between operations  2.01 us (1%)
    ppermute x12, starting transfers between devices, to_level(): return lax.ppermute(x, 'dp', [(j, j ^ m * PLANE) for j in range(places)])  37.8 us
    ppermute x12, waiting for transfers between devices, to_level(): return lax.ppermute(x, 'dp', [(j, j ^ m * PLANE) for j in range(places)])  35.8 us
    ppermute x15, waiting for transfers between devices, to_plane(): return lax.ppermute(x, 'dp', [(j, j ^ k) for j in range(places)])  23.7 us
    pallas_call x3, Pallas kernels, kernel_call(): pl.pallas_call(body, out_shape=out_shapes, in_specs=[smem] * in_smem + [v...  22.5 us
    ppermute x15, starting transfers between devices, to_plane(): return lax.ppermute(x, 'dp', [(j, j ^ k) for j in range(places)])  20.1 us
    unnamed x37, local copies, waits for them, and re-layouts  5.54 us
  transfers between devices with their start and end apart: 30, of which 15 were waited for; matrix products, arithmetic and copies ran while one was open for 14% of the time, Pallas kernels for 6%

profile of v1, /device:TPU:0, one launch (start us, length us, event | category | flops | bytes accessed | tf_op | source)
XLA Modules:
  0.0 176.8 jit_solution(18164555226889891096)
XLA Ops:
  0.7 1.4 reduce_sum.45
  2.7 1.2 maximum_maximum_fusion
  4.0 3.0 %collective-permute-start = (bf16[272,768]{1,0:T(8,128)(2,1)S(1)}, bf16[272,768]{1,0:T(8,128)(2,1)S(1)}, u32[]{:S(2)}, u32[]{:S(2)}) collective-permute-start(bf16[272,768]{1,0:T(8,128)(2,1)S(1)} %maximum_maximum_fusion), channel_id=1, source_target_pairs={{0,2},{2,0},{4,6},{6,4},{8,10},{10,8},{12,14},{14,12},{16,18},{18,... | collective-permute-start | bytes 1253384 | tf_op jit(solution)/shard_map/ppermute | solution.py:233
  7.0 1.5 collective-permute-start.1
  8.5 0.8 dynamic-slice_bitcast_fusion.7
  9.3 0.9 constant_dynamic-slice_fusion.8
  10.2 1.4 dynamic-slice_bitcast_fusion.23
  12.9 2.9 %collective-permute-start.4 = (bf16[48,1280]{1,0:T(8,128)(2,1)}, bf16[48,1280]{1,0:T(8,128)(2,1)S(1)}, u32[]{:S(2)}, u32[]{:S(2)}) collective-permute-start(bf16[48,1280]{1,0:T(8,128)(2,1)} %pad_maximum_fusion.15), channel_id=1, source_target_pairs={{0,6},{2,4},{4,2},{6,0},{8,14},{10,12},{12,10},{14,8},{16,22},{18,... | collective-permute-start | bytes 368648 | tf_op jit(solution)/shard_map/ppermute | solution.py:233
  21.1 0.8 dynamic_slice.121
  23.8 0.8 maximum_select_fusion.2
  25.3 0.8 stack.53.params_ref
  26.1 1.9 %collective-permute-done.2 = bf16[272,768]{1,0:T(8,128)(2,1)S(1)} collective-permute-done((bf16[272,768]{1,0:T(8,128)(2,1)S(1)}, bf16[272,768]{1,0:T(8,128)(2,1)S(1)}, u32[]{:S(2)}, u32[]{:S(2)}) %collective-permute-start.2) | collective-permute-done | bytes 417824 | tf_op jit(solution)/shard_map/ppermute | solution.py:233
  28.0 1.5 collective-permute-start.6
  30.5 1.9 %collective-permute-done.5 = bf16[48,1280]{1,0:T(8,128)(2,1)} collective-permute-done((bf16[48,1280]{1,0:T(8,128)(2,1)}, bf16[48,1280]{1,0:T(8,128)(2,1)}, u32[]{:S(2)}, u32[]{:S(2)}) %collective-permute-start.5) | collective-permute-done | bytes 122912 | tf_op jit(solution)/shard_map/ppermute | solution.py:233
  32.9 1.0 broadcast_select_fusion.23
  33.9 3.7 %collective-permute-start.10 = (bf16[192,512]{1,0:T(8,128)(2,1)S(1)}, bf16[192,512]{1,0:T(8,128)(2,1)S(1)}, u32[]{:S(2)}, u32[]{:S(2)}) collective-permute-start(bf16[192,512]{1,0:T(8,128)(2,1)S(1)} %pad_maximum_fusion.10), channel_id=1, source_target_pairs={{0,24},{2,26},{4,28},{6,30},{8,16},{10,18},{12,20},{14,22},{16,8},... | collective-permute-start | bytes 589832 | tf_op jit(solution)/shard_map/ppermute | solution.py:236
  37.6 0.8 collective-permute-start.12
  38.5 3.7 %collective-permute-start.7 = (bf16[192,768]{1,0:T(8,128)(2,1)S(1)}, bf16[192,768]{1,0:T(8,128)(2,1)S(1)}, u32[]{:S(2)}, u32[]{:S(2)}) collective-permute-start(bf16[192,768]{1,0:T(8,128)(2,1)S(1)} %slice.261), channel_id=1, source_target_pairs={{0,24},{2,26},{4,28},{6,30},{8,16},{10,18},{12,20},{14,22},{16,8},... | collective-permute-start | bytes 884744 | tf_op jit(solution)/shard_map/ppermute | solution.py:236
  42.1 1.6 collective-permute-done.10
  43.7 18.6 %collective-permute-start.8 = (bf16[192,768]{1,0:T(8,128)(2,1)S(1)}, bf16[192,768]{1,0:T(8,128)(2,1)S(1)}, u32[]{:S(2)}, u32[]{:S(2)}) collective-permute-start(bf16[192,768]{1,0:T(8,128)(2,1)S(1)} %slice.261), channel_id=1, source_target_pairs={{0,16},{2,18},{4,20},{6,22},{8,24},{10,26},{12,28},{14,30},{16,0},... | collective-permute-start | bytes 884744 | tf_op jit(solution)/shard_map/ppermute | solution.py:236
  62.3 1.6 collective-permute-done.11
  66.3 2.0 %maximum_convert_fusion.length_ref = s32[4]{0:T(128)S(1)} fusion(bf16[1]{0:T(256)(128)(2,1)} %bitcast.4, bf16[1]{0:T(256)(128)(2,1)} %bitcast.3, bf16[1]{0:T(256)(128)(2,1)} %bitcast.2, bf16[1]{0:T(256)(128)(2,1)} %bitcast.1), kind=kLoop, calls=%fused_computation.159 | loop fusion | flops 32 | bytes 24 | tf_op jit(solution)/shard_map/convert_element_type | solution.py:280
  68.3 10.4 %collective-permute-done.8 = bf16[192,768]{1,0:T(8,128)(2,1)S(1)} collective-permute-done((bf16[192,768]{1,0:T(8,128)(2,1)S(1)}, bf16[192,768]{1,0:T(8,128)(2,1)S(1)}, u32[]{:S(2)}, u32[]{:S(2)}) %collective-permute-start.8) | collective-permute-done | bytes 294944 | tf_op jit(solution)/shard_map/ppermute | solution.py:236
  78.9 1.2 copy-done.7
  80.1 4.9 %shard_map.254 = (bf16[1024,768]{1,0:T(8,128)(2,1)S(1)}, bf16[1024,768]{1,0:T(8,128)(2,1)S(1)}, bf16[1024,768]{1,0:T(8,128)(2,1)S(1)}, bf16[1024,768]{1,0:T(8,128)(2,1)}, f32[1,768]{1,0:T(1,128)S(1)}) custom-call(s32[1]{0:T(128)} %bitcast.half_ref, s32[4]{0:T(128)S(1)} %maximum_convert_fusion.length_ref, f32[8,768]{1,0:T(8,128)S(1)} %stack.53.params_ref, ...), custom_call_target="tpu_custom_call" | custom-call | flops 15728640 | bytes 9464852 | tf_op jit(solution)/shard_map/pallas_call | solution.py:190
  85.0 1.1 copy-done.1
  86.2 1.2 copy-done.2
  87.3 1.4 copy-done.3
  88.7 7.2 %shard_map.255 = (bf16[1024,128]{1,0:T(8,128)(2,1)S(1)}, bf16[1024,384]{1,0:T(8,128)(2,1)S(1)}, bf16[768,512]{1,0:T(8,128)(2,1)S(1)}, f32[1,384]{1,0:T(1,128)S(1)}) custom-call(s32[4]{0:T(128)S(1)} %maximum_convert_fusion.length_ref, bf16[1024,768]{1,0:T(8,128)(2,1)S(1)} %get-tuple-element.30.x1_ref, bf16[1024,768]{1,0:T(8,128)(2,1)S(1)} %copy-done.3, ...), custom_call_target="tpu_custom_call" | custom-call | flops 2415919104 | bytes 6163472 | tf_op jit(solution)/shard_map/pallas_call | solution.py:190
  96.1 3.0 %collective-permute-start.25 = (bf16[192,512]{1,0:T(8,128)(2,1)S(1)}, bf16[192,512]{1,0:T(8,128)(2,1)S(1)}, u32[]{:S(2)}, u32[]{:S(2)}) collective-permute-start(bf16[192,512]{1,0:T(8,128)(2,1)S(1)} %get-tuple-element.66), channel_id=1, source_target_pairs={{0,16},{2,18},{4,20},{6,22},{8,24},{10,26},{12,28},{14,30},{16,0},... | collective-permute-start | bytes 589832 | tf_op jit(solution)/shard_map/ppermute | solution.py:236
  99.1 1.3 collective-permute-start.26
  100.5 10.4 %shard_map.256 = (bf16[2,4,128,768]{3,2,1,0:T(8,128)(2,1)S(1)}, bf16[2,4,128,768]{3,2,1,0:T(8,128)(2,1)}, bf16[768,768]{1,0:T(8,128)(2,1)S(1)}, f32[16,768]{1,0:T(8,128)S(1)}) custom-call(s32[1]{0:T(128)} %bitcast.half_ref, f32[8,768]{1,0:T(8,128)S(1)} %stack.53.params_ref, bf16[1024,768]{1,0:T(8,128)(2,1)} %copy-done.1, bf16[1024,768]{1,0:T(8,128)(2,1)} %copy-done.2, ...), custom_call_target="tpu_custom_call" | custom-call | flops 3623878656 | bytes 12138500 | tf_op jit(solution)/shard_map/pallas_call | solution.py:190
  110.9 1.9 %collective-permute-done.25 = bf16[192,512]{1,0:T(8,128)(2,1)S(1)} collective-permute-done((bf16[192,512]{1,0:T(8,128)(2,1)S(1)}, bf16[192,512]{1,0:T(8,128)(2,1)S(1)}, u32[]{:S(2)}, u32[]{:S(2)}) %collective-permute-start.25) | collective-permute-done | bytes 196640 | tf_op jit(solution)/shard_map/ppermute | solution.py:236
  113.0 1.4 collective-permute-start.27
  114.9 1.6 collective-permute-start.29
  116.6 3.4 %collective-permute-start.17 = (bf16[208,768]{1,0:T(8,128)(2,1)S(1)}, bf16[208,768]{1,0:T(8,128)(2,1)S(1)}, u32[]{:S(2)}, u32[]{:S(2)}) collective-permute-start(bf16[208,768]{1,0:T(8,128)(2,1)S(1)} %get-tuple-element.136), channel_id=1, source_target_pairs={{0,8},{2,10},{4,12},{6,14},{8,0},{10,2},{12,4},{14,6},{16,24},{18,... | collective-permute-start | bytes 958472 | tf_op jit(solution)/shard_map/ppermute | solution.py:236
  120.1 2.4 %collective-permute-start.19 = (bf16[208,768]{1,0:T(8,128)(2,1)S(1)}, bf16[208,768]{1,0:T(8,128)(2,1)S(1)}, u32[]{:S(2)}, u32[]{:S(2)}) collective-permute-start(bf16[208,768]{1,0:T(8,128)(2,1)S(1)} %get-tuple-element.138), channel_id=1, source_target_pairs={{0,24},{2,26},{4,28},{6,30},{8,16},{10,18},{12,20},{14,22},{16,8},... | collective-permute-start | bytes 958472 | tf_op jit(solution)/shard_map/ppermute | solution.py:236
  123.3 8.5 %collective-permute-done.17 = bf16[208,768]{1,0:T(8,128)(2,1)S(1)} collective-permute-done((bf16[208,768]{1,0:T(8,128)(2,1)S(1)}, bf16[208,768]{1,0:T(8,128)(2,1)S(1)}, u32[]{:S(2)}, u32[]{:S(2)}) %collective-permute-start.17) | collective-permute-done | bytes 319520 | tf_op jit(solution)/shard_map/ppermute | solution.py:236
  131.9 11.8 %collective-permute-done.18 = bf16[208,768]{1,0:T(8,128)(2,1)S(1)} collective-permute-done((bf16[208,768]{1,0:T(8,128)(2,1)S(1)}, bf16[208,768]{1,0:T(8,128)(2,1)S(1)}, u32[]{:S(2)}, u32[]{:S(2)}) %collective-permute-start.18) | collective-permute-done | bytes 319520 | tf_op jit(solution)/shard_map/ppermute | solution.py:236
  144.2 1.7 collective-permute-start.21
  145.9 1.6 collective-permute-start.22
  148.8 2.6 %collective-permute-done.22 = bf16[64,768]{1,0:T(8,128)(2,1)S(1)} collective-permute-done((bf16[64,768]{1,0:T(8,128)(2,1)S(1)}, bf16[64,768]{1,0:T(8,128)(2,1)S(1)}, u32[]{:S(2)}, u32[]{:S(2)}) %collective-permute-start.22) | collective-permute-done | bytes 98336 | tf_op jit(solution)/shard_map/ppermute | solution.py:233
  153.7 1.4 collective-permute-start.14
  155.1 0.9 collective-permute-start.15
  155.9 1.3 collective-permute-start.16
  159.1 6.5 %collective-permute-done.14 = bf16[2,128,768]{2,1,0:T(8,128)(2,1)S(1)} collective-permute-done((bf16[2,128,768]{2,1,0:T(8,128)(2,1)S(1)}, bf16[2,128,768]{2,1,0:T(8,128)(2,1)S(1)}, u32[]{:S(2)}, u32[]{:S(2)}) %collective-permute-start.14) | collective-permute-done | bytes 393248 | tf_op jit(solution)/shard_map/ppermute | solution.py:233
  165.7 9.1 %collective-permute-done.15 = bf16[2,128,768]{2,1,0:T(8,128)(2,1)S(1)} collective-permute-done((bf16[2,128,768]{2,1,0:T(8,128)(2,1)S(1)}, bf16[2,128,768]{2,1,0:T(8,128)(2,1)S(1)}, u32[]{:S(2)}, u32[]{:S(2)}) %collective-permute-start.15) | collective-permute-done | bytes 393248 | tf_op jit(solution)/shard_map/ppermute | solution.py:233
  175.3 1.0 fusion.8
  (144 shorter events, 22.0 us)
Async XLA Ops:
  0.6 17.1 %copy-start = (f32[3,384]{1,0:T(4,128)S(1)}, f32[3,384]{1,0:T(4,128)}, u32[]{:S(2)}) copy-start(f32[3,384]{1,0:T(4,128)} %param.23) | copy-start | bytes 13828
  0.7 16.4 %copy-start.4 = (bf16[128,768]{1,0:T(8,128)(2,1)S(1)}, bf16[128,768]{1,0:T(8,128)(2,1)}, u32[]{:S(2)}) copy-start(bf16[128,768]{1,0:T(8,128)(2,1)} %param.15) | copy-start | bytes 589828
  0.7 16.3 %copy-start.6 = (bf16[128,768]{1,0:T(8,128)(2,1)S(1)}, bf16[128,768]{1,0:T(8,128)(2,1)}, u32[]{:S(2)}) copy-start(bf16[128,768]{1,0:T(8,128)(2,1)} %param.16) | copy-start | bytes 589828
  0.7 10.9 %copy-start.8 = (bf16[3,48,384]{2,1,0:T(8,128)(2,1)S(1)}, bf16[3,48,384]{2,1,0:T(8,128)(2,1)}, u32[]{:S(2)}) copy-start(bf16[3,48,384]{2,1,0:T(8,128)(2,1)} %param.22) | copy-start | bytes 331780
  3.9 13.9 %copy-start.12 = (f32[768]{0:T(1024)S(1)}, f32[768]{0:T(1024)}, u32[]{:S(2)}) copy-start(f32[768]{0:T(1024)} %param.18) | copy-start | bytes 9220
  3.9 14.4 %copy-start.13 = (f32[768]{0:T(1024)S(1)}, f32[768]{0:T(1024)}, u32[]{:S(2)}) copy-start(f32[768]{0:T(1024)} %param.19) | copy-start | bytes 9220
  3.9 15.0 %copy-start.14 = (f32[768]{0:T(1024)S(1)}, f32[768]{0:T(1024)}, u32[]{:S(2)}) copy-start(f32[768]{0:T(1024)} %param.20) | copy-start | bytes 9220
  3.9 15.6 %copy-start.15 = (f32[768]{0:T(1024)S(1)}, f32[768]{0:T(1024)}, u32[]{:S(2)}) copy-start(f32[768]{0:T(1024)} %param.21) | copy-start | bytes 9220
  4.0 26.2 %collective-permute-start = (bf16[272,768]{1,0:T(8,128)(2,1)S(1)}, bf16[272,768]{1,0:T(8,128)(2,1)S(1)}, u32[]{:S(2)}, u32[]{:S(2)}) collective-permute-start(bf16[272,768]{1,0:T(8,128)(2,1)S(1)} %maximum_maximum_fusion), channel_id=1, source_target_pairs={{0,2},{2,0},{4,6},{6,4},{8,10},{10,8},{12,14},{14,12},{16,18},{18,... | collective-permute-start | bytes 1253384 | tf_op jit(solution)/shard_map/ppermute | solution.py:233
  7.0 23.2 %collective-permute-start.1 = (bf16[272,768]{1,0:T(8,128)(2,1)S(1)}, bf16[272,768]{1,0:T(8,128)(2,1)S(1)}, u32[]{:S(2)}, u32[]{:S(2)}) collective-permute-start(bf16[272,768]{1,0:T(8,128)(2,1)S(1)} %maximum_maximum_fusion), channel_id=1, source_target_pairs={{0,4},{2,6},{4,0},{6,2},{8,12},{10,14},{12,8},{14,10},{16,20},{18,... | collective-permute-start | bytes 1253384 | tf_op jit(solution)/shard_map/ppermute | solution.py:233
  8.5 19.5 %collective-permute-start.2 = (bf16[272,768]{1,0:T(8,128)(2,1)S(1)}, bf16[272,768]{1,0:T(8,128)(2,1)S(1)}, u32[]{:S(2)}, u32[]{:S(2)}) collective-permute-start(bf16[272,768]{1,0:T(8,128)(2,1)S(1)} %maximum_maximum_fusion), channel_id=1, source_target_pairs={{0,6},{2,4},{4,2},{6,0},{8,14},{10,12},{12,10},{14,8},{16,22},{18,... | collective-permute-start | bytes 1253384 | tf_op jit(solution)/shard_map/ppermute | solution.py:233
  12.9 17.6 %collective-permute-start.4 = (bf16[48,1280]{1,0:T(8,128)(2,1)}, bf16[48,1280]{1,0:T(8,128)(2,1)S(1)}, u32[]{:S(2)}, u32[]{:S(2)}) collective-permute-start(bf16[48,1280]{1,0:T(8,128)(2,1)} %pad_maximum_fusion.15), channel_id=1, source_target_pairs={{0,6},{2,4},{4,2},{6,0},{8,14},{10,12},{12,10},{14,8},{16,22},{18,... | collective-permute-start | bytes 368648 | tf_op jit(solution)/shard_map/ppermute | solution.py:233
  16.5 15.9 %collective-permute-start.5 = (bf16[48,1280]{1,0:T(8,128)(2,1)}, bf16[48,1280]{1,0:T(8,128)(2,1)}, u32[]{:S(2)}, u32[]{:S(2)}) collective-permute-start(bf16[48,1280]{1,0:T(8,128)(2,1)} %pad_maximum_fusion.16), channel_id=1, source_target_pairs={{0,4},{2,6},{4,0},{6,2},{8,12},{10,14},{12,8},{14,10},{16,20},{18,... | collective-permute-start | bytes 368648 | tf_op jit(solution)/shard_map/ppermute | solution.py:233
  28.0 4.9 %collective-permute-start.6 = (bf16[48,1280]{1,0:T(8,128)(2,1)S(1)}, bf16[48,1280]{1,0:T(8,128)(2,1)S(1)}, u32[]{:S(2)}, u32[]{:S(2)}) collective-permute-start(bf16[48,1280]{1,0:T(8,128)(2,1)S(1)} %pad_maximum_fusion.17), channel_id=1, source_target_pairs={{0,2},{2,0},{4,6},{6,4},{8,10},{10,8},{12,14},{14,12},{16,18},{18,... | collective-permute-start | bytes 368648 | tf_op jit(solution)/shard_map/ppermute | solution.py:233
  30.4 8.0 %copy-start.5 = (bf16[4,256,768]{2,1,0:T(8,128)(2,1)}, bf16[4,256,768]{2,1,0:T(8,128)(2,1)S(1)}, u32[]{:S(2)}) copy-start(bf16[4,256,768]{2,1,0:T(8,128)(2,1)S(1)} %pad_maximum_fusion.own_ref) | copy-start | bytes 4718596
  30.4 48.5 %collective-permute-start.3 = (bf16[4,256,768]{2,1,0:T(8,128)(2,1)S(1)}, bf16[4,256,768]{2,1,0:T(8,128)(2,1)S(1)}, u32[]{:S(2)}, u32[]{:S(2)}) collective-permute-start(bf16[4,256,768]{2,1,0:T(8,128)(2,1)S(1)} %pad_maximum_fusion.own_ref), channel_id=1, source_target_pairs={{0,1},{1,0},{2,3},{3,2},{4,5},{5,4},{6,7},{7,6},{8,9},{9,8},{10,11... | collective-permute-start | bytes 4718600 | tf_op jit(solution)/shard_map/ppermute | solution.py:239
  33.9 9.8 %collective-permute-start.10 = (bf16[192,512]{1,0:T(8,128)(2,1)S(1)}, bf16[192,512]{1,0:T(8,128)(2,1)S(1)}, u32[]{:S(2)}, u32[]{:S(2)}) collective-permute-start(bf16[192,512]{1,0:T(8,128)(2,1)S(1)} %pad_maximum_fusion.10), channel_id=1, source_target_pairs={{0,24},{2,26},{4,28},{6,30},{8,16},{10,18},{12,20},{14,22},{16,8},... | collective-permute-start | bytes 589832 | tf_op jit(solution)/shard_map/ppermute | solution.py:236
  37.6 26.3 %collective-permute-start.11 = (bf16[192,512]{1,0:T(8,128)(2,1)S(1)}, bf16[192,512]{1,0:T(8,128)(2,1)S(1)}, u32[]{:S(2)}, u32[]{:S(2)}) collective-permute-start(bf16[192,512]{1,0:T(8,128)(2,1)S(1)} %pad_maximum_fusion.10), channel_id=1, source_target_pairs={{0,16},{2,18},{4,20},{6,22},{8,24},{10,26},{12,28},{14,30},{16,0},... | collective-permute-start | bytes 589832 | tf_op jit(solution)/shard_map/ppermute | solution.py:236
  37.6 27.0 %collective-permute-start.12 = (bf16[192,512]{1,0:T(8,128)(2,1)S(1)}, bf16[192,512]{1,0:T(8,128)(2,1)S(1)}, u32[]{:S(2)}, u32[]{:S(2)}) collective-permute-start(bf16[192,512]{1,0:T(8,128)(2,1)S(1)} %pad_maximum_fusion.10), channel_id=1, source_target_pairs={{0,8},{2,10},{4,12},{6,14},{8,0},{10,2},{12,4},{14,6},{16,24},{18,... | collective-permute-start | bytes 589832 | tf_op jit(solution)/shard_map/ppermute | solution.py:236
  38.5 29.9 %collective-permute-start.7 = (bf16[192,768]{1,0:T(8,128)(2,1)S(1)}, bf16[192,768]{1,0:T(8,128)(2,1)S(1)}, u32[]{:S(2)}, u32[]{:S(2)}) collective-permute-start(bf16[192,768]{1,0:T(8,128)(2,1)S(1)} %slice.261), channel_id=1, source_target_pairs={{0,24},{2,26},{4,28},{6,30},{8,16},{10,18},{12,20},{14,22},{16,8},... | collective-permute-start | bytes 884744 | tf_op jit(solution)/shard_map/ppermute | solution.py:236
  43.7 35.0 %collective-permute-start.8 = (bf16[192,768]{1,0:T(8,128)(2,1)S(1)}, bf16[192,768]{1,0:T(8,128)(2,1)S(1)}, u32[]{:S(2)}, u32[]{:S(2)}) collective-permute-start(bf16[192,768]{1,0:T(8,128)(2,1)S(1)} %slice.261), channel_id=1, source_target_pairs={{0,16},{2,18},{4,20},{6,22},{8,24},{10,26},{12,28},{14,30},{16,0},... | collective-permute-start | bytes 884744 | tf_op jit(solution)/shard_map/ppermute | solution.py:236
  63.9 14.8 %collective-permute-start.9 = (bf16[192,768]{1,0:T(8,128)(2,1)S(1)}, bf16[192,768]{1,0:T(8,128)(2,1)S(1)}, u32[]{:S(2)}, u32[]{:S(2)}) collective-permute-start(bf16[192,768]{1,0:T(8,128)(2,1)S(1)} %slice.261), channel_id=1, source_target_pairs={{0,8},{2,10},{4,12},{6,14},{8,0},{10,2},{12,4},{14,6},{16,24},{18,... | collective-permute-start | bytes 884744 | tf_op jit(solution)/shard_map/ppermute | solution.py:236
  78.9 1.2 copy-start.7
  85.0 1.1 copy-start.1
  86.2 1.2 copy-start.2
  87.3 1.4 copy-start.3
  96.0 14.9 %collective-permute-start.24 = (bf16[192,512]{1,0:T(8,128)(2,1)S(1)}, bf16[192,512]{1,0:T(8,128)(2,1)S(1)}, u32[]{:S(2)}, u32[]{:S(2)}) collective-permute-start(bf16[192,512]{1,0:T(8,128)(2,1)S(1)} %get-tuple-element.64), channel_id=1, source_target_pairs={{0,8},{2,10},{4,12},{6,14},{8,0},{10,2},{12,4},{14,6},{16,24},{18,... | collective-permute-start | bytes 589832 | tf_op jit(solution)/shard_map/ppermute | solution.py:236
  96.1 16.7 %collective-permute-start.25 = (bf16[192,512]{1,0:T(8,128)(2,1)S(1)}, bf16[192,512]{1,0:T(8,128)(2,1)S(1)}, u32[]{:S(2)}, u32[]{:S(2)}) collective-permute-start(bf16[192,512]{1,0:T(8,128)(2,1)S(1)} %get-tuple-element.66), channel_id=1, source_target_pairs={{0,16},{2,18},{4,20},{6,22},{8,24},{10,26},{12,28},{14,30},{16,0},... | collective-permute-start | bytes 589832 | tf_op jit(solution)/shard_map/ppermute | solution.py:236
  99.1 13.7 %collective-permute-start.26 = (bf16[192,512]{1,0:T(8,128)(2,1)S(1)}, bf16[192,512]{1,0:T(8,128)(2,1)S(1)}, u32[]{:S(2)}, u32[]{:S(2)}) collective-permute-start(bf16[192,512]{1,0:T(8,128)(2,1)S(1)} %get-tuple-element.65), channel_id=1, source_target_pairs={{0,24},{2,26},{4,28},{6,30},{8,16},{10,18},{12,20},{14,22},{16,8},... | collective-permute-start | bytes 589832 | tf_op jit(solution)/shard_map/ppermute | solution.py:236
  110.9 11.5 %copy-start.16 = (bf16[2,4,128,768]{3,2,1,0:T(8,128)(2,1)S(1)}, bf16[2,4,128,768]{3,2,1,0:T(8,128)(2,1)}, u32[]{:S(2)}) copy-start(bf16[2,4,128,768]{3,2,1,0:T(8,128)(2,1)} %get-tuple-element.36) | copy-start | bytes 4718596
  113.0 7.1 %collective-permute-start.27 = (bf16[48,512]{1,0:T(8,128)(2,1)S(1)}, bf16[48,512]{1,0:T(8,128)(2,1)S(1)}, u32[]{:S(2)}, u32[]{:S(2)}) collective-permute-start(bf16[48,512]{1,0:T(8,128)(2,1)S(1)} %get-tuple-element.96), channel_id=1, source_target_pairs={{0,6},{2,4},{4,2},{6,0},{8,14},{10,12},{12,10},{14,8},{16,22},{18,... | collective-permute-start | bytes 147464 | tf_op jit(solution)/shard_map/ppermute | solution.py:233
  114.4 8.1 %collective-permute-start.28 = (bf16[48,512]{1,0:T(8,128)(2,1)S(1)}, bf16[48,512]{1,0:T(8,128)(2,1)S(1)}, u32[]{:S(2)}, u32[]{:S(2)}) collective-permute-start(bf16[48,512]{1,0:T(8,128)(2,1)S(1)} %get-tuple-element.95), channel_id=1, source_target_pairs={{0,4},{2,6},{4,0},{6,2},{8,12},{10,14},{12,8},{14,10},{16,20},{18,... | collective-permute-start | bytes 147464 | tf_op jit(solution)/shard_map/ppermute | solution.py:233
  114.9 7.6 %collective-permute-start.29 = (bf16[48,512]{1,0:T(8,128)(2,1)S(1)}, bf16[48,512]{1,0:T(8,128)(2,1)S(1)}, u32[]{:S(2)}, u32[]{:S(2)}) collective-permute-start(bf16[48,512]{1,0:T(8,128)(2,1)S(1)} %get-tuple-element.94), channel_id=1, source_target_pairs={{0,2},{2,0},{4,6},{6,4},{8,10},{10,8},{12,14},{14,12},{16,18},{18,... | collective-permute-start | bytes 147464 | tf_op jit(solution)/shard_map/ppermute | solution.py:233
  116.6 15.3 %collective-permute-start.17 = (bf16[208,768]{1,0:T(8,128)(2,1)S(1)}, bf16[208,768]{1,0:T(8,128)(2,1)S(1)}, u32[]{:S(2)}, u32[]{:S(2)}) collective-permute-start(bf16[208,768]{1,0:T(8,128)(2,1)S(1)} %get-tuple-element.136), channel_id=1, source_target_pairs={{0,8},{2,10},{4,12},{6,14},{8,0},{10,2},{12,4},{14,6},{16,24},{18,... | collective-permute-start | bytes 958472 | tf_op jit(solution)/shard_map/ppermute | solution.py:236
  120.0 23.7 %collective-permute-start.18 = (bf16[208,768]{1,0:T(8,128)(2,1)S(1)}, bf16[208,768]{1,0:T(8,128)(2,1)S(1)}, u32[]{:S(2)}, u32[]{:S(2)}) collective-permute-start(bf16[208,768]{1,0:T(8,128)(2,1)S(1)} %get-tuple-element.137), channel_id=1, source_target_pairs={{0,16},{2,18},{4,20},{6,22},{8,24},{10,26},{12,28},{14,30},{16,0},... | collective-permute-start | bytes 958472 | tf_op jit(solution)/shard_map/ppermute | solution.py:236
  120.1 23.6 %collective-permute-start.19 = (bf16[208,768]{1,0:T(8,128)(2,1)S(1)}, bf16[208,768]{1,0:T(8,128)(2,1)S(1)}, u32[]{:S(2)}, u32[]{:S(2)}) collective-permute-start(bf16[208,768]{1,0:T(8,128)(2,1)S(1)} %get-tuple-element.138), channel_id=1, source_target_pairs={{0,24},{2,26},{4,28},{6,30},{8,16},{10,18},{12,20},{14,22},{16,8},... | collective-permute-start | bytes 958472 | tf_op jit(solution)/shard_map/ppermute | solution.py:236
  122.5 30.7 %collective-permute-start.13 = (bf16[2,4,128,768]{3,2,1,0:T(8,128)(2,1)S(1)}, bf16[2,4,128,768]{3,2,1,0:T(8,128)(2,1)S(1)}, u32[]{:S(2)}, u32[]{:S(2)}) collective-permute-start(bf16[2,4,128,768]{3,2,1,0:T(8,128)(2,1)S(1)} %copy-done.16), channel_id=1, source_target_pairs={{0,1},{1,0},{2,3},{3,2},{4,5},{5,4},{6,7},{7,6},{8,9},{9,8},{10,11... | collective-permute-start | bytes 4718600 | tf_op jit(solution)/shard_map/ppermute | solution.py:239
  144.0 4.7 %collective-permute-start.20 = (bf16[64,768]{1,0:T(8,128)(2,1)S(1)}, bf16[64,768]{1,0:T(8,128)(2,1)S(1)}, u32[]{:S(2)}, u32[]{:S(2)}) collective-permute-start(bf16[64,768]{1,0:T(8,128)(2,1)S(1)} %get-tuple-element.133), channel_id=1, source_target_pairs={{0,2},{2,0},{4,6},{6,4},{8,10},{10,8},{12,14},{14,12},{16,18},{18,... | collective-permute-start | bytes 294920 | tf_op jit(solution)/shard_map/ppermute | solution.py:233
  144.2 4.6 %collective-permute-start.21 = (bf16[64,768]{1,0:T(8,128)(2,1)S(1)}, bf16[64,768]{1,0:T(8,128)(2,1)S(1)}, u32[]{:S(2)}, u32[]{:S(2)}) collective-permute-start(bf16[64,768]{1,0:T(8,128)(2,1)S(1)} %get-tuple-element.134), channel_id=1, source_target_pairs={{0,4},{2,6},{4,0},{6,2},{8,12},{10,14},{12,8},{14,10},{16,20},{18,... | collective-permute-start | bytes 294920 | tf_op jit(solution)/shard_map/ppermute | solution.py:233
  145.9 5.5 %collective-permute-start.22 = (bf16[64,768]{1,0:T(8,128)(2,1)S(1)}, bf16[64,768]{1,0:T(8,128)(2,1)S(1)}, u32[]{:S(2)}, u32[]{:S(2)}) collective-permute-start(bf16[64,768]{1,0:T(8,128)(2,1)S(1)} %get-tuple-element.135), channel_id=1, source_target_pairs={{0,6},{2,4},{4,2},{6,0},{8,14},{10,12},{12,10},{14,8},{16,22},{18,... | collective-permute-start | bytes 294920 | tf_op jit(solution)/shard_map/ppermute | solution.py:233
  151.4 7.1 %collective-permute-start.23 = (f32[5,768]{1,0:T(8,128)S(1)}, f32[5,768]{1,0:T(8,128)S(1)}, u32[]{:S(2)}, u32[]{:S(2)}) collective-permute-start(f32[5,768]{1,0:T(8,128)S(1)} %add_add_fusion), channel_id=1, source_target_pairs={{0,1},{1,0},{2,3},{3,2},{4,5},{5,4},{6,7},{7,6},{8,9},{9,8},{10,11... | collective-permute-start | bytes 46088 | tf_op jit(solution)/shard_map/ppermute | solution.py:239
  153.7 12.0 %collective-permute-start.14 = (bf16[2,128,768]{2,1,0:T(8,128)(2,1)S(1)}, bf16[2,128,768]{2,1,0:T(8,128)(2,1)S(1)}, u32[]{:S(2)}, u32[]{:S(2)}) collective-permute-start(bf16[2,128,768]{2,1,0:T(8,128)(2,1)S(1)} %get-tuple-element.51), channel_id=1, source_target_pairs={{0,2},{2,0},{4,6},{6,4},{8,10},{10,8},{12,14},{14,12},{16,18},{18,... | collective-permute-start | bytes 1179656 | tf_op jit(solution)/shard_map/ppermute | solution.py:233
  155.1 19.7 %collective-permute-start.15 = (bf16[2,128,768]{2,1,0:T(8,128)(2,1)S(1)}, bf16[2,128,768]{2,1,0:T(8,128)(2,1)S(1)}, u32[]{:S(2)}, u32[]{:S(2)}) collective-permute-start(bf16[2,128,768]{2,1,0:T(8,128)(2,1)S(1)} %get-tuple-element.53), channel_id=1, source_target_pairs={{0,4},{2,6},{4,0},{6,2},{8,12},{10,14},{12,8},{14,10},{16,20},{18,... | collective-permute-start | bytes 1179656 | tf_op jit(solution)/shard_map/ppermute | solution.py:233
  155.9 18.8 %collective-permute-start.16 = (bf16[2,128,768]{2,1,0:T(8,128)(2,1)S(1)}, bf16[2,128,768]{2,1,0:T(8,128)(2,1)S(1)}, u32[]{:S(2)}, u32[]{:S(2)}) collective-permute-start(bf16[2,128,768]{2,1,0:T(8,128)(2,1)S(1)} %get-tuple-element.52), channel_id=1, source_target_pairs={{0,6},{2,4},{4,2},{6,0},{8,14},{10,12},{12,10},{14,8},{16,22},{18,... | collective-permute-start | bytes 1179656 | tf_op jit(solution)/shard_map/ppermute | solution.py:233
  159.1 17.1 %copy-start.9 = (f32[768]{0:T(1024)}, f32[768]{0:T(1024)S(1)}, u32[]{:S(2)}) copy-start(f32[768]{0:T(1024)S(1)} %get-tuple-element.181) | copy-start | bytes 9220
  159.1 16.1 %copy-start.10 = (f32[768]{0:T(1024)S(1)}, f32[768]{0:T(1024)}, u32[]{:S(2)}) copy-start(f32[768]{0:T(1024)} %param.29) | copy-start | bytes 9220
  159.1 16.1 %copy-start.11 = (f32[768]{0:T(1024)S(1)}, f32[768]{0:T(1024)}, u32[]{:S(2)}) copy-start(f32[768]{0:T(1024)} %param.25) | copy-start | bytes 9220

commit v2 on v1

v2 whole, which is shorter than its diff:
```python
import math
from functools import partial

import jax
import jax.numpy as jnp
import numpy as np
from jax import lax
from jax.experimental import pallas as pl
from jax.experimental.pallas import tpu as pltpu
from jax.sharding import PartitionSpec as P

HD = 64
ROT = 16
PLANE = 4
BLK = 2 * HD
NOTES = 16
eps = 1e-05
F32 = jnp.float32
BF16 = jnp.bfloat16


def dot(a, b):
    return jnp.dot(a, b, preferred_element_type=F32)


def dot_nt(a, b):
    return lax.dot_general(a, b, (((1,), (1,)), ((), ())), preferred_element_type=F32)


def dot_tn(a, b):
    return lax.dot_general(a, b, (((0,), (0,)), ((), ())), preferred_element_type=F32)


def xor_sorted(parts, index):
    parts = list(parts)
    bit = 1
    while bit < len(parts):
        swap = (index & bit) != 0
        parts = [jnp.where(swap, parts[j ^ bit], parts[j]) for j in range(len(parts))]
        bit *= 2
    return parts


def tree_sum(parts):
    parts = list(parts)
    while len(parts) > 1:
        parts = [parts[j] + parts[j + 1] for j in range(0, len(parts), 2)]
    return parts[0]


def rotary_tables(rows):
    half = ROT // 2
    inverse = np.float32(10000.0) ** (-np.arange(half, dtype=np.float32) * np.float32(2.0 / ROT))
    angle = np.arange(rows, dtype=np.float32)[:, None] * inverse.astype(np.float32)[None, :]
    cos, sin = np.cos(angle), np.sin(angle)
    rest = np.ones((rows, HD - ROT), np.float32)
    none = np.zeros((rows, half), np.float32)
    keep = np.concatenate([cos, cos, rest], axis=1)
    low = np.concatenate([-sin, none, 0.0 * rest], axis=1)
    high = np.concatenate([none, sin, 0.0 * rest], axis=1)
    return tuple(
        np.concatenate([t] * (BLK // HD), axis=1).astype(np.float32) for t in (keep, low, high)
    )


def share_kernel(place_ref, qkv_ref, out_ref, up_ref, down_ref, *share_refs):
    head_blocks = out_ref.shape[1] // BLK
    width = up_ref.shape[1] // PLANE
    for k in range(PLANE):
        place = place_ref[0] ^ k
        at = pl.ds(pl.multiple_of(jnp.minimum(place, head_blocks - 1) * BLK, BLK), BLK)
        for c in range(4):
            block = qkv_ref[c, :, at] if c < 3 else out_ref[:, at]
            block = jnp.where(place < head_blocks, block.astype(F32), 0.0)
            share_refs[k][:, c * BLK : (c + 1) * BLK] = block.astype(BF16)
        at = pl.ds(pl.multiple_of(place * width, BLK), width)
        share_refs[k][:, 4 * BLK : 4 * BLK + width] = up_ref[:, at]
        share_refs[k][:, 4 * BLK + width :] = down_ref[:, at]


def place_rows(place_ref, piece_refs, to_ref):
    plane_at, level_at = place_ref[0], place_ref[1]
    owned = piece_refs[0].shape[0] // PLANE
    for m, piece_ref in enumerate(piece_refs):
        for k in range(PLANE):
            at = ((level_at ^ m) * PLANE + (plane_at ^ k)) * owned
            to_ref[pl.ds(pl.multiple_of(at, owned), owned), :] = piece_ref[k * owned : (k + 1) * owned, :]


def take_rows(place_ref, from_ref, m, k, owned):
    at = ((place_ref[1] ^ m) * PLANE + (place_ref[0] ^ k)) * owned
    return from_ref[pl.ds(pl.multiple_of(at, owned), owned), :]


def rows_kernel(half_ref, params_ref, *refs):
    own_refs, peer_refs = refs[:2], refs[2:4]
    x1_ref, x2_ref, xh_ref, g_ref, g_own_ref, length_ref, bo_ref = refs[4:]
    half = half_ref[0]
    own_rows = g_own_ref.shape[0]
    slots = 2 * own_rows
    message_rows = own_refs[0].shape[0] // 2
    params = params_ref[...]
    length_ref[...] = jnp.zeros_like(length_ref)
    for k in range(PLANE):
        start = (k % 2) * message_rows
        length = own_refs[k // 2][start + slots : start + slots + NOTES, :].astype(F32)
        length = jnp.sum(length[0:1], axis=-1, keepdims=True)
        length_ref[k : k + 1, :] = jnp.broadcast_to(length, (1, length_ref.shape[1]))
        for which, parts in enumerate((own_refs, peer_refs)):
            part = half if which == 0 else 1 - half
            ref = parts[k // 2]
            x = ref[start : start + own_rows, :].astype(F32)
            centre = jnp.mean(x, axis=-1, keepdims=True)
            off = x - centre
            spread = jnp.mean(off * off, axis=-1, keepdims=True)
            xh = off * lax.rsqrt(spread + eps)
            at = pl.ds(pl.multiple_of(k * slots + part * own_rows, own_rows), own_rows)
            x1_ref[at, :] = (xh * params[0:1] + params[1:2]).astype(BF16)
            x2_ref[at, :] = (xh * params[2:3] + params[3:4]).astype(BF16)
            xh_ref[at, :] = xh.astype(BF16)
            row = lax.broadcasted_iota(jnp.int32, (own_rows, 1), 0) + part * own_rows
            g = ref[start + own_rows : start + slots, :].astype(F32)
            g = jnp.where(row.astype(F32) < length, g, 0.0)
            g_ref[at, :] = g.astype(BF16)
            if k == 0 and which == 0:
                g_own_ref[...] = g.astype(BF16)
                bo_ref[...] = jnp.sum(g, axis=0, keepdims=True)


def attention_kernel(levels, *refs):
    place_ref, length_ref, x1_ref, g_ref, bias_ref, keep_ref, low_ref, high_ref = refs[:8]
    pieces = refs[8 : 8 + max(levels, 1)]
    att_ref, gp_ref, wa_ref, gb_ref = refs[8 + len(pieces) : 12 + len(pieces)]
    message_refs, gw_ref = refs[12 + len(pieces) : -1], refs[-1]
    if levels:
        place_rows(place_ref, pieces, wa_ref)
    else:
        wa_ref[...] = pieces[0][...]
        gw_ref = message_refs[0]
    slots = keep_ref.shape[0]
    keep, low, high = keep_ref[...], low_ref[...], high_ref[...]

    def turn(x, sign):
        return x * keep + sign * (
            pltpu.roll(x, BLK - ROT // 2, 1) * low + pltpu.roll(x, ROT // 2, 1) * high
        )

    lane = lax.broadcasted_iota(jnp.int32, (slots, BLK), 1)
    first = lane < HD
    q_row = lax.broadcasted_iota(jnp.int32, (2 * slots, slots), 0) & (slots - 1)
    k_row = lax.broadcasted_iota(jnp.int32, (2 * slots, slots), 1)

    def stacked(x):
        zero = jnp.zeros_like(x)
        return jnp.concatenate([jnp.where(first, x, zero), jnp.where(first, zero, x)], axis=0)

    def joined(x):
        return jnp.where(first, x[:slots], x[slots:])

    total = jnp.zeros((1, 3 * BLK), F32)
    for k in range(PLANE):
        at = pl.ds(k * slots, slots)
        proj = dot(x1_ref[at, :], wa_ref[:, : 3 * BLK]) + bias_ref[...]
        query = stacked((turn(proj[:, :BLK], 1.0) * HD**-0.5).astype(BF16))
        key = turn(proj[:, BLK : 2 * BLK], 1.0).astype(BF16)
        value = proj[:, 2 * BLK :].astype(BF16)
        ga = stacked(dot(g_ref[at, :], wa_ref[:, 3 * BLK :]).astype(BF16))
        logits = dot_nt(query, key)
        live = k_row.astype(F32) < length_ref[k : k + 1, 0:1]
        allowed = (k_row <= q_row) & (live | (k_row == q_row))
        logits = jnp.where(allowed, logits, -1000000000.0)
        weights = jnp.exp(logits - jnp.max(logits, axis=-1, keepdims=True))
        probs = weights / jnp.sum(weights, axis=-1, keepdims=True)
        rounded = probs.astype(BF16)
        att_ref[at, :] = joined(dot(rounded, value)).astype(BF16)
        grad_probs = dot_nt(ga, value)
        inner = jnp.sum(probs * grad_probs, axis=-1, keepdims=True)
        grad_logits = (probs * (grad_probs - inner)).astype(BF16)
        grad_query = joined(dot(grad_logits, key)) * HD**-0.5
        grad_key = dot_tn(grad_logits, query)
        grad_value = dot_tn(rounded, ga)
        gp = jnp.concatenate([turn(grad_query, -1.0), turn(grad_key, -1.0), grad_value], axis=1).astype(BF16)
        gp_ref[at, :] = gp
        total = total + jnp.sum(gp.astype(F32), axis=0, keepdims=True)
    gb_ref[...] = total
    gw_ref[:, : 3 * BLK] = dot_tn(x1_ref[...], gp_ref[...]).astype(BF16)
    gw_ref[:, 3 * BLK :] = dot_tn(g_ref[...], att_ref[...]).astype(BF16)
    if levels:
        owned = pieces[0].shape[0] // PLANE
        for m in range(levels):
            for k in range(PLANE):
                message_refs[m][k * owned : (k + 1) * owned, :] = take_rows(place_ref, gw_ref, m, k, owned)


def feed_kernel(levels, *refs):
    place_ref, half_ref, params_ref, x2_ref, xh_ref, g_ref, wa_ref, att_ref, gp_ref = refs[:9]
    bias_ref, gb_ref, bo_ref = refs[9:12]
    pieces = refs[12 : 12 + max(levels, 1)]
    keep_ref, send_ref, notes_ref = refs[12 + len(pieces) : 15 + len(pieces)]
    message_refs = refs[15 + len(pieces) : -5]
    wf_ref, gw_ref, act_ref, gh_ref, stage_ref = refs[-5:]
    width = bias_ref.shape[1]
    if levels:
        place_rows(place_ref, pieces, wf_ref)
    else:
        wf_ref[...] = pieces[0][...]
        gw_ref = message_refs[0]
    half = half_ref[0]
    own_rows = keep_ref.shape[2]
    slots = 2 * own_rows
    params = params_ref[...]
    gain1, gain2 = params[0:1], params[2:3]
    sums = [jnp.zeros((1, x2_ref.shape[1]), F32) for _ in range(4)]
    gb_up = jnp.zeros((1, width), F32)
    for k in range(PLANE):
        at = pl.ds(k * slots, slots)
        hidden = dot(x2_ref[at, :], wf_ref[:, :width]) + bias_ref[...]
        grad_act = dot(g_ref[at, :], wf_ref[:, width:])
        part = 0.5 + 0.5 * lax.erf(hidden * (0.5**0.5))
        act = (hidden * part).astype(BF16)
        slope = part + hidden * jnp.exp(-0.5 * hidden * hidden) * (2.0 * math.pi) ** -0.5
        gh = (grad_act * slope).astype(BF16)
        act_ref[at, :] = act
        gh_ref[at, :] = gh
        gb_up = gb_up + jnp.sum(gh.astype(F32), axis=0, keepdims=True)
        stage_ref[0] = dot_nt(act, wf_ref[:, width:]) + dot_nt(att_ref[at, :], wa_ref[:, 3 * BLK :])
        g1 = dot_nt(gp_ref[at, :], wa_ref[:, : 3 * BLK])
        g2 = dot_nt(gh, wf_ref[:, :width])
        stage_ref[1] = gain1 * g1 + gain2 * g2
        xh = xh_ref[at, :].astype(F32)
        for j, term in enumerate((g1 * xh, g1, g2 * xh, g2)):
            sums[j] = sums[j] + jnp.sum(term, axis=0, keepdims=True)
        mine = pl.ds(pl.multiple_of(half * own_rows, own_rows), own_rows)
        other = pl.ds(pl.multiple_of((1 - half) * own_rows, own_rows), own_rows)
        for j in range(2):
            keep_ref[j, k] = stage_ref[j, mine, :].astype(BF16)
            send_ref[j, k] = stage_ref[j, other, :].astype(BF16)
    gw_ref[:, :width] = dot_tn(x2_ref[...], gh_ref[...]).astype(BF16)
    gw_ref[:, width:] = dot_tn(g_ref[...], act_ref[...]).astype(BF16)
    notes_ref[...] = jnp.zeros_like(notes_ref)
    notes_ref[0:1, :width] = gb_up
    notes_ref[0:1, width:] = gb_ref[...]
    notes_ref[1:2, :] = bo_ref[...]
    for j in range(4):
        notes_ref[2 + j : 3 + j, :] = sums[j]
    if levels:
        owned = pieces[0].shape[0] // PLANE
        notes = notes_ref[...].astype(BF16)
        for m in range(levels):
            for k in range(PLANE):
                message_refs[m][k * owned : (k + 1) * owned, :] = take_rows(place_ref, gw_ref, m, k, owned)
            message_refs[m][PLANE * owned :, :] = notes


def combine_kernel(inner_ref, *refs):
    head_refs, feed_refs, out_refs = refs[:4], refs[4:8], refs[8:]
    owned = head_refs[0].shape[0] // PLANE
    head_columns = head_refs[0].shape[1]
    inner = inner_ref[0] != 0

    def summed(refs, rows):
        own, near, middle, far = [ref[rows, :].astype(F32) for ref in refs]
        return (own + near) + (jnp.where(inner, 0.0, middle) + far)

    at = pl.ds(PLANE * owned, NOTES)
    own, near, middle, far = [ref[at, :].astype(F32) for ref in feed_refs]
    passed = feed_refs[3][PLANE * owned + NOTES :, :].astype(F32)
    notes = ((own + near) + (jnp.where(inner, passed, middle) + far)).astype(BF16)
    for k, out_ref in enumerate(out_refs):
        rows = pl.ds(k * owned, owned)
        out_ref[:owned, :head_columns] = summed(head_refs, rows).astype(out_ref.dtype)
        out_ref[:owned, head_columns:] = summed(feed_refs, rows).astype(out_ref.dtype)
        out_ref[owned:, :head_columns] = jnp.zeros((NOTES, head_columns), out_ref.dtype)
        out_ref[owned:, head_columns:] = notes.astype(out_ref.dtype)


def owner_kernel(place_ref, *refs):
    part_refs = refs[:PLANE]
    up_ref, down_ref, qkv_ref, out_ref, b_up_ref, b_qkv_ref, common_ref = refs[PLANE:]
    owned = up_ref.shape[0]
    width = up_ref.shape[1] // PLANE
    head_blocks = out_ref.shape[1] // BLK
    start = 4 * BLK
    for k, part_ref in enumerate(part_refs):
        place = place_ref[0] ^ k
        at = pl.ds(pl.multiple_of(place * width, BLK), width)
        up_ref[:, at] = part_ref[:owned, start : start + width].astype(F32)
        down_ref[:, at] = part_ref[:owned, start + width :].astype(F32)
        notes = part_ref[owned:, start:].astype(F32)
        b_up_ref[:, at] = notes[0:1, :width]

        @pl.when(place < head_blocks)
        def _():
            at = pl.ds(pl.multiple_of(place * BLK, BLK), BLK)
            for c in range(3):
                qkv_ref[c, :, at] = part_ref[:owned, c * BLK : (c + 1) * BLK].astype(F32)
                b_qkv_ref[c : c + 1, at] = notes[0:1, width + c * BLK : width + (c + 1) * BLK]
            out_ref[:, at] = part_ref[:owned, 3 * BLK : 4 * BLK].astype(F32)

    common_ref[...] = tree_sum([part_ref[owned:, start:].astype(F32) for part_ref in part_refs])


def kernel_call(body, out_shapes, in_smem, operands, scratch=(), micros=1.0):
    vmem = pl.BlockSpec(memory_space=pltpu.VMEM)
    smem = pl.BlockSpec(memory_space=pltpu.SMEM)
    return pl.pallas_call(
        body,
        out_shape=out_shapes,
        in_specs=[smem] * in_smem + [vmem] * (len(operands) - in_smem),
        out_specs=[vmem] * len(out_shapes),
        scratch_shapes=list(scratch),
        compiler_params=pltpu.CompilerParams(vmem_limit_bytes=48 * 2**20),
        cost_estimate=pl.CostEstimate(flops=int(micros * 1e9), bytes_accessed=1, transcendentals=0),
    )(*operands)


def per_device(
    residual,
    cotangent,
    seq_lengths,
    gain_attn,
    shift_attn,
    gain_mlp,
    shift_mlp,
    w_qkv,
    b_qkv,
    w_out,
    b_out,
    w_up,
    b_up,
    w_down,
    b_down,
):
    places = lax.axis_size("dp")
    levels = places // PLANE
    index = lax.axis_index("dp")
    half = lax.axis_index("tensor")
    plane_at = index % PLANE
    level_at = index // PLANE
    own_rows, model = residual.shape
    slots = 2 * own_rows
    rows_all = PLANE * slots
    owned = w_up.shape[0]
    width = w_up.shape[1] // PLANE
    head_blocks = w_out.shape[0] // BLK
    direct = levels if levels == 4 and owned % 16 == 0 else 0
    level_groups = [[lev * PLANE + j for lev in range(levels)] for j in range(PLANE)]
    shape = jax.ShapeDtypeStruct

    def to_plane(x, k):
        return lax.ppermute(x, "dp", [(j, j ^ k) for j in range(places)])

    def to_level(x, m):
        return lax.ppermute(x, "dp", [(j, j ^ (m * PLANE)) for j in range(places)])

    def to_peer(x):
        return lax.ppermute(x, "tensor", [(0, 1), (1, 0)])

    inner = (level_at == 1) | (level_at == 2)
    passing = [(0, 2), (3, 1), (1, 0), (2, 3)]

    def to_pass(x, back=False):
        pairs = [(b, a) if back else (a, b) for a, b in passing]
        return lax.ppermute(x, "dp", [(a * PLANE + j, b * PLANE + j) for a, b in pairs for j in range(PLANE)])

    def gather_line(x):
        near, far = to_level(x, 1), to_level(x, 3)
        return near, far, to_pass(jnp.where(inner, far, x))

    place_s = jnp.stack([plane_at, level_at]).astype(jnp.int32)
    half_s = half.astype(jnp.int32).reshape(1)

    shares = kernel_call(
        share_kernel,
        [shape((owned, 4 * BLK + 2 * width), BF16)] * PLANE,
        1,
        (place_s, w_qkv, w_out.T, w_up, w_down.T),
    )
    received = [to_plane(shares[k], k) for k in range(1, PLANE)]
    if direct:
        every = jnp.concatenate([shares[0]] + received, axis=0)
        head_own, feed_own = every[:, : 4 * BLK], every[:, 4 * BLK :]
        near, far, middle = gather_line(head_own)
        head_pieces = [head_own, near, middle, far]
        feed_own, _ = lax.optimization_barrier((feed_own, far))
        near, far, middle = gather_line(feed_own)
        feed_pieces = [feed_own, near, middle, far]
    else:
        every = jnp.concatenate(xor_sorted([shares[0]] + received, plane_at), axis=0)
        every = lax.all_gather(every, "dp", axis=0, tiled=True, axis_index_groups=level_groups)
        head_pieces, feed_pieces = [every[:, : 4 * BLK]], [every[:, 4 * BLK :]]

    notes = jnp.pad(seq_lengths.astype(BF16), ((0, NOTES - 1), (0, model - seq_lengths.shape[1])))
    message = jnp.concatenate([residual, cotangent, notes], axis=0)
    message, _ = lax.optimization_barrier((message, shares))
    pair = jnp.concatenate([message, to_plane(message, 1)], axis=0)
    other_pair = to_plane(pair, 2)
    peers = to_peer(pair), to_peer(other_pair)

    params = jnp.stack([gain_attn, shift_attn, gain_mlp, shift_mlp] + [jnp.zeros_like(gain_attn)] * 4)
    x1, x2, xh, g, g_own, lengths, bo = kernel_call(
        rows_kernel,
        [shape((rows_all, model), BF16)] * 4
        + [shape((own_rows, model), BF16), shape((8, 128), F32), shape((1, model), F32)],
        1,
        (half_s, params, pair, other_pair, *peers),
        micros=5,
    )

    block_at = jnp.minimum(plane_at, head_blocks - 1) * BLK
    bias_heads = lax.dynamic_slice_in_dim(b_qkv, block_at, BLK, 1).reshape(1, 3 * BLK)
    head_message = shape((PLANE * owned if direct else model, 4 * BLK), BF16)
    att, gp, wa, gb, *head_messages = kernel_call(
        partial(attention_kernel, direct),
        [
            shape((rows_all, BLK), BF16),
            shape((rows_all, 3 * BLK), BF16),
            shape((model, 4 * BLK), BF16),
            shape((1, 3 * BLK), F32),
        ]
        + [head_message] * max(direct, 1),
        1,
        (place_s, lengths, x1, g, bias_heads, *rotary_tables(slots), *head_pieces),
        scratch=[pltpu.VMEM((model, 4 * BLK), BF16)],
        micros=8,
    )

    bias_up = lax.dynamic_slice_in_dim(b_up, plane_at * width, width, 0).reshape(1, width)
    feed_message = shape((PLANE * owned + NOTES if direct else model, 2 * width), BF16)
    keep, send, notes, *feed_messages = kernel_call(
        partial(feed_kernel, direct),
        [
            shape((2, PLANE, own_rows, model), BF16),
            shape((2, PLANE, own_rows, model), BF16),
            shape((NOTES, model), F32),
        ]
        + [feed_message] * max(direct, 1),
        2,
        (place_s, half_s, params, x2, xh, g, wa, att, gp, bias_up, gb, bo, *feed_pieces),
        scratch=[
            pltpu.VMEM((model, 2 * width), BF16),
            pltpu.VMEM((model, 2 * width), BF16),
            pltpu.VMEM((rows_all, width), BF16),
            pltpu.VMEM((rows_all, width), BF16),
            pltpu.VMEM((2, slots, model), F32),
        ],
        micros=10.5,
    )

    summed = (keep.astype(F32) + to_peer(send).astype(F32)).astype(BF16)
    outgoing = [summed[:, k] for k in range(PLANE)]

    if direct:
        head_mid = to_pass(head_messages[2], back=True)
        head_near = to_level(head_messages[1], 1)
        feed_messages, head_mid = lax.optimization_barrier((feed_messages, head_mid))
        relayed = head_messages[3].astype(F32) + jnp.where(inner, head_mid.astype(F32), 0.0)
        head_far = to_level(relayed.astype(BF16), 3)
        feed_mid = to_pass(feed_messages[2], back=True)
        feed_near = to_level(feed_messages[1], 1)
        (feed_mid, head_mid), outgoing = lax.optimization_barrier(((feed_mid, head_mid), outgoing))
        rows = PLANE * owned
        relayed = feed_messages[3].astype(F32) + jnp.where(inner, feed_mid.astype(F32), 0.0)
        relayed = [relayed[:rows].astype(BF16), feed_messages[3][rows:], feed_mid[rows:]]
        feed_far = to_level(jnp.concatenate(relayed, axis=0), 3)
        columns = 4 * BLK + 2 * width
        backs = kernel_call(
            combine_kernel,
            [shape((owned + NOTES, columns), F32)] + [shape((owned + NOTES, columns), BF16)] * (PLANE - 1),
            1,
            (
                inner.astype(jnp.int32).reshape(1),
                *(head_messages[0], head_near, head_mid, head_far),
                *(feed_messages[0], feed_near, feed_mid, feed_far),
            ),
        )
    else:
        sums = jnp.concatenate([head_messages[0], feed_messages[0]], axis=1)
        sums = lax.psum_scatter(sums, "dp", scatter_dimension=0, tiled=True, axis_index_groups=level_groups)
        notes = lax.all_gather(notes.astype(BF16), "dp", axis=0, axis_index_groups=level_groups)
        notes = jnp.sum(notes.astype(F32), axis=0).astype(BF16)
        notes = jnp.concatenate([jnp.zeros((NOTES, 4 * BLK), BF16), notes], axis=1)
        sums = sums.reshape(PLANE, owned, 4 * BLK + 2 * width)
        backs = [
            jnp.concatenate([lax.dynamic_index_in_dim(sums, plane_at ^ k, 0, keepdims=False), notes], axis=0)
            for k in range(PLANE)
        ]
    parts = [outgoing[0]] + [to_plane(outgoing[k], k) for k in range(1, PLANE)]
    backs, parts = lax.optimization_barrier((backs, parts))
    backs = [backs[0]] + [to_plane(backs[k], k) for k in range(1, PLANE)]
    grad_up, grad_down, grad_qkv, grad_out_w, grad_b_up, grad_b_qkv, common = kernel_call(
        owner_kernel,
        [
            shape((owned, PLANE * width), F32),
            shape((owned, PLANE * width), F32),
            shape((3, owned, head_blocks * BLK), F32),
            shape((owned, head_blocks * BLK), F32),
            shape((1, PLANE * width), F32),
            shape((3, head_blocks * BLK), F32),
            shape((NOTES, model), F32),
        ],
        1,
        (place_s, *backs),
    )
    common = common + to_peer(common)

    branch, grad_norm = tree_sum([part.astype(F32) for part in parts])
    residual_f = residual.astype(F32)
    result = (residual_f + (branch + b_out + b_down)).astype(BF16)
    centre = jnp.mean(residual_f, axis=-1, keepdims=True)
    off = residual_f - centre
    scale = lax.rsqrt(jnp.mean(off * off, axis=-1, keepdims=True) + eps)
    xh_own = off * scale
    grad_residual = g_own.astype(F32) + scale * (
        grad_norm
        - jnp.mean(grad_norm, axis=-1, keepdims=True)
        - xh_own * jnp.mean(grad_norm * xh_own, axis=-1, keepdims=True)
    )
    return (
        result,
        grad_residual,
        common[2],
        common[3],
        common[4],
        common[5],
        grad_qkv,
        grad_b_qkv,
        grad_out_w.T,
        common[1],
        grad_up,
        grad_b_up[0],
        grad_down.T,
        common[1],
    )


def solution(mesh):
    return jax.shard_map(
        per_device,
        mesh=mesh,
        in_specs=(
            P(("dp", "tensor"), None),
            P(("dp", "tensor"), None),
            P("dp", None),
            P(),
            P(),
            P(),
            P(),
            P(None, "dp", "tensor"),
            P(None, "tensor"),
            P("tensor", "dp"),
            P(),
            P("dp", "tensor"),
            P("tensor"),
            P("tensor", "dp"),
            P(),
        ),
        out_specs=(
            P(("dp", "tensor"), None),
            P(("dp", "tensor"), None),
            P(),
            P(),
            P(),
            P(),
            P(None, "dp", "tensor"),
            P(None, "tensor"),
            P("tensor", "dp"),
            P(),
            P("dp", "tensor"),
            P("tensor"),
            P("tensor", "dp"),
            P(),
        ),
        check_vma=False,
    )
```

time: 180 us -> 156 us (0.87); the launches traced: 177 us -> 155 us
  other arithmetic: 18.1 us -> 7.24 us
  starting transfers between devices: 58 us -> 47.3 us
  local copies, waits for them, and re-layouts: 16.6 us -> 7.28 us
  waiting for transfers between devices: 59.5 us -> 65.7 us
  Pallas kernels: 22.5 us -> 26.6 us
    ppermute x12 -> x8, waiting for transfers between devices: 35.8 us -> 18.8 us  [to_level(): return lax.ppermute(x, 'dp', [(j, j ^ m * PLANE) for j in range(places)])]
    ppermute x12 -> x8, starting transfers between devices: 37.8 us -> 21.6 us  [to_level(): return lax.ppermute(x, 'dp', [(j, j ^ m * PLANE) for j in range(places)])]
    ppermute x15 -> x11, waiting for transfers between devices: 23.7 us -> 36.3 us  [to_plane(): return lax.ppermute(x, 'dp', [(j, j ^ k) for j in range(places)])]
    ppermute x0 -> x4, waiting for transfers between devices: none -> 10.7 us  [to_pass(): lax.ppermute(x, 'dp', [(a * PLANE + j, b * PLANE + j) for a, b in pairs f...]
    ppermute x0 -> x4, starting transfers between devices: none -> 9.81 us  [to_pass(): lax.ppermute(x, 'dp', [(a * PLANE + j, b * PLANE + j) for a, b in pairs f...]
    ppermute x15 -> x11, starting transfers between devices: 20.1 us -> 15.3 us  [to_plane(): return lax.ppermute(x, 'dp', [(j, j ^ k) for j in range(places)])]
    pallas_call x3 -> x6, Pallas kernels: 22.5 us -> 26.6 us  [kernel_call(): pl.pallas_call(body, out_shape=out_shapes, in_specs=[smem] * in_smem + [v...]
    concatenate x12 -> x2, other arithmetic: 4.67 us -> 1.07 us  [the longest x1 1.05 us: per_device(): message = jnp.concatenate([residual, cotangent, notes], axis=0)]
  transfers between devices with their start and end apart: 30 -> 27, of which waited for: 15 -> 13; matrix products, arithmetic and copies ran while one was open for 14% -> 4% of each run, Pallas kernels for 6% -> 9%
where the time goes in v2:
time: 156 us; the launch traced here: 155 us
  waiting for transfers between devices  65.7 us (42%)
  starting transfers between devices  47.3 us (30%)
  Pallas kernels  26.6 us (17%)
  local copies, waits for them, and re-layouts  7.28 us (5%)
  other arithmetic  7.24 us (5%)
    ppermute x11, waiting for transfers between devices, to_plane(): return lax.ppermute(x, 'dp', [(j, j ^ k) for j in range(places)])  36.3 us
    pallas_call x6, Pallas kernels, kernel_call(): pl.pallas_call(body, out_shape=out_shapes, in_specs=[smem] * in_smem + [v...  26.6 us
    ppermute x8, starting transfers between devices, to_level(): return lax.ppermute(x, 'dp', [(j, j ^ m * PLANE) for j in range(places)])  21.6 us
    ppermute x8, waiting for transfers between devices, to_level(): return lax.ppermute(x, 'dp', [(j, j ^ m * PLANE) for j in range(places)])  18.8 us
    ppermute x11, starting transfers between devices, to_plane(): return lax.ppermute(x, 'dp', [(j, j ^ k) for j in range(places)])  15.3 us
    ppermute x4, waiting for transfers between devices, to_pass(): lax.ppermute(x, 'dp', [(a * PLANE + j, b * PLANE + j) for a, b in pairs f...  10.7 us
    ppermute x4, starting transfers between devices, to_pass(): lax.ppermute(x, 'dp', [(a * PLANE + j, b * PLANE + j) for a, b in pairs f...  9.81 us
    unnamed x51, local copies, waits for them, and re-layouts  5.62 us
  transfers between devices with their start and end apart: 27, of which 13 were waited for; matrix products, arithmetic and copies ran while one was open for 4% of the time, Pallas kernels for 9%

profile of v2, /device:TPU:0, one launch (start us, length us, event | category | flops | bytes accessed | tf_op | source)
XLA Modules:
  0.0 155.2 jit_solution(12150137512237865579)
XLA Ops:
  0.7 0.7 convert_element_type.53
  1.4 1.0 fusion.5
  2.5 0.9 copy-done.3
  3.4 0.9 copy-done.4
  4.3 0.9 copy-done.5
  5.2 0.8 copy-done.6
  6.0 0.6 shard_map.281
  6.6 3.0 %collective-permute-start = (bf16[272,768]{1,0:T(8,128)(2,1)S(1)}, bf16[272,768]{1,0:T(8,128)(2,1)S(1)}, u32[]{:S(2)}, u32[]{:S(2)}) collective-permute-start(bf16[272,768]{1,0:T(8,128)(2,1)S(1)} %fusion.5), channel_id=1, source_target_pairs={{0,2},{2,0},{4,6},{6,4},{8,10},{10,8},{12,14},{14,12},{16,18},{18,... | collective-permute-start | bytes 1253384 | tf_op jit(solution)/shard_map/ppermute | solution.py:351
  9.7 9.6 %collective-permute-done = bf16[272,768]{1,0:T(8,128)(2,1)S(1)} collective-permute-done((bf16[272,768]{1,0:T(8,128)(2,1)S(1)}, bf16[272,768]{1,0:T(8,128)(2,1)S(1)}, u32[]{:S(2)}, u32[]{:S(2)}) %collective-permute-start) | collective-permute-done | bytes 417824 | tf_op jit(solution)/shard_map/ppermute | solution.py:351
  19.3 1.8 %collective-permute-start.1 = (bf16[544,768]{1,0:T(8,128)(2,1)S(1)}, bf16[544,768]{1,0:T(8,128)(2,1)}, u32[]{:S(2)}, u32[]{:S(2)}) collective-permute-start(bf16[544,768]{1,0:T(8,128)(2,1)S(1)} %constant_dynamic-update-slice_fusion.refs_0_), channel_id=1, source_target_pairs={{0,4},{2,6},{4,0},{6,2},{8,12},{10,14},{12,8},{14,10},{16,20},{18,... | collective-permute-start | bytes 2506760 | tf_op jit(solution)/shard_map/ppermute | solution.py:351
  21.1 1.5 collective-permute-start.4
  23.1 1.5 collective-permute-start.6
  24.6 2.6 %collective-permute-done.4 = bf16[48,1280]{1,0:T(8,128)(2,1)S(1)} collective-permute-done((bf16[48,1280]{1,0:T(8,128)(2,1)S(1)}, bf16[48,1280]{1,0:T(8,128)(2,1)S(1)}, u32[]{:S(2)}, u32[]{:S(2)}) %collective-permute-start.4) | collective-permute-done | bytes 122912 | tf_op jit(solution)/shard_map/ppermute | solution.py:351
  27.2 17.2 %collective-permute-done.5 = bf16[48,1280]{1,0:T(8,128)(2,1)S(1)} collective-permute-done((bf16[48,1280]{1,0:T(8,128)(2,1)S(1)}, bf16[48,1280]{1,0:T(8,128)(2,1)S(1)}, u32[]{:S(2)}, u32[]{:S(2)}) %collective-permute-start.5) | collective-permute-done | bytes 122912 | tf_op jit(solution)/shard_map/ppermute | solution.py:351
  45.0 3.6 %collective-permute-start.8 = (bf16[192,512]{1,0:T(8,128)(2,1)S(1)}, bf16[192,512]{1,0:T(8,128)(2,1)S(1)}, u32[]{:S(2)}, u32[]{:S(2)}) collective-permute-start(bf16[192,512]{1,0:T(8,128)(2,1)S(1)} %slice.58.refs_8_), channel_id=1, source_target_pairs={{0,24},{2,26},{4,28},{6,30},{8,16},{10,18},{12,20},{14,22},{16,8},... | collective-permute-start | bytes 589832 | tf_op jit(solution)/shard_map/ppermute | solution.py:354
  48.6 5.2 %collective-permute-done.8.refs_11_ = bf16[192,512]{1,0:T(8,128)(2,1)S(1)} collective-permute-done((bf16[192,512]{1,0:T(8,128)(2,1)S(1)}, bf16[192,512]{1,0:T(8,128)(2,1)S(1)}, u32[]{:S(2)}, u32[]{:S(2)}) %collective-permute-start.8) | collective-permute-done | bytes 196640 | tf_op jit(solution)/shard_map/ppermute | solution.py:354
  53.9 3.5 %collective-permute-start.12 = (bf16[192,768]{1,0:T(8,128)(2,1)S(1)}, bf16[192,768]{1,0:T(8,128)(2,1)S(1)}, u32[]{:S(2)}, u32[]{:S(2)}) collective-permute-start(bf16[192,768]{1,0:T(8,128)(2,1)S(1)} %slice.59.refs_12_), channel_id=1, source_target_pairs={{0,24},{2,26},{4,28},{6,30},{8,16},{10,18},{12,20},{14,22},{16,8},... | collective-permute-start | bytes 884744 | tf_op jit(solution)/shard_map/ppermute | solution.py:354
  57.5 0.8 dynamic_slice.7
  58.3 1.9 %collective-permute-start.7 = (bf16[192,512]{1,0:T(8,128)(2,1)S(1)}, bf16[192,512]{1,0:T(8,128)(2,1)S(1)}, u32[]{:S(2)}, u32[]{:S(2)}) collective-permute-start(bf16[192,512]{1,0:T(8,128)(2,1)S(1)} %slice.58.refs_8_), channel_id=1, source_target_pairs={{0,8},{2,10},{4,12},{6,14},{8,0},{10,2},{12,4},{14,6},{16,24},{18,... | collective-permute-start | bytes 589832 | tf_op jit(solution)/shard_map/ppermute | solution.py:354
  60.4 5.2 %collective-permute-done.12.refs_15_ = bf16[192,768]{1,0:T(8,128)(2,1)S(1)} collective-permute-done((bf16[192,768]{1,0:T(8,128)(2,1)S(1)}, bf16[192,768]{1,0:T(8,128)(2,1)S(1)}, u32[]{:S(2)}, u32[]{:S(2)}) %collective-permute-start.12) | collective-permute-done | bytes 294944 | tf_op jit(solution)/shard_map/ppermute | solution.py:354
  65.6 7.1 %collective-permute-start.9 = (bf16[192,512]{1,0:T(8,128)(2,1)S(1)}, bf16[192,512]{1,0:T(8,128)(2,1)S(1)}, u32[]{:S(2)}, u32[]{:S(2)}) collective-permute-start(bf16[192,512]{1,0:T(8,128)(2,1)S(1)} %broadcast_select_fusion.1), channel_id=1, source_target_pairs={{0,16},{2,18},{4,20},{6,22},{24,8},{26,10},{28,12},{30,14},{8,0},{... | collective-permute-start | bytes 589832 | tf_op jit(solution)/shard_map/ppermute | solution.py:364
  72.9 5.7 %shard_map.282 = (bf16[1024,768]{1,0:T(8,128)(2,1)S(1)}, bf16[1024,768]{1,0:T(8,128)(2,1)}, bf16[1024,768]{1,0:T(8,128)(2,1)}, bf16[1024,768]{1,0:T(8,128)(2,1)}...) custom-call(s32[1]{0:T(128)} %bitcast.3.half_ref.refs_1_, ...), custom_call_target="tpu_custom_call" | custom-call | flops 5000000000 | bytes 1 | tf_op jit(solution)/shard_map/pallas_call | solution.py:306
  78.7 8.0 %shard_map.283 = (bf16[1024,128]{1,0:T(8,128)(2,1)S(1)}, bf16[1024,384]{1,0:T(8,128)(2,1)S(1)}, bf16[768,512]{1,0:T(8,128)(2,1)S(1)}, f32[1,384]{1,0:T(1,128)S(1...) custom-call(s32[2]{0:T(128)S(1)} %pad_add_fusion.place_ref.refs_0_, ...), custom_call_target="tpu_custom_call" | custom-call | flops 8000000000 | bytes 1 | tf_op jit(solution)/shard_map/pallas_call | solution.py:306
  86.7 0.7 copy-done.12
  87.4 10.5 %shard_map.284 = (bf16[2,4,128,768]{3,2,1,0:T(8,128)(2,1)S(1)}, bf16[2,4,128,768]{3,2,1,0:T(8,128)(2,1)}, f32[16,768]{1,0:T(8,128)}, bf16[208,768]{1,0:T(8,128)(...) custom-call(s32[2]{0:T(128)S(1)} %pad_add_fusion.place_ref.refs_0_, ...), custom_call_target="tpu_custom_call" | custom-call | flops 10499999744 | bytes 1 | tf_op jit(solution)/shard_map/pallas_call | solution.py:306
  97.9 0.7 copy-done.10
  98.6 1.0 convert_reduce_fusion
  99.6 1.9 %collective-permute-start.14 = (bf16[192,512]{1,0:T(8,128)(2,1)}, bf16[192,512]{1,0:T(8,128)(2,1)S(1)}, u32[]{:S(2)}, u32[]{:S(2)}) collective-permute-start(bf16[192,512]{1,0:T(8,128)(2,1)} %copy-done.2), channel_id=1, source_target_pairs={{16,0},{18,2},{20,4},{22,6},{8,24},{10,26},{12,28},{14,30},{0,8},{... | collective-permute-start | bytes 589832 | tf_op jit(solution)/shard_map/ppermute | solution.py:364
  101.6 2.2 %collective-permute-start.10 = (bf16[192,512]{1,0:T(8,128)(2,1)}, bf16[192,512]{1,0:T(8,128)(2,1)S(1)}, u32[]{:S(2)}, u32[]{:S(2)}) collective-permute-start(bf16[192,512]{1,0:T(8,128)(2,1)} %copy-done.1), channel_id=1, source_target_pairs={{0,8},{2,10},{4,12},{6,14},{8,0},{10,2},{12,4},{14,6},{16,24},{18,... | collective-permute-start | bytes 589832 | tf_op jit(solution)/shard_map/ppermute | solution.py:354
  103.7 5.0 %collective-permute-done.14.refs_2_ = bf16[192,512]{1,0:T(8,128)(2,1)S(1)} collective-permute-done((bf16[192,512]{1,0:T(8,128)(2,1)}, bf16[192,512]{1,0:T(8,128)(2,1)S(1)}, u32[]{:S(2)}, u32[]{:S(2)}) %collective-permute-start.14) | collective-permute-done | bytes 196640 | tf_op jit(solution)/shard_map/ppermute | solution.py:364
  108.7 0.7 collective-permute-start.15
  109.6 2.8 %collective-permute-start.17 = (bf16[192,512]{1,0:T(8,128)(2,1)S(1)}, bf16[192,512]{1,0:T(8,128)(2,1)S(1)}, u32[]{:S(2)}, u32[]{:S(2)}) collective-permute-start(bf16[192,512]{1,0:T(8,128)(2,1)S(1)} %add_convert_fusion.2), channel_id=1, source_target_pairs={{0,24},{2,26},{4,28},{6,30},{8,16},{10,18},{12,20},{14,22},{16,8},... | collective-permute-start | bytes 589832 | tf_op jit(solution)/shard_map/ppermute | solution.py:354
  112.5 1.8 %add_convert_fusion = bf16[2,4,128,768]{3,2,1,0:T(8,128)(2,1)S(1)} fusion(bf16[2,4,128,768]{3,2,1,0:T(8,128)(2,1)} %collective-permute-done.16, bf16[2,4,128,768]{3,2,1,0:T(8,128)(2,1)S(1)} %get-tuple-element.96), kind=kLoop, calls=%fused_computation | loop fusion | flops 3145728 | bytes 4718592 | tf_op jit(solution)/shard_map/convert_element_type | solution.py:450
  114.5 5.6 %collective-permute-done.15.refs_6_ = bf16[208,768]{1,0:T(8,128)(2,1)S(1)} collective-permute-done((bf16[208,768]{1,0:T(8,128)(2,1)S(1)}, bf16[208,768]{1,0:T(8,128)(2,1)S(1)}, u32[]{:S(2)}, u32[]{:S(2)}) %collective-permute-start.15) | collective-permute-done | bytes 319520 | tf_op jit(solution)/shard_map/ppermute | solution.py:364
  120.2 7.3 %collective-permute-start.19 = (bf16[224,768]{1,0:T(8,128)(2,1)S(1)}, bf16[224,768]{1,0:T(8,128)(2,1)S(1)}, u32[]{:S(2)}, u32[]{:S(2)}) collective-permute-start(bf16[224,768]{1,0:T(8,128)(2,1)S(1)} %pad_maximum_fusion), channel_id=1, source_target_pairs={{0,24},{2,26},{4,28},{6,30},{8,16},{10,18},{12,20},{14,22},{16,8},... | collective-permute-start | bytes 1032200 | tf_op jit(solution)/shard_map/ppermute | solution.py:354
  127.5 1.5 collective-permute-start.20
  129.0 1.5 collective-permute-start.21
  131.2 8.3 %collective-permute-done.19.refs_7_ = bf16[224,768]{1,0:T(8,128)(2,1)S(1)} collective-permute-done((bf16[224,768]{1,0:T(8,128)(2,1)S(1)}, bf16[224,768]{1,0:T(8,128)(2,1)S(1)}, u32[]{:S(2)}, u32[]{:S(2)}) %collective-permute-start.19) | collective-permute-done | bytes 344096 | tf_op jit(solution)/shard_map/ppermute | solution.py:354
  139.8 1.5 collective-permute-done.21
  141.3 1.2 collective-permute-start.23
  142.5 1.8 %collective-permute-start.24 = (bf16[64,1280]{1,0:T(8,128)(2,1)S(1)}, bf16[64,1280]{1,0:T(8,128)(2,1)S(1)}, u32[]{:S(2)}, u32[]{:S(2)}) collective-permute-start(bf16[64,1280]{1,0:T(8,128)(2,1)S(1)} %get-tuple-element.119), channel_id=1, source_target_pairs={{0,4},{2,6},{4,0},{6,2},{8,12},{10,14},{12,8},{14,10},{16,20},{18,... | collective-permute-start | bytes 491528 | tf_op jit(solution)/shard_map/ppermute | solution.py:351
  145.4 2.7 %collective-permute-done.23.refs_1_ = bf16[64,1280]{1,0:T(8,128)(2,1)S(1)} collective-permute-done((bf16[64,1280]{1,0:T(8,128)(2,1)S(1)}, bf16[64,1280]{1,0:T(8,128)(2,1)S(1)}, u32[]{:S(2)}, u32[]{:S(2)}) %collective-permute-start.23) | collective-permute-done | bytes 163872 | tf_op jit(solution)/shard_map/ppermute | solution.py:351
  148.1 1.5 collective-permute-done.24.refs_2_
  149.6 1.2 collective-permute-done.25.refs_3_
  150.8 1.5 shard_map.286
  152.3 1.0 fusion.9
  153.3 0.6 reduce.6
  153.9 0.6 slice_reduce_fusion.1
  (99 shorter events, 4.9 us)
Async XLA Ops:
  0.6 56.8 %copy-start = (f32[3,384]{1,0:T(4,128)S(1)}, f32[3,384]{1,0:T(4,128)}, u32[]{:S(2)}) copy-start(f32[3,384]{1,0:T(4,128)} %param.26) | copy-start | bytes 13828
  2.5 0.9 copy-start.3
  3.4 0.9 copy-start.4
  4.3 0.9 copy-start.5
  5.2 0.8 copy-start.6
  6.6 12.6 %collective-permute-start = (bf16[272,768]{1,0:T(8,128)(2,1)S(1)}, bf16[272,768]{1,0:T(8,128)(2,1)S(1)}, u32[]{:S(2)}, u32[]{:S(2)}) collective-permute-start(bf16[272,768]{1,0:T(8,128)(2,1)S(1)} %fusion.5), channel_id=1, source_target_pairs={{0,2},{2,0},{4,6},{6,4},{8,10},{10,8},{12,14},{14,12},{16,18},{18,... | collective-permute-start | bytes 1253384 | tf_op jit(solution)/shard_map/ppermute | solution.py:351
  9.6 47.8 %copy-start.18 = (f32[768]{0:T(1024)S(1)}, f32[768]{0:T(1024)}, u32[]{:S(2)}) copy-start(f32[768]{0:T(1024)} %param.21) | copy-start | bytes 9220
  9.6 47.8 %copy-start.19 = (f32[768]{0:T(1024)S(1)}, f32[768]{0:T(1024)}, u32[]{:S(2)}) copy-start(f32[768]{0:T(1024)} %param.22) | copy-start | bytes 9220
  9.6 47.8 %copy-start.20 = (f32[768]{0:T(1024)S(1)}, f32[768]{0:T(1024)}, u32[]{:S(2)}) copy-start(f32[768]{0:T(1024)} %param.23) | copy-start | bytes 9220
  9.6 47.8 %copy-start.21 = (f32[768]{0:T(1024)S(1)}, f32[768]{0:T(1024)}, u32[]{:S(2)}) copy-start(f32[768]{0:T(1024)} %param.24) | copy-start | bytes 9220
  19.3 25.2 %collective-permute-start.1 = (bf16[544,768]{1,0:T(8,128)(2,1)S(1)}, bf16[544,768]{1,0:T(8,128)(2,1)}, u32[]{:S(2)}, u32[]{:S(2)}) collective-permute-start(bf16[544,768]{1,0:T(8,128)(2,1)S(1)} %constant_dynamic-update-slice_fusion.refs_0_), channel_id=1, source_target_pairs={{0,4},{2,6},{4,0},{6,2},{8,12},{10,14},{12,8},{14,10},{16,20},{18,... | collective-permute-start | bytes 2506760 | tf_op jit(solution)/shard_map/ppermute | solution.py:351
  21.1 6.1 %collective-permute-start.4 = (bf16[48,1280]{1,0:T(8,128)(2,1)S(1)}, bf16[48,1280]{1,0:T(8,128)(2,1)S(1)}, u32[]{:S(2)}, u32[]{:S(2)}) collective-permute-start(bf16[48,1280]{1,0:T(8,128)(2,1)S(1)} %get-tuple-element.72), channel_id=1, source_target_pairs={{0,2},{2,0},{4,6},{6,4},{8,10},{10,8},{12,14},{14,12},{16,18},{18,... | collective-permute-start | bytes 368648 | tf_op jit(solution)/shard_map/ppermute | solution.py:351
  22.6 21.8 %collective-permute-start.5 = (bf16[48,1280]{1,0:T(8,128)(2,1)S(1)}, bf16[48,1280]{1,0:T(8,128)(2,1)S(1)}, u32[]{:S(2)}, u32[]{:S(2)}) collective-permute-start(bf16[48,1280]{1,0:T(8,128)(2,1)S(1)} %get-tuple-element.73), channel_id=1, source_target_pairs={{0,4},{2,6},{4,0},{6,2},{8,12},{10,14},{12,8},{14,10},{16,20},{18,... | collective-permute-start | bytes 368648 | tf_op jit(solution)/shard_map/ppermute | solution.py:351
  23.1 21.9 %collective-permute-start.6 = (bf16[48,1280]{1,0:T(8,128)(2,1)S(1)}, bf16[48,1280]{1,0:T(8,128)(2,1)S(1)}, u32[]{:S(2)}, u32[]{:S(2)}) collective-permute-start(bf16[48,1280]{1,0:T(8,128)(2,1)S(1)} %get-tuple-element.74), channel_id=1, source_target_pairs={{0,6},{2,4},{4,2},{6,0},{8,14},{10,12},{12,10},{14,8},{16,22},{18,... | collective-permute-start | bytes 368648 | tf_op jit(solution)/shard_map/ppermute | solution.py:351
  44.4 28.4 %collective-permute-start.2 = (bf16[544,768]{1,0:T(8,128)(2,1)S(1)}, bf16[544,768]{1,0:T(8,128)(2,1)}, u32[]{:S(2)}, u32[]{:S(2)}) collective-permute-start(bf16[544,768]{1,0:T(8,128)(2,1)S(1)} %constant_dynamic-update-slice_fusion.refs_0_), channel_id=1, source_target_pairs={{0,1},{1,0},{2,3},{3,2},{4,5},{5,4},{6,7},{7,6},{8,9},{9,8},{10,11... | collective-permute-start | bytes 2506760 | tf_op jit(solution)/shard_map/ppermute | solution.py:357
  44.5 28.4 %collective-permute-start.3 = (bf16[544,768]{1,0:T(8,128)(2,1)}, bf16[544,768]{1,0:T(8,128)(2,1)}, u32[]{:S(2)}, u32[]{:S(2)}) collective-permute-start(bf16[544,768]{1,0:T(8,128)(2,1)} %collective-permute-done.1.refs_1_), channel_id=1, source_target_pairs={{0,1},{1,0},{2,3},{3,2},{4,5},{5,4},{6,7},{7,6},{8,9},{9,8},{10,11... | collective-permute-start | bytes 2506760 | tf_op jit(solution)/shard_map/ppermute | solution.py:357
  45.0 8.9 %collective-permute-start.8 = (bf16[192,512]{1,0:T(8,128)(2,1)S(1)}, bf16[192,512]{1,0:T(8,128)(2,1)S(1)}, u32[]{:S(2)}, u32[]{:S(2)}) collective-permute-start(bf16[192,512]{1,0:T(8,128)(2,1)S(1)} %slice.58.refs_8_), channel_id=1, source_target_pairs={{0,24},{2,26},{4,28},{6,30},{8,16},{10,18},{12,20},{14,22},{16,8},... | collective-permute-start | bytes 589832 | tf_op jit(solution)/shard_map/ppermute | solution.py:354
  53.9 11.8 %collective-permute-start.12 = (bf16[192,768]{1,0:T(8,128)(2,1)S(1)}, bf16[192,768]{1,0:T(8,128)(2,1)S(1)}, u32[]{:S(2)}, u32[]{:S(2)}) collective-permute-start(bf16[192,768]{1,0:T(8,128)(2,1)S(1)} %slice.59.refs_12_), channel_id=1, source_target_pairs={{0,24},{2,26},{4,28},{6,30},{8,16},{10,18},{12,20},{14,22},{16,8},... | collective-permute-start | bytes 884744 | tf_op jit(solution)/shard_map/ppermute | solution.py:354
  58.3 20.3 %collective-permute-start.7 = (bf16[192,512]{1,0:T(8,128)(2,1)S(1)}, bf16[192,512]{1,0:T(8,128)(2,1)S(1)}, u32[]{:S(2)}, u32[]{:S(2)}) collective-permute-start(bf16[192,512]{1,0:T(8,128)(2,1)S(1)} %slice.58.refs_8_), channel_id=1, source_target_pairs={{0,8},{2,10},{4,12},{6,14},{8,0},{10,2},{12,4},{14,6},{16,24},{18,... | collective-permute-start | bytes 589832 | tf_op jit(solution)/shard_map/ppermute | solution.py:354
  60.2 27.1 %collective-permute-start.11 = (bf16[192,768]{1,0:T(8,128)(2,1)S(1)}, bf16[192,768]{1,0:T(8,128)(2,1)S(1)}, u32[]{:S(2)}, u32[]{:S(2)}) collective-permute-start(bf16[192,768]{1,0:T(8,128)(2,1)S(1)} %slice.59.refs_12_), channel_id=1, source_target_pairs={{0,8},{2,10},{4,12},{6,14},{8,0},{10,2},{12,4},{14,6},{16,24},{18,... | collective-permute-start | bytes 884744 | tf_op jit(solution)/shard_map/ppermute | solution.py:354
  65.6 13.0 %collective-permute-start.9 = (bf16[192,512]{1,0:T(8,128)(2,1)S(1)}, bf16[192,512]{1,0:T(8,128)(2,1)S(1)}, u32[]{:S(2)}, u32[]{:S(2)}) collective-permute-start(bf16[192,512]{1,0:T(8,128)(2,1)S(1)} %broadcast_select_fusion.1), channel_id=1, source_target_pairs={{0,16},{2,18},{4,20},{6,22},{24,8},{26,10},{28,12},{30,14},{8,0},{... | collective-permute-start | bytes 589832 | tf_op jit(solution)/shard_map/ppermute | solution.py:364
  72.8 14.6 %collective-permute-start.13 = (bf16[192,768]{1,0:T(8,128)(2,1)S(1)}, bf16[192,768]{1,0:T(8,128)(2,1)S(1)}, u32[]{:S(2)}, u32[]{:S(2)}) collective-permute-start(bf16[192,768]{1,0:T(8,128)(2,1)S(1)} %broadcast_select_fusion), channel_id=1, source_target_pairs={{0,16},{2,18},{4,20},{6,22},{24,8},{26,10},{28,12},{30,14},{8,0},{... | collective-permute-start | bytes 884744 | tf_op jit(solution)/shard_map/ppermute | solution.py:364
  72.8 5.9 %copy-start.7 = (f32[256,128]{1,0:T(8,128)S(1)}, f32[256,128]{1,0:T(8,128)}, u32[]{:S(2)}) copy-start(f32[256,128]{1,0:T(8,128)} %constant.62.clone.refs_5_) | copy-start | bytes 393220
  72.8 5.8 %copy-start.8 = (f32[256,128]{1,0:T(8,128)S(1)}, f32[256,128]{1,0:T(8,128)}, u32[]{:S(2)}) copy-start(f32[256,128]{1,0:T(8,128)} %constant.63.clone.refs_6_) | copy-start | bytes 393220
  72.9 5.8 %copy-start.9 = (f32[256,128]{1,0:T(8,128)S(1)}, f32[256,128]{1,0:T(8,128)}, u32[]{:S(2)}) copy-start(f32[256,128]{1,0:T(8,128)} %constant.64.clone.refs_7_) | copy-start | bytes 393220
  86.7 0.7 copy-start.12
  87.4 10.5 %copy-start.1 = (bf16[192,512]{1,0:T(8,128)(2,1)}, bf16[192,512]{1,0:T(8,128)(2,1)S(1)}, u32[]{:S(2)}) copy-start(bf16[192,512]{1,0:T(8,128)(2,1)S(1)} %get-tuple-element.80) | copy-start | bytes 589828
  87.4 10.5 %copy-start.2 = (bf16[192,512]{1,0:T(8,128)(2,1)}, bf16[192,512]{1,0:T(8,128)(2,1)S(1)}, u32[]{:S(2)}) copy-start(bf16[192,512]{1,0:T(8,128)(2,1)S(1)} %get-tuple-element.93) | copy-start | bytes 589828
  97.9 0.7 copy-start.10
  98.6 13.9 %collective-permute-start.16 = (bf16[2,4,128,768]{3,2,1,0:T(8,128)(2,1)}, bf16[2,4,128,768]{3,2,1,0:T(8,128)(2,1)}, u32[]{:S(2)}, u32[]{:S(2)}) collective-permute-start(bf16[2,4,128,768]{3,2,1,0:T(8,128)(2,1)} %get-tuple-element.97), channel_id=1, source_target_pairs={{0,1},{1,0},{2,3},{3,2},{4,5},{5,4},{6,7},{7,6},{8,9},{9,8},{10,11... | collective-permute-start | bytes 4718600 | tf_op jit(solution)/shard_map/ppermute | solution.py:357
  99.6 9.1 %collective-permute-start.14 = (bf16[192,512]{1,0:T(8,128)(2,1)}, bf16[192,512]{1,0:T(8,128)(2,1)S(1)}, u32[]{:S(2)}, u32[]{:S(2)}) collective-permute-start(bf16[192,512]{1,0:T(8,128)(2,1)} %copy-done.2), channel_id=1, source_target_pairs={{16,0},{18,2},{20,4},{22,6},{8,24},{10,26},{12,28},{14,30},{0,8},{... | collective-permute-start | bytes 589832 | tf_op jit(solution)/shard_map/ppermute | solution.py:364
  101.6 27.4 %collective-permute-start.10 = (bf16[192,512]{1,0:T(8,128)(2,1)}, bf16[192,512]{1,0:T(8,128)(2,1)S(1)}, u32[]{:S(2)}, u32[]{:S(2)}) collective-permute-start(bf16[192,512]{1,0:T(8,128)(2,1)} %copy-done.1), channel_id=1, source_target_pairs={{0,8},{2,10},{4,12},{6,14},{8,0},{10,2},{12,4},{14,6},{16,24},{18,... | collective-permute-start | bytes 589832 | tf_op jit(solution)/shard_map/ppermute | solution.py:354
  108.7 11.3 %collective-permute-start.15 = (bf16[208,768]{1,0:T(8,128)(2,1)S(1)}, bf16[208,768]{1,0:T(8,128)(2,1)S(1)}, u32[]{:S(2)}, u32[]{:S(2)}) collective-permute-start(bf16[208,768]{1,0:T(8,128)(2,1)S(1)} %get-tuple-element.94), channel_id=1, source_target_pairs={{16,0},{18,2},{20,4},{22,6},{8,24},{10,26},{12,28},{14,30},{0,8},{... | collective-permute-start | bytes 958472 | tf_op jit(solution)/shard_map/ppermute | solution.py:364
  109.6 20.9 %collective-permute-start.17 = (bf16[192,512]{1,0:T(8,128)(2,1)S(1)}, bf16[192,512]{1,0:T(8,128)(2,1)S(1)}, u32[]{:S(2)}, u32[]{:S(2)}) collective-permute-start(bf16[192,512]{1,0:T(8,128)(2,1)S(1)} %add_convert_fusion.2), channel_id=1, source_target_pairs={{0,24},{2,26},{4,28},{6,30},{8,16},{10,18},{12,20},{14,22},{16,8},... | collective-permute-start | bytes 589832 | tf_op jit(solution)/shard_map/ppermute | solution.py:354
  112.4 18.8 %collective-permute-start.18 = (bf16[208,768]{1,0:T(8,128)(2,1)S(1)}, bf16[208,768]{1,0:T(8,128)(2,1)S(1)}, u32[]{:S(2)}, u32[]{:S(2)}) collective-permute-start(bf16[208,768]{1,0:T(8,128)(2,1)S(1)} %get-tuple-element.101), channel_id=1, source_target_pairs={{0,8},{2,10},{4,12},{6,14},{8,0},{10,2},{12,4},{14,6},{16,24},{18,... | collective-permute-start | bytes 958472 | tf_op jit(solution)/shard_map/ppermute | solution.py:354
  114.5 16.5 %copy-start.14 = (bf16[128,768]{1,0:T(8,128)(2,1)S(1)}, bf16[128,768]{1,0:T(8,128)(2,1)}, u32[]{:S(2)}) copy-start(bf16[128,768]{1,0:T(8,128)(2,1)} %param.18) | copy-start | bytes 589828
  114.5 25.0 %copy-start.11 = (bf16[208,768]{1,0:T(8,128)(2,1)S(1)}, bf16[208,768]{1,0:T(8,128)(2,1)}, u32[]{:S(2)}) copy-start(bf16[208,768]{1,0:T(8,128)(2,1)} %copy-done.10) | copy-start | bytes 958468
  114.5 25.0 %copy-start.13 = (bf16[192,512]{1,0:T(8,128)(2,1)S(1)}, bf16[192,512]{1,0:T(8,128)(2,1)}, u32[]{:S(2)}) copy-start(bf16[192,512]{1,0:T(8,128)(2,1)} %copy-done.12) | copy-start | bytes 589828
  120.2 19.3 %collective-permute-start.19 = (bf16[224,768]{1,0:T(8,128)(2,1)S(1)}, bf16[224,768]{1,0:T(8,128)(2,1)S(1)}, u32[]{:S(2)}, u32[]{:S(2)}) collective-permute-start(bf16[224,768]{1,0:T(8,128)(2,1)S(1)} %pad_maximum_fusion), channel_id=1, source_target_pairs={{0,24},{2,26},{4,28},{6,30},{8,16},{10,18},{12,20},{14,22},{16,8},... | collective-permute-start | bytes 1032200 | tf_op jit(solution)/shard_map/ppermute | solution.py:354
  127.5 12.3 %collective-permute-start.20 = (bf16[2,128,768]{2,1,0:T(8,128)(2,1)S(1)}, bf16[2,128,768]{2,1,0:T(8,128)(2,1)S(1)}, u32[]{:S(2)}, u32[]{:S(2)}) collective-permute-start(bf16[2,128,768]{2,1,0:T(8,128)(2,1)S(1)} %get-tuple-element.109), channel_id=1, source_target_pairs={{0,2},{2,0},{4,6},{6,4},{8,10},{10,8},{12,14},{14,12},{16,18},{18,... | collective-permute-start | bytes 1179656 | tf_op jit(solution)/shard_map/ppermute | solution.py:351
  129.0 12.3 %collective-permute-start.21 = (bf16[2,128,768]{2,1,0:T(8,128)(2,1)S(1)}, bf16[2,128,768]{2,1,0:T(8,128)(2,1)S(1)}, u32[]{:S(2)}, u32[]{:S(2)}) collective-permute-start(bf16[2,128,768]{2,1,0:T(8,128)(2,1)S(1)} %get-tuple-element.110), channel_id=1, source_target_pairs={{0,4},{2,6},{4,0},{6,2},{8,12},{10,14},{12,8},{14,10},{16,20},{18,... | collective-permute-start | bytes 1179656 | tf_op jit(solution)/shard_map/ppermute | solution.py:351
  130.5 10.8 %collective-permute-start.22 = (bf16[2,128,768]{2,1,0:T(8,128)(2,1)S(1)}, bf16[2,128,768]{2,1,0:T(8,128)(2,1)S(1)}, u32[]{:S(2)}, u32[]{:S(2)}) collective-permute-start(bf16[2,128,768]{2,1,0:T(8,128)(2,1)S(1)} %get-tuple-element.111), channel_id=1, source_target_pairs={{0,6},{2,4},{4,2},{6,0},{8,14},{10,12},{12,10},{14,8},{16,22},{18,... | collective-permute-start | bytes 1179656 | tf_op jit(solution)/shard_map/ppermute | solution.py:351
  141.3 6.7 %collective-permute-start.23 = (bf16[64,1280]{1,0:T(8,128)(2,1)S(1)}, bf16[64,1280]{1,0:T(8,128)(2,1)S(1)}, u32[]{:S(2)}, u32[]{:S(2)}) collective-permute-start(bf16[64,1280]{1,0:T(8,128)(2,1)S(1)} %get-tuple-element.118), channel_id=1, source_target_pairs={{0,2},{2,0},{4,6},{6,4},{8,10},{10,8},{12,14},{14,12},{16,18},{18,... | collective-permute-start | bytes 491528 | tf_op jit(solution)/shard_map/ppermute | solution.py:351
  142.5 7.0 %collective-permute-start.24 = (bf16[64,1280]{1,0:T(8,128)(2,1)S(1)}, bf16[64,1280]{1,0:T(8,128)(2,1)S(1)}, u32[]{:S(2)}, u32[]{:S(2)}) collective-permute-start(bf16[64,1280]{1,0:T(8,128)(2,1)S(1)} %get-tuple-element.119), channel_id=1, source_target_pairs={{0,4},{2,6},{4,0},{6,2},{8,12},{10,14},{12,8},{14,10},{16,20},{18,... | collective-permute-start | bytes 491528 | tf_op jit(solution)/shard_map/ppermute | solution.py:351
  144.3 6.5 %collective-permute-start.25 = (bf16[64,1280]{1,0:T(8,128)(2,1)S(1)}, bf16[64,1280]{1,0:T(8,128)(2,1)S(1)}, u32[]{:S(2)}, u32[]{:S(2)}) collective-permute-start(bf16[64,1280]{1,0:T(8,128)(2,1)S(1)} %get-tuple-element.120), channel_id=1, source_target_pairs={{0,6},{2,4},{4,2},{6,0},{8,14},{10,12},{12,10},{14,8},{16,22},{18,... | collective-permute-start | bytes 491528 | tf_op jit(solution)/shard_map/ppermute | solution.py:351
  145.4 7.0 %copy-start.16 = (f32[768]{0:T(1024)S(1)}, f32[768]{0:T(1024)}, u32[]{:S(2)}) copy-start(f32[768]{0:T(1024)} %param.32) | copy-start | bytes 9220
  145.4 7.0 %copy-start.17 = (f32[768]{0:T(1024)S(1)}, f32[768]{0:T(1024)}, u32[]{:S(2)}) copy-start(f32[768]{0:T(1024)} %param.28) | copy-start | bytes 9220
  152.3 1.6 %collective-permute-start.26 = (f32[16,768]{1,0:T(8,128)S(1)}, f32[16,768]{1,0:T(8,128)S(1)}, u32[]{:S(2)}, u32[]{:S(2)}) collective-permute-start(f32[16,768]{1,0:T(8,128)S(1)} %get-tuple-element.121), channel_id=1, source_target_pairs={{0,1},{1,0},{2,3},{3,2},{4,5},{5,4},{6,7},{7,6},{8,9},{9,8},{10,11... | collective-permute-start | bytes 147464 | tf_op jit(solution)/shard_map/ppermute | solution.py:357
  (1 other events, 0.6 us)

commit v3 on v2

v3 whole, which is shorter than its diff:
```python
import math
from functools import partial

import jax
import jax.numpy as jnp
import numpy as np
from jax import lax
from jax.experimental import pallas as pl
from jax.experimental.pallas import tpu as pltpu
from jax.sharding import PartitionSpec as P

HD = 64
ROT = 16
PLANE = 4
BLK = 2 * HD
NOTES = 16
eps = 1e-05
F32 = jnp.float32
BF16 = jnp.bfloat16


def dot(a, b):
    return jnp.dot(a, b, preferred_element_type=F32)


def dot_nt(a, b):
    return lax.dot_general(a, b, (((1,), (1,)), ((), ())), preferred_element_type=F32)


def dot_tn(a, b):
    return lax.dot_general(a, b, (((0,), (0,)), ((), ())), preferred_element_type=F32)


def place():
    index = lax.axis_index("dp")
    return index % PLANE, index // PLANE


def is_inner():
    level = place()[1]
    return (level == 1) | (level == 2)


def xor_sorted(parts, index):
    parts = list(parts)
    bit = 1
    while bit < len(parts):
        swap = (index & bit) != 0
        parts = [jnp.where(swap, parts[j ^ bit], parts[j]) for j in range(len(parts))]
        bit *= 2
    return parts


def tree_sum(parts):
    parts = list(parts)
    while len(parts) > 1:
        parts = [parts[j] + parts[j + 1] for j in range(0, len(parts), 2)]
    return parts[0]


def rotary_tables(rows):
    half = ROT // 2
    inverse = np.float32(10000.0) ** (-np.arange(half, dtype=np.float32) * np.float32(2.0 / ROT))
    angle = np.arange(rows, dtype=np.float32)[:, None] * inverse.astype(np.float32)[None, :]
    cos, sin = np.cos(angle), np.sin(angle)
    rest = np.ones((rows, HD - ROT), np.float32)
    none = np.zeros((rows, half), np.float32)
    keep = np.concatenate([cos, cos, rest], axis=1)
    low = np.concatenate([-sin, none, 0.0 * rest], axis=1)
    high = np.concatenate([none, sin, 0.0 * rest], axis=1)
    return tuple(
        np.concatenate([t] * (BLK // HD), axis=1).astype(np.float32) for t in (keep, low, high)
    )


def share_kernel(*refs):
    whole_refs, share_refs = refs[:4], refs[4 : 4 + PLANE]
    held_refs, arrived = refs[4 + PLANE : -1], refs[-1]
    copies = [
        pltpu.make_async_copy(whole, held, arrived.at[j])
        for j, (whole, held) in enumerate(zip(whole_refs, held_refs))
    ]
    for copy in copies:
        copy.start()
    for copy in copies:
        copy.wait()
    qkv_ref, out_ref, up_ref, down_ref = held_refs
    head_blocks = out_ref.shape[1] // BLK
    width = up_ref.shape[1] // PLANE
    for k in range(PLANE):
        other = place()[0] ^ k
        at = pl.ds(pl.multiple_of(jnp.minimum(other, head_blocks - 1) * BLK, BLK), BLK)
        for c in range(4):
            block = qkv_ref[c, :, at] if c < 3 else out_ref[:, at]
            block = jnp.where(other < head_blocks, block.astype(F32), 0.0)
            share_refs[k][:, c * BLK : (c + 1) * BLK] = block.astype(BF16)
        at = pl.ds(pl.multiple_of(other * width, BLK), width)
        share_refs[k][:, 4 * BLK : 4 * BLK + width] = up_ref[:, at]
        share_refs[k][:, 4 * BLK + width :] = down_ref[:, at]


def rows_at(m, k, owned):
    plane_at, level_at = place()
    return pl.ds(pl.multiple_of(((level_at ^ m) * PLANE + (plane_at ^ k)) * owned, owned), owned)


def rows_kernel(params_ref, own_ref, peer_ref, x1_ref, x2_ref, xh_ref, g_ref, g_own_ref, length_ref, bo_ref):
    half = lax.axis_index("tensor")
    own_rows = g_own_ref.shape[0]
    slots = 2 * own_rows
    params = params_ref[...]
    length_ref[...] = jnp.zeros_like(length_ref)
    for k in range(PLANE):
        start = k * (slots + NOTES)
        length = own_ref[start + slots : start + slots + NOTES, :].astype(F32)
        length = jnp.sum(length[0:1], axis=-1, keepdims=True)
        length_ref[k : k + 1, :] = jnp.broadcast_to(length, (1, length_ref.shape[1]))
        for which, ref in enumerate((own_ref, peer_ref)):
            part = half if which == 0 else 1 - half
            x = ref[start : start + own_rows, :].astype(F32)
            centre = jnp.mean(x, axis=-1, keepdims=True)
            off = x - centre
            spread = jnp.mean(off * off, axis=-1, keepdims=True)
            xh = off * lax.rsqrt(spread + eps)
            at = pl.ds(pl.multiple_of(k * slots + part * own_rows, own_rows), own_rows)
            x1_ref[at, :] = (xh * params[0:1] + params[1:2]).astype(BF16)
            x2_ref[at, :] = (xh * params[2:3] + params[3:4]).astype(BF16)
            xh_ref[at, :] = xh.astype(BF16)
            row = lax.broadcasted_iota(jnp.int32, (own_rows, 1), 0) + part * own_rows
            g = ref[start + own_rows : start + slots, :].astype(F32)
            g = jnp.where(row.astype(F32) < length, g, 0.0)
            g_ref[at, :] = g.astype(BF16)
            if k == 0 and which == 0:
                g_own_ref[...] = g.astype(BF16)
                bo_ref[...] = jnp.sum(g, axis=0, keepdims=True)


def layer_kernel(levels, *refs):
    length_ref, x1_ref, x2_ref, g_ref, bias_ref, bias_up_ref, keep_ref, low_ref, high_ref = refs[:9]
    pieces = refs[9 : 9 + max(2 * levels, 1)]
    att_ref, gp_ref, act_ref, gh_ref, w_ref, gb_ref = refs[9 + len(pieces) : 15 + len(pieces)]
    message_refs, gw_ref = refs[15 + len(pieces) : -1], refs[-1]
    if levels:
        owned = pieces[0].shape[0]
        for m in range(levels):
            w_ref[rows_at(m, 0, owned), :] = pieces[m][...]
            for k in range(1, PLANE):
                w_ref[rows_at(m, k, owned), :] = pieces[levels + m][(k - 1) * owned : k * owned, :]
    else:
        w_ref[...] = pieces[0][...]
        gw_ref = message_refs[0]
    heads, width = 4 * BLK, bias_up_ref.shape[1]
    slots = keep_ref.shape[0]
    keep, low, high = keep_ref[...], low_ref[...], high_ref[...]

    def turn(x, sign):
        return x * keep + sign * (
            pltpu.roll(x, BLK - ROT // 2, 1) * low + pltpu.roll(x, ROT // 2, 1) * high
        )

    lane = lax.broadcasted_iota(jnp.int32, (slots, BLK), 1)
    first = lane < HD
    q_row = lax.broadcasted_iota(jnp.int32, (2 * slots, slots), 0) & (slots - 1)
    k_row = lax.broadcasted_iota(jnp.int32, (2 * slots, slots), 1)

    def stacked(x):
        zero = jnp.zeros_like(x)
        return jnp.concatenate([jnp.where(first, x, zero), jnp.where(first, zero, x)], axis=0)

    def joined(x):
        return jnp.where(first, x[:slots], x[slots:])

    total = jnp.zeros((1, 3 * BLK), F32)
    for k in range(PLANE):
        at = pl.ds(k * slots, slots)
        proj = dot(x1_ref[at, :], w_ref[:, : 3 * BLK]) + bias_ref[...]
        query = stacked((turn(proj[:, :BLK], 1.0) * HD**-0.5).astype(BF16))
        key = turn(proj[:, BLK : 2 * BLK], 1.0).astype(BF16)
        value = proj[:, 2 * BLK :].astype(BF16)
        ga = stacked(dot(g_ref[at, :], w_ref[:, 3 * BLK : heads]).astype(BF16))
        logits = dot_nt(query, key)
        live = k_row.astype(F32) < length_ref[k : k + 1, 0:1]
        allowed = (k_row <= q_row) & (live | (k_row == q_row))
        logits = jnp.where(allowed, logits, -1000000000.0)
        weights = jnp.exp(logits - jnp.max(logits, axis=-1, keepdims=True))
        probs = weights / jnp.sum(weights, axis=-1, keepdims=True)
        rounded = probs.astype(BF16)
        att_ref[at, :] = joined(dot(rounded, value)).astype(BF16)
        grad_probs = dot_nt(ga, value)
        inner = jnp.sum(probs * grad_probs, axis=-1, keepdims=True)
        grad_logits = (probs * (grad_probs - inner)).astype(BF16)
        grad_query = joined(dot(grad_logits, key)) * HD**-0.5
        grad_key = dot_tn(grad_logits, query)
        grad_value = dot_tn(rounded, ga)
        gp = jnp.concatenate([turn(grad_query, -1.0), turn(grad_key, -1.0), grad_value], axis=1).astype(BF16)
        gp_ref[at, :] = gp
        total = total + jnp.sum(gp.astype(F32), axis=0, keepdims=True)
    gb_ref[:, width:] = total
    total = jnp.zeros((1, width), F32)
    for k in range(PLANE):
        at = pl.ds(k * slots, slots)
        hidden = dot(x2_ref[at, :], w_ref[:, heads : heads + width]) + bias_up_ref[...]
        grad_act = dot(g_ref[at, :], w_ref[:, heads + width :])
        part = 0.5 + 0.5 * lax.erf(hidden * (0.5**0.5))
        act_ref[at, :] = (hidden * part).astype(BF16)
        slope = part + hidden * jnp.exp(-0.5 * hidden * hidden) * (2.0 * math.pi) ** -0.5
        gh = (grad_act * slope).astype(BF16)
        gh_ref[at, :] = gh
        total = total + jnp.sum(gh.astype(F32), axis=0, keepdims=True)
    gb_ref[:, :width] = total
    gw_ref[:, : 3 * BLK] = dot_tn(x1_ref[...], gp_ref[...]).astype(BF16)
    gw_ref[:, 3 * BLK : heads] = dot_tn(g_ref[...], att_ref[...]).astype(BF16)
    gw_ref[:, heads : heads + width] = dot_tn(x2_ref[...], gh_ref[...]).astype(BF16)
    gw_ref[:, heads + width :] = dot_tn(g_ref[...], act_ref[...]).astype(BF16)
    if levels:
        for m in range(levels):
            for k in range(PLANE):
                message_refs[m][k * owned : (k + 1) * owned, :] = gw_ref[rows_at(m, k, owned), :]


def products_kernel(
    params_ref, xh_ref, w_ref, act_ref, gh_ref, att_ref, gp_ref, gb_ref, bo_ref, keep_ref, send_ref, stage_ref
):
    half = lax.axis_index("tensor")
    slots = stage_ref.shape[1]
    own_rows = slots // 2
    heads, width = 4 * BLK, act_ref.shape[1]
    params = params_ref[...]
    gain1, gain2 = params[0:1], params[2:3]
    sums = [jnp.zeros((1, xh_ref.shape[1]), F32) for _ in range(4)]
    for k in range(PLANE):
        at = pl.ds(k * slots, slots)
        stage_ref[0] = dot_nt(act_ref[at, :], w_ref[:, heads + width :]) + dot_nt(
            att_ref[at, :], w_ref[:, 3 * BLK : heads]
        )
        g1 = dot_nt(gp_ref[at, :], w_ref[:, : 3 * BLK])
        g2 = dot_nt(gh_ref[at, :], w_ref[:, heads : heads + width])
        stage_ref[1] = gain1 * g1 + gain2 * g2
        xh = xh_ref[at, :].astype(F32)
        for j, term in enumerate((g1 * xh, g1, g2 * xh, g2)):
            sums[j] = sums[j] + jnp.sum(term, axis=0, keepdims=True)
        mine = pl.ds(pl.multiple_of(half * own_rows, own_rows), own_rows)
        other = pl.ds(pl.multiple_of((1 - half) * own_rows, own_rows), own_rows)
        for j in range(2):
            to = pl.ds(k * slots + j * own_rows, own_rows)
            keep_ref[to, :] = stage_ref[j, mine, :].astype(BF16)
            send_ref[to, :] = stage_ref[j, other, :].astype(BF16)
    zero = jnp.zeros((NOTES - 6, xh_ref.shape[1]), F32)
    notes = jnp.concatenate([gb_ref[...], bo_ref[...]] + sums + [zero], axis=0).astype(BF16)
    keep_ref[PLANE * slots :, :] = notes
    send_ref[PLANE * slots :, :] = notes


def pair_kernel(levels, keep_ref, peer_ref, *refs):
    notes_ref, out_refs = refs[-PLANE - 1], refs[-PLANE:]
    slots = out_refs[0].shape[0]
    notes = keep_ref[PLANE * slots :, :].astype(F32)
    row = lax.broadcasted_iota(jnp.int32, notes.shape, 0)
    notes = notes + jnp.where(row == 0, 0.0, peer_ref[PLANE * slots :, :].astype(F32))
    notes = notes.astype(BF16)
    notes_ref[...] = notes
    for k, out_ref in enumerate(out_refs):
        at = pl.ds(k * slots, slots)
        out_ref[...] = (keep_ref[at, :].astype(F32) + peer_ref[at, :].astype(F32)).astype(BF16)
    if levels:
        passed_ref, near_ref, far_ref, to_near_ref, to_far_ref = refs[:5]
        rows, columns = near_ref.shape
        passed = jnp.where(is_inner(), passed_ref[...].astype(F32), 0.0)
        to_near_ref[:rows, :] = near_ref[...]
        to_far_ref[:rows, :] = (far_ref[...].astype(F32) + passed).astype(BF16)
        notes = jnp.concatenate([jnp.zeros((NOTES, columns - notes.shape[1]), BF16), notes], axis=1)
        to_near_ref[rows:, :] = notes
        to_far_ref[rows:, :] = notes


def rows_out_kernel(residual_ref, g_ref, b_out_ref, b_down_ref, *refs):
    part_refs, (result_ref, grad_ref) = refs[:PLANE], refs[PLANE:]
    own_rows = residual_ref.shape[0]
    branch = tree_sum([ref[:own_rows, :].astype(F32) for ref in part_refs])
    x = residual_ref[...].astype(F32)
    result_ref[...] = (x + (branch + b_out_ref[...] + b_down_ref[...])).astype(BF16)
    off = x - jnp.mean(x, axis=-1, keepdims=True)
    scale = lax.rsqrt(jnp.mean(off * off, axis=-1, keepdims=True) + eps)
    xh = off * scale
    grad = tree_sum([ref[own_rows:, :].astype(F32) for ref in part_refs])
    grad = grad - jnp.mean(grad, axis=-1, keepdims=True) - xh * jnp.mean(grad * xh, axis=-1, keepdims=True)
    grad_ref[...] = g_ref[...].astype(F32) + scale * grad


def combine_kernel(own_ref, near_ref, passed_ref, far_ref, notes_ref, notes_middle_ref, *out_refs):
    rows = own_ref.shape[0]
    owned = rows // PLANE
    columns, model = own_ref.shape[1], notes_ref.shape[1]
    passed_here = jnp.logical_not(is_inner())
    own, middle = notes_ref[...].astype(F32), notes_middle_ref[...].astype(F32)
    near, far = [ref[rows:, columns - model :].astype(F32) for ref in (near_ref, far_ref)]
    notes = ((own + near) + (middle + far)).astype(BF16)
    for k, out_ref in enumerate(out_refs):
        at = pl.ds(k * owned, owned)
        total = own_ref[at, :].astype(F32) + near_ref[at, :].astype(F32) + far_ref[at, :].astype(F32)
        total = total + jnp.where(passed_here, passed_ref[at, :].astype(F32), 0.0)
        out_ref[:owned, :] = total.astype(out_ref.dtype)
        out_ref[owned:, : columns - model] = jnp.zeros((NOTES, columns - model), out_ref.dtype)
        out_ref[owned:, columns - model :] = notes.astype(out_ref.dtype)


def owner_kernel(*refs):
    part_refs = refs[:PLANE]
    up_ref, down_ref, qkv_ref, out_ref, b_up_ref, b_qkv_ref, common_ref = refs[PLANE:]
    owned = up_ref.shape[0]
    width = up_ref.shape[1] // PLANE
    head_blocks = out_ref.shape[1] // BLK
    start = 4 * BLK
    for k, part_ref in enumerate(part_refs):
        other = place()[0] ^ k
        at = pl.ds(pl.multiple_of(other * width, BLK), width)
        up_ref[:, at] = part_ref[:owned, start : start + width].astype(F32)
        down_ref[:, at] = part_ref[:owned, start + width :].astype(F32)
        notes = part_ref[owned:, start:].astype(F32)
        b_up_ref[:, at] = notes[0:1, :width]

        @pl.when(other < head_blocks)
        def _():
            at = pl.ds(pl.multiple_of(other * BLK, BLK), BLK)
            for c in range(3):
                qkv_ref[c, :, at] = part_ref[:owned, c * BLK : (c + 1) * BLK].astype(F32)
                b_qkv_ref[c : c + 1, at] = notes[0:1, width + c * BLK : width + (c + 1) * BLK]
            out_ref[:, at] = part_ref[:owned, 3 * BLK : 4 * BLK].astype(F32)

    common_ref[...] = tree_sum([ref[owned:, start:].astype(F32) for ref in part_refs])


def kernel_call(body, out_shapes, operands, scratch=(), micros=1.0, space=pltpu.VMEM, limit=20):
    vmem = pl.BlockSpec(memory_space=pltpu.VMEM)
    taken = pl.BlockSpec(memory_space=space)
    return pl.pallas_call(
        body,
        out_shape=out_shapes,
        in_specs=[taken] * len(operands),
        out_specs=[vmem] * len(out_shapes),
        scratch_shapes=list(scratch),
        compiler_params=pltpu.CompilerParams(vmem_limit_bytes=limit * 2**20),
        cost_estimate=pl.CostEstimate(flops=int(micros * 1e9), bytes_accessed=1, transcendentals=0),
    )(*operands)


def per_device(
    residual,
    cotangent,
    seq_lengths,
    gain_attn,
    shift_attn,
    gain_mlp,
    shift_mlp,
    w_qkv,
    b_qkv,
    w_out,
    b_out,
    w_up,
    b_up,
    w_down,
    b_down,
):
    places = lax.axis_size("dp")
    levels = places // PLANE
    plane_at = place()[0]
    own_rows, model = residual.shape
    slots = 2 * own_rows
    rows_all = PLANE * slots
    owned = w_up.shape[0]
    width = w_up.shape[1] // PLANE
    head_blocks = w_out.shape[0] // BLK
    columns = 4 * BLK + 2 * width
    direct = levels if levels == 4 and owned % 16 == 0 else 0
    level_groups = [[lev * PLANE + j for lev in range(levels)] for j in range(PLANE)]
    shape = jax.ShapeDtypeStruct

    def to_plane(x, k):
        return lax.ppermute(x, "dp", [(j, j ^ k) for j in range(places)])

    def to_level(x, m):
        return lax.ppermute(x, "dp", [(j, j ^ (m * PLANE)) for j in range(places)])

    def to_peer(x):
        return lax.ppermute(x, "tensor", [(0, 1), (1, 0)])

    passing = [(0, 2), (3, 1), (1, 0), (2, 3)]

    def to_pass(x, back=False):
        pairs = [(b, a) if back else (a, b) for a, b in passing]
        return lax.ppermute(x, "dp", [(a * PLANE + j, b * PLANE + j) for a, b in pairs for j in range(PLANE)])

    held = (w_qkv, w_out.T, w_up, w_down.T)
    shares = kernel_call(
        share_kernel,
        [shape((owned, columns), BF16)] * PLANE,
        held,
        scratch=[pltpu.VMEM(a.shape, a.dtype) for a in held] + [pltpu.SemaphoreType.DMA((4,))],
        space=pl.ANY,
        limit=63,
    )
    received = [to_plane(shares[k], k) for k in range(1, PLANE)]
    residual_m, cotangent_m, lengths_m, _ = lax.optimization_barrier((residual, cotangent, seq_lengths, shares))
    notes = jnp.pad(lengths_m.astype(BF16), ((0, NOTES - 1), (0, model - seq_lengths.shape[1])))
    message = jnp.concatenate([residual_m, cotangent_m, notes], axis=0)
    if direct:
        own = shares[0]
        own_near, own_far = to_level(own, 1), to_level(own, 3)
        received, own, own_near, own_far, message = lax.optimization_barrier(
            (received, own, own_near, own_far, message)
        )
        others = jnp.concatenate(received, axis=0)
        near, far = to_level(others, 1), to_level(others, 3)
        own_mid = to_pass(jnp.where(is_inner(), own_far, own))
    messages = [message] + [to_plane(message, k) for k in range(1, PLANE)]
    if direct:
        messages, own_mid, near, far = lax.optimization_barrier((messages, own_mid, near, far))
        mid = to_pass(jnp.where(is_inner(), far, others))
        pieces = [own, own_near, own_mid, own_far, others, near, mid, far]
    else:
        every = jnp.concatenate(xor_sorted([shares[0]] + received, plane_at), axis=0)
        pieces = [lax.all_gather(every, "dp", axis=0, tiled=True, axis_index_groups=level_groups)]
    rows = jnp.concatenate(messages, axis=0)
    params = jnp.stack([gain_attn, shift_attn, gain_mlp, shift_mlp] + [jnp.zeros_like(gain_attn)] * 4)
    x1, x2, xh, g, g_own, lengths, bo = kernel_call(
        rows_kernel,
        [shape((rows_all, model), BF16)] * 4
        + [shape((own_rows, model), BF16), shape((8, 128), F32), shape((1, model), F32)],
        (params, rows, to_peer(rows)),
        micros=4,
    )

    block_at = jnp.minimum(plane_at, head_blocks - 1) * BLK
    bias_heads = lax.dynamic_slice_in_dim(b_qkv, block_at, BLK, 1).reshape(1, 3 * BLK)
    bias_up = lax.dynamic_slice_in_dim(b_up, plane_at * width, width, 0).reshape(1, width)
    att, gp, act, gh, w, gb, *messages = kernel_call(
        partial(layer_kernel, direct),
        [
            shape((rows_all, BLK), BF16),
            shape((rows_all, 3 * BLK), BF16),
            shape((rows_all, width), BF16),
            shape((rows_all, width), BF16),
            shape((model, columns), BF16),
            shape((1, width + 3 * BLK), F32),
        ]
        + [shape((PLANE * owned if direct else model, columns), BF16)] * max(direct, 1),
        (lengths, x1, x2, g, bias_heads, bias_up, *rotary_tables(slots), *pieces),
        scratch=[pltpu.VMEM((model, columns), BF16)],
        micros=12,
        limit=30,
    )
    if direct:
        passed = to_pass(messages[2], back=True)
    keep, send = kernel_call(
        products_kernel,
        [shape((rows_all + NOTES, model), BF16)] * 2,
        (params, xh, w, act, gh, att, gp, gb, bo),
        scratch=[pltpu.VMEM((2, slots, model), F32)],
        micros=4,
    )
    from_peer = to_peer(send)
    extra, extra_shapes = (), []
    if direct:
        passed, from_peer = lax.optimization_barrier((passed, from_peer))
        extra = (passed, messages[1], messages[3])
        extra_shapes = [shape((PLANE * owned + NOTES, columns), BF16)] * 2
    laid = kernel_call(
        partial(pair_kernel, direct),
        extra_shapes + [shape((NOTES, model), BF16)] + [shape((slots, model), BF16)] * PLANE,
        (keep, from_peer, *extra),
        micros=2,
    )

    notes, outgoing = laid[-PLANE - 1], laid[-PLANE:]

    parts = [outgoing[0]] + [to_plane(outgoing[k], k) for k in range(1, PLANE)]
    if direct:
        near, far = to_level(laid[0], 1), to_level(laid[1], 3)
        notes_after, parts[1] = lax.optimization_barrier((notes, parts[1]))
        notes_mid = to_level(notes_after, 2)
        parts, near, far, notes_mid = lax.optimization_barrier((parts, near, far, notes_mid))
        backs = kernel_call(
            combine_kernel,
            [shape((owned + NOTES, columns), F32)] + [shape((owned + NOTES, columns), BF16)] * (PLANE - 1),
            (messages[0], near, passed, far, notes, notes_mid),
        )
    else:
        sums = lax.psum_scatter(
            messages[0], "dp", scatter_dimension=0, tiled=True, axis_index_groups=level_groups
        ).reshape(PLANE, owned, columns)
        notes = lax.all_gather(notes, "dp", axis=0, axis_index_groups=level_groups)
        notes = jnp.sum(notes.astype(F32), axis=0).astype(BF16)
        notes = jnp.concatenate([jnp.zeros((NOTES, columns - model), BF16), notes], axis=1)
        backs = [
            jnp.concatenate([lax.dynamic_index_in_dim(sums, plane_at ^ k, 0, keepdims=False), notes], axis=0)
            for k in range(PLANE)
        ]
    backs = [backs[0]] + [to_plane(backs[k], k) for k in range(1, PLANE)]
    result, grad_residual = kernel_call(
        rows_out_kernel,
        [shape((own_rows, model), BF16), shape((own_rows, model), F32)],
        (residual, g_own, b_out.reshape(1, model), b_down.reshape(1, model), *parts),
    )
    grad_up, grad_down, grad_qkv, grad_out_w, grad_b_up, grad_b_qkv, common = kernel_call(
        owner_kernel,
        [
            shape((owned, PLANE * width), F32),
            shape((owned, PLANE * width), F32),
            shape((3, owned, head_blocks * BLK), F32),
            shape((owned, head_blocks * BLK), F32),
            shape((1, PLANE * width), F32),
            shape((3, head_blocks * BLK), F32),
            shape((NOTES, model), F32),
        ],
        backs,
    )
    return (
        result,
        grad_residual,
        common[2],
        common[3],
        common[4],
        common[5],
        grad_qkv,
        grad_b_qkv,
        grad_out_w.T,
        common[1],
        grad_up,
        grad_b_up[0],
        grad_down.T,
        common[1],
    )


def solution(mesh):
    return jax.shard_map(
        per_device,
        mesh=mesh,
        in_specs=(
            P(("dp", "tensor"), None),
            P(("dp", "tensor"), None),
            P("dp", None),
            P(),
            P(),
            P(),
            P(),
            P(None, "dp", "tensor"),
            P(None, "tensor"),
            P("tensor", "dp"),
            P(),
            P("dp", "tensor"),
            P("tensor"),
            P("tensor", "dp"),
            P(),
        ),
        out_specs=(
            P(("dp", "tensor"), None),
            P(("dp", "tensor"), None),
            P(),
            P(),
            P(),
            P(),
            P(None, "dp", "tensor"),
            P(None, "tensor"),
            P("tensor", "dp"),
            P(),
            P("dp", "tensor"),
            P("tensor"),
            P("tensor", "dp"),
            P(),
        ),
        check_vma=False,
    )
```

time: 156 us -> 123 us (0.79)
  starting transfers between devices: 47.3 us -> 27 us
  other arithmetic: 7.24 us -> 1.63 us
  local copies, waits for them, and re-layouts: 7.28 us -> 2.32 us
  Pallas kernels: 26.6 us -> 23.1 us
    ppermute x4 -> x3, waiting for transfers between devices: 10.7 us -> 26.8 us  [to_pass(): lax.ppermute(x, 'dp', [(a * PLANE + j, b * PLANE + j) for a, b in pairs f...]
    ppermute x11 -> x12, waiting for transfers between devices: 36.3 us -> 21.5 us  [to_plane(): return lax.ppermute(x, 'dp', [(j, j ^ k) for j in range(places)])]
    ppermute x8 -> x7, starting transfers between devices: 21.6 us -> 11.3 us  [to_level(): return lax.ppermute(x, 'dp', [(j, j ^ m * PLANE) for j in range(places)])]
    ppermute x4 -> x3, starting transfers between devices: 9.81 us -> 1.52 us  [to_pass(): lax.ppermute(x, 'dp', [(a * PLANE + j, b * PLANE + j) for a, b in pairs f...]
    unnamed x51 -> x38, local copies, waits for them, and re-layouts: 5.62 us -> 0.8 us
    pallas_call x6 -> x8, Pallas kernels: 26.6 us -> 23.1 us  [kernel_call(): pl.pallas_call(body, out_shape=out_shapes, in_specs=[taken] * len(operand...]
    convert_element_type x3 -> x1, other arithmetic: 2.56 us -> 0.01 us  [per_device(): lengths_m.astype(BF16)]
    ppermute x4 -> x2, waiting for transfers between devices: 0.01 us -> 2.02 us  [to_peer(): return lax.ppermute(x, 'tensor', [(0, 1), (1, 0)])]
  transfers between devices with their start and end apart: 27 -> 24, of which waited for: 13 -> 13; matrix products, arithmetic and copies ran while one was open for 4% -> 2% of each run, Pallas kernels for 9% -> 4%
where the time goes in v3:
time: 123 us; the launch traced here: 122 us
  waiting for transfers between devices  67.2 us (55%)
  starting transfers between devices  27 us (22%)
  Pallas kernels  23.1 us (19%)
  local copies, waits for them, and re-layouts  2.32 us (2%)
  other arithmetic  1.63 us (1%)
    ppermute x3, waiting for transfers between devices, to_pass(): lax.ppermute(x, 'dp', [(a * PLANE + j, b * PLANE + j) for a, b in pairs f...  26.8 us
    pallas_call x8, Pallas kernels, kernel_call(): pl.pallas_call(body, out_shape=out_shapes, in_specs=[taken] * len(operand...  23.1 us
    ppermute x12, waiting for transfers between devices, to_plane(): return lax.ppermute(x, 'dp', [(j, j ^ k) for j in range(places)])  21.5 us
    ppermute x7, waiting for transfers between devices, to_level(): return lax.ppermute(x, 'dp', [(j, j ^ m * PLANE) for j in range(places)])  16.9 us
    ppermute x12, starting transfers between devices, to_plane(): return lax.ppermute(x, 'dp', [(j, j ^ k) for j in range(places)])  14 us
    ppermute x7, starting transfers between devices, to_level(): return lax.ppermute(x, 'dp', [(j, j ^ m * PLANE) for j in range(places)])  11.3 us
  transfers between devices with their start and end apart: 24, of which 13 were waited for; matrix products, arithmetic and copies ran while one was open for 2% of the time, Pallas kernels for 4%

profile of v3, /device:TPU:0, one launch (start us, length us, event | category | flops | bytes accessed | tf_op | source)
XLA Modules:
  0.0 122.3 jit_solution(6794851202854658787)
XLA Ops:
  0.7 2.0 %shard_map.281 = (bf16[48,1280]{1,0:T(8,128)(2,1)}, bf16[48,1280]{1,0:T(8,128)(2,1)}, bf16[48,1280]{1,0:T(8,128)(2,1)}, bf16[48,1280]{1,0:T(8,128)(2,1)}) custom-call(bf16[3,48,384]{2,1,0:T(8,128)(2,1)} %refs_0_.1, bf16[48,384]{1,0:T(8,128)(2,1)} %bitcast.12, bf16[48,1536]{1,0:T(8,128)(2,1)} %refs_2_.1, bf16[48,1536]{1,0:T(8,128)(2,1)} %bitcast.11), custom_call_target="tpu_custom_call" | custom-call | flops 1000000000 | bytes 1 | tf_op jit(solution)/shard_map/pallas_call | solution.py:336
  2.7 3.1 %collective-permute-start.3 = (bf16[48,1280]{1,0:T(8,128)(2,1)}, bf16[48,1280]{1,0:T(8,128)(2,1)S(1)}, u32[]{:S(2)}, u32[]{:S(2)}) collective-permute-start(bf16[48,1280]{1,0:T(8,128)(2,1)} %get-tuple-element.94.refs_9_), channel_id=1, source_target_pairs={{0,8},{2,10},{4,12},{6,14},{8,0},{10,2},{12,4},{14,6},{16,24},{18,... | collective-permute-start | bytes 368648 | tf_op jit(solution)/shard_map/ppermute | solution.py:382
  5.8 2.5 %collective-permute-start.4 = (bf16[48,1280]{1,0:T(8,128)(2,1)}, bf16[48,1280]{1,0:T(8,128)(2,1)S(1)}, u32[]{:S(2)}, u32[]{:S(2)}) collective-permute-start(bf16[48,1280]{1,0:T(8,128)(2,1)} %get-tuple-element.94.refs_9_), channel_id=1, source_target_pairs={{0,24},{2,26},{4,28},{6,30},{8,16},{10,18},{12,20},{14,22},{16,8},... | collective-permute-start | bytes 368648 | tf_op jit(solution)/shard_map/ppermute | solution.py:382
  8.2 1.5 %collective-permute-start = (bf16[48,1280]{1,0:T(8,128)(2,1)}, bf16[48,1280]{1,0:T(8,128)(2,1)S(1)}, u32[]{:S(2)}, u32[]{:S(2)}) collective-permute-start(bf16[48,1280]{1,0:T(8,128)(2,1)} %get-tuple-element.85), channel_id=1, source_target_pairs={{0,2},{2,0},{4,6},{6,4},{8,10},{10,8},{12,14},{14,12},{16,18},{18,... | collective-permute-start | bytes 368648 | tf_op jit(solution)/shard_map/ppermute | solution.py:379
  9.7 1.5 %collective-permute-start.1 = (bf16[48,1280]{1,0:T(8,128)(2,1)}, bf16[48,1280]{1,0:T(8,128)(2,1)S(1)}, u32[]{:S(2)}, u32[]{:S(2)}) collective-permute-start(bf16[48,1280]{1,0:T(8,128)(2,1)} %get-tuple-element.86), channel_id=1, source_target_pairs={{0,4},{2,6},{4,0},{6,2},{8,12},{10,14},{12,8},{14,10},{16,20},{18,... | collective-permute-start | bytes 368648 | tf_op jit(solution)/shard_map/ppermute | solution.py:379
  11.2 0.5 collective-permute-start.2
  11.8 2.4 %collective-permute-done.4.refs_12_ = bf16[48,1280]{1,0:T(8,128)(2,1)S(1)} collective-permute-done((bf16[48,1280]{1,0:T(8,128)(2,1)}, bf16[48,1280]{1,0:T(8,128)(2,1)S(1)}, u32[]{:S(2)}, u32[]{:S(2)}) %collective-permute-start.4) | collective-permute-done | bytes 122912 | tf_op jit(solution)/shard_map/ppermute | solution.py:382
  14.2 3.2 %collective-permute-done.1 = bf16[48,1280]{1,0:T(8,128)(2,1)S(1)} collective-permute-done((bf16[48,1280]{1,0:T(8,128)(2,1)}, bf16[48,1280]{1,0:T(8,128)(2,1)S(1)}, u32[]{:S(2)}, u32[]{:S(2)}) %collective-permute-start.1) | collective-permute-done | bytes 122912 | tf_op jit(solution)/shard_map/ppermute | solution.py:379
  17.5 0.7 collective-permute-start.5
  18.1 0.8 collective-permute-start.6
  19.0 2.0 %collective-permute-start.7 = (bf16[272,768]{1,0:T(8,128)(2,1)S(1)}, bf16[272,768]{1,0:T(8,128)(2,1)S(1)}, u32[]{:S(2)}, u32[]{:S(2)}) collective-permute-start(bf16[272,768]{1,0:T(8,128)(2,1)S(1)} %fusion.1), channel_id=1, source_target_pairs={{0,6},{2,4},{4,2},{6,0},{8,14},{10,12},{12,10},{14,8},{16,22},{18,... | collective-permute-start | bytes 1253384 | tf_op jit(solution)/shard_map/ppermute | solution.py:379
  21.0 0.9 broadcast_select_fusion.1
  22.0 2.2 %collective-permute-start.10 = (bf16[144,1280]{1,0:T(8,128)(2,1)S(1)}, bf16[144,1280]{1,0:T(8,128)(2,1)S(1)}, u32[]{:S(2)}, u32[]{:S(2)}) collective-permute-start(bf16[144,1280]{1,0:T(8,128)(2,1)S(1)} %constant_dynamic-update-slice_fusion.refs_13_), channel_id=1, source_target_pairs={{0,24},{2,26},{4,28},{6,30},{8,16},{10,18},{12,20},{14,22},{16,8},... | collective-permute-start | bytes 1105928 | tf_op jit(solution)/shard_map/ppermute | solution.py:382
  24.2 8.1 %collective-permute-done.8.refs_11_ = bf16[48,1280]{1,0:T(8,128)(2,1)S(1)} collective-permute-done((bf16[48,1280]{1,0:T(8,128)(2,1)S(1)}, bf16[48,1280]{1,0:T(8,128)(2,1)S(1)}, u32[]{:S(2)}, u32[]{:S(2)}) %collective-permute-start.8) | collective-permute-done | bytes 122912 | tf_op jit(solution)/shard_map/ppermute | solution.py:391
  32.4 3.9 %collective-permute-done.10.refs_16_ = bf16[144,1280]{1,0:T(8,128)(2,1)S(1)} collective-permute-done((bf16[144,1280]{1,0:T(8,128)(2,1)S(1)}, bf16[144,1280]{1,0:T(8,128)(2,1)S(1)}, u32[]{:S(2)}, u32[]{:S(2)}) %collective-permute-start.10) | collective-permute-done | bytes 368672 | tf_op jit(solution)/shard_map/ppermute | solution.py:382
  36.2 4.7 %collective-permute-done.9.refs_14_ = bf16[144,1280]{1,0:T(8,128)(2,1)S(1)} collective-permute-done((bf16[144,1280]{1,0:T(8,128)(2,1)S(1)}, bf16[144,1280]{1,0:T(8,128)(2,1)S(1)}, u32[]{:S(2)}, u32[]{:S(2)}) %collective-permute-start.9) | collective-permute-done | bytes 368672 | tf_op jit(solution)/shard_map/ppermute | solution.py:382
  41.1 0.1 collective-permute-start.11
  41.3 0.8 dynamic_slice.7
  42.2 0.6 collective-permute-start.12
  42.8 2.0 %collective-permute-done.11.peer_ref = bf16[1088,768]{1,0:T(8,128)(2,1)} collective-permute-done((bf16[1088,768]{1,0:T(8,128)(2,1)S(1)}, bf16[1088,768]{1,0:T(8,128)(2,1)}, u32[]{:S(2)}, u32[]{:S(2)}) %collective-permute-start.11) | collective-permute-done | bytes 1671200 | tf_op jit(solution)/shard_map/ppermute | solution.py:385
  44.8 3.4 %shard_map.282 = (bf16[1024,768]{1,0:T(8,128)(2,1)S(1)}, bf16[1024,768]{1,0:T(8,128)(2,1)S(1)}, bf16[1024,768]{1,0:T(8,128)(2,1)S(1)}, bf16[1024,768]{1,0:T(8,12...) custom-call(f32[8,768]{1,0:T(8,128)S(1)} %stack.23.params_ref, ...), custom_call_target="tpu_custom_call" | custom-call | flops 4000000000 | bytes 1 | tf_op jit(solution)/shard_map/pallas_call | solution.py:336
  48.2 5.0 %collective-permute-done.12.refs_15_ = bf16[144,1280]{1,0:T(8,128)(2,1)S(1)} collective-permute-done((bf16[144,1280]{1,0:T(8,128)(2,1)S(1)}, bf16[144,1280]{1,0:T(8,128)(2,1)S(1)}, u32[]{:S(2)}, u32[]{:S(2)}) %collective-permute-start.12) | collective-permute-done | bytes 368672 | tf_op jit(solution)/shard_map/ppermute | solution.py:391
  53.2 10.1 %shard_map.283 = (bf16[1024,128]{1,0:T(8,128)(2,1)S(1)}, bf16[1024,384]{1,0:T(8,128)(2,1)S(1)}, bf16[1024,384]{1,0:T(8,128)(2,1)S(1)}, bf16[1024,384]{1,0:T(8,12...) custom-call(f32[8,128]{1,0:T(8,128)S(1)} %get-tuple-element.104.refs, ...), custom_call_target="tpu_custom_call" | custom-call | flops 12000000000 | bytes 1 | tf_op jit(solution)/shard_map/pallas_call | solution.py:336
  63.3 4.6 %shard_map.284 = (bf16[1040,768]{1,0:T(8,128)(2,1)S(1)}, bf16[1040,768]{1,0:T(8,128)(2,1)S(1)}) custom-call(f32[8,768]{1,0:T(8,128)S(1)} %stack.23.params_ref, bf16[1024,768]{1,0:T(8,128)(2,1)S(1)} %get-tuple-element.103.xh_ref, bf16[768,1280]{1,0:T(8,128)(2,1)S(1)} %get-tuple-element.112.w_ref, bf16[1024,384]{1,0:T(8,128)(2,1)S(1)} %get-tuple-element.113.act_ref, ...), custom_call_target="tpu_custom_call" | custom-call | flops 4000000000 | bytes 1 | tf_op jit(solution)/shard_map/pallas_call | solution.py:336
  68.0 0.1 collective-permute-start.14
  68.0 0.9 collective-permute-start.13
  68.9 13.6 %collective-permute-done.13.refs_0_.passed_ref = bf16[192,1280]{1,0:T(8,128)(2,1)S(1)} collective-permute-done((bf16[192,1280]{1,0:T(8,128)(2,1)S(1)}, bf16[192,1280]{1,0:T(8,128)(2,1)S(1)}, u32[]{:S(2)}, u32[]{:S(2)}) %collective-permute-start.13) | collective-permute-done | bytes 491552 | tf_op jit(solution)/shard_map/ppermute | solution.py:391
  82.6 0.5 shard_map.285
  83.1 0.1 collective-permute-start.18
  83.2 2.0 %collective-permute-start.19 = (bf16[208,1280]{1,0:T(8,128)(2,1)S(1)}, bf16[208,1280]{1,0:T(8,128)(2,1)S(1)}, u32[]{:S(2)}, u32[]{:S(2)}) collective-permute-start(bf16[208,1280]{1,0:T(8,128)(2,1)S(1)} %get-tuple-element.133), channel_id=1, source_target_pairs={{0,24},{2,26},{4,28},{6,30},{8,16},{10,18},{12,20},{14,22},{16,8},... | collective-permute-start | bytes 1597448 | tf_op jit(solution)/shard_map/ppermute | solution.py:382
  85.1 0.9 collective-permute-start.15
  86.1 0.8 collective-permute-start.16
  86.8 1.8 %collective-permute-start.17 = (bf16[256,768]{1,0:T(8,128)(2,1)S(1)}, bf16[256,768]{1,0:T(8,128)(2,1)S(1)}, u32[]{:S(2)}, u32[]{:S(2)}) collective-permute-start(bf16[256,768]{1,0:T(8,128)(2,1)S(1)} %get-tuple-element.131), channel_id=1, source_target_pairs={{0,6},{2,4},{4,2},{6,0},{8,14},{10,12},{12,10},{14,8},{16,22},{18,... | collective-permute-start | bytes 1179656 | tf_op jit(solution)/shard_map/ppermute | solution.py:379
  88.6 8.6 %collective-permute-done.15.refs_1_ = bf16[256,768]{1,0:T(8,128)(2,1)S(1)} collective-permute-done((bf16[256,768]{1,0:T(8,128)(2,1)S(1)}, bf16[256,768]{1,0:T(8,128)(2,1)S(1)}, u32[]{:S(2)}, u32[]{:S(2)}) %collective-permute-start.15) | collective-permute-done | bytes 393248 | tf_op jit(solution)/shard_map/ppermute | solution.py:379
  97.2 1.5 %collective-permute-start.20 = (bf16[16,768]{1,0:T(8,128)(2,1)S(1)}, bf16[16,768]{1,0:T(8,128)(2,1)S(1)}, u32[]{:S(2)}, u32[]{:S(2)}) collective-permute-start(bf16[16,768]{1,0:T(8,128)(2,1)S(1)} %get-tuple-element.134.notes_ref), channel_id=1, source_target_pairs={{0,16},{2,18},{4,20},{6,22},{8,24},{10,26},{12,28},{14,30},{16,0},... | collective-permute-start | bytes 73736 | tf_op jit(solution)/shard_map/ppermute | solution.py:382
  98.7 5.8 %collective-permute-done.16.refs_2_ = bf16[256,768]{1,0:T(8,128)(2,1)S(1)} collective-permute-done((bf16[256,768]{1,0:T(8,128)(2,1)S(1)}, bf16[256,768]{1,0:T(8,128)(2,1)S(1)}, u32[]{:S(2)}, u32[]{:S(2)}) %collective-permute-start.16) | collective-permute-done | bytes 393248 | tf_op jit(solution)/shard_map/ppermute | solution.py:379
  104.5 6.0 %collective-permute-done.20.notes_middle_ref = bf16[16,768]{1,0:T(8,128)(2,1)S(1)} collective-permute-done((bf16[16,768]{1,0:T(8,128)(2,1)S(1)}, bf16[16,768]{1,0:T(8,128)(2,1)S(1)}, u32[]{:S(2)}, u32[]{:S(2)}) %collective-permute-start.20) | collective-permute-done | bytes 24608 | tf_op jit(solution)/shard_map/ppermute | solution.py:382
  110.5 0.3 shard_map.287
  110.8 1.0 collective-permute-start.21
  111.8 0.8 collective-permute-start.22
  112.6 1.8 %collective-permute-start.23 = (bf16[64,1280]{1,0:T(8,128)(2,1)S(1)}, bf16[64,1280]{1,0:T(8,128)(2,1)S(1)}, u32[]{:S(2)}, u32[]{:S(2)}) collective-permute-start(bf16[64,1280]{1,0:T(8,128)(2,1)S(1)} %get-tuple-element.148), channel_id=1, source_target_pairs={{0,6},{2,4},{4,2},{6,0},{8,14},{10,12},{12,10},{14,8},{16,22},{18,... | collective-permute-start | bytes 491528 | tf_op jit(solution)/shard_map/ppermute | solution.py:379
  114.4 1.2 shard_map.286
  115.6 1.6 %collective-permute-done.21.refs_1_ = bf16[64,1280]{1,0:T(8,128)(2,1)S(1)} collective-permute-done((bf16[64,1280]{1,0:T(8,128)(2,1)S(1)}, bf16[64,1280]{1,0:T(8,128)(2,1)S(1)}, u32[]{:S(2)}, u32[]{:S(2)}) %collective-permute-start.21) | collective-permute-done | bytes 163872 | tf_op jit(solution)/shard_map/ppermute | solution.py:379
  117.2 2.3 %collective-permute-done.22.refs_2_ = bf16[64,1280]{1,0:T(8,128)(2,1)S(1)} collective-permute-done((bf16[64,1280]{1,0:T(8,128)(2,1)S(1)}, bf16[64,1280]{1,0:T(8,128)(2,1)S(1)}, u32[]{:S(2)}, u32[]{:S(2)}) %collective-permute-start.22) | collective-permute-done | bytes 163872 | tf_op jit(solution)/shard_map/ppermute | solution.py:379
  119.5 1.0 shard_map.288
  120.5 0.6 slice_reduce_fusion
  121.1 0.6 reduce.5
  121.7 0.6 copy.41
  (64 shorter events, 0.5 us)
Async XLA Ops:
  0.6 40.6 %copy-start = (f32[3,384]{1,0:T(4,128)S(1)}, f32[3,384]{1,0:T(4,128)}, u32[]{:S(2)}) copy-start(f32[3,384]{1,0:T(4,128)} %param.26) | copy-start | bytes 13828
  0.7 11.1 %copy-start.14 = (s32[1,4]{1,0:T(1,128)S(1)}, s32[1,4]{1,0:T(1,128)}, u32[]{:S(2)}) copy-start(s32[1,4]{1,0:T(1,128)} %param.20) | copy-start | bytes 52
  0.7 11.1 %copy-start.1 = (bf16[128,768]{1,0:T(8,128)(2,1)S(1)}, bf16[128,768]{1,0:T(8,128)(2,1)}, u32[]{:S(2)}) copy-start(bf16[128,768]{1,0:T(8,128)(2,1)} %residual_ref.1) | copy-start | bytes 589828
  0.7 11.1 %copy-start.6 = (bf16[128,768]{1,0:T(8,128)(2,1)S(1)}, bf16[128,768]{1,0:T(8,128)(2,1)}, u32[]{:S(2)}) copy-start(bf16[128,768]{1,0:T(8,128)(2,1)} %param.19) | copy-start | bytes 589828
  2.7 9.1 %collective-permute-start.3 = (bf16[48,1280]{1,0:T(8,128)(2,1)}, bf16[48,1280]{1,0:T(8,128)(2,1)S(1)}, u32[]{:S(2)}, u32[]{:S(2)}) collective-permute-start(bf16[48,1280]{1,0:T(8,128)(2,1)} %get-tuple-element.94.refs_9_), channel_id=1, source_target_pairs={{0,8},{2,10},{4,12},{6,14},{8,0},{10,2},{12,4},{14,6},{16,24},{18,... | collective-permute-start | bytes 368648 | tf_op jit(solution)/shard_map/ppermute | solution.py:382
  5.8 8.5 %collective-permute-start.4 = (bf16[48,1280]{1,0:T(8,128)(2,1)}, bf16[48,1280]{1,0:T(8,128)(2,1)S(1)}, u32[]{:S(2)}, u32[]{:S(2)}) collective-permute-start(bf16[48,1280]{1,0:T(8,128)(2,1)} %get-tuple-element.94.refs_9_), channel_id=1, source_target_pairs={{0,24},{2,26},{4,28},{6,30},{8,16},{10,18},{12,20},{14,22},{16,8},... | collective-permute-start | bytes 368648 | tf_op jit(solution)/shard_map/ppermute | solution.py:382
  8.2 6.0 %collective-permute-start = (bf16[48,1280]{1,0:T(8,128)(2,1)}, bf16[48,1280]{1,0:T(8,128)(2,1)S(1)}, u32[]{:S(2)}, u32[]{:S(2)}) collective-permute-start(bf16[48,1280]{1,0:T(8,128)(2,1)} %get-tuple-element.85), channel_id=1, source_target_pairs={{0,2},{2,0},{4,6},{6,4},{8,10},{10,8},{12,14},{14,12},{16,18},{18,... | collective-permute-start | bytes 368648 | tf_op jit(solution)/shard_map/ppermute | solution.py:379
  9.7 7.7 %collective-permute-start.1 = (bf16[48,1280]{1,0:T(8,128)(2,1)}, bf16[48,1280]{1,0:T(8,128)(2,1)S(1)}, u32[]{:S(2)}, u32[]{:S(2)}) collective-permute-start(bf16[48,1280]{1,0:T(8,128)(2,1)} %get-tuple-element.86), channel_id=1, source_target_pairs={{0,4},{2,6},{4,0},{6,2},{8,12},{10,14},{12,8},{14,10},{16,20},{18,... | collective-permute-start | bytes 368648 | tf_op jit(solution)/shard_map/ppermute | solution.py:379
  11.2 6.2 %collective-permute-start.2 = (bf16[48,1280]{1,0:T(8,128)(2,1)}, bf16[48,1280]{1,0:T(8,128)(2,1)S(1)}, u32[]{:S(2)}, u32[]{:S(2)}) collective-permute-start(bf16[48,1280]{1,0:T(8,128)(2,1)} %get-tuple-element.87), channel_id=1, source_target_pairs={{0,6},{2,4},{4,2},{6,0},{8,14},{10,12},{12,10},{14,8},{16,22},{18,... | collective-permute-start | bytes 368648 | tf_op jit(solution)/shard_map/ppermute | solution.py:379
  17.5 23.4 %collective-permute-start.5 = (bf16[272,768]{1,0:T(8,128)(2,1)S(1)}, bf16[272,768]{1,0:T(8,128)(2,1)S(1)}, u32[]{:S(2)}, u32[]{:S(2)}) collective-permute-start(bf16[272,768]{1,0:T(8,128)(2,1)S(1)} %fusion.1), channel_id=1, source_target_pairs={{0,2},{2,0},{4,6},{6,4},{8,10},{10,8},{12,14},{14,12},{16,18},{18,... | collective-permute-start | bytes 1253384 | tf_op jit(solution)/shard_map/ppermute | solution.py:379
  18.1 22.8 %collective-permute-start.6 = (bf16[272,768]{1,0:T(8,128)(2,1)S(1)}, bf16[272,768]{1,0:T(8,128)(2,1)S(1)}, u32[]{:S(2)}, u32[]{:S(2)}) collective-permute-start(bf16[272,768]{1,0:T(8,128)(2,1)S(1)} %fusion.1), channel_id=1, source_target_pairs={{0,4},{2,6},{4,0},{6,2},{8,12},{10,14},{12,8},{14,10},{16,20},{18,... | collective-permute-start | bytes 1253384 | tf_op jit(solution)/shard_map/ppermute | solution.py:379
  19.0 21.9 %collective-permute-start.7 = (bf16[272,768]{1,0:T(8,128)(2,1)S(1)}, bf16[272,768]{1,0:T(8,128)(2,1)S(1)}, u32[]{:S(2)}, u32[]{:S(2)}) collective-permute-start(bf16[272,768]{1,0:T(8,128)(2,1)S(1)} %fusion.1), channel_id=1, source_target_pairs={{0,6},{2,4},{4,2},{6,0},{8,14},{10,12},{12,10},{14,8},{16,22},{18,... | collective-permute-start | bytes 1253384 | tf_op jit(solution)/shard_map/ppermute | solution.py:379
  21.9 10.5 %collective-permute-start.8 = (bf16[48,1280]{1,0:T(8,128)(2,1)S(1)}, bf16[48,1280]{1,0:T(8,128)(2,1)S(1)}, u32[]{:S(2)}, u32[]{:S(2)}) collective-permute-start(bf16[48,1280]{1,0:T(8,128)(2,1)S(1)} %broadcast_select_fusion.1), channel_id=1, source_target_pairs={{0,16},{2,18},{4,20},{6,22},{24,8},{26,10},{28,12},{30,14},{8,0},{... | collective-permute-start | bytes 368648 | tf_op jit(solution)/shard_map/ppermute | solution.py:391
  22.0 19.2 %copy-start.8 = (f32[768]{0:T(1024)S(1)}, f32[768]{0:T(1024)}, u32[]{:S(2)}) copy-start(f32[768]{0:T(1024)} %param.21) | copy-start | bytes 9220
  22.0 19.2 %copy-start.9 = (f32[768]{0:T(1024)S(1)}, f32[768]{0:T(1024)}, u32[]{:S(2)}) copy-start(f32[768]{0:T(1024)} %param.22) | copy-start | bytes 9220
  22.0 19.2 %copy-start.10 = (f32[768]{0:T(1024)S(1)}, f32[768]{0:T(1024)}, u32[]{:S(2)}) copy-start(f32[768]{0:T(1024)} %param.23) | copy-start | bytes 9220
  22.0 19.2 %copy-start.11 = (f32[768]{0:T(1024)S(1)}, f32[768]{0:T(1024)}, u32[]{:S(2)}) copy-start(f32[768]{0:T(1024)} %param.24) | copy-start | bytes 9220
  22.0 14.2 %collective-permute-start.10 = (bf16[144,1280]{1,0:T(8,128)(2,1)S(1)}, bf16[144,1280]{1,0:T(8,128)(2,1)S(1)}, u32[]{:S(2)}, u32[]{:S(2)}) collective-permute-start(bf16[144,1280]{1,0:T(8,128)(2,1)S(1)} %constant_dynamic-update-slice_fusion.refs_13_), channel_id=1, source_target_pairs={{0,24},{2,26},{4,28},{6,30},{8,16},{10,18},{12,20},{14,22},{16,8},... | collective-permute-start | bytes 1105928 | tf_op jit(solution)/shard_map/ppermute | solution.py:382
  32.4 8.5 %collective-permute-start.9 = (bf16[144,1280]{1,0:T(8,128)(2,1)S(1)}, bf16[144,1280]{1,0:T(8,128)(2,1)S(1)}, u32[]{:S(2)}, u32[]{:S(2)}) collective-permute-start(bf16[144,1280]{1,0:T(8,128)(2,1)S(1)} %constant_dynamic-update-slice_fusion.refs_13_), channel_id=1, source_target_pairs={{0,8},{2,10},{4,12},{6,14},{8,0},{10,2},{12,4},{14,6},{16,24},{18,... | collective-permute-start | bytes 1105928 | tf_op jit(solution)/shard_map/ppermute | solution.py:382
  41.1 3.7 %collective-permute-start.11 = (bf16[1088,768]{1,0:T(8,128)(2,1)S(1)}, bf16[1088,768]{1,0:T(8,128)(2,1)}, u32[]{:S(2)}, u32[]{:S(2)}) collective-permute-start(bf16[1088,768]{1,0:T(8,128)(2,1)S(1)} %constant_dynamic-update-slice_fusion.3.own_ref), channel_id=1, source_target_pairs={{0,1},{1,0},{2,3},{3,2},{4,5},{5,4},{6,7},{7,6},{8,9},{9,8},{10,11... | collective-permute-start | bytes 5013512 | tf_op jit(solution)/shard_map/ppermute | solution.py:385
  42.2 11.1 %copy-start.2 = (bf16[48,1280]{1,0:T(8,128)(2,1)S(1)}, bf16[48,1280]{1,0:T(8,128)(2,1)}, u32[]{:S(2)}) copy-start(bf16[48,1280]{1,0:T(8,128)(2,1)} %get-tuple-element.94.refs_9_) | copy-start | bytes 368644
  42.2 11.0 %copy-start.3 = (f32[256,128]{1,0:T(8,128)S(1)}, f32[256,128]{1,0:T(8,128)}, u32[]{:S(2)}) copy-start(f32[256,128]{1,0:T(8,128)} %constant.53.clone.refs_6_) | copy-start | bytes 393220
  42.2 11.0 %copy-start.4 = (f32[256,128]{1,0:T(8,128)S(1)}, f32[256,128]{1,0:T(8,128)}, u32[]{:S(2)}) copy-start(f32[256,128]{1,0:T(8,128)} %constant.54.clone.refs_7_) | copy-start | bytes 393220
  42.2 11.0 %copy-start.5 = (f32[256,128]{1,0:T(8,128)S(1)}, f32[256,128]{1,0:T(8,128)}, u32[]{:S(2)}) copy-start(f32[256,128]{1,0:T(8,128)} %constant.55.clone.refs_8_) | copy-start | bytes 393220
  42.2 11.0 %collective-permute-start.12 = (bf16[144,1280]{1,0:T(8,128)(2,1)S(1)}, bf16[144,1280]{1,0:T(8,128)(2,1)S(1)}, u32[]{:S(2)}, u32[]{:S(2)}) collective-permute-start(bf16[144,1280]{1,0:T(8,128)(2,1)S(1)} %broadcast_select_fusion), channel_id=1, source_target_pairs={{0,16},{2,18},{4,20},{6,22},{24,8},{26,10},{28,12},{30,14},{8,0},{... | collective-permute-start | bytes 1105928 | tf_op jit(solution)/shard_map/ppermute | solution.py:391
  68.0 14.6 %collective-permute-start.14 = (bf16[1040,768]{1,0:T(8,128)(2,1)S(1)}, bf16[1040,768]{1,0:T(8,128)(2,1)S(1)}, u32[]{:S(2)}, u32[]{:S(2)}) collective-permute-start(bf16[1040,768]{1,0:T(8,128)(2,1)S(1)} %get-tuple-element.121), channel_id=1, source_target_pairs={{0,1},{1,0},{2,3},{3,2},{4,5},{5,4},{6,7},{7,6},{8,9},{9,8},{10,11... | collective-permute-start | bytes 4792328 | tf_op jit(solution)/shard_map/ppermute | solution.py:385
  68.0 14.5 %collective-permute-start.13 = (bf16[192,1280]{1,0:T(8,128)(2,1)S(1)}, bf16[192,1280]{1,0:T(8,128)(2,1)S(1)}, u32[]{:S(2)}, u32[]{:S(2)}) collective-permute-start(bf16[192,1280]{1,0:T(8,128)(2,1)S(1)} %get-tuple-element.120), channel_id=1, source_target_pairs={{16,0},{18,2},{20,4},{22,6},{8,24},{10,26},{12,28},{14,30},{0,8},{... | collective-permute-start | bytes 1474568 | tf_op jit(solution)/shard_map/ppermute | solution.py:391
  83.1 27.4 %collective-permute-start.18 = (bf16[208,1280]{1,0:T(8,128)(2,1)S(1)}, bf16[208,1280]{1,0:T(8,128)(2,1)S(1)}, u32[]{:S(2)}, u32[]{:S(2)}) collective-permute-start(bf16[208,1280]{1,0:T(8,128)(2,1)S(1)} %get-tuple-element.132), channel_id=1, source_target_pairs={{0,8},{2,10},{4,12},{6,14},{8,0},{10,2},{12,4},{14,6},{16,24},{18,... | collective-permute-start | bytes 1597448 | tf_op jit(solution)/shard_map/ppermute | solution.py:382
  83.2 27.3 %collective-permute-start.19 = (bf16[208,1280]{1,0:T(8,128)(2,1)S(1)}, bf16[208,1280]{1,0:T(8,128)(2,1)S(1)}, u32[]{:S(2)}, u32[]{:S(2)}) collective-permute-start(bf16[208,1280]{1,0:T(8,128)(2,1)S(1)} %get-tuple-element.133), channel_id=1, source_target_pairs={{0,24},{2,26},{4,28},{6,30},{8,16},{10,18},{12,20},{14,22},{16,8},... | collective-permute-start | bytes 1597448 | tf_op jit(solution)/shard_map/ppermute | solution.py:382
  85.1 12.1 %collective-permute-start.15 = (bf16[256,768]{1,0:T(8,128)(2,1)S(1)}, bf16[256,768]{1,0:T(8,128)(2,1)S(1)}, u32[]{:S(2)}, u32[]{:S(2)}) collective-permute-start(bf16[256,768]{1,0:T(8,128)(2,1)S(1)} %get-tuple-element.128), channel_id=1, source_target_pairs={{0,2},{2,0},{4,6},{6,4},{8,10},{10,8},{12,14},{14,12},{16,18},{18,... | collective-permute-start | bytes 1179656 | tf_op jit(solution)/shard_map/ppermute | solution.py:379
  86.1 18.5 %collective-permute-start.16 = (bf16[256,768]{1,0:T(8,128)(2,1)S(1)}, bf16[256,768]{1,0:T(8,128)(2,1)S(1)}, u32[]{:S(2)}, u32[]{:S(2)}) collective-permute-start(bf16[256,768]{1,0:T(8,128)(2,1)S(1)} %get-tuple-element.130), channel_id=1, source_target_pairs={{0,4},{2,6},{4,0},{6,2},{8,12},{10,14},{12,8},{14,10},{16,20},{18,... | collective-permute-start | bytes 1179656 | tf_op jit(solution)/shard_map/ppermute | solution.py:379
  86.8 17.7 %collective-permute-start.17 = (bf16[256,768]{1,0:T(8,128)(2,1)S(1)}, bf16[256,768]{1,0:T(8,128)(2,1)S(1)}, u32[]{:S(2)}, u32[]{:S(2)}) collective-permute-start(bf16[256,768]{1,0:T(8,128)(2,1)S(1)} %get-tuple-element.131), channel_id=1, source_target_pairs={{0,6},{2,4},{4,2},{6,0},{8,14},{10,12},{12,10},{14,8},{16,22},{18,... | collective-permute-start | bytes 1179656 | tf_op jit(solution)/shard_map/ppermute | solution.py:379
  97.2 13.3 %collective-permute-start.20 = (bf16[16,768]{1,0:T(8,128)(2,1)S(1)}, bf16[16,768]{1,0:T(8,128)(2,1)S(1)}, u32[]{:S(2)}, u32[]{:S(2)}) collective-permute-start(bf16[16,768]{1,0:T(8,128)(2,1)S(1)} %get-tuple-element.134.notes_ref), channel_id=1, source_target_pairs={{0,16},{2,18},{4,20},{6,22},{8,24},{10,26},{12,28},{14,30},{16,0},... | collective-permute-start | bytes 73736 | tf_op jit(solution)/shard_map/ppermute | solution.py:382
  110.5 3.9 %copy-start.12 = (f32[768]{0:T(1024)S(1)}, f32[768]{0:T(1024)}, u32[]{:S(2)}) copy-start(f32[768]{0:T(1024)} %param.28) | copy-start | bytes 9220
  110.5 3.9 %copy-start.13 = (f32[768]{0:T(1024)S(1)}, f32[768]{0:T(1024)}, u32[]{:S(2)}) copy-start(f32[768]{0:T(1024)} %param.32) | copy-start | bytes 9220
  110.8 6.4 %collective-permute-start.21 = (bf16[64,1280]{1,0:T(8,128)(2,1)S(1)}, bf16[64,1280]{1,0:T(8,128)(2,1)S(1)}, u32[]{:S(2)}, u32[]{:S(2)}) collective-permute-start(bf16[64,1280]{1,0:T(8,128)(2,1)S(1)} %get-tuple-element.146), channel_id=1, source_target_pairs={{0,2},{2,0},{4,6},{6,4},{8,10},{10,8},{12,14},{14,12},{16,18},{18,... | collective-permute-start | bytes 491528 | tf_op jit(solution)/shard_map/ppermute | solution.py:379
  111.8 7.7 %collective-permute-start.22 = (bf16[64,1280]{1,0:T(8,128)(2,1)S(1)}, bf16[64,1280]{1,0:T(8,128)(2,1)S(1)}, u32[]{:S(2)}, u32[]{:S(2)}) collective-permute-start(bf16[64,1280]{1,0:T(8,128)(2,1)S(1)} %get-tuple-element.147), channel_id=1, source_target_pairs={{0,4},{2,6},{4,0},{6,2},{8,12},{10,14},{12,8},{14,10},{16,20},{18,... | collective-permute-start | bytes 491528 | tf_op jit(solution)/shard_map/ppermute | solution.py:379
  112.6 6.9 %collective-permute-start.23 = (bf16[64,1280]{1,0:T(8,128)(2,1)S(1)}, bf16[64,1280]{1,0:T(8,128)(2,1)S(1)}, u32[]{:S(2)}, u32[]{:S(2)}) collective-permute-start(bf16[64,1280]{1,0:T(8,128)(2,1)S(1)} %get-tuple-element.148), channel_id=1, source_target_pairs={{0,6},{2,4},{4,2},{6,0},{8,14},{10,12},{12,10},{14,8},{16,22},{18,... | collective-permute-start | bytes 491528 | tf_op jit(solution)/shard_map/ppermute | solution.py:379
  121.1 1.2 copy-start.7

commit v4 on v3

--- a/solution.py
+++ b/solution.py
@@ -89,14 +89,16 @@
     width = up_ref.shape[1] // PLANE
     for k in range(PLANE):
         other = place()[0] ^ k
+        heads, out = 3 * BLK, 3 * BLK + width
         at = pl.ds(pl.multiple_of(jnp.minimum(other, head_blocks - 1) * BLK, BLK), BLK)
         for c in range(4):
             block = qkv_ref[c, :, at] if c < 3 else out_ref[:, at]
             block = jnp.where(other < head_blocks, block.astype(F32), 0.0)
-            share_refs[k][:, c * BLK : (c + 1) * BLK] = block.astype(BF16)
+            start = c * BLK if c < 3 else out
+            share_refs[k][:, start : start + BLK] = block.astype(BF16)
         at = pl.ds(pl.multiple_of(other * width, BLK), width)
-        share_refs[k][:, 4 * BLK : 4 * BLK + width] = up_ref[:, at]
-        share_refs[k][:, 4 * BLK + width :] = down_ref[:, at]
+        share_refs[k][:, heads:out] = up_ref[:, at]
+        share_refs[k][:, out + BLK :] = down_ref[:, at]
 
 
 def rows_at(m, k, owned):
@@ -138,8 +140,8 @@
 def layer_kernel(levels, *refs):
     length_ref, x1_ref, x2_ref, g_ref, bias_ref, bias_up_ref, keep_ref, low_ref, high_ref = refs[:9]
     pieces = refs[9 : 9 + max(2 * levels, 1)]
-    att_ref, gp_ref, act_ref, gh_ref, w_ref, gb_ref = refs[9 + len(pieces) : 15 + len(pieces)]
-    message_refs, gw_ref = refs[15 + len(pieces) : -1], refs[-1]
+    za_ref, gp_ref, gh_ref, w_ref, gb_ref = refs[9 + len(pieces) : 14 + len(pieces)]
+    message_refs, gw_ref = refs[14 + len(pieces) : -1], refs[-1]
     if levels:
         owned = pieces[0].shape[0]
         for m in range(levels):
@@ -149,7 +151,8 @@
     else:
         w_ref[...] = pieces[0][...]
         gw_ref = message_refs[0]
-    heads, width = 4 * BLK, bias_up_ref.shape[1]
+    width = bias_up_ref.shape[1]
+    heads, out = 3 * BLK, 3 * BLK + width
     slots = keep_ref.shape[0]
     keep, low, high = keep_ref[...], low_ref[...], high_ref[...]
 
@@ -171,13 +174,16 @@
         return jnp.where(first, x[:slots], x[slots:])
 
     total = jnp.zeros((1, 3 * BLK), F32)
+    total_up = jnp.zeros((1, width), F32)
     for k in range(PLANE):
         at = pl.ds(k * slots, slots)
-        proj = dot(x1_ref[at, :], w_ref[:, : 3 * BLK]) + bias_ref[...]
+        proj = dot(x1_ref[at, :], w_ref[:, :heads]) + bias_ref[...]
+        hidden = dot(x2_ref[at, :], w_ref[:, heads:out]) + bias_up_ref[...]
+        back = dot(g_ref[at, :], w_ref[:, out:])
         query = stacked((turn(proj[:, :BLK], 1.0) * HD**-0.5).astype(BF16))
         key = turn(proj[:, BLK : 2 * BLK], 1.0).astype(BF16)
         value = proj[:, 2 * BLK :].astype(BF16)
-        ga = stacked(dot(g_ref[at, :], w_ref[:, 3 * BLK : heads]).astype(BF16))
+        ga = stacked(back[:, :BLK].astype(BF16))
         logits = dot_nt(query, key)
         live = k_row.astype(F32) < length_ref[k : k + 1, 0:1]
         allowed = (k_row <= q_row) & (live | (k_row == q_row))
@@ -185,7 +191,7 @@
         weights = jnp.exp(logits - jnp.max(logits, axis=-1, keepdims=True))
         probs = weights / jnp.sum(weights, axis=-1, keepdims=True)
         rounded = probs.astype(BF16)
-        att_ref[at, :] = joined(dot(rounded, value)).astype(BF16)
+        za_ref[at, :BLK] = joined(dot(rounded, value)).astype(BF16)
         grad_probs = dot_nt(ga, value)
         inner = jnp.sum(probs * grad_probs, axis=-1, keepdims=True)
         grad_logits = (probs * (grad_probs - inner)).astype(BF16)
@@ -195,23 +201,17 @@
         gp = jnp.concatenate([turn(grad_query, -1.0), turn(grad_key, -1.0), grad_value], axis=1).astype(BF16)
         gp_ref[at, :] = gp
         total = total + jnp.sum(gp.astype(F32), axis=0, keepdims=True)
+        part = 0.5 + 0.5 * lax.erf(hidden * (0.5**0.5))
+        za_ref[at, BLK:] = (hidden * part).astype(BF16)
+        slope = part + hidden * jnp.exp(-0.5 * hidden * hidden) * (2.0 * math.pi) ** -0.5
+        gh = (back[:, BLK:] * slope).astype(BF16)
+        gh_ref[at, :] = gh
+        total_up = total_up + jnp.sum(gh.astype(F32), axis=0, keepdims=True)
+    gb_ref[:, :width] = total_up
     gb_ref[:, width:] = total
-    total = jnp.zeros((1, width), F32)
-    for k in range(PLANE):
-        at = pl.ds(k * slots, slots)
-        hidden = dot(x2_ref[at, :], w_ref[:, heads : heads + width]) + bias_up_ref[...]
-        grad_act = dot(g_ref[at, :], w_ref[:, heads + width :])
-        part = 0.5 + 0.5 * lax.erf(hidden * (0.5**0.5))
-        act_ref[at, :] = (hidden * part).astype(BF16)
-        slope = part + hidden * jnp.exp(-0.5 * hidden * hidden) * (2.0 * math.pi) ** -0.5
-        gh = (grad_act * slope).astype(BF16)
-        gh_ref[at, :] = gh
-        total = total + jnp.sum(gh.astype(F32), axis=0, keepdims=True)
-    gb_ref[:, :width] = total
-    gw_ref[:, : 3 * BLK] = dot_tn(x1_ref[...], gp_ref[...]).astype(BF16)
-    gw_ref[:, 3 * BLK : heads] = dot_tn(g_ref[...], att_ref[...]).astype(BF16)
-    gw_ref[:, heads : heads + width] = dot_tn(x2_ref[...], gh_ref[...]).astype(BF16)
-    gw_ref[:, heads + width :] = dot_tn(g_ref[...], act_ref[...]).astype(BF16)
+    gw_ref[:, :heads] = dot_tn(x1_ref[...], gp_ref[...]).astype(BF16)
+    gw_ref[:, heads:out] = dot_tn(x2_ref[...], gh_ref[...]).astype(BF16)
+    gw_ref[:, out:] = dot_tn(g_ref[...], za_ref[...]).astype(BF16)
     if levels:
         for m in range(levels):
             for k in range(PLANE):
@@ -219,22 +219,20 @@
 
 
 def products_kernel(
-    params_ref, xh_ref, w_ref, act_ref, gh_ref, att_ref, gp_ref, gb_ref, bo_ref, keep_ref, send_ref, stage_ref
+    params_ref, xh_ref, w_ref, za_ref, gp_ref, gh_ref, gb_ref, bo_ref, keep_ref, send_ref, stage_ref
 ):
     half = lax.axis_index("tensor")
     slots = stage_ref.shape[1]
     own_rows = slots // 2
-    heads, width = 4 * BLK, act_ref.shape[1]
+    heads, out = 3 * BLK, 3 * BLK + gh_ref.shape[1]
     params = params_ref[...]
     gain1, gain2 = params[0:1], params[2:3]
     sums = [jnp.zeros((1, xh_ref.shape[1]), F32) for _ in range(4)]
     for k in range(PLANE):
         at = pl.ds(k * slots, slots)
-        stage_ref[0] = dot_nt(act_ref[at, :], w_ref[:, heads + width :]) + dot_nt(
-            att_ref[at, :], w_ref[:, 3 * BLK : heads]
-        )
-        g1 = dot_nt(gp_ref[at, :], w_ref[:, : 3 * BLK])
-        g2 = dot_nt(gh_ref[at, :], w_ref[:, heads : heads + width])
+        stage_ref[0] = dot_nt(za_ref[at, :], w_ref[:, out:])
+        g1 = dot_nt(gp_ref[at, :], w_ref[:, :heads])
+        g2 = dot_nt(gh_ref[at, :], w_ref[:, heads:out])
         stage_ref[1] = gain1 * g1 + gain2 * g2
         xh = xh_ref[at, :].astype(F32)
         for j, term in enumerate((g1 * xh, g1, g2 * xh, g2)):
@@ -251,6 +249,21 @@
     send_ref[PLANE * slots :, :] = notes
 
 
+def join_kernel(*refs):
+    owned = refs[0].shape[0]
+    for k, ref in enumerate(refs[:-1]):
+        refs[-1][k * owned : (k + 1) * owned, :] = ref[...]
+
+
+def choose_kernel(own_ref, far_ref, out_ref):
+    out_ref[...] = jnp.where(is_inner(), far_ref[...].astype(F32), own_ref[...].astype(F32)).astype(BF16)
+
+
+def relay_kernel(far_ref, passed_ref, out_ref):
+    passed = jnp.where(is_inner(), passed_ref[...].astype(F32), 0.0)
+    out_ref[...] = (far_ref[...].astype(F32) + passed).astype(BF16)
+
+
 def pair_kernel(levels, keep_ref, peer_ref, *refs):
     notes_ref, out_refs = refs[-PLANE - 1], refs[-PLANE:]
     slots = out_refs[0].shape[0]
@@ -263,11 +276,10 @@
         at = pl.ds(k * slots, slots)
         out_ref[...] = (keep_ref[at, :].astype(F32) + peer_ref[at, :].astype(F32)).astype(BF16)
     if levels:
-        passed_ref, near_ref, far_ref, to_near_ref, to_far_ref = refs[:5]
+        near_ref, far_ref, to_near_ref, to_far_ref = refs[:4]
         rows, columns = near_ref.shape
-        passed = jnp.where(is_inner(), passed_ref[...].astype(F32), 0.0)
         to_near_ref[:rows, :] = near_ref[...]
-        to_far_ref[:rows, :] = (far_ref[...].astype(F32) + passed).astype(BF16)
+        to_far_ref[:rows, :] = far_ref[...]
         notes = jnp.concatenate([jnp.zeros((NOTES, columns - notes.shape[1]), BF16), notes], axis=1)
         to_near_ref[rows:, :] = notes
         to_far_ref[rows:, :] = notes
@@ -306,18 +318,22 @@
 
 def owner_kernel(*refs):
     part_refs = refs[:PLANE]
-    up_ref, down_ref, qkv_ref, out_ref, b_up_ref, b_qkv_ref, common_ref = refs[PLANE:]
+    up_ref, down_ref, qkv_ref, out_ref, b_up_ref, b_qkv_ref = refs[PLANE : PLANE + 6]
+    common_refs = refs[PLANE + 6 :]
     owned = up_ref.shape[0]
     width = up_ref.shape[1] // PLANE
     head_blocks = out_ref.shape[1] // BLK
-    start = 4 * BLK
+    heads, out = 3 * BLK, 3 * BLK + width
+    all_notes = []
     for k, part_ref in enumerate(part_refs):
         other = place()[0] ^ k
         at = pl.ds(pl.multiple_of(other * width, BLK), width)
-        up_ref[:, at] = part_ref[:owned, start : start + width].astype(F32)
-        down_ref[:, at] = part_ref[:owned, start + width :].astype(F32)
-        notes = part_ref[owned:, start:].astype(F32)
-        b_up_ref[:, at] = notes[0:1, :width]
+        up_ref[:, at] = part_ref[:owned, heads:out].astype(F32)
+        down_ref[:, at] = part_ref[:owned, out + BLK :].astype(F32)
+        notes = part_ref[owned:, part_ref.shape[1] - common_refs[0].shape[0] * BLK :].astype(F32)
+        all_notes.append(notes)
+        for j in range(width // BLK):
+            b_up_ref[pl.ds(other * (width // BLK) + j, 1), :] = notes[0:1, j * BLK : (j + 1) * BLK]
 
         @pl.when(other < head_blocks)
         def _():
@@ -325,9 +341,12 @@
             for c in range(3):
                 qkv_ref[c, :, at] = part_ref[:owned, c * BLK : (c + 1) * BLK].astype(F32)
                 b_qkv_ref[c : c + 1, at] = notes[0:1, width + c * BLK : width + (c + 1) * BLK]
-            out_ref[:, at] = part_ref[:owned, 3 * BLK : 4 * BLK].astype(F32)
-
-    common_ref[...] = tree_sum([ref[owned:, start:].astype(F32) for ref in part_refs])
+            out_ref[:, at] = part_ref[:owned, out : out + BLK].astype(F32)
+
+    common = tree_sum(all_notes)
+    for row, common_ref in zip((1, 1, 2, 3, 4, 5), common_refs):
+        for j in range(common_ref.shape[0]):
+            common_ref[j : j + 1, :] = common[row : row + 1, j * BLK : (j + 1) * BLK]
 
 
 def kernel_call(body, out_shapes, operands, scratch=(), micros=1.0, space=pltpu.VMEM, limit=20):
@@ -406,16 +425,17 @@
     if direct:
         own = shares[0]
         own_near, own_far = to_level(own, 1), to_level(own, 3)
-        received, own, own_near, own_far, message = lax.optimization_barrier(
-            (received, own, own_near, own_far, message)
+        others = kernel_call(join_kernel, [shape(((PLANE - 1) * owned, columns), BF16)], received, micros=20)[0]
+        others, own, own_near, own_far, message = lax.optimization_barrier(
+            (others, own, own_near, own_far, message)
         )
-        others = jnp.concatenate(received, axis=0)
         near, far = to_level(others, 1), to_level(others, 3)
-        own_mid = to_pass(jnp.where(is_inner(), own_far, own))
+        own_mid = to_pass(kernel_call(choose_kernel, [shape(own.shape, BF16)], (own, own_far))[0])
     messages = [message] + [to_plane(message, k) for k in range(1, PLANE)]
     if direct:
-        messages, own_mid, near, far = lax.optimization_barrier((messages, own_mid, near, far))
-        mid = to_pass(jnp.where(is_inner(), far, others))
+        chosen = kernel_call(choose_kernel, [shape(others.shape, BF16)], (others, far), micros=20)[0]
+        messages, own_mid, near, far, chosen = lax.optimization_barrier((messages, own_mid, near, far, chosen))
+        mid = to_pass(chosen)
         pieces = [own, own_near, own_mid, own_far, others, near, mid, far]
     else:
         every = jnp.concatenate(xor_sorted([shares[0]] + received, plane_at), axis=0)
@@ -433,12 +453,11 @@
     block_at = jnp.minimum(plane_at, head_blocks - 1) * BLK
     bias_heads = lax.dynamic_slice_in_dim(b_qkv, block_at, BLK, 1).reshape(1, 3 * BLK)
     bias_up = lax.dynamic_slice_in_dim(b_up, plane_at * width, width, 0).reshape(1, width)
-    att, gp, act, gh, w, gb, *messages = kernel_call(
+    za, gp, gh, w, gb, *messages = kernel_call(
         partial(layer_kernel, direct),
         [
-            shape((rows_all, BLK), BF16),
+            shape((rows_all, BLK + width), BF16),
             shape((rows_all, 3 * BLK), BF16),
-            shape((rows_all, width), BF16),
             shape((rows_all, width), BF16),
             shape((model, columns), BF16),
             shape((1, width + 3 * BLK), F32),
@@ -454,15 +473,18 @@
     keep, send = kernel_call(
         products_kernel,
         [shape((rows_all + NOTES, model), BF16)] * 2,
-        (params, xh, w, act, gh, att, gp, gb, bo),
+        (params, xh, w, za, gp, gh, gb, bo),
         scratch=[pltpu.VMEM((2, slots, model), F32)],
         micros=4,
     )
     from_peer = to_peer(send)
     extra, extra_shapes = (), []
     if direct:
-        passed, from_peer = lax.optimization_barrier((passed, from_peer))
-        extra = (passed, messages[1], messages[3])
+        relayed = kernel_call(
+            relay_kernel, [shape((PLANE * owned, columns), BF16)], (messages[3], passed), micros=20
+        )[0]
+        relayed, from_peer = lax.optimization_barrier((relayed, from_peer))
+        extra = (messages[1], relayed)
         extra_shapes = [shape((PLANE * owned + NOTES, columns), BF16)] * 2
     laid = kernel_call(
         partial(pair_kernel, direct),
@@ -501,32 +523,30 @@
         [shape((own_rows, model), BF16), shape((own_rows, model), F32)],
         (residual, g_own, b_out.reshape(1, model), b_down.reshape(1, model), *parts),
     )
-    grad_up, grad_down, grad_qkv, grad_out_w, grad_b_up, grad_b_qkv, common = kernel_call(
+    grad_up, grad_down, grad_qkv, grad_out_w, grad_b_up, grad_b_qkv, *common = kernel_call(
         owner_kernel,
         [
             shape((owned, PLANE * width), F32),
             shape((owned, PLANE * width), F32),
             shape((3, owned, head_blocks * BLK), F32),
             shape((owned, head_blocks * BLK), F32),
-            shape((1, PLANE * width), F32),
+            shape((PLANE * width // BLK, BLK), F32),
             shape((3, head_blocks * BLK), F32),
-            shape((NOTES, model), F32),
-        ],
+        ]
+        + [shape((model // BLK, BLK), F32)] * 6,
         backs,
     )
+    common = [total.reshape(model) for total in common]
     return (
         result,
         grad_residual,
-        common[2],
-        common[3],
-        common[4],
-        common[5],
+        *common[2:],
         grad_qkv,
         grad_b_qkv,
         grad_out_w.T,
-        common[1],
+        common[0],
         grad_up,
-        grad_b_up[0],
+        grad_b_up.reshape(PLANE * width),
         grad_down.T,
         common[1],
     )

time: 123 us -> 112 us (0.911)
  waiting for transfers between devices: 67.2 us -> 54.8 us
  starting transfers between devices: 27 us -> 32.6 us
  Pallas kernels: 23.1 us -> 21.1 us
  other arithmetic: 1.63 us -> 0.03 us
    ppermute x3, waiting for transfers between devices: 26.8 us -> 16.5 us  [to_pass(): lax.ppermute(x, 'dp', [(a * PLANE + j, b * PLANE + j) for a, b in pairs f...]
    ppermute x3, starting transfers between devices: 1.52 us -> 8.01 us  [to_pass(): lax.ppermute(x, 'dp', [(a * PLANE + j, b * PLANE + j) for a, b in pairs f...]
    ppermute x7, waiting for transfers between devices: 16.9 us -> 13.4 us  [to_level(): return lax.ppermute(x, 'dp', [(j, j ^ m * PLANE) for j in range(places)])]
    ppermute x12, waiting for transfers between devices: 21.5 us -> 24 us  [to_plane(): return lax.ppermute(x, 'dp', [(j, j ^ k) for j in range(places)])]
    pallas_call x8 -> x12, Pallas kernels: 23.1 us -> 21.1 us  [kernel_call(): pl.pallas_call(body, out_shape=out_shapes, in_specs=[taken] * len(operand...]
  transfers between devices with their start and end apart: 24 -> 24, of which waited for: 13 -> 12; matrix products, arithmetic and copies ran while one was open for 2% -> 1% of each run, Pallas kernels for 4% -> 8%
where the time goes in v4:
time: 112 us
  waiting for transfers between devices  54.8 us (49%)
  starting transfers between devices  32.6 us (29%)
  Pallas kernels  21.1 us (19%)
  local copies, waits for them, and re-layouts  2.19 us (2%)
  between operations  1.25 us (1%)
    ppermute x12, waiting for transfers between devices, to_plane(): return lax.ppermute(x, 'dp', [(j, j ^ k) for j in range(places)])  24 us
    pallas_call x12, Pallas kernels, kernel_call(): pl.pallas_call(body, out_shape=out_shapes, in_specs=[taken] * len(operand...  21.1 us
    ppermute x3, waiting for transfers between devices, to_pass(): lax.ppermute(x, 'dp', [(a * PLANE + j, b * PLANE + j) for a, b in pairs f...  16.5 us
    ppermute x12, starting transfers between devices, to_plane(): return lax.ppermute(x, 'dp', [(j, j ^ k) for j in range(places)])  14 us
    ppermute x7, waiting for transfers between devices, to_level(): return lax.ppermute(x, 'dp', [(j, j ^ m * PLANE) for j in range(places)])  13.4 us
    ppermute x7, starting transfers between devices, to_level(): return lax.ppermute(x, 'dp', [(j, j ^ m * PLANE) for j in range(places)])  10.5 us
    ppermute x3, starting transfers between devices, to_pass(): lax.ppermute(x, 'dp', [(a * PLANE + j, b * PLANE + j) for a, b in pairs f...  8.01 us
  transfers between devices with their start and end apart: 24, of which 12 were waited for; matrix products, arithmetic and copies ran while one was open for 1% of the time, Pallas kernels for 8%

profile of v4, /device:TPU:0, one launch (start us, length us, event | category | flops | bytes accessed | tf_op | source)
XLA Modules:
  0.0 112.0 jit_solution(14202601955608239250)
XLA Ops:
  0.6 0.0 copy-start
  0.7 2.0 %shard_map.281 = (bf16[48,1280]{1,0:T(8,128)(2,1)}, bf16[48,1280]{1,0:T(8,128)(2,1)}, bf16[48,1280]{1,0:T(8,128)(2,1)}, bf16[48,1280]{1,0:T(8,128)(2,1)}) custom-call(bf16[3,48,384]{2,1,0:T(8,128)(2,1)} %refs_0_.1, bf16[48,384]{1,0:T(8,128)(2,1)} %bitcast.19, bf16[48,1536]{1,0:T(8,128)(2,1)} %refs_2_.1, bf16[48,1536]{1,0:T(8,128)(2,1)} %bitcast.18), custom_call_target="tpu_custom_call" | custom-call | flops 1000000000 | bytes 1 | tf_op jit(solution)/shard_map/pallas_call | solution.py:355
  2.7 3.1 %collective-permute-start.3 = (bf16[48,1280]{1,0:T(8,128)(2,1)}, bf16[48,1280]{1,0:T(8,128)(2,1)S(1)}, u32[]{:S(2)}, u32[]{:S(2)}) collective-permute-start(bf16[48,1280]{1,0:T(8,128)(2,1)} %get-tuple-element.96.own_ref.refs_9_), channel_id=1, source_target_pairs={{0,8},{2,10},{4,12},{6,14},{8,0},{10,2},{12,4},{14,6},{16,24},{18,... | collective-permute-start | bytes 368648 | tf_op jit(solution)/shard_map/ppermute | solution.py:401
  5.8 2.5 %collective-permute-start.4 = (bf16[48,1280]{1,0:T(8,128)(2,1)}, bf16[48,1280]{1,0:T(8,128)(2,1)S(1)}, u32[]{:S(2)}, u32[]{:S(2)}) collective-permute-start(bf16[48,1280]{1,0:T(8,128)(2,1)} %get-tuple-element.96.own_ref.refs_9_), channel_id=1, source_target_pairs={{0,24},{2,26},{4,28},{6,30},{8,16},{10,18},{12,20},{14,22},{16,8},... | collective-permute-start | bytes 368648 | tf_op jit(solution)/shard_map/ppermute | solution.py:401
  8.2 1.5 %collective-permute-start = (bf16[48,1280]{1,0:T(8,128)(2,1)}, bf16[48,1280]{1,0:T(8,128)(2,1)S(1)}, u32[]{:S(2)}, u32[]{:S(2)}) collective-permute-start(bf16[48,1280]{1,0:T(8,128)(2,1)} %get-tuple-element.88), channel_id=1, source_target_pairs={{0,2},{2,0},{4,6},{6,4},{8,10},{10,8},{12,14},{14,12},{16,18},{18,... | collective-permute-start | bytes 368648 | tf_op jit(solution)/shard_map/ppermute | solution.py:398
  9.7 1.5 %collective-permute-start.1 = (bf16[48,1280]{1,0:T(8,128)(2,1)}, bf16[48,1280]{1,0:T(8,128)(2,1)S(1)}, u32[]{:S(2)}, u32[]{:S(2)}) collective-permute-start(bf16[48,1280]{1,0:T(8,128)(2,1)} %get-tuple-element.89), channel_id=1, source_target_pairs={{0,4},{2,6},{4,0},{6,2},{8,12},{10,14},{12,8},{14,10},{16,20},{18,... | collective-permute-start | bytes 368648 | tf_op jit(solution)/shard_map/ppermute | solution.py:398
  11.2 0.5 collective-permute-start.2
  11.8 2.2 %collective-permute-done.refs_0_ = bf16[48,1280]{1,0:T(8,128)(2,1)S(1)} collective-permute-done((bf16[48,1280]{1,0:T(8,128)(2,1)}, bf16[48,1280]{1,0:T(8,128)(2,1)S(1)}, u32[]{:S(2)}, u32[]{:S(2)}) %collective-permute-start) | collective-permute-done | bytes 122912 | tf_op jit(solution)/shard_map/ppermute | solution.py:398
  14.0 3.5 %collective-permute-done.1.refs_1_ = bf16[48,1280]{1,0:T(8,128)(2,1)S(1)} collective-permute-done((bf16[48,1280]{1,0:T(8,128)(2,1)}, bf16[48,1280]{1,0:T(8,128)(2,1)S(1)}, u32[]{:S(2)}, u32[]{:S(2)}) %collective-permute-start.1) | collective-permute-done | bytes 122912 | tf_op jit(solution)/shard_map/ppermute | solution.py:398
  17.5 0.6 copy-done.3
  18.2 1.3 %collective-permute-start.10 = (bf16[144,1280]{1,0:T(8,128)(2,1)S(1)}, bf16[144,1280]{1,0:T(8,128)(2,1)S(1)}, u32[]{:S(2)}, u32[]{:S(2)}) collective-permute-start(bf16[144,1280]{1,0:T(8,128)(2,1)S(1)} %shard_map.282.own_ref.refs_13_), channel_id=1, source_target_pairs={{0,24},{2,26},{4,28},{6,30},{8,16},{10,18},{12,20},{14,22},{16,8},... | collective-permute-start | bytes 1105928 | tf_op jit(solution)/shard_map/ppermute | solution.py:401
  19.5 0.7 collective-permute-start.5
  20.2 0.8 collective-permute-start.6
  21.0 2.0 %collective-permute-start.7 = (bf16[272,768]{1,0:T(8,128)(2,1)S(1)}, bf16[272,768]{1,0:T(8,128)(2,1)S(1)}, u32[]{:S(2)}, u32[]{:S(2)}) collective-permute-start(bf16[272,768]{1,0:T(8,128)(2,1)S(1)} %fusion.1), channel_id=1, source_target_pairs={{0,6},{2,4},{4,2},{6,0},{8,14},{10,12},{12,10},{14,8},{16,22},{18,... | collective-permute-start | bytes 1253384 | tf_op jit(solution)/shard_map/ppermute | solution.py:398
  23.1 8.5 %collective-permute-done.10.far_ref.refs_16_ = bf16[144,1280]{1,0:T(8,128)(2,1)S(1)} collective-permute-done((bf16[144,1280]{1,0:T(8,128)(2,1)S(1)}, bf16[144,1280]{1,0:T(8,128)(2,1)S(1)}, u32[]{:S(2)}, u32[]{:S(2)}) %collective-permute-start.10) | collective-permute-done | bytes 368672 | tf_op jit(solution)/shard_map/ppermute | solution.py:401
  31.5 3.4 %collective-permute-start.8 = (bf16[48,1280]{1,0:T(8,128)(2,1)S(1)}, bf16[48,1280]{1,0:T(8,128)(2,1)S(1)}, u32[]{:S(2)}, u32[]{:S(2)}) collective-permute-start(bf16[48,1280]{1,0:T(8,128)(2,1)S(1)} %shard_map.283), channel_id=1, source_target_pairs={{0,16},{2,18},{4,20},{6,22},{24,8},{26,10},{28,12},{30,14},{8,0},{... | collective-permute-start | bytes 368648 | tf_op jit(solution)/shard_map/ppermute | solution.py:410
  35.0 0.1 shard_map.284
  35.1 4.0 %collective-permute-done.8.refs_11_ = bf16[48,1280]{1,0:T(8,128)(2,1)S(1)} collective-permute-done((bf16[48,1280]{1,0:T(8,128)(2,1)S(1)}, bf16[48,1280]{1,0:T(8,128)(2,1)S(1)}, u32[]{:S(2)}, u32[]{:S(2)}) %collective-permute-start.8) | collective-permute-done | bytes 122912 | tf_op jit(solution)/shard_map/ppermute | solution.py:410
  39.3 0.5 copy-done.7
  39.9 0.8 dynamic_slice.7
  40.8 1.7 %collective-permute-start.12 = (bf16[144,1280]{1,0:T(8,128)(2,1)S(1)}, bf16[144,1280]{1,0:T(8,128)(2,1)S(1)}, u32[]{:S(2)}, u32[]{:S(2)}) collective-permute-start(bf16[144,1280]{1,0:T(8,128)(2,1)S(1)} %shard_map.284), channel_id=1, source_target_pairs={{0,16},{2,18},{4,20},{6,22},{24,8},{26,10},{28,12},{30,14},{8,0},{... | collective-permute-start | bytes 1105928 | tf_op jit(solution)/shard_map/ppermute | solution.py:410
  42.5 1.0 collective-permute-done.11.peer_ref
  43.4 3.4 %shard_map.285 = (bf16[1024,768]{1,0:T(8,128)(2,1)S(1)}, bf16[1024,768]{1,0:T(8,128)(2,1)S(1)}, bf16[1024,768]{1,0:T(8,128)(2,1)S(1)}, bf16[1024,768]{1,0:T(8,12...) custom-call(f32[8,768]{1,0:T(8,128)S(1)} %stack.23.params_ref, ...), custom_call_target="tpu_custom_call" | custom-call | flops 4000000000 | bytes 1 | tf_op jit(solution)/shard_map/pallas_call | solution.py:355
  46.8 5.2 %collective-permute-done.12.refs_15_ = bf16[144,1280]{1,0:T(8,128)(2,1)S(1)} collective-permute-done((bf16[144,1280]{1,0:T(8,128)(2,1)S(1)}, bf16[144,1280]{1,0:T(8,128)(2,1)S(1)}, u32[]{:S(2)}, u32[]{:S(2)}) %collective-permute-start.12) | collective-permute-done | bytes 368672 | tf_op jit(solution)/shard_map/ppermute | solution.py:410
  52.0 8.7 %shard_map.286 = (bf16[1024,512]{1,0:T(8,128)(2,1)S(1)}, bf16[1024,384]{1,0:T(8,128)(2,1)S(1)}, bf16[1024,384]{1,0:T(8,128)(2,1)S(1)}, bf16[768,1280]{1,0:T(8,12...) custom-call(f32[8,128]{1,0:T(8,128)S(1)} %get-tuple-element.105.refs, ...), custom_call_target="tpu_custom_call" | custom-call | flops 12000000000 | bytes 1 | tf_op jit(solution)/shard_map/pallas_call | solution.py:355
  60.7 2.9 %collective-permute-start.13 = (bf16[192,1280]{1,0:T(8,128)(2,1)S(1)}, bf16[192,1280]{1,0:T(8,128)(2,1)S(1)}, u32[]{:S(2)}, u32[]{:S(2)}) collective-permute-start(bf16[192,1280]{1,0:T(8,128)(2,1)S(1)} %get-tuple-element.122), channel_id=1, source_target_pairs={{16,0},{18,2},{20,4},{22,6},{8,24},{10,26},{12,28},{14,30},{0,8},{... | collective-permute-start | bytes 1474568 | tf_op jit(solution)/shard_map/ppermute | solution.py:410
  63.6 3.9 %shard_map.287 = (bf16[1040,768]{1,0:T(8,128)(2,1)S(1)}, bf16[1040,768]{1,0:T(8,128)(2,1)S(1)}) custom-call(f32[8,768]{1,0:T(8,128)S(1)} %stack.23.params_ref, bf16[1024,768]{1,0:T(8,128)(2,1)S(1)} %get-tuple-element.104.xh_ref, bf16[768,1280]{1,0:T(8,128)(2,1)S(1)} %get-tuple-element.114.w_ref, bf16[1024,512]{1,0:T(8,128)(2,1)S(1)} %get-tuple-element.115.za_ref, ...), custom_call_target="tpu_custom_call" | custom-call | flops 4000000000 | bytes 1 | tf_op jit(solution)/shard_map/pallas_call | solution.py:355
  67.4 0.1 collective-permute-start.14
  67.5 7.3 %collective-permute-done.13.passed_ref = bf16[192,1280]{1,0:T(8,128)(2,1)S(1)} collective-permute-done((bf16[192,1280]{1,0:T(8,128)(2,1)S(1)}, bf16[192,1280]{1,0:T(8,128)(2,1)S(1)}, u32[]{:S(2)}, u32[]{:S(2)}) %collective-permute-start.13) | collective-permute-done | bytes 491552 | tf_op jit(solution)/shard_map/ppermute | solution.py:410
  74.8 0.2 shard_map.288.refs_1_
  75.0 0.4 shard_map.289
  75.4 1.7 %collective-permute-start.18 = (bf16[208,1280]{1,0:T(8,128)(2,1)S(1)}, bf16[208,1280]{1,0:T(8,128)(2,1)S(1)}, u32[]{:S(2)}, u32[]{:S(2)}) collective-permute-start(bf16[208,1280]{1,0:T(8,128)(2,1)S(1)} %get-tuple-element.133), channel_id=1, source_target_pairs={{0,8},{2,10},{4,12},{6,14},{8,0},{10,2},{12,4},{14,6},{16,24},{18,... | collective-permute-start | bytes 1597448 | tf_op jit(solution)/shard_map/ppermute | solution.py:401
  77.1 1.2 %collective-permute-start.19 = (bf16[208,1280]{1,0:T(8,128)(2,1)S(1)}, bf16[208,1280]{1,0:T(8,128)(2,1)S(1)}, u32[]{:S(2)}, u32[]{:S(2)}) collective-permute-start(bf16[208,1280]{1,0:T(8,128)(2,1)S(1)} %get-tuple-element.134), channel_id=1, source_target_pairs={{0,24},{2,26},{4,28},{6,30},{8,16},{10,18},{12,20},{14,22},{16,8},... | collective-permute-start | bytes 1597448 | tf_op jit(solution)/shard_map/ppermute | solution.py:401
  78.3 1.5 %collective-permute-start.15 = (bf16[256,768]{1,0:T(8,128)(2,1)S(1)}, bf16[256,768]{1,0:T(8,128)(2,1)S(1)}, u32[]{:S(2)}, u32[]{:S(2)}) collective-permute-start(bf16[256,768]{1,0:T(8,128)(2,1)S(1)} %get-tuple-element.129), channel_id=1, source_target_pairs={{0,2},{2,0},{4,6},{6,4},{8,10},{10,8},{12,14},{14,12},{16,18},{18,... | collective-permute-start | bytes 1179656 | tf_op jit(solution)/shard_map/ppermute | solution.py:398
  79.8 0.5 collective-permute-start.16
  80.3 1.5 %collective-permute-start.17 = (bf16[256,768]{1,0:T(8,128)(2,1)S(1)}, bf16[256,768]{1,0:T(8,128)(2,1)S(1)}, u32[]{:S(2)}, u32[]{:S(2)}) collective-permute-start(bf16[256,768]{1,0:T(8,128)(2,1)S(1)} %get-tuple-element.132), channel_id=1, source_target_pairs={{0,6},{2,4},{4,2},{6,0},{8,14},{10,12},{12,10},{14,8},{16,22},{18,... | collective-permute-start | bytes 1179656 | tf_op jit(solution)/shard_map/ppermute | solution.py:398
  81.8 8.6 %collective-permute-done.15.refs_1_ = bf16[256,768]{1,0:T(8,128)(2,1)S(1)} collective-permute-done((bf16[256,768]{1,0:T(8,128)(2,1)S(1)}, bf16[256,768]{1,0:T(8,128)(2,1)S(1)}, u32[]{:S(2)}, u32[]{:S(2)}) %collective-permute-start.15) | collective-permute-done | bytes 393248 | tf_op jit(solution)/shard_map/ppermute | solution.py:398
  90.3 0.7 collective-permute-start.20
  91.0 6.2 %collective-permute-done.16.refs_2_ = bf16[256,768]{1,0:T(8,128)(2,1)S(1)} collective-permute-done((bf16[256,768]{1,0:T(8,128)(2,1)S(1)}, bf16[256,768]{1,0:T(8,128)(2,1)S(1)}, u32[]{:S(2)}, u32[]{:S(2)}) %collective-permute-start.16) | collective-permute-done | bytes 393248 | tf_op jit(solution)/shard_map/ppermute | solution.py:398
  97.2 4.9 %collective-permute-done.20.notes_middle_ref = bf16[16,768]{1,0:T(8,128)(2,1)S(1)} collective-permute-done((bf16[16,768]{1,0:T(8,128)(2,1)S(1)}, bf16[16,768]{1,0:T(8,128)(2,1)S(1)}, u32[]{:S(2)}, u32[]{:S(2)}) %collective-permute-start.20) | collective-permute-done | bytes 24608 | tf_op jit(solution)/shard_map/ppermute | solution.py:401
  102.1 0.3 shard_map.291
  102.4 1.3 %collective-permute-start.21 = (bf16[64,1280]{1,0:T(8,128)(2,1)S(1)}, bf16[64,1280]{1,0:T(8,128)(2,1)S(1)}, u32[]{:S(2)}, u32[]{:S(2)}) collective-permute-start(bf16[64,1280]{1,0:T(8,128)(2,1)S(1)} %get-tuple-element.147), channel_id=1, source_target_pairs={{0,2},{2,0},{4,6},{6,4},{8,10},{10,8},{12,14},{14,12},{16,18},{18,... | collective-permute-start | bytes 491528 | tf_op jit(solution)/shard_map/ppermute | solution.py:398
  103.7 0.4 collective-permute-start.22
  104.1 1.9 %collective-permute-start.23 = (bf16[64,1280]{1,0:T(8,128)(2,1)S(1)}, bf16[64,1280]{1,0:T(8,128)(2,1)S(1)}, u32[]{:S(2)}, u32[]{:S(2)}) collective-permute-start(bf16[64,1280]{1,0:T(8,128)(2,1)S(1)} %get-tuple-element.149), channel_id=1, source_target_pairs={{0,6},{2,4},{4,2},{6,0},{8,14},{10,12},{12,10},{14,8},{16,22},{18,... | collective-permute-start | bytes 491528 | tf_op jit(solution)/shard_map/ppermute | solution.py:398
  106.0 1.2 %shard_map.290 = (bf16[128,768]{1,0:T(8,128)(2,1)}, f32[128,768]{1,0:T(8,128)}) custom-call(bf16[128,768]{1,0:T(8,128)(2,1)S(1)} %copy-done.1, bf16[128,768]{1,0:T(8,128)(2,1)S(1)} %get-tuple-element.103.g_ref, f32[1,768]{1,0:T(1,128)S(1)} %reshape.61.b_out_ref, f32[1,768]{1,0:T(1,128)S(1)} %reshape.62.b_down_ref, ...), custom_call_target="tpu_custom_call" | custom-call | flops 1000000000 | bytes 1 | tf_op jit(solution)/shard_map/pallas_call | solution.py:355
  107.2 0.6 collective-permute-done.21.refs_1_
  107.8 3.0 %collective-permute-done.22.refs_2_ = bf16[64,1280]{1,0:T(8,128)(2,1)S(1)} collective-permute-done((bf16[64,1280]{1,0:T(8,128)(2,1)S(1)}, bf16[64,1280]{1,0:T(8,128)(2,1)S(1)}, u32[]{:S(2)}, u32[]{:S(2)}) %collective-permute-start.22) | collective-permute-done | bytes 163872 | tf_op jit(solution)/shard_map/ppermute | solution.py:398
  110.8 1.0 shard_map.292
  (70 shorter events, 0.4 us)
Async XLA Ops:
  0.6 39.2 %copy-start = (f32[3,384]{1,0:T(4,128)S(1)}, f32[3,384]{1,0:T(4,128)}, u32[]{:S(2)}) copy-start(f32[3,384]{1,0:T(4,128)} %param.26) | copy-start | bytes 13828
  0.7 11.1 %copy-start.19 = (s32[1,4]{1,0:T(1,128)S(1)}, s32[1,4]{1,0:T(1,128)}, u32[]{:S(2)}) copy-start(s32[1,4]{1,0:T(1,128)} %param.20) | copy-start | bytes 52
  0.7 11.1 %copy-start.1 = (bf16[128,768]{1,0:T(8,128)(2,1)S(1)}, bf16[128,768]{1,0:T(8,128)(2,1)}, u32[]{:S(2)}) copy-start(bf16[128,768]{1,0:T(8,128)(2,1)} %residual_ref.1) | copy-start | bytes 589828
  0.7 11.1 %copy-start.12 = (bf16[128,768]{1,0:T(8,128)(2,1)S(1)}, bf16[128,768]{1,0:T(8,128)(2,1)}, u32[]{:S(2)}) copy-start(bf16[128,768]{1,0:T(8,128)(2,1)} %param.19) | copy-start | bytes 589828
  2.7 14.8 %collective-permute-start.3 = (bf16[48,1280]{1,0:T(8,128)(2,1)}, bf16[48,1280]{1,0:T(8,128)(2,1)S(1)}, u32[]{:S(2)}, u32[]{:S(2)}) collective-permute-start(bf16[48,1280]{1,0:T(8,128)(2,1)} %get-tuple-element.96.own_ref.refs_9_), channel_id=1, source_target_pairs={{0,8},{2,10},{4,12},{6,14},{8,0},{10,2},{12,4},{14,6},{16,24},{18,... | collective-permute-start | bytes 368648 | tf_op jit(solution)/shard_map/ppermute | solution.py:401
  5.8 12.4 %collective-permute-start.4 = (bf16[48,1280]{1,0:T(8,128)(2,1)}, bf16[48,1280]{1,0:T(8,128)(2,1)S(1)}, u32[]{:S(2)}, u32[]{:S(2)}) collective-permute-start(bf16[48,1280]{1,0:T(8,128)(2,1)} %get-tuple-element.96.own_ref.refs_9_), channel_id=1, source_target_pairs={{0,24},{2,26},{4,28},{6,30},{8,16},{10,18},{12,20},{14,22},{16,8},... | collective-permute-start | bytes 368648 | tf_op jit(solution)/shard_map/ppermute | solution.py:401
  8.2 5.7 %collective-permute-start = (bf16[48,1280]{1,0:T(8,128)(2,1)}, bf16[48,1280]{1,0:T(8,128)(2,1)S(1)}, u32[]{:S(2)}, u32[]{:S(2)}) collective-permute-start(bf16[48,1280]{1,0:T(8,128)(2,1)} %get-tuple-element.88), channel_id=1, source_target_pairs={{0,2},{2,0},{4,6},{6,4},{8,10},{10,8},{12,14},{14,12},{16,18},{18,... | collective-permute-start | bytes 368648 | tf_op jit(solution)/shard_map/ppermute | solution.py:398
  9.7 7.7 %collective-permute-start.1 = (bf16[48,1280]{1,0:T(8,128)(2,1)}, bf16[48,1280]{1,0:T(8,128)(2,1)S(1)}, u32[]{:S(2)}, u32[]{:S(2)}) collective-permute-start(bf16[48,1280]{1,0:T(8,128)(2,1)} %get-tuple-element.89), channel_id=1, source_target_pairs={{0,4},{2,6},{4,0},{6,2},{8,12},{10,14},{12,8},{14,10},{16,20},{18,... | collective-permute-start | bytes 368648 | tf_op jit(solution)/shard_map/ppermute | solution.py:398
  11.2 6.2 %collective-permute-start.2 = (bf16[48,1280]{1,0:T(8,128)(2,1)}, bf16[48,1280]{1,0:T(8,128)(2,1)S(1)}, u32[]{:S(2)}, u32[]{:S(2)}) collective-permute-start(bf16[48,1280]{1,0:T(8,128)(2,1)} %get-tuple-element.90), channel_id=1, source_target_pairs={{0,6},{2,4},{4,2},{6,0},{8,14},{10,12},{12,10},{14,8},{16,22},{18,... | collective-permute-start | bytes 368648 | tf_op jit(solution)/shard_map/ppermute | solution.py:398
  11.8 11.2 %copy-start.2 = (bf16[48,1280]{1,0:T(8,128)(2,1)S(1)}, bf16[48,1280]{1,0:T(8,128)(2,1)}, u32[]{:S(2)}) copy-start(bf16[48,1280]{1,0:T(8,128)(2,1)} %get-tuple-element.96.own_ref.refs_9_) | copy-start | bytes 368644
  17.5 0.7 copy-start.3
  18.1 4.9 %copy-start.5 = (bf16[48,1280]{1,0:T(8,128)(2,1)}, bf16[48,1280]{1,0:T(8,128)(2,1)S(1)}, u32[]{:S(2)}) copy-start(bf16[48,1280]{1,0:T(8,128)(2,1)S(1)} %collective-permute-done.4.far_ref.refs_12_) | copy-start | bytes 368644
  18.2 13.4 %collective-permute-start.10 = (bf16[144,1280]{1,0:T(8,128)(2,1)S(1)}, bf16[144,1280]{1,0:T(8,128)(2,1)S(1)}, u32[]{:S(2)}, u32[]{:S(2)}) collective-permute-start(bf16[144,1280]{1,0:T(8,128)(2,1)S(1)} %shard_map.282.own_ref.refs_13_), channel_id=1, source_target_pairs={{0,24},{2,26},{4,28},{6,30},{8,16},{10,18},{12,20},{14,22},{16,8},... | collective-permute-start | bytes 1105928 | tf_op jit(solution)/shard_map/ppermute | solution.py:401
  19.5 19.6 %collective-permute-start.5 = (bf16[272,768]{1,0:T(8,128)(2,1)S(1)}, bf16[272,768]{1,0:T(8,128)(2,1)S(1)}, u32[]{:S(2)}, u32[]{:S(2)}) collective-permute-start(bf16[272,768]{1,0:T(8,128)(2,1)S(1)} %fusion.1), channel_id=1, source_target_pairs={{0,2},{2,0},{4,6},{6,4},{8,10},{10,8},{12,14},{14,12},{16,18},{18,... | collective-permute-start | bytes 1253384 | tf_op jit(solution)/shard_map/ppermute | solution.py:398
  20.2 18.9 %collective-permute-start.6 = (bf16[272,768]{1,0:T(8,128)(2,1)S(1)}, bf16[272,768]{1,0:T(8,128)(2,1)S(1)}, u32[]{:S(2)}, u32[]{:S(2)}) collective-permute-start(bf16[272,768]{1,0:T(8,128)(2,1)S(1)} %fusion.1), channel_id=1, source_target_pairs={{0,4},{2,6},{4,0},{6,2},{8,12},{10,14},{12,8},{14,10},{16,20},{18,... | collective-permute-start | bytes 1253384 | tf_op jit(solution)/shard_map/ppermute | solution.py:398
  21.0 18.1 %collective-permute-start.7 = (bf16[272,768]{1,0:T(8,128)(2,1)S(1)}, bf16[272,768]{1,0:T(8,128)(2,1)S(1)}, u32[]{:S(2)}, u32[]{:S(2)}) collective-permute-start(bf16[272,768]{1,0:T(8,128)(2,1)S(1)} %fusion.1), channel_id=1, source_target_pairs={{0,6},{2,4},{4,2},{6,0},{8,14},{10,12},{12,10},{14,8},{16,22},{18,... | collective-permute-start | bytes 1253384 | tf_op jit(solution)/shard_map/ppermute | solution.py:398
  23.0 16.1 %collective-permute-start.9 = (bf16[144,1280]{1,0:T(8,128)(2,1)S(1)}, bf16[144,1280]{1,0:T(8,128)(2,1)S(1)}, u32[]{:S(2)}, u32[]{:S(2)}) collective-permute-start(bf16[144,1280]{1,0:T(8,128)(2,1)S(1)} %shard_map.282.own_ref.refs_13_), channel_id=1, source_target_pairs={{0,8},{2,10},{4,12},{6,14},{8,0},{10,2},{12,4},{14,6},{16,24},{18,... | collective-permute-start | bytes 1105928 | tf_op jit(solution)/shard_map/ppermute | solution.py:401
  31.5 7.6 %collective-permute-start.8 = (bf16[48,1280]{1,0:T(8,128)(2,1)S(1)}, bf16[48,1280]{1,0:T(8,128)(2,1)S(1)}, u32[]{:S(2)}, u32[]{:S(2)}) collective-permute-start(bf16[48,1280]{1,0:T(8,128)(2,1)S(1)} %shard_map.283), channel_id=1, source_target_pairs={{0,16},{2,18},{4,20},{6,22},{24,8},{26,10},{28,12},{30,14},{8,0},{... | collective-permute-start | bytes 368648 | tf_op jit(solution)/shard_map/ppermute | solution.py:410
  35.1 4.7 %copy-start.13 = (f32[768]{0:T(1024)S(1)}, f32[768]{0:T(1024)}, u32[]{:S(2)}) copy-start(f32[768]{0:T(1024)} %param.21) | copy-start | bytes 9220
  35.1 4.7 %copy-start.14 = (f32[768]{0:T(1024)S(1)}, f32[768]{0:T(1024)}, u32[]{:S(2)}) copy-start(f32[768]{0:T(1024)} %param.22) | copy-start | bytes 9220
  35.1 4.7 %copy-start.15 = (f32[768]{0:T(1024)S(1)}, f32[768]{0:T(1024)}, u32[]{:S(2)}) copy-start(f32[768]{0:T(1024)} %param.23) | copy-start | bytes 9220
  35.1 4.7 %copy-start.16 = (f32[768]{0:T(1024)S(1)}, f32[768]{0:T(1024)}, u32[]{:S(2)}) copy-start(f32[768]{0:T(1024)} %param.24) | copy-start | bytes 9220
  39.1 0.6 copy-start.7
  39.7 3.7 %collective-permute-start.11 = (bf16[1088,768]{1,0:T(8,128)(2,1)S(1)}, bf16[1088,768]{1,0:T(8,128)(2,1)}, u32[]{:S(2)}, u32[]{:S(2)}) collective-permute-start(bf16[1088,768]{1,0:T(8,128)(2,1)S(1)} %constant_dynamic-update-slice_fusion.own_ref), channel_id=1, source_target_pairs={{0,1},{1,0},{2,3},{3,2},{4,5},{5,4},{6,7},{7,6},{8,9},{9,8},{10,11... | collective-permute-start | bytes 5013512 | tf_op jit(solution)/shard_map/ppermute | solution.py:404
  40.7 11.3 %copy-start.4 = (bf16[48,1280]{1,0:T(8,128)(2,1)S(1)}, bf16[48,1280]{1,0:T(8,128)(2,1)}, u32[]{:S(2)}) copy-start(bf16[48,1280]{1,0:T(8,128)(2,1)} %copy-done.3) | copy-start | bytes 368644
  40.7 11.3 %copy-start.6 = (bf16[48,1280]{1,0:T(8,128)(2,1)S(1)}, bf16[48,1280]{1,0:T(8,128)(2,1)}, u32[]{:S(2)}) copy-start(bf16[48,1280]{1,0:T(8,128)(2,1)} %copy-done.5) | copy-start | bytes 368644
  40.7 11.3 %copy-start.8 = (bf16[48,1280]{1,0:T(8,128)(2,1)S(1)}, bf16[48,1280]{1,0:T(8,128)(2,1)}, u32[]{:S(2)}) copy-start(bf16[48,1280]{1,0:T(8,128)(2,1)} %copy-done.7) | copy-start | bytes 368644
  40.7 11.3 %copy-start.9 = (f32[256,128]{1,0:T(8,128)S(1)}, f32[256,128]{1,0:T(8,128)}, u32[]{:S(2)}) copy-start(f32[256,128]{1,0:T(8,128)} %constant.38.clone.refs_6_) | copy-start | bytes 393220
  40.8 11.3 %copy-start.10 = (f32[256,128]{1,0:T(8,128)S(1)}, f32[256,128]{1,0:T(8,128)}, u32[]{:S(2)}) copy-start(f32[256,128]{1,0:T(8,128)} %constant.39.clone.refs_7_) | copy-start | bytes 393220
  40.8 11.3 %copy-start.11 = (f32[256,128]{1,0:T(8,128)S(1)}, f32[256,128]{1,0:T(8,128)}, u32[]{:S(2)}) copy-start(f32[256,128]{1,0:T(8,128)} %constant.40.clone.refs_8_) | copy-start | bytes 393220
  40.8 11.2 %collective-permute-start.12 = (bf16[144,1280]{1,0:T(8,128)(2,1)S(1)}, bf16[144,1280]{1,0:T(8,128)(2,1)S(1)}, u32[]{:S(2)}, u32[]{:S(2)}) collective-permute-start(bf16[144,1280]{1,0:T(8,128)(2,1)S(1)} %shard_map.284), channel_id=1, source_target_pairs={{0,16},{2,18},{4,20},{6,22},{24,8},{26,10},{28,12},{30,14},{8,0},{... | collective-permute-start | bytes 1105928 | tf_op jit(solution)/shard_map/ppermute | solution.py:410
  60.7 14.1 %collective-permute-start.13 = (bf16[192,1280]{1,0:T(8,128)(2,1)S(1)}, bf16[192,1280]{1,0:T(8,128)(2,1)S(1)}, u32[]{:S(2)}, u32[]{:S(2)}) collective-permute-start(bf16[192,1280]{1,0:T(8,128)(2,1)S(1)} %get-tuple-element.122), channel_id=1, source_target_pairs={{16,0},{18,2},{20,4},{22,6},{8,24},{10,26},{12,28},{14,30},{0,8},{... | collective-permute-start | bytes 1474568 | tf_op jit(solution)/shard_map/ppermute | solution.py:410
  67.4 7.5 %collective-permute-start.14 = (bf16[1040,768]{1,0:T(8,128)(2,1)S(1)}, bf16[1040,768]{1,0:T(8,128)(2,1)S(1)}, u32[]{:S(2)}, u32[]{:S(2)}) collective-permute-start(bf16[1040,768]{1,0:T(8,128)(2,1)S(1)} %get-tuple-element.123), channel_id=1, source_target_pairs={{0,1},{1,0},{2,3},{3,2},{4,5},{5,4},{6,7},{7,6},{8,9},{9,8},{10,11... | collective-permute-start | bytes 4792328 | tf_op jit(solution)/shard_map/ppermute | solution.py:404
  75.4 26.7 %collective-permute-start.18 = (bf16[208,1280]{1,0:T(8,128)(2,1)S(1)}, bf16[208,1280]{1,0:T(8,128)(2,1)S(1)}, u32[]{:S(2)}, u32[]{:S(2)}) collective-permute-start(bf16[208,1280]{1,0:T(8,128)(2,1)S(1)} %get-tuple-element.133), channel_id=1, source_target_pairs={{0,8},{2,10},{4,12},{6,14},{8,0},{10,2},{12,4},{14,6},{16,24},{18,... | collective-permute-start | bytes 1597448 | tf_op jit(solution)/shard_map/ppermute | solution.py:401
  77.1 25.0 %collective-permute-start.19 = (bf16[208,1280]{1,0:T(8,128)(2,1)S(1)}, bf16[208,1280]{1,0:T(8,128)(2,1)S(1)}, u32[]{:S(2)}, u32[]{:S(2)}) collective-permute-start(bf16[208,1280]{1,0:T(8,128)(2,1)S(1)} %get-tuple-element.134), channel_id=1, source_target_pairs={{0,24},{2,26},{4,28},{6,30},{8,16},{10,18},{12,20},{14,22},{16,8},... | collective-permute-start | bytes 1597448 | tf_op jit(solution)/shard_map/ppermute | solution.py:401
  78.3 12.1 %collective-permute-start.15 = (bf16[256,768]{1,0:T(8,128)(2,1)S(1)}, bf16[256,768]{1,0:T(8,128)(2,1)S(1)}, u32[]{:S(2)}, u32[]{:S(2)}) collective-permute-start(bf16[256,768]{1,0:T(8,128)(2,1)S(1)} %get-tuple-element.129), channel_id=1, source_target_pairs={{0,2},{2,0},{4,6},{6,4},{8,10},{10,8},{12,14},{14,12},{16,18},{18,... | collective-permute-start | bytes 1179656 | tf_op jit(solution)/shard_map/ppermute | solution.py:398
  79.8 17.4 %collective-permute-start.16 = (bf16[256,768]{1,0:T(8,128)(2,1)S(1)}, bf16[256,768]{1,0:T(8,128)(2,1)S(1)}, u32[]{:S(2)}, u32[]{:S(2)}) collective-permute-start(bf16[256,768]{1,0:T(8,128)(2,1)S(1)} %get-tuple-element.131), channel_id=1, source_target_pairs={{0,4},{2,6},{4,0},{6,2},{8,12},{10,14},{12,8},{14,10},{16,20},{18,... | collective-permute-start | bytes 1179656 | tf_op jit(solution)/shard_map/ppermute | solution.py:398
  80.3 17.0 %collective-permute-start.17 = (bf16[256,768]{1,0:T(8,128)(2,1)S(1)}, bf16[256,768]{1,0:T(8,128)(2,1)S(1)}, u32[]{:S(2)}, u32[]{:S(2)}) collective-permute-start(bf16[256,768]{1,0:T(8,128)(2,1)S(1)} %get-tuple-element.132), channel_id=1, source_target_pairs={{0,6},{2,4},{4,2},{6,0},{8,14},{10,12},{12,10},{14,8},{16,22},{18,... | collective-permute-start | bytes 1179656 | tf_op jit(solution)/shard_map/ppermute | solution.py:398
  90.3 11.7 %collective-permute-start.20 = (bf16[16,768]{1,0:T(8,128)(2,1)S(1)}, bf16[16,768]{1,0:T(8,128)(2,1)S(1)}, u32[]{:S(2)}, u32[]{:S(2)}) collective-permute-start(bf16[16,768]{1,0:T(8,128)(2,1)S(1)} %get-tuple-element.135.notes_ref), channel_id=1, source_target_pairs={{0,16},{2,18},{4,20},{6,22},{8,24},{10,26},{12,28},{14,30},{16,0},... | collective-permute-start | bytes 73736 | tf_op jit(solution)/shard_map/ppermute | solution.py:401
  102.1 3.9 %copy-start.17 = (f32[768]{0:T(1024)S(1)}, f32[768]{0:T(1024)}, u32[]{:S(2)}) copy-start(f32[768]{0:T(1024)} %param.28) | copy-start | bytes 9220
  102.1 3.9 %copy-start.18 = (f32[768]{0:T(1024)S(1)}, f32[768]{0:T(1024)}, u32[]{:S(2)}) copy-start(f32[768]{0:T(1024)} %param.32) | copy-start | bytes 9220
  102.4 5.4 %collective-permute-start.21 = (bf16[64,1280]{1,0:T(8,128)(2,1)S(1)}, bf16[64,1280]{1,0:T(8,128)(2,1)S(1)}, u32[]{:S(2)}, u32[]{:S(2)}) collective-permute-start(bf16[64,1280]{1,0:T(8,128)(2,1)S(1)} %get-tuple-element.147), channel_id=1, source_target_pairs={{0,2},{2,0},{4,6},{6,4},{8,10},{10,8},{12,14},{14,12},{16,18},{18,... | collective-permute-start | bytes 491528 | tf_op jit(solution)/shard_map/ppermute | solution.py:398
  103.7 7.1 %collective-permute-start.22 = (bf16[64,1280]{1,0:T(8,128)(2,1)S(1)}, bf16[64,1280]{1,0:T(8,128)(2,1)S(1)}, u32[]{:S(2)}, u32[]{:S(2)}) collective-permute-start(bf16[64,1280]{1,0:T(8,128)(2,1)S(1)} %get-tuple-element.148), channel_id=1, source_target_pairs={{0,4},{2,6},{4,0},{6,2},{8,12},{10,14},{12,8},{14,10},{16,20},{18,... | collective-permute-start | bytes 491528 | tf_op jit(solution)/shard_map/ppermute | solution.py:398
  104.1 6.7 %collective-permute-start.23 = (bf16[64,1280]{1,0:T(8,128)(2,1)S(1)}, bf16[64,1280]{1,0:T(8,128)(2,1)S(1)}, u32[]{:S(2)}, u32[]{:S(2)}) collective-permute-start(bf16[64,1280]{1,0:T(8,128)(2,1)S(1)} %get-tuple-element.149), channel_id=1, source_target_pairs={{0,6},{2,4},{4,2},{6,0},{8,14},{10,12},{12,10},{14,8},{16,22},{18,... | collective-permute-start | bytes 491528 | tf_op jit(solution)/shard_map/ppermute | solution.py:398

commit v5 on v4

--- a/solution.py
+++ b/solution.py
@@ -139,15 +139,17 @@
 
 def layer_kernel(levels, *refs):
     length_ref, x1_ref, x2_ref, g_ref, bias_ref, bias_up_ref, keep_ref, low_ref, high_ref = refs[:9]
-    pieces = refs[9 : 9 + max(2 * levels, 1)]
+    pieces = refs[9 : 9 + (7 if levels else 1)]
     za_ref, gp_ref, gh_ref, w_ref, gb_ref = refs[9 + len(pieces) : 14 + len(pieces)]
     message_refs, gw_ref = refs[14 + len(pieces) : -1], refs[-1]
     if levels:
         owned = pieces[0].shape[0]
-        for m in range(levels):
-            w_ref[rows_at(m, 0, owned), :] = pieces[m][...]
+        for own, others, m in ((0, 3, 0), (1, 4, 1), (2, 5, 3)):
+            w_ref[rows_at(m, 0, owned), :] = pieces[own][...]
             for k in range(1, PLANE):
-                w_ref[rows_at(m, k, owned), :] = pieces[levels + m][(k - 1) * owned : k * owned, :]
+                w_ref[rows_at(m, k, owned), :] = pieces[others][(k - 1) * owned : k * owned, :]
+        for k in range(PLANE):
+            w_ref[rows_at(2, k, owned), :] = pieces[6][k * owned : (k + 1) * owned, :]
     else:
         w_ref[...] = pieces[0][...]
         gw_ref = message_refs[0]
@@ -219,7 +221,7 @@
 
 
 def products_kernel(
-    params_ref, xh_ref, w_ref, za_ref, gp_ref, gh_ref, gb_ref, bo_ref, keep_ref, send_ref, stage_ref
+    params_ref, xh_ref, w_ref, za_ref, gp_ref, gh_ref, gb_ref, bo_ref, keep_ref, send_ref, notes_ref, stage_ref
 ):
     half = lax.axis_index("tensor")
     slots = stage_ref.shape[1]
@@ -244,9 +246,7 @@
             keep_ref[to, :] = stage_ref[j, mine, :].astype(BF16)
             send_ref[to, :] = stage_ref[j, other, :].astype(BF16)
     zero = jnp.zeros((NOTES - 6, xh_ref.shape[1]), F32)
-    notes = jnp.concatenate([gb_ref[...], bo_ref[...]] + sums + [zero], axis=0).astype(BF16)
-    keep_ref[PLANE * slots :, :] = notes
-    send_ref[PLANE * slots :, :] = notes
+    notes_ref[...] = jnp.concatenate([gb_ref[...], bo_ref[...]] + sums + [zero], axis=0).astype(BF16)
 
 
 def join_kernel(*refs):
@@ -255,8 +255,11 @@
         refs[-1][k * owned : (k + 1) * owned, :] = ref[...]
 
 
-def choose_kernel(own_ref, far_ref, out_ref):
-    out_ref[...] = jnp.where(is_inner(), far_ref[...].astype(F32), own_ref[...].astype(F32)).astype(BF16)
+def choose_kernel(own_ref, own_far_ref, others_ref, far_ref, out_ref):
+    owned = own_ref.shape[0]
+    for at, mine, afar in ((0, own_ref, own_far_ref), (owned, others_ref, far_ref)):
+        rows = pl.ds(at, mine.shape[0])
+        out_ref[rows, :] = jnp.where(is_inner(), afar[...].astype(F32), mine[...].astype(F32)).astype(BF16)
 
 
 def relay_kernel(far_ref, passed_ref, out_ref):
@@ -264,87 +267,72 @@
     out_ref[...] = (far_ref[...].astype(F32) + passed).astype(BF16)
 
 
-def pair_kernel(levels, keep_ref, peer_ref, *refs):
-    notes_ref, out_refs = refs[-PLANE - 1], refs[-PLANE:]
-    slots = out_refs[0].shape[0]
-    notes = keep_ref[PLANE * slots :, :].astype(F32)
-    row = lax.broadcasted_iota(jnp.int32, notes.shape, 0)
-    notes = notes + jnp.where(row == 0, 0.0, peer_ref[PLANE * slots :, :].astype(F32))
-    notes = notes.astype(BF16)
-    notes_ref[...] = notes
+def pair_kernel(keep_ref, peer_ref, *refs):
+    note_refs, out_refs = refs[:-PLANE], refs[-PLANE:]
+    slots = out_refs[0].shape[0] - NOTES
+    notes = tree_sum([ref[...].astype(F32) for ref in note_refs]).astype(BF16)
     for k, out_ref in enumerate(out_refs):
         at = pl.ds(k * slots, slots)
-        out_ref[...] = (keep_ref[at, :].astype(F32) + peer_ref[at, :].astype(F32)).astype(BF16)
-    if levels:
-        near_ref, far_ref, to_near_ref, to_far_ref = refs[:4]
-        rows, columns = near_ref.shape
-        to_near_ref[:rows, :] = near_ref[...]
-        to_far_ref[:rows, :] = far_ref[...]
-        notes = jnp.concatenate([jnp.zeros((NOTES, columns - notes.shape[1]), BF16), notes], axis=1)
-        to_near_ref[rows:, :] = notes
-        to_far_ref[rows:, :] = notes
+        out_ref[:slots, :] = (keep_ref[at, :].astype(F32) + peer_ref[at, :].astype(F32)).astype(BF16)
+        out_ref[slots:, :] = notes
 
 
 def rows_out_kernel(residual_ref, g_ref, b_out_ref, b_down_ref, *refs):
-    part_refs, (result_ref, grad_ref) = refs[:PLANE], refs[PLANE:]
+    part_refs, (result_ref, grad_ref, notes_ref) = refs[:PLANE], refs[PLANE:]
     own_rows = residual_ref.shape[0]
+    slots = 2 * own_rows
     branch = tree_sum([ref[:own_rows, :].astype(F32) for ref in part_refs])
     x = residual_ref[...].astype(F32)
     result_ref[...] = (x + (branch + b_out_ref[...] + b_down_ref[...])).astype(BF16)
     off = x - jnp.mean(x, axis=-1, keepdims=True)
     scale = lax.rsqrt(jnp.mean(off * off, axis=-1, keepdims=True) + eps)
     xh = off * scale
-    grad = tree_sum([ref[own_rows:, :].astype(F32) for ref in part_refs])
+    grad = tree_sum([ref[own_rows:slots, :].astype(F32) for ref in part_refs])
     grad = grad - jnp.mean(grad, axis=-1, keepdims=True) - xh * jnp.mean(grad * xh, axis=-1, keepdims=True)
     grad_ref[...] = g_ref[...].astype(F32) + scale * grad
-
-
-def combine_kernel(own_ref, near_ref, passed_ref, far_ref, notes_ref, notes_middle_ref, *out_refs):
-    rows = own_ref.shape[0]
-    owned = rows // PLANE
-    columns, model = own_ref.shape[1], notes_ref.shape[1]
+    notes = [ref[slots:, :].astype(F32) for ref in part_refs]
+    zero = jnp.zeros((NOTES - PLANE - 5, x.shape[1]), F32)
+    notes = jnp.concatenate([note[0:1] for note in notes] + [tree_sum(notes)[1:6], zero], axis=0)
+    notes_ref[...] = notes
+
+
+def combine_kernel(own_ref, near_ref, passed_ref, far_ref, *out_refs):
+    owned = own_ref.shape[0] // PLANE
     passed_here = jnp.logical_not(is_inner())
-    own, middle = notes_ref[...].astype(F32), notes_middle_ref[...].astype(F32)
-    near, far = [ref[rows:, columns - model :].astype(F32) for ref in (near_ref, far_ref)]
-    notes = ((own + near) + (middle + far)).astype(BF16)
     for k, out_ref in enumerate(out_refs):
         at = pl.ds(k * owned, owned)
         total = own_ref[at, :].astype(F32) + near_ref[at, :].astype(F32) + far_ref[at, :].astype(F32)
         total = total + jnp.where(passed_here, passed_ref[at, :].astype(F32), 0.0)
-        out_ref[:owned, :] = total.astype(out_ref.dtype)
-        out_ref[owned:, : columns - model] = jnp.zeros((NOTES, columns - model), out_ref.dtype)
-        out_ref[owned:, columns - model :] = notes.astype(out_ref.dtype)
+        out_ref[...] = total.astype(out_ref.dtype)
 
 
 def owner_kernel(*refs):
-    part_refs = refs[:PLANE]
-    up_ref, down_ref, qkv_ref, out_ref, b_up_ref, b_qkv_ref = refs[PLANE : PLANE + 6]
-    common_refs = refs[PLANE + 6 :]
-    owned = up_ref.shape[0]
+    part_refs, (notes_ref, peer_notes_ref) = refs[:PLANE], refs[PLANE:-12]
+    up_ref, down_ref, qkv_ref, out_ref, b_up_ref, b_qkv_ref = refs[-12:-6]
+    common_refs = refs[-6:]
     width = up_ref.shape[1] // PLANE
     head_blocks = out_ref.shape[1] // BLK
     heads, out = 3 * BLK, 3 * BLK + width
-    all_notes = []
+    notes = notes_ref[...]
+    common = notes + peer_notes_ref[...]
     for k, part_ref in enumerate(part_refs):
         other = place()[0] ^ k
         at = pl.ds(pl.multiple_of(other * width, BLK), width)
-        up_ref[:, at] = part_ref[:owned, heads:out].astype(F32)
-        down_ref[:, at] = part_ref[:owned, out + BLK :].astype(F32)
-        notes = part_ref[owned:, part_ref.shape[1] - common_refs[0].shape[0] * BLK :].astype(F32)
-        all_notes.append(notes)
+        up_ref[:, at] = part_ref[:, heads:out].astype(F32)
+        down_ref[:, at] = part_ref[:, out + BLK :].astype(F32)
         for j in range(width // BLK):
-            b_up_ref[pl.ds(other * (width // BLK) + j, 1), :] = notes[0:1, j * BLK : (j + 1) * BLK]
+            b_up_ref[pl.ds(other * (width // BLK) + j, 1), :] = notes[k : k + 1, j * BLK : (j + 1) * BLK]
 
         @pl.when(other < head_blocks)
         def _():
             at = pl.ds(pl.multiple_of(other * BLK, BLK), BLK)
             for c in range(3):
-                qkv_ref[c, :, at] = part_ref[:owned, c * BLK : (c + 1) * BLK].astype(F32)
-                b_qkv_ref[c : c + 1, at] = notes[0:1, width + c * BLK : width + (c + 1) * BLK]
-            out_ref[:, at] = part_ref[:owned, out : out + BLK].astype(F32)
-
-    common = tree_sum(all_notes)
-    for row, common_ref in zip((1, 1, 2, 3, 4, 5), common_refs):
+                qkv_ref[c, :, at] = part_ref[:, c * BLK : (c + 1) * BLK].astype(F32)
+                b_qkv_ref[c : c + 1, at] = notes[k : k + 1, width + c * BLK : width + (c + 1) * BLK]
+            out_ref[:, at] = part_ref[:, out : out + BLK].astype(F32)
+
+    for row, common_ref in zip((0, 0, 1, 2, 3, 4), common_refs):
+        row = PLANE + row
         for j in range(common_ref.shape[0]):
             common_ref[j : j + 1, :] = common[row : row + 1, j * BLK : (j + 1) * BLK]
 
@@ -426,17 +414,19 @@
         own = shares[0]
         own_near, own_far = to_level(own, 1), to_level(own, 3)
         others = kernel_call(join_kernel, [shape(((PLANE - 1) * owned, columns), BF16)], received, micros=20)[0]
-        others, own, own_near, own_far, message = lax.optimization_barrier(
-            (others, own, own_near, own_far, message)
-        )
+        others, message = lax.optimization_barrier((others, message))
         near, far = to_level(others, 1), to_level(others, 3)
-        own_mid = to_pass(kernel_call(choose_kernel, [shape(own.shape, BF16)], (own, own_far))[0])
+        near, far = lax.optimization_barrier((near, far))
+        message, own_near, own_far = lax.optimization_barrier((message, own_near, own_far))
+        chosen = kernel_call(
+            choose_kernel,
+            [shape((PLANE * owned, columns), BF16)],
+            (own, own_far, others, far),
+            micros=20,
+        )[0]
     messages = [message] + [to_plane(message, k) for k in range(1, PLANE)]
     if direct:
-        chosen = kernel_call(choose_kernel, [shape(others.shape, BF16)], (others, far), micros=20)[0]
-        messages, own_mid, near, far, chosen = lax.optimization_barrier((messages, own_mid, near, far, chosen))
-        mid = to_pass(chosen)
-        pieces = [own, own_near, own_mid, own_far, others, near, mid, far]
+        pieces = [own, own_near, own_far, others, near, far, to_pass(chosen)]
     else:
         every = jnp.concatenate(xor_sorted([shares[0]] + received, plane_at), axis=0)
         pieces = [lax.all_gather(every, "dp", axis=0, tiled=True, axis_index_groups=level_groups)]
@@ -447,7 +437,7 @@
         [shape((rows_all, model), BF16)] * 4
         + [shape((own_rows, model), BF16), shape((8, 128), F32), shape((1, model), F32)],
         (params, rows, to_peer(rows)),
-        micros=4,
+        micros=1,
     )
 
     block_at = jnp.minimum(plane_at, head_blocks - 1) * BLK
@@ -470,57 +460,48 @@
     )
     if direct:
         passed = to_pass(messages[2], back=True)
-    keep, send = kernel_call(
+    keep, send, notes = kernel_call(
         products_kernel,
-        [shape((rows_all + NOTES, model), BF16)] * 2,
+        [shape((rows_all, model), BF16)] * 2 + [shape((NOTES, model), BF16)],
         (params, xh, w, za, gp, gh, gb, bo),
         scratch=[pltpu.VMEM((2, slots, model), F32)],
         micros=4,
     )
     from_peer = to_peer(send)
-    extra, extra_shapes = (), []
     if direct:
+        notes = [notes] + [to_level(notes, m) for m in range(1, levels)]
         relayed = kernel_call(
             relay_kernel, [shape((PLANE * owned, columns), BF16)], (messages[3], passed), micros=20
         )[0]
-        relayed, from_peer = lax.optimization_barrier((relayed, from_peer))
-        extra = (messages[1], relayed)
-        extra_shapes = [shape((PLANE * owned + NOTES, columns), BF16)] * 2
-    laid = kernel_call(
-        partial(pair_kernel, direct),
-        extra_shapes + [shape((NOTES, model), BF16)] + [shape((slots, model), BF16)] * PLANE,
-        (keep, from_peer, *extra),
+        relayed, from_peer, messages = lax.optimization_barrier((relayed, from_peer, messages))
+    else:
+        notes = lax.all_gather(notes, "dp", axis=0, axis_index_groups=level_groups)
+        notes = [jnp.sum(notes.astype(F32), axis=0)]
+    outgoing = kernel_call(
+        pair_kernel,
+        [shape((slots + NOTES, model), BF16)] * PLANE,
+        (keep, from_peer, *notes),
         micros=2,
     )
-
-    notes, outgoing = laid[-PLANE - 1], laid[-PLANE:]
-
     parts = [outgoing[0]] + [to_plane(outgoing[k], k) for k in range(1, PLANE)]
+
     if direct:
-        near, far = to_level(laid[0], 1), to_level(laid[1], 3)
-        notes_after, parts[1] = lax.optimization_barrier((notes, parts[1]))
-        notes_mid = to_level(notes_after, 2)
-        parts, near, far, notes_mid = lax.optimization_barrier((parts, near, far, notes_mid))
+        near, far = to_level(messages[1], 1), to_level(relayed, 3)
+        parts, near, far = lax.optimization_barrier((parts, near, far))
         backs = kernel_call(
             combine_kernel,
-            [shape((owned + NOTES, columns), F32)] + [shape((owned + NOTES, columns), BF16)] * (PLANE - 1),
-            (messages[0], near, passed, far, notes, notes_mid),
+            [shape((owned, columns), F32)] + [shape((owned, columns), BF16)] * (PLANE - 1),
+            (messages[0], near, passed, far),
         )
     else:
         sums = lax.psum_scatter(
             messages[0], "dp", scatter_dimension=0, tiled=True, axis_index_groups=level_groups
         ).reshape(PLANE, owned, columns)
-        notes = lax.all_gather(notes, "dp", axis=0, axis_index_groups=level_groups)
-        notes = jnp.sum(notes.astype(F32), axis=0).astype(BF16)
-        notes = jnp.concatenate([jnp.zeros((NOTES, columns - model), BF16), notes], axis=1)
-        backs = [
-            jnp.concatenate([lax.dynamic_index_in_dim(sums, plane_at ^ k, 0, keepdims=False), notes], axis=0)
-            for k in range(PLANE)
-        ]
+        backs = [lax.dynamic_index_in_dim(sums, plane_at ^ k, 0, keepdims=False) for k in range(PLANE)]
     backs = [backs[0]] + [to_plane(backs[k], k) for k in range(1, PLANE)]
-    result, grad_residual = kernel_call(
+    result, grad_residual, notes = kernel_call(
         rows_out_kernel,
-        [shape((own_rows, model), BF16), shape((own_rows, model), F32)],
+        [shape((own_rows, model), BF16), shape((own_rows, model), F32), shape((NOTES, model), F32)],
         (residual, g_own, b_out.reshape(1, model), b_down.reshape(1, model), *parts),
     )
     grad_up, grad_down, grad_qkv, grad_out_w, grad_b_up, grad_b_qkv, *common = kernel_call(
@@ -534,7 +515,7 @@
             shape((3, head_blocks * BLK), F32),
         ]
         + [shape((model // BLK, BLK), F32)] * 6,
-        backs,
+        (*backs, notes, to_peer(notes)),
     )
     common = [total.reshape(model) for total in common]
     return (

time: 112 us -> 109 us (0.973)
  waiting for transfers between devices: 54.8 us -> 50.9 us
  starting transfers between devices: 32.6 us -> 34.3 us
    ppermute x3 -> x2, waiting for transfers between devices: 16.5 us -> 11.2 us  [to_pass(): lax.ppermute(x, 'dp', [(a * PLANE + j, b * PLANE + j) for a, b in pairs f...]
    ppermute x7 -> x9, starting transfers between devices: 10.5 us -> 14.7 us  [to_level(): return lax.ppermute(x, 'dp', [(j, j ^ m * PLANE) for j in range(places)])]
    ppermute x3 -> x2, starting transfers between devices: 8.01 us -> 5.42 us  [to_pass(): lax.ppermute(x, 'dp', [(a * PLANE + j, b * PLANE + j) for a, b in pairs f...]
    ppermute x7 -> x9, waiting for transfers between devices: 13.4 us -> 13.7 us  [to_level(): return lax.ppermute(x, 'dp', [(j, j ^ m * PLANE) for j in range(places)])]
    pallas_call x12 -> x11, Pallas kernels: 21.1 us -> 21 us  [kernel_call(): pl.pallas_call(body, out_shape=out_shapes, in_specs=[taken] * len(operand...]
  transfers between devices with their start and end apart: 24 -> 26, of which waited for: 12 -> 12; matrix products, arithmetic and copies ran while one was open for 1% -> 1% of each run, Pallas kernels for 8% -> 8%
where the time goes in v5:
time: 109 us
  waiting for transfers between devices  50.9 us (47%)
  starting transfers between devices  34.3 us (31%)
  Pallas kernels  21 us (19%)
  between operations  1.25 us (1%)
  local copies, waits for them, and re-layouts  1.09 us (1%)
    ppermute x12, waiting for transfers between devices, to_plane(): return lax.ppermute(x, 'dp', [(j, j ^ k) for j in range(places)])  24.7 us
    pallas_call x11, Pallas kernels, kernel_call(): pl.pallas_call(body, out_shape=out_shapes, in_specs=[taken] * len(operand...  21 us
    ppermute x9, starting transfers between devices, to_level(): return lax.ppermute(x, 'dp', [(j, j ^ m * PLANE) for j in range(places)])  14.7 us
    ppermute x12, starting transfers between devices, to_plane(): return lax.ppermute(x, 'dp', [(j, j ^ k) for j in range(places)])  14.1 us
    ppermute x9, waiting for transfers between devices, to_level(): return lax.ppermute(x, 'dp', [(j, j ^ m * PLANE) for j in range(places)])  13.7 us
    ppermute x2, waiting for transfers between devices, to_pass(): lax.ppermute(x, 'dp', [(a * PLANE + j, b * PLANE + j) for a, b in pairs f...  11.2 us
    ppermute x2, starting transfers between devices, to_pass(): lax.ppermute(x, 'dp', [(a * PLANE + j, b * PLANE + j) for a, b in pairs f...  5.42 us
  transfers between devices with their start and end apart: 26, of which 12 were waited for; matrix products, arithmetic and copies ran while one was open for 1% of the time, Pallas kernels for 8%

profile of v5, /device:TPU:0, one launch (start us, length us, event | category | flops | bytes accessed | tf_op | source)
XLA Modules:
  0.0 108.5 jit_solution(3264981663647329027)
XLA Ops:
  0.6 0.0 copy-start
  0.7 2.0 %shard_map.281 = (bf16[48,1280]{1,0:T(8,128)(2,1)}, bf16[48,1280]{1,0:T(8,128)(2,1)}, bf16[48,1280]{1,0:T(8,128)(2,1)}, bf16[48,1280]{1,0:T(8,128)(2,1)}) custom-call(bf16[3,48,384]{2,1,0:T(8,128)(2,1)} %refs_0_.1, bf16[48,384]{1,0:T(8,128)(2,1)} %bitcast.19, bf16[48,1536]{1,0:T(8,128)(2,1)} %refs_2_.1, bf16[48,1536]{1,0:T(8,128)(2,1)} %bitcast.18), custom_call_target="tpu_custom_call" | custom-call | flops 1000000000 | bytes 1 | tf_op jit(solution)/shard_map/pallas_call | solution.py:343
  2.7 3.1 %collective-permute-start.3 = (bf16[48,1280]{1,0:T(8,128)(2,1)}, bf16[48,1280]{1,0:T(8,128)(2,1)S(1)}, u32[]{:S(2)}, u32[]{:S(2)}) collective-permute-start(bf16[48,1280]{1,0:T(8,128)(2,1)} %get-tuple-element.83.own_ref.refs_9_), channel_id=1, source_target_pairs={{0,8},{2,10},{4,12},{6,14},{8,0},{10,2},{12,4},{14,6},{16,24},{18,... | collective-permute-start | bytes 368648 | tf_op jit(solution)/shard_map/ppermute | solution.py:389
  5.8 2.5 %collective-permute-start.4 = (bf16[48,1280]{1,0:T(8,128)(2,1)}, bf16[48,1280]{1,0:T(8,128)(2,1)S(1)}, u32[]{:S(2)}, u32[]{:S(2)}) collective-permute-start(bf16[48,1280]{1,0:T(8,128)(2,1)} %get-tuple-element.83.own_ref.refs_9_), channel_id=1, source_target_pairs={{0,24},{2,26},{4,28},{6,30},{8,16},{10,18},{12,20},{14,22},{16,8},... | collective-permute-start | bytes 368648 | tf_op jit(solution)/shard_map/ppermute | solution.py:389
  8.2 1.5 %collective-permute-start = (bf16[48,1280]{1,0:T(8,128)(2,1)}, bf16[48,1280]{1,0:T(8,128)(2,1)S(1)}, u32[]{:S(2)}, u32[]{:S(2)}) collective-permute-start(bf16[48,1280]{1,0:T(8,128)(2,1)} %get-tuple-element.80), channel_id=1, source_target_pairs={{0,2},{2,0},{4,6},{6,4},{8,10},{10,8},{12,14},{14,12},{16,18},{18,... | collective-permute-start | bytes 368648 | tf_op jit(solution)/shard_map/ppermute | solution.py:386
  9.7 1.5 %collective-permute-start.1 = (bf16[48,1280]{1,0:T(8,128)(2,1)}, bf16[48,1280]{1,0:T(8,128)(2,1)S(1)}, u32[]{:S(2)}, u32[]{:S(2)}) collective-permute-start(bf16[48,1280]{1,0:T(8,128)(2,1)} %get-tuple-element.81), channel_id=1, source_target_pairs={{0,4},{2,6},{4,0},{6,2},{8,12},{10,14},{12,8},{14,10},{16,20},{18,... | collective-permute-start | bytes 368648 | tf_op jit(solution)/shard_map/ppermute | solution.py:386
  11.2 0.5 collective-permute-start.2
  11.8 2.2 %collective-permute-done.refs_0_ = bf16[48,1280]{1,0:T(8,128)(2,1)S(1)} collective-permute-done((bf16[48,1280]{1,0:T(8,128)(2,1)}, bf16[48,1280]{1,0:T(8,128)(2,1)S(1)}, u32[]{:S(2)}, u32[]{:S(2)}) %collective-permute-start) | collective-permute-done | bytes 122912 | tf_op jit(solution)/shard_map/ppermute | solution.py:386
  14.0 3.5 %collective-permute-done.1.refs_1_ = bf16[48,1280]{1,0:T(8,128)(2,1)S(1)} collective-permute-done((bf16[48,1280]{1,0:T(8,128)(2,1)}, bf16[48,1280]{1,0:T(8,128)(2,1)S(1)}, u32[]{:S(2)}, u32[]{:S(2)}) %collective-permute-start.1) | collective-permute-done | bytes 122912 | tf_op jit(solution)/shard_map/ppermute | solution.py:386
  17.5 0.8 collective-permute-start.5
  18.3 1.3 %collective-permute-start.10 = (bf16[144,1280]{1,0:T(8,128)(2,1)S(1)}, bf16[144,1280]{1,0:T(8,128)(2,1)S(1)}, u32[]{:S(2)}, u32[]{:S(2)}) collective-permute-start(bf16[144,1280]{1,0:T(8,128)(2,1)S(1)} %shard_map.282.others_ref.refs_12_), channel_id=1, source_target_pairs={{0,24},{2,26},{4,28},{6,30},{8,16},{10,18},{12,20},{14,22},{16,8},... | collective-permute-start | bytes 1105928 | tf_op jit(solution)/shard_map/ppermute | solution.py:389
  19.6 0.8 collective-permute-start.6
  20.4 2.0 %collective-permute-start.7 = (bf16[272,768]{1,0:T(8,128)(2,1)S(1)}, bf16[272,768]{1,0:T(8,128)(2,1)S(1)}, u32[]{:S(2)}, u32[]{:S(2)}) collective-permute-start(bf16[272,768]{1,0:T(8,128)(2,1)S(1)} %fusion.1), channel_id=1, source_target_pairs={{0,6},{2,4},{4,2},{6,0},{8,14},{10,12},{12,10},{14,8},{16,22},{18,... | collective-permute-start | bytes 1253384 | tf_op jit(solution)/shard_map/ppermute | solution.py:386
  22.5 9.1 %collective-permute-done.10.far_ref.refs_14_ = bf16[144,1280]{1,0:T(8,128)(2,1)S(1)} collective-permute-done((bf16[144,1280]{1,0:T(8,128)(2,1)S(1)}, bf16[144,1280]{1,0:T(8,128)(2,1)S(1)}, u32[]{:S(2)}, u32[]{:S(2)}) %collective-permute-start.10) | collective-permute-done | bytes 368672 | tf_op jit(solution)/shard_map/ppermute | solution.py:389
  31.6 4.1 %collective-permute-done.9.refs_13_ = bf16[144,1280]{1,0:T(8,128)(2,1)S(1)} collective-permute-done((bf16[144,1280]{1,0:T(8,128)(2,1)S(1)}, bf16[144,1280]{1,0:T(8,128)(2,1)S(1)}, u32[]{:S(2)}, u32[]{:S(2)}) %collective-permute-start.9) | collective-permute-done | bytes 368672 | tf_op jit(solution)/shard_map/ppermute | solution.py:389
  35.8 2.1 %collective-permute-done.6 = bf16[272,768]{1,0:T(8,128)(2,1)S(1)} collective-permute-done((bf16[272,768]{1,0:T(8,128)(2,1)S(1)}, bf16[272,768]{1,0:T(8,128)(2,1)S(1)}, u32[]{:S(2)}, u32[]{:S(2)}) %collective-permute-start.6) | collective-permute-done | bytes 417824 | tf_op jit(solution)/shard_map/ppermute | solution.py:386
  38.0 0.1 collective-permute-start.8
  38.1 0.1 shard_map.284
  38.2 2.8 %collective-permute-start.11 = (bf16[192,1280]{1,0:T(8,128)(2,1)S(1)}, bf16[192,1280]{1,0:T(8,128)(2,1)S(1)}, u32[]{:S(2)}, u32[]{:S(2)}) collective-permute-start(bf16[192,1280]{1,0:T(8,128)(2,1)S(1)} %shard_map.284), channel_id=1, source_target_pairs={{0,16},{2,18},{4,20},{6,22},{24,8},{26,10},{28,12},{30,14},{8,0},{... | collective-permute-start | bytes 1474568 | tf_op jit(solution)/shard_map/ppermute | solution.py:398
  41.1 0.8 dynamic_slice.7
  42.1 3.4 %shard_map.283 = (bf16[1024,768]{1,0:T(8,128)(2,1)S(1)}, bf16[1024,768]{1,0:T(8,128)(2,1)S(1)}, bf16[1024,768]{1,0:T(8,128)(2,1)S(1)}, bf16[1024,768]{1,0:T(8,12...) custom-call(f32[8,768]{1,0:T(8,128)S(1)} %stack.23.params_ref, ...), custom_call_target="tpu_custom_call" | custom-call | flops 1000000000 | bytes 1 | tf_op jit(solution)/shard_map/pallas_call | solution.py:343
  45.5 6.6 %collective-permute-done.11.refs_15_ = bf16[192,1280]{1,0:T(8,128)(2,1)S(1)} collective-permute-done((bf16[192,1280]{1,0:T(8,128)(2,1)S(1)}, bf16[192,1280]{1,0:T(8,128)(2,1)S(1)}, u32[]{:S(2)}, u32[]{:S(2)}) %collective-permute-start.11) | collective-permute-done | bytes 491552 | tf_op jit(solution)/shard_map/ppermute | solution.py:398
  52.2 8.5 %shard_map.285 = (bf16[1024,512]{1,0:T(8,128)(2,1)S(1)}, bf16[1024,384]{1,0:T(8,128)(2,1)S(1)}, bf16[1024,384]{1,0:T(8,128)(2,1)S(1)}, bf16[768,1280]{1,0:T(8,12...) custom-call(f32[8,128]{1,0:T(8,128)S(1)} %get-tuple-element.91.refs_, ...), custom_call_target="tpu_custom_call" | custom-call | flops 12000000000 | bytes 1 | tf_op jit(solution)/shard_map/pallas_call | solution.py:343
  60.7 2.6 %collective-permute-start.12 = (bf16[192,1280]{1,0:T(8,128)(2,1)S(1)}, bf16[192,1280]{1,0:T(8,128)(2,1)S(1)}, u32[]{:S(2)}, u32[]{:S(2)}) collective-permute-start(bf16[192,1280]{1,0:T(8,128)(2,1)S(1)} %get-tuple-element.108), channel_id=1, source_target_pairs={{16,0},{18,2},{20,4},{22,6},{8,24},{10,26},{12,28},{14,30},{0,8},{... | collective-permute-start | bytes 1474568 | tf_op jit(solution)/shard_map/ppermute | solution.py:398
  63.3 3.8 %shard_map.286 = (bf16[1024,768]{1,0:T(8,128)(2,1)S(1)}, bf16[1024,768]{1,0:T(8,128)(2,1)S(1)}, bf16[16,768]{1,0:T(8,128)(2,1)S(1)}) custom-call(f32[8,768]{1,0:T(8,128)S(1)} %stack.23.params_ref, bf16[1024,768]{1,0:T(8,128)(2,1)S(1)} %get-tuple-element.90.xh_ref, bf16[768,1280]{1,0:T(8,128)(2,1)S(1)} %get-tuple-element.100.w_ref, ...), custom_call_target="tpu_custom_call" | custom-call | flops 4000000000 | bytes 1 | tf_op jit(solution)/shard_map/pallas_call | solution.py:343
  67.1 0.5 collective-permute-start.14
  67.6 2.6 %collective-permute-start.15 = (bf16[16,768]{1,0:T(8,128)(2,1)S(1)}, bf16[16,768]{1,0:T(8,128)(2,1)S(1)}, u32[]{:S(2)}, u32[]{:S(2)}) collective-permute-start(bf16[16,768]{1,0:T(8,128)(2,1)S(1)} %get-tuple-element.113.refs_0_), channel_id=1, source_target_pairs={{0,16},{2,18},{4,20},{6,22},{8,24},{10,26},{12,28},{14,30},{16,0},... | collective-permute-start | bytes 73736 | tf_op jit(solution)/shard_map/ppermute | solution.py:389
  70.2 1.3 %collective-permute-start.16 = (bf16[16,768]{1,0:T(8,128)(2,1)S(1)}, bf16[16,768]{1,0:T(8,128)(2,1)S(1)}, u32[]{:S(2)}, u32[]{:S(2)}) collective-permute-start(bf16[16,768]{1,0:T(8,128)(2,1)S(1)} %get-tuple-element.113.refs_0_), channel_id=1, source_target_pairs={{0,24},{2,26},{4,28},{6,30},{8,16},{10,18},{12,20},{14,22},{16,8},... | collective-permute-start | bytes 73736 | tf_op jit(solution)/shard_map/ppermute | solution.py:389
  71.6 4.6 %collective-permute-done.12.passed_ref = bf16[192,1280]{1,0:T(8,128)(2,1)S(1)} collective-permute-done((bf16[192,1280]{1,0:T(8,128)(2,1)S(1)}, bf16[192,1280]{1,0:T(8,128)(2,1)S(1)}, u32[]{:S(2)}, u32[]{:S(2)}) %collective-permute-start.12) | collective-permute-done | bytes 491552 | tf_op jit(solution)/shard_map/ppermute | solution.py:398
  76.2 0.2 shard_map.287
  76.3 0.8 collective-permute-start.20
  77.2 2.5 %collective-permute-start.21 = (bf16[192,1280]{1,0:T(8,128)(2,1)S(1)}, bf16[192,1280]{1,0:T(8,128)(2,1)S(1)}, u32[]{:S(2)}, u32[]{:S(2)}) collective-permute-start(bf16[192,1280]{1,0:T(8,128)(2,1)S(1)} %shard_map.287), channel_id=1, source_target_pairs={{0,24},{2,26},{4,28},{6,30},{8,16},{10,18},{12,20},{14,22},{16,8},... | collective-permute-start | bytes 1474568 | tf_op jit(solution)/shard_map/ppermute | solution.py:389
  79.7 0.4 shard_map.288
  80.1 1.2 %collective-permute-start.17 = (bf16[272,768]{1,0:T(8,128)(2,1)S(1)}, bf16[272,768]{1,0:T(8,128)(2,1)S(1)}, u32[]{:S(2)}, u32[]{:S(2)}) collective-permute-start(bf16[272,768]{1,0:T(8,128)(2,1)S(1)} %get-tuple-element.115), channel_id=1, source_target_pairs={{0,2},{2,0},{4,6},{6,4},{8,10},{10,8},{12,14},{14,12},{16,18},{18,... | collective-permute-start | bytes 1253384 | tf_op jit(solution)/shard_map/ppermute | solution.py:386
  81.3 0.5 collective-permute-start.18
  81.8 1.9 %collective-permute-start.19 = (bf16[272,768]{1,0:T(8,128)(2,1)S(1)}, bf16[272,768]{1,0:T(8,128)(2,1)S(1)}, u32[]{:S(2)}, u32[]{:S(2)}) collective-permute-start(bf16[272,768]{1,0:T(8,128)(2,1)S(1)} %get-tuple-element.117), channel_id=1, source_target_pairs={{0,6},{2,4},{4,2},{6,0},{8,14},{10,12},{12,10},{14,8},{16,22},{18,... | collective-permute-start | bytes 1253384 | tf_op jit(solution)/shard_map/ppermute | solution.py:386
  83.7 9.1 %collective-permute-done.17.refs_1_ = bf16[272,768]{1,0:T(8,128)(2,1)S(1)} collective-permute-done((bf16[272,768]{1,0:T(8,128)(2,1)S(1)}, bf16[272,768]{1,0:T(8,128)(2,1)S(1)}, u32[]{:S(2)}, u32[]{:S(2)}) %collective-permute-start.17) | collective-permute-done | bytes 417824 | tf_op jit(solution)/shard_map/ppermute | solution.py:386
  92.7 6.4 %collective-permute-done.18.refs_2_ = bf16[272,768]{1,0:T(8,128)(2,1)S(1)} collective-permute-done((bf16[272,768]{1,0:T(8,128)(2,1)S(1)}, bf16[272,768]{1,0:T(8,128)(2,1)S(1)}, u32[]{:S(2)}, u32[]{:S(2)}) %collective-permute-start.18) | collective-permute-done | bytes 417824 | tf_op jit(solution)/shard_map/ppermute | solution.py:386
  99.2 0.4 collective-permute-done.21.far_ref
  99.6 0.3 shard_map.290
  99.9 1.2 %collective-permute-start.22 = (bf16[48,1280]{1,0:T(8,128)(2,1)S(1)}, bf16[48,1280]{1,0:T(8,128)(2,1)S(1)}, u32[]{:S(2)}, u32[]{:S(2)}) collective-permute-start(bf16[48,1280]{1,0:T(8,128)(2,1)S(1)} %get-tuple-element.130), channel_id=1, source_target_pairs={{0,2},{2,0},{4,6},{6,4},{8,10},{10,8},{12,14},{14,12},{16,18},{18,... | collective-permute-start | bytes 368648 | tf_op jit(solution)/shard_map/ppermute | solution.py:386
  101.1 0.5 collective-permute-start.23
  101.6 1.9 %collective-permute-start.24 = (bf16[48,1280]{1,0:T(8,128)(2,1)S(1)}, bf16[48,1280]{1,0:T(8,128)(2,1)S(1)}, u32[]{:S(2)}, u32[]{:S(2)}) collective-permute-start(bf16[48,1280]{1,0:T(8,128)(2,1)S(1)} %get-tuple-element.132), channel_id=1, source_target_pairs={{0,6},{2,4},{4,2},{6,0},{8,14},{10,12},{12,10},{14,8},{16,22},{18,... | collective-permute-start | bytes 368648 | tf_op jit(solution)/shard_map/ppermute | solution.py:386
  103.4 1.2 %shard_map.289 = (bf16[128,768]{1,0:T(8,128)(2,1)}, f32[128,768]{1,0:T(8,128)}, f32[16,768]{1,0:T(8,128)S(1)}) custom-call(bf16[128,768]{1,0:T(8,128)(2,1)S(1)} %copy-done.1, bf16[128,768]{1,0:T(8,128)(2,1)S(1)} %get-tuple-element.89.g_ref, f32[1,768]{1,0:T(1,128)S(1)} %reshape.61.b_out_ref, f32[1,768]{1,0:T(1,128)S(1)} %reshape.62.b_down_ref, ...), custom_call_target="tpu_custom_call" | custom-call | flops 1000000000 | bytes 1 | tf_op jit(solution)/shard_map/pallas_call | solution.py:343
  104.7 1.2 %collective-permute-done.25.refs_5_ = f32[16,768]{1,0:T(8,128)S(1)} collective-permute-done((f32[16,768]{1,0:T(8,128)S(1)}, f32[16,768]{1,0:T(8,128)S(1)}, u32[]{:S(2)}, u32[]{:S(2)}) %collective-permute-start.25) | collective-permute-done | bytes 49184 | tf_op jit(solution)/shard_map/ppermute | solution.py:392
  105.9 0.0 collective-permute-done.23.refs_2_
  105.9 1.4 %collective-permute-done.24.refs_3_ = bf16[48,1280]{1,0:T(8,128)(2,1)S(1)} collective-permute-done((bf16[48,1280]{1,0:T(8,128)(2,1)S(1)}, bf16[48,1280]{1,0:T(8,128)(2,1)S(1)}, u32[]{:S(2)}, u32[]{:S(2)}) %collective-permute-start.24) | collective-permute-done | bytes 122912 | tf_op jit(solution)/shard_map/ppermute | solution.py:386
  107.4 1.0 shard_map.291
  (73 shorter events, 0.4 us)
Async XLA Ops:
  0.6 40.5 %copy-start = (f32[3,384]{1,0:T(4,128)S(1)}, f32[3,384]{1,0:T(4,128)}, u32[]{:S(2)}) copy-start(f32[3,384]{1,0:T(4,128)} %param.26) | copy-start | bytes 13828
  0.7 11.1 %copy-start.19 = (s32[1,4]{1,0:T(1,128)S(1)}, s32[1,4]{1,0:T(1,128)}, u32[]{:S(2)}) copy-start(s32[1,4]{1,0:T(1,128)} %param.20) | copy-start | bytes 52
  0.7 11.1 %copy-start.1 = (bf16[128,768]{1,0:T(8,128)(2,1)S(1)}, bf16[128,768]{1,0:T(8,128)(2,1)}, u32[]{:S(2)}) copy-start(bf16[128,768]{1,0:T(8,128)(2,1)} %residual_ref.1) | copy-start | bytes 589828
  0.7 11.1 %copy-start.12 = (bf16[128,768]{1,0:T(8,128)(2,1)S(1)}, bf16[128,768]{1,0:T(8,128)(2,1)}, u32[]{:S(2)}) copy-start(bf16[128,768]{1,0:T(8,128)(2,1)} %param.19) | copy-start | bytes 589828
  2.7 14.8 %collective-permute-start.3 = (bf16[48,1280]{1,0:T(8,128)(2,1)}, bf16[48,1280]{1,0:T(8,128)(2,1)S(1)}, u32[]{:S(2)}, u32[]{:S(2)}) collective-permute-start(bf16[48,1280]{1,0:T(8,128)(2,1)} %get-tuple-element.83.own_ref.refs_9_), channel_id=1, source_target_pairs={{0,8},{2,10},{4,12},{6,14},{8,0},{10,2},{12,4},{14,6},{16,24},{18,... | collective-permute-start | bytes 368648 | tf_op jit(solution)/shard_map/ppermute | solution.py:389
  5.8 11.7 %collective-permute-start.4 = (bf16[48,1280]{1,0:T(8,128)(2,1)}, bf16[48,1280]{1,0:T(8,128)(2,1)S(1)}, u32[]{:S(2)}, u32[]{:S(2)}) collective-permute-start(bf16[48,1280]{1,0:T(8,128)(2,1)} %get-tuple-element.83.own_ref.refs_9_), channel_id=1, source_target_pairs={{0,24},{2,26},{4,28},{6,30},{8,16},{10,18},{12,20},{14,22},{16,8},... | collective-permute-start | bytes 368648 | tf_op jit(solution)/shard_map/ppermute | solution.py:389
  8.2 5.7 %collective-permute-start = (bf16[48,1280]{1,0:T(8,128)(2,1)}, bf16[48,1280]{1,0:T(8,128)(2,1)S(1)}, u32[]{:S(2)}, u32[]{:S(2)}) collective-permute-start(bf16[48,1280]{1,0:T(8,128)(2,1)} %get-tuple-element.80), channel_id=1, source_target_pairs={{0,2},{2,0},{4,6},{6,4},{8,10},{10,8},{12,14},{14,12},{16,18},{18,... | collective-permute-start | bytes 368648 | tf_op jit(solution)/shard_map/ppermute | solution.py:386
  9.7 7.7 %collective-permute-start.1 = (bf16[48,1280]{1,0:T(8,128)(2,1)}, bf16[48,1280]{1,0:T(8,128)(2,1)S(1)}, u32[]{:S(2)}, u32[]{:S(2)}) collective-permute-start(bf16[48,1280]{1,0:T(8,128)(2,1)} %get-tuple-element.81), channel_id=1, source_target_pairs={{0,4},{2,6},{4,0},{6,2},{8,12},{10,14},{12,8},{14,10},{16,20},{18,... | collective-permute-start | bytes 368648 | tf_op jit(solution)/shard_map/ppermute | solution.py:386
  11.2 6.2 %collective-permute-start.2 = (bf16[48,1280]{1,0:T(8,128)(2,1)}, bf16[48,1280]{1,0:T(8,128)(2,1)S(1)}, u32[]{:S(2)}, u32[]{:S(2)}) collective-permute-start(bf16[48,1280]{1,0:T(8,128)(2,1)} %get-tuple-element.82), channel_id=1, source_target_pairs={{0,6},{2,4},{4,2},{6,0},{8,14},{10,12},{12,10},{14,8},{16,22},{18,... | collective-permute-start | bytes 368648 | tf_op jit(solution)/shard_map/ppermute | solution.py:386
  17.5 20.6 %copy-start.6 = (bf16[48,1280]{1,0:T(8,128)(2,1)S(1)}, bf16[48,1280]{1,0:T(8,128)(2,1)}, u32[]{:S(2)}) copy-start(bf16[48,1280]{1,0:T(8,128)(2,1)} %get-tuple-element.83.own_ref.refs_9_) | copy-start | bytes 368644
  17.5 20.5 %copy-start.7 = (bf16[48,1280]{1,0:T(8,128)(2,1)}, bf16[48,1280]{1,0:T(8,128)(2,1)S(1)}, u32[]{:S(2)}) copy-start(bf16[48,1280]{1,0:T(8,128)(2,1)S(1)} %collective-permute-done.4.own_far_ref.refs_11_) | copy-start | bytes 368644
  17.5 18.2 %collective-permute-start.5 = (bf16[272,768]{1,0:T(8,128)(2,1)S(1)}, bf16[272,768]{1,0:T(8,128)(2,1)S(1)}, u32[]{:S(2)}, u32[]{:S(2)}) collective-permute-start(bf16[272,768]{1,0:T(8,128)(2,1)S(1)} %fusion.1), channel_id=1, source_target_pairs={{0,2},{2,0},{4,6},{6,4},{8,10},{10,8},{12,14},{14,12},{16,18},{18,... | collective-permute-start | bytes 1253384 | tf_op jit(solution)/shard_map/ppermute | solution.py:386
  18.3 13.3 %collective-permute-start.10 = (bf16[144,1280]{1,0:T(8,128)(2,1)S(1)}, bf16[144,1280]{1,0:T(8,128)(2,1)S(1)}, u32[]{:S(2)}, u32[]{:S(2)}) collective-permute-start(bf16[144,1280]{1,0:T(8,128)(2,1)S(1)} %shard_map.282.others_ref.refs_12_), channel_id=1, source_target_pairs={{0,24},{2,26},{4,28},{6,30},{8,16},{10,18},{12,20},{14,22},{16,8},... | collective-permute-start | bytes 1105928 | tf_op jit(solution)/shard_map/ppermute | solution.py:389
  19.6 16.1 %collective-permute-start.9 = (bf16[144,1280]{1,0:T(8,128)(2,1)S(1)}, bf16[144,1280]{1,0:T(8,128)(2,1)S(1)}, u32[]{:S(2)}, u32[]{:S(2)}) collective-permute-start(bf16[144,1280]{1,0:T(8,128)(2,1)S(1)} %shard_map.282.others_ref.refs_12_), channel_id=1, source_target_pairs={{0,8},{2,10},{4,12},{6,14},{8,0},{10,2},{12,4},{14,6},{16,24},{18,... | collective-permute-start | bytes 1105928 | tf_op jit(solution)/shard_map/ppermute | solution.py:389
  19.6 18.2 %collective-permute-start.6 = (bf16[272,768]{1,0:T(8,128)(2,1)S(1)}, bf16[272,768]{1,0:T(8,128)(2,1)S(1)}, u32[]{:S(2)}, u32[]{:S(2)}) collective-permute-start(bf16[272,768]{1,0:T(8,128)(2,1)S(1)} %fusion.1), channel_id=1, source_target_pairs={{0,4},{2,6},{4,0},{6,2},{8,12},{10,14},{12,8},{14,10},{16,20},{18,... | collective-permute-start | bytes 1253384 | tf_op jit(solution)/shard_map/ppermute | solution.py:386
  20.4 17.4 %collective-permute-start.7 = (bf16[272,768]{1,0:T(8,128)(2,1)S(1)}, bf16[272,768]{1,0:T(8,128)(2,1)S(1)}, u32[]{:S(2)}, u32[]{:S(2)}) collective-permute-start(bf16[272,768]{1,0:T(8,128)(2,1)S(1)} %fusion.1), channel_id=1, source_target_pairs={{0,6},{2,4},{4,2},{6,0},{8,14},{10,12},{12,10},{14,8},{16,22},{18,... | collective-permute-start | bytes 1253384 | tf_op jit(solution)/shard_map/ppermute | solution.py:386
  31.6 6.6 %copy-start.2 = (bf16[144,1280]{1,0:T(8,128)(2,1)}, bf16[144,1280]{1,0:T(8,128)(2,1)S(1)}, u32[]{:S(2)}) copy-start(bf16[144,1280]{1,0:T(8,128)(2,1)S(1)} %collective-permute-done.10.far_ref.refs_14_) | copy-start | bytes 1105924
  35.7 2.3 %copy-start.4 = (bf16[144,1280]{1,0:T(8,128)(2,1)}, bf16[144,1280]{1,0:T(8,128)(2,1)S(1)}, u32[]{:S(2)}) copy-start(bf16[144,1280]{1,0:T(8,128)(2,1)S(1)} %collective-permute-done.9.refs_13_) | copy-start | bytes 1105924
  37.9 3.1 %copy-start.13 = (f32[768]{0:T(1024)S(1)}, f32[768]{0:T(1024)}, u32[]{:S(2)}) copy-start(f32[768]{0:T(1024)} %param.21) | copy-start | bytes 9220
  37.9 3.1 %copy-start.14 = (f32[768]{0:T(1024)S(1)}, f32[768]{0:T(1024)}, u32[]{:S(2)}) copy-start(f32[768]{0:T(1024)} %param.22) | copy-start | bytes 9220
  37.9 3.1 %copy-start.15 = (f32[768]{0:T(1024)S(1)}, f32[768]{0:T(1024)}, u32[]{:S(2)}) copy-start(f32[768]{0:T(1024)} %param.23) | copy-start | bytes 9220
  37.9 3.1 %copy-start.16 = (f32[768]{0:T(1024)S(1)}, f32[768]{0:T(1024)}, u32[]{:S(2)}) copy-start(f32[768]{0:T(1024)} %param.24) | copy-start | bytes 9220
  38.0 4.1 %collective-permute-start.8 = (bf16[1088,768]{1,0:T(8,128)(2,1)S(1)}, bf16[1088,768]{1,0:T(8,128)(2,1)}, u32[]{:S(2)}, u32[]{:S(2)}) collective-permute-start(bf16[1088,768]{1,0:T(8,128)(2,1)S(1)} %constant_dynamic-update-slice_fusion.own_ref), channel_id=1, source_target_pairs={{0,1},{1,0},{2,3},{3,2},{4,5},{5,4},{6,7},{7,6},{8,9},{9,8},{10,11... | collective-permute-start | bytes 5013512 | tf_op jit(solution)/shard_map/ppermute | solution.py:392
  38.2 13.9 %collective-permute-start.11 = (bf16[192,1280]{1,0:T(8,128)(2,1)S(1)}, bf16[192,1280]{1,0:T(8,128)(2,1)S(1)}, u32[]{:S(2)}, u32[]{:S(2)}) collective-permute-start(bf16[192,1280]{1,0:T(8,128)(2,1)S(1)} %shard_map.284), channel_id=1, source_target_pairs={{0,16},{2,18},{4,20},{6,22},{24,8},{26,10},{28,12},{30,14},{8,0},{... | collective-permute-start | bytes 1474568 | tf_op jit(solution)/shard_map/ppermute | solution.py:398
  42.0 10.2 %copy-start.3 = (bf16[144,1280]{1,0:T(8,128)(2,1)S(1)}, bf16[144,1280]{1,0:T(8,128)(2,1)}, u32[]{:S(2)}) copy-start(bf16[144,1280]{1,0:T(8,128)(2,1)} %copy-done.2) | copy-start | bytes 1105924
  42.0 10.2 %copy-start.5 = (bf16[144,1280]{1,0:T(8,128)(2,1)S(1)}, bf16[144,1280]{1,0:T(8,128)(2,1)}, u32[]{:S(2)}) copy-start(bf16[144,1280]{1,0:T(8,128)(2,1)} %copy-done.4) | copy-start | bytes 1105924
  42.0 10.2 %copy-start.8 = (bf16[48,1280]{1,0:T(8,128)(2,1)S(1)}, bf16[48,1280]{1,0:T(8,128)(2,1)}, u32[]{:S(2)}) copy-start(bf16[48,1280]{1,0:T(8,128)(2,1)} %copy-done.7) | copy-start | bytes 368644
  42.0 10.1 %copy-start.9 = (f32[256,128]{1,0:T(8,128)S(1)}, f32[256,128]{1,0:T(8,128)}, u32[]{:S(2)}) copy-start(f32[256,128]{1,0:T(8,128)} %constant.38.clone.refs_6_) | copy-start | bytes 393220
  42.0 10.1 %copy-start.10 = (f32[256,128]{1,0:T(8,128)S(1)}, f32[256,128]{1,0:T(8,128)}, u32[]{:S(2)}) copy-start(f32[256,128]{1,0:T(8,128)} %constant.39.clone.refs_7_) | copy-start | bytes 393220
  42.0 10.1 %copy-start.11 = (f32[256,128]{1,0:T(8,128)S(1)}, f32[256,128]{1,0:T(8,128)}, u32[]{:S(2)}) copy-start(f32[256,128]{1,0:T(8,128)} %constant.40.clone.refs_8_) | copy-start | bytes 393220
  60.7 15.5 %collective-permute-start.12 = (bf16[192,1280]{1,0:T(8,128)(2,1)S(1)}, bf16[192,1280]{1,0:T(8,128)(2,1)S(1)}, u32[]{:S(2)}, u32[]{:S(2)}) collective-permute-start(bf16[192,1280]{1,0:T(8,128)(2,1)S(1)} %get-tuple-element.108), channel_id=1, source_target_pairs={{16,0},{18,2},{20,4},{22,6},{8,24},{10,26},{12,28},{14,30},{0,8},{... | collective-permute-start | bytes 1474568 | tf_op jit(solution)/shard_map/ppermute | solution.py:398
  67.1 12.5 %collective-permute-start.14 = (bf16[16,768]{1,0:T(8,128)(2,1)S(1)}, bf16[16,768]{1,0:T(8,128)(2,1)S(1)}, u32[]{:S(2)}, u32[]{:S(2)}) collective-permute-start(bf16[16,768]{1,0:T(8,128)(2,1)S(1)} %get-tuple-element.113.refs_0_), channel_id=1, source_target_pairs={{0,8},{2,10},{4,12},{6,14},{8,0},{10,2},{12,4},{14,6},{16,24},{18,... | collective-permute-start | bytes 73736 | tf_op jit(solution)/shard_map/ppermute | solution.py:389
  67.6 12.1 %collective-permute-start.15 = (bf16[16,768]{1,0:T(8,128)(2,1)S(1)}, bf16[16,768]{1,0:T(8,128)(2,1)S(1)}, u32[]{:S(2)}, u32[]{:S(2)}) collective-permute-start(bf16[16,768]{1,0:T(8,128)(2,1)S(1)} %get-tuple-element.113.refs_0_), channel_id=1, source_target_pairs={{0,16},{2,18},{4,20},{6,22},{8,24},{10,26},{12,28},{14,30},{16,0},... | collective-permute-start | bytes 73736 | tf_op jit(solution)/shard_map/ppermute | solution.py:389
  70.2 9.4 %collective-permute-start.16 = (bf16[16,768]{1,0:T(8,128)(2,1)S(1)}, bf16[16,768]{1,0:T(8,128)(2,1)S(1)}, u32[]{:S(2)}, u32[]{:S(2)}) collective-permute-start(bf16[16,768]{1,0:T(8,128)(2,1)S(1)} %get-tuple-element.113.refs_0_), channel_id=1, source_target_pairs={{0,24},{2,26},{4,28},{6,30},{8,16},{10,18},{12,20},{14,22},{16,8},... | collective-permute-start | bytes 73736 | tf_op jit(solution)/shard_map/ppermute | solution.py:389
  71.6 4.8 %collective-permute-start.13 = (bf16[1024,768]{1,0:T(8,128)(2,1)S(1)}, bf16[1024,768]{1,0:T(8,128)(2,1)S(1)}, u32[]{:S(2)}, u32[]{:S(2)}) collective-permute-start(bf16[1024,768]{1,0:T(8,128)(2,1)S(1)} %get-tuple-element.109), channel_id=1, source_target_pairs={{0,1},{1,0},{2,3},{3,2},{4,5},{5,4},{6,7},{7,6},{8,9},{9,8},{10,11... | collective-permute-start | bytes 4718600 | tf_op jit(solution)/shard_map/ppermute | solution.py:392
  76.3 22.8 %collective-permute-start.20 = (bf16[192,1280]{1,0:T(8,128)(2,1)S(1)}, bf16[192,1280]{1,0:T(8,128)(2,1)S(1)}, u32[]{:S(2)}, u32[]{:S(2)}) collective-permute-start(bf16[192,1280]{1,0:T(8,128)(2,1)S(1)} %get-tuple-element.118), channel_id=1, source_target_pairs={{0,8},{2,10},{4,12},{6,14},{8,0},{10,2},{12,4},{14,6},{16,24},{18,... | collective-permute-start | bytes 1474568 | tf_op jit(solution)/shard_map/ppermute | solution.py:389
  77.2 22.5 %collective-permute-start.21 = (bf16[192,1280]{1,0:T(8,128)(2,1)S(1)}, bf16[192,1280]{1,0:T(8,128)(2,1)S(1)}, u32[]{:S(2)}, u32[]{:S(2)}) collective-permute-start(bf16[192,1280]{1,0:T(8,128)(2,1)S(1)} %shard_map.287), channel_id=1, source_target_pairs={{0,24},{2,26},{4,28},{6,30},{8,16},{10,18},{12,20},{14,22},{16,8},... | collective-permute-start | bytes 1474568 | tf_op jit(solution)/shard_map/ppermute | solution.py:389
  79.6 4.0 %copy-start.17 = (f32[768]{0:T(1024)S(1)}, f32[768]{0:T(1024)}, u32[]{:S(2)}) copy-start(f32[768]{0:T(1024)} %param.28) | copy-start | bytes 9220
  79.7 4.0 %copy-start.18 = (f32[768]{0:T(1024)S(1)}, f32[768]{0:T(1024)}, u32[]{:S(2)}) copy-start(f32[768]{0:T(1024)} %param.32) | copy-start | bytes 9220
  80.1 12.6 %collective-permute-start.17 = (bf16[272,768]{1,0:T(8,128)(2,1)S(1)}, bf16[272,768]{1,0:T(8,128)(2,1)S(1)}, u32[]{:S(2)}, u32[]{:S(2)}) collective-permute-start(bf16[272,768]{1,0:T(8,128)(2,1)S(1)} %get-tuple-element.115), channel_id=1, source_target_pairs={{0,2},{2,0},{4,6},{6,4},{8,10},{10,8},{12,14},{14,12},{16,18},{18,... | collective-permute-start | bytes 1253384 | tf_op jit(solution)/shard_map/ppermute | solution.py:386
  81.3 17.9 %collective-permute-start.18 = (bf16[272,768]{1,0:T(8,128)(2,1)S(1)}, bf16[272,768]{1,0:T(8,128)(2,1)S(1)}, u32[]{:S(2)}, u32[]{:S(2)}) collective-permute-start(bf16[272,768]{1,0:T(8,128)(2,1)S(1)} %get-tuple-element.116), channel_id=1, source_target_pairs={{0,4},{2,6},{4,0},{6,2},{8,12},{10,14},{12,8},{14,10},{16,20},{18,... | collective-permute-start | bytes 1253384 | tf_op jit(solution)/shard_map/ppermute | solution.py:386
  81.8 17.4 %collective-permute-start.19 = (bf16[272,768]{1,0:T(8,128)(2,1)S(1)}, bf16[272,768]{1,0:T(8,128)(2,1)S(1)}, u32[]{:S(2)}, u32[]{:S(2)}) collective-permute-start(bf16[272,768]{1,0:T(8,128)(2,1)S(1)} %get-tuple-element.117), channel_id=1, source_target_pairs={{0,6},{2,4},{4,2},{6,0},{8,14},{10,12},{12,10},{14,8},{16,22},{18,... | collective-permute-start | bytes 1253384 | tf_op jit(solution)/shard_map/ppermute | solution.py:386
  99.9 6.0 %collective-permute-start.22 = (bf16[48,1280]{1,0:T(8,128)(2,1)S(1)}, bf16[48,1280]{1,0:T(8,128)(2,1)S(1)}, u32[]{:S(2)}, u32[]{:S(2)}) collective-permute-start(bf16[48,1280]{1,0:T(8,128)(2,1)S(1)} %get-tuple-element.130), channel_id=1, source_target_pairs={{0,2},{2,0},{4,6},{6,4},{8,10},{10,8},{12,14},{14,12},{16,18},{18,... | collective-permute-start | bytes 368648 | tf_op jit(solution)/shard_map/ppermute | solution.py:386
  101.1 4.9 %collective-permute-start.23 = (bf16[48,1280]{1,0:T(8,128)(2,1)S(1)}, bf16[48,1280]{1,0:T(8,128)(2,1)S(1)}, u32[]{:S(2)}, u32[]{:S(2)}) collective-permute-start(bf16[48,1280]{1,0:T(8,128)(2,1)S(1)} %get-tuple-element.131), channel_id=1, source_target_pairs={{0,4},{2,6},{4,0},{6,2},{8,12},{10,14},{12,8},{14,10},{16,20},{18,... | collective-permute-start | bytes 368648 | tf_op jit(solution)/shard_map/ppermute | solution.py:386
  101.6 5.8 %collective-permute-start.24 = (bf16[48,1280]{1,0:T(8,128)(2,1)S(1)}, bf16[48,1280]{1,0:T(8,128)(2,1)S(1)}, u32[]{:S(2)}, u32[]{:S(2)}) collective-permute-start(bf16[48,1280]{1,0:T(8,128)(2,1)S(1)} %get-tuple-element.132), channel_id=1, source_target_pairs={{0,6},{2,4},{4,2},{6,0},{8,14},{10,12},{12,10},{14,8},{16,22},{18,... | collective-permute-start | bytes 368648 | tf_op jit(solution)/shard_map/ppermute | solution.py:386
  104.7 1.2 %collective-permute-start.25 = (f32[16,768]{1,0:T(8,128)S(1)}, f32[16,768]{1,0:T(8,128)S(1)}, u32[]{:S(2)}, u32[]{:S(2)}) collective-permute-start(f32[16,768]{1,0:T(8,128)S(1)} %get-tuple-element.133.refs_4_), channel_id=1, source_target_pairs={{0,1},{1,0},{2,3},{3,2},{4,5},{5,4},{6,7},{7,6},{8,9},{9,8},{10,11... | collective-permute-start | bytes 147464 | tf_op jit(solution)/shard_map/ppermute | solution.py:392

commit v6 on v5

--- a/solution.py
+++ b/solution.py
@@ -14,6 +14,7 @@
 PLANE = 4
 BLK = 2 * HD
 NOTES = 16
+MARK = 16384.0
 eps = 1e-05
 F32 = jnp.float32
 BF16 = jnp.bfloat16
@@ -113,10 +114,8 @@
     params = params_ref[...]
     length_ref[...] = jnp.zeros_like(length_ref)
     for k in range(PLANE):
-        start = k * (slots + NOTES)
-        length = own_ref[start + slots : start + slots + NOTES, :].astype(F32)
-        length = jnp.sum(length[0:1], axis=-1, keepdims=True)
-        length_ref[k : k + 1, :] = jnp.broadcast_to(length, (1, length_ref.shape[1]))
+        start = k * slots
+        count = jnp.zeros((1, 1), F32)
         for which, ref in enumerate((own_ref, peer_ref)):
             part = half if which == 0 else 1 - half
             x = ref[start : start + own_rows, :].astype(F32)
@@ -128,28 +127,30 @@
             x1_ref[at, :] = (xh * params[0:1] + params[1:2]).astype(BF16)
             x2_ref[at, :] = (xh * params[2:3] + params[3:4]).astype(BF16)
             xh_ref[at, :] = xh.astype(BF16)
-            row = lax.broadcasted_iota(jnp.int32, (own_rows, 1), 0) + part * own_rows
             g = ref[start + own_rows : start + slots, :].astype(F32)
-            g = jnp.where(row.astype(F32) < length, g, 0.0)
+            live = g[:, 0:1] < 0.5 * MARK
+            count = count + jnp.sum(jnp.where(live, 1.0, 0.0), axis=0, keepdims=True)
+            g = jnp.where(live, g, 0.0)
             g_ref[at, :] = g.astype(BF16)
             if k == 0 and which == 0:
                 g_own_ref[...] = g.astype(BF16)
                 bo_ref[...] = jnp.sum(g, axis=0, keepdims=True)
+        length_ref[k : k + 1, :] = jnp.broadcast_to(count, (1, length_ref.shape[1]))
 
 
 def layer_kernel(levels, *refs):
     length_ref, x1_ref, x2_ref, g_ref, bias_ref, bias_up_ref, keep_ref, low_ref, high_ref = refs[:9]
-    pieces = refs[9 : 9 + (7 if levels else 1)]
+    pieces = refs[9 : 9 + (5 if levels else 1)]
     za_ref, gp_ref, gh_ref, w_ref, gb_ref = refs[9 + len(pieces) : 14 + len(pieces)]
     message_refs, gw_ref = refs[14 + len(pieces) : -1], refs[-1]
     if levels:
-        owned = pieces[0].shape[0]
-        for own, others, m in ((0, 3, 0), (1, 4, 1), (2, 5, 3)):
-            w_ref[rows_at(m, 0, owned), :] = pieces[own][...]
-            for k in range(1, PLANE):
-                w_ref[rows_at(m, k, owned), :] = pieces[others][(k - 1) * owned : k * owned, :]
-        for k in range(PLANE):
-            w_ref[rows_at(2, k, owned), :] = pieces[6][k * owned : (k + 1) * owned, :]
+        owned = pieces[3].shape[0]
+        for m in range(3):
+            for k in range(PLANE):
+                w_ref[rows_at(m, k, owned), :] = pieces[m][k * owned : (k + 1) * owned, :]
+        w_ref[rows_at(3, 0, owned), :] = pieces[3][...]
+        for k in range(1, PLANE):
+            w_ref[rows_at(3, k, owned), :] = pieces[4][(k - 1) * owned : k * owned, :]
     else:
         w_ref[...] = pieces[0][...]
         gw_ref = message_refs[0]
@@ -250,9 +251,12 @@
 
 
 def join_kernel(*refs):
-    owned = refs[0].shape[0]
-    for k, ref in enumerate(refs[:-1]):
-        refs[-1][k * owned : (k + 1) * owned, :] = ref[...]
+    part_refs, (every_ref, others_ref) = refs[:PLANE], refs[PLANE:]
+    owned = part_refs[0].shape[0]
+    for k, ref in enumerate(part_refs):
+        every_ref[k * owned : (k + 1) * owned, :] = ref[...]
+        if k:
+            others_ref[(k - 1) * owned : k * owned, :] = ref[...]
 
 
 def choose_kernel(own_ref, own_far_ref, others_ref, far_ref, out_ref):
@@ -408,16 +412,22 @@
     )
     received = [to_plane(shares[k], k) for k in range(1, PLANE)]
     residual_m, cotangent_m, lengths_m, _ = lax.optimization_barrier((residual, cotangent, seq_lengths, shares))
-    notes = jnp.pad(lengths_m.astype(BF16), ((0, NOTES - 1), (0, model - seq_lengths.shape[1])))
-    message = jnp.concatenate([residual_m, cotangent_m, notes], axis=0)
+    row = lax.axis_index("tensor") * own_rows + jnp.arange(own_rows, dtype=jnp.int32)
+    live = (row < jnp.sum(lengths_m[0]))[:, None]
+    message = jnp.concatenate([residual_m, jnp.where(live, cotangent_m, jnp.asarray(MARK, BF16))], axis=0)
     if direct:
         own = shares[0]
-        own_near, own_far = to_level(own, 1), to_level(own, 3)
-        others = kernel_call(join_kernel, [shape(((PLANE - 1) * owned, columns), BF16)], received, micros=20)[0]
-        others, message = lax.optimization_barrier((others, message))
-        near, far = to_level(others, 1), to_level(others, 3)
+        own_far = to_level(own, 3)
+        every, others = kernel_call(
+            join_kernel,
+            [shape((PLANE * owned, columns), BF16), shape(((PLANE - 1) * owned, columns), BF16)],
+            (own, *received),
+            micros=20,
+        )
+        every, others, message = lax.optimization_barrier((every, others, message))
+        near, far = to_level(every, 1), to_level(others, 3)
         near, far = lax.optimization_barrier((near, far))
-        message, own_near, own_far = lax.optimization_barrier((message, own_near, own_far))
+        message, own_far = lax.optimization_barrier((message, own_far))
         chosen = kernel_call(
             choose_kernel,
             [shape((PLANE * owned, columns), BF16)],
@@ -426,7 +436,7 @@
         )[0]
     messages = [message] + [to_plane(message, k) for k in range(1, PLANE)]
     if direct:
-        pieces = [own, own_near, own_far, others, near, far, to_pass(chosen)]
+        pieces = [every, near, to_pass(chosen), own_far, far]
     else:
         every = jnp.concatenate(xor_sorted([shares[0]] + received, plane_at), axis=0)
         pieces = [lax.all_gather(every, "dp", axis=0, tiled=True, axis_index_groups=level_groups)]

time: 109 us -> 108 us (level)
  waiting for transfers between devices: 50.9 us -> 46.6 us
  Pallas kernels: 21 us -> 22.9 us
  other arithmetic: 0.03 us -> 1.4 us
    ppermute x9 -> x8, waiting for transfers between devices: 13.7 us -> 5.61 us  [to_level(): return lax.ppermute(x, 'dp', [(j, j ^ m * PLANE) for j in range(places)])]
    ppermute x12, waiting for transfers between devices: 24.7 us -> 31.1 us  [to_plane(): return lax.ppermute(x, 'dp', [(j, j ^ k) for j in range(places)])]
    ppermute x2, waiting for transfers between devices: 11.2 us -> 7.48 us  [to_pass(): lax.ppermute(x, 'dp', [(a * PLANE + j, b * PLANE + j) for a, b in pairs f...]
    ppermute x2, starting transfers between devices: 5.42 us -> 2.88 us  [to_pass(): lax.ppermute(x, 'dp', [(a * PLANE + j, b * PLANE + j) for a, b in pairs f...]
    pallas_call x11, Pallas kernels: 21 us -> 22.9 us  [kernel_call(): pl.pallas_call(body, out_shape=out_shapes, in_specs=[taken] * len(operand...]
    ppermute x3, waiting for transfers between devices: 1.23 us -> 2.43 us  [to_peer(): return lax.ppermute(x, 'tensor', [(0, 1), (1, 0)])]
    ppermute x9 -> x8, starting transfers between devices: 14.7 us -> 15.2 us  [to_level(): return lax.ppermute(x, 'dp', [(j, j ^ m * PLANE) for j in range(places)])]
  transfers between devices with their start and end apart: 26 -> 25, of which waited for: 12 -> 13; matrix products, arithmetic and copies ran while one was open for 1% -> 2% of each run, Pallas kernels for 8% -> 9%
where the time goes in v6:
time: 108 us; the launch traced here: 107 us
  waiting for transfers between devices  46.6 us (43%)
  starting transfers between devices  33.3 us (31%)
  Pallas kernels  22.9 us (21%)
  local copies, waits for them, and re-layouts  1.95 us (2%)
  other arithmetic  1.4 us (1%)
  between operations  1.17 us (1%)
    ppermute x12, waiting for transfers between devices, to_plane(): return lax.ppermute(x, 'dp', [(j, j ^ k) for j in range(places)])  31.1 us
    pallas_call x11, Pallas kernels, kernel_call(): pl.pallas_call(body, out_shape=out_shapes, in_specs=[taken] * len(operand...  22.9 us
    ppermute x12, starting transfers between devices, to_plane(): return lax.ppermute(x, 'dp', [(j, j ^ k) for j in range(places)])  15.2 us
    ppermute x8, starting transfers between devices, to_level(): return lax.ppermute(x, 'dp', [(j, j ^ m * PLANE) for j in range(places)])  15.2 us
    ppermute x2, waiting for transfers between devices, to_pass(): lax.ppermute(x, 'dp', [(a * PLANE + j, b * PLANE + j) for a, b in pairs f...  7.48 us
    ppermute x8, waiting for transfers between devices, to_level(): return lax.ppermute(x, 'dp', [(j, j ^ m * PLANE) for j in range(places)])  5.61 us
    ppermute x2, starting transfers between devices, to_pass(): lax.ppermute(x, 'dp', [(a * PLANE + j, b * PLANE + j) for a, b in pairs f...  2.88 us
    ppermute x3, waiting for transfers between devices, to_peer(): return lax.ppermute(x, 'tensor', [(0, 1), (1, 0)])  2.43 us
  transfers between devices with their start and end apart: 25, of which 13 were waited for; matrix products, arithmetic and copies ran while one was open for 2% of the time, Pallas kernels for 9%

profile of v6, /device:TPU:0, one launch (start us, length us, event | category | flops | bytes accessed | tf_op | source)
XLA Modules:
  0.0 107.4 jit_solution(15441706586403488113)
XLA Ops:
  0.7 2.0 %shard_map.281 = (bf16[48,1280]{1,0:T(8,128)(2,1)}, bf16[48,1280]{1,0:T(8,128)(2,1)}, bf16[48,1280]{1,0:T(8,128)(2,1)}, bf16[48,1280]{1,0:T(8,128)(2,1)}) custom-call(bf16[3,48,384]{2,1,0:T(8,128)(2,1)} %refs_0_.1, bf16[48,384]{1,0:T(8,128)(2,1)} %bitcast.19, bf16[48,1536]{1,0:T(8,128)(2,1)} %refs_2_.1, bf16[48,1536]{1,0:T(8,128)(2,1)} %bitcast.18), custom_call_target="tpu_custom_call" | custom-call | flops 1000000000 | bytes 1 | tf_op jit(solution)/shard_map/pallas_call | solution.py:347
  2.7 3.0 %collective-permute-start = (bf16[48,1280]{1,0:T(8,128)(2,1)}, bf16[48,1280]{1,0:T(8,128)(2,1)S(1)}, u32[]{:S(2)}, u32[]{:S(2)}) collective-permute-start(bf16[48,1280]{1,0:T(8,128)(2,1)} %get-tuple-element.83), channel_id=1, source_target_pairs={{0,2},{2,0},{4,6},{6,4},{8,10},{10,8},{12,14},{14,12},{16,18},{18,... | collective-permute-start | bytes 368648 | tf_op jit(solution)/shard_map/ppermute | solution.py:390
  5.7 1.5 %collective-permute-start.1 = (bf16[48,1280]{1,0:T(8,128)(2,1)}, bf16[48,1280]{1,0:T(8,128)(2,1)S(1)}, u32[]{:S(2)}, u32[]{:S(2)}) collective-permute-start(bf16[48,1280]{1,0:T(8,128)(2,1)} %get-tuple-element.84), channel_id=1, source_target_pairs={{0,4},{2,6},{4,0},{6,2},{8,12},{10,14},{12,8},{14,10},{16,20},{18,... | collective-permute-start | bytes 368648 | tf_op jit(solution)/shard_map/ppermute | solution.py:390
  7.2 4.1 %collective-permute-start.3 = (bf16[48,1280]{1,0:T(8,128)(2,1)}, bf16[48,1280]{1,0:T(8,128)(2,1)S(1)}, u32[]{:S(2)}, u32[]{:S(2)}) collective-permute-start(bf16[48,1280]{1,0:T(8,128)(2,1)} %get-tuple-element.82.refs_0_.own_ref), channel_id=1, source_target_pairs={{0,24},{2,26},{4,28},{6,30},{8,16},{10,18},{12,20},{14,22},{16,8},... | collective-permute-start | bytes 368648 | tf_op jit(solution)/shard_map/ppermute | solution.py:393
  11.3 0.6 reduce_sum.9
  11.9 0.7 add_compare_fusion
  12.6 0.1 broadcast_select_fusion
  12.7 0.7 collective-permute-done.1.refs_2_
  13.4 0.9 copy-done.2
  14.4 1.8 %collective-permute-start.4 = (bf16[256,768]{1,0:T(8,128)(2,1)S(1)}, bf16[256,768]{1,0:T(8,128)(2,1)S(1)}, u32[]{:S(2)}, u32[]{:S(2)}) collective-permute-start(bf16[256,768]{1,0:T(8,128)(2,1)S(1)} %pad_maximum_fusion), channel_id=1, source_target_pairs={{0,2},{2,0},{4,6},{6,4},{8,10},{10,8},{12,14},{14,12},{16,18},{18,... | collective-permute-start | bytes 1179656 | tf_op jit(solution)/shard_map/ppermute | solution.py:390
  16.2 1.5 %collective-permute-start.5 = (bf16[256,768]{1,0:T(8,128)(2,1)S(1)}, bf16[256,768]{1,0:T(8,128)(2,1)S(1)}, u32[]{:S(2)}, u32[]{:S(2)}) collective-permute-start(bf16[256,768]{1,0:T(8,128)(2,1)S(1)} %pad_maximum_fusion), channel_id=1, source_target_pairs={{0,4},{2,6},{4,0},{6,2},{8,12},{10,14},{12,8},{14,10},{16,20},{18,... | collective-permute-start | bytes 1179656 | tf_op jit(solution)/shard_map/ppermute | solution.py:390
  17.7 0.2 collective-permute-start.6
  17.9 1.9 %collective-permute-start.8 = (bf16[192,1280]{1,0:T(8,128)(2,1)S(1)}, bf16[192,1280]{1,0:T(8,128)(2,1)S(1)}, u32[]{:S(2)}, u32[]{:S(2)}) collective-permute-start(bf16[192,1280]{1,0:T(8,128)(2,1)S(1)} %get-tuple-element.99.refs_9_), channel_id=1, source_target_pairs={{0,8},{2,10},{4,12},{6,14},{8,0},{10,2},{12,4},{14,6},{16,24},{18,... | collective-permute-start | bytes 1474568 | tf_op jit(solution)/shard_map/ppermute | solution.py:393
  19.8 3.1 %collective-permute-start.9 = (bf16[144,1280]{1,0:T(8,128)(2,1)S(1)}, bf16[144,1280]{1,0:T(8,128)(2,1)S(1)}, u32[]{:S(2)}, u32[]{:S(2)}) collective-permute-start(bf16[144,1280]{1,0:T(8,128)(2,1)S(1)} %get-tuple-element.100.others_ref), channel_id=1, source_target_pairs={{0,24},{2,26},{4,28},{6,30},{8,16},{10,18},{12,20},{14,22},{16,8},... | collective-permute-start | bytes 1105928 | tf_op jit(solution)/shard_map/ppermute | solution.py:393
  22.9 3.6 %collective-permute-done.4 = bf16[256,768]{1,0:T(8,128)(2,1)S(1)} collective-permute-done((bf16[256,768]{1,0:T(8,128)(2,1)S(1)}, bf16[256,768]{1,0:T(8,128)(2,1)S(1)}, u32[]{:S(2)}, u32[]{:S(2)}) %collective-permute-start.4) | collective-permute-done | bytes 393248 | tf_op jit(solution)/shard_map/ppermute | solution.py:390
  26.5 7.2 %collective-permute-done.5 = bf16[256,768]{1,0:T(8,128)(2,1)S(1)} collective-permute-done((bf16[256,768]{1,0:T(8,128)(2,1)S(1)}, bf16[256,768]{1,0:T(8,128)(2,1)S(1)}, u32[]{:S(2)}, u32[]{:S(2)}) %collective-permute-start.5) | collective-permute-done | bytes 393248 | tf_op jit(solution)/shard_map/ppermute | solution.py:390
  33.9 4.7 %collective-permute-done.9.far_ref.refs_13_ = bf16[144,1280]{1,0:T(8,128)(2,1)S(1)} collective-permute-done((bf16[144,1280]{1,0:T(8,128)(2,1)S(1)}, bf16[144,1280]{1,0:T(8,128)(2,1)S(1)}, u32[]{:S(2)}, u32[]{:S(2)}) %collective-permute-start.9) | collective-permute-done | bytes 368672 | tf_op jit(solution)/shard_map/ppermute | solution.py:393
  38.6 0.9 shard_map.284
  39.6 0.8 dynamic_slice.7
  40.5 3.5 %shard_map.283 = (bf16[1024,768]{1,0:T(8,128)(2,1)S(1)}, bf16[1024,768]{1,0:T(8,128)(2,1)S(1)}, bf16[1024,768]{1,0:T(8,128)(2,1)S(1)}, bf16[1024,768]{1,0:T(8,12...) custom-call(f32[8,768]{1,0:T(8,128)S(1)} %stack.23.params_ref, ...), custom_call_target="tpu_custom_call" | custom-call | flops 1000000000 | bytes 1 | tf_op jit(solution)/shard_map/pallas_call | solution.py:347
  44.0 5.4 %collective-permute-done.10.refs_11_ = bf16[192,1280]{1,0:T(8,128)(2,1)} collective-permute-done((bf16[192,1280]{1,0:T(8,128)(2,1)}, bf16[192,1280]{1,0:T(8,128)(2,1)}, u32[]{:S(2)}, u32[]{:S(2)}) %collective-permute-start.10) | collective-permute-done | bytes 491552 | tf_op jit(solution)/shard_map/ppermute | solution.py:402
  49.4 9.7 %shard_map.285 = (bf16[1024,512]{1,0:T(8,128)(2,1)S(1)}, bf16[1024,384]{1,0:T(8,128)(2,1)S(1)}, bf16[1024,384]{1,0:T(8,128)(2,1)S(1)}, bf16[768,1280]{1,0:T(8,12...) custom-call(f32[8,128]{1,0:T(8,128)S(1)} %get-tuple-element.95.refs_, ...), custom_call_target="tpu_custom_call" | custom-call | flops 12000000000 | bytes 1 | tf_op jit(solution)/shard_map/pallas_call | solution.py:347
  59.1 2.9 %collective-permute-start.11 = (bf16[192,1280]{1,0:T(8,128)(2,1)S(1)}, bf16[192,1280]{1,0:T(8,128)(2,1)S(1)}, u32[]{:S(2)}, u32[]{:S(2)}) collective-permute-start(bf16[192,1280]{1,0:T(8,128)(2,1)S(1)} %get-tuple-element.112), channel_id=1, source_target_pairs={{16,0},{18,2},{20,4},{22,6},{8,24},{10,26},{12,28},{14,30},{0,8},{... | collective-permute-start | bytes 1474568 | tf_op jit(solution)/shard_map/ppermute | solution.py:402
  62.0 3.8 %shard_map.286 = (bf16[1024,768]{1,0:T(8,128)(2,1)S(1)}, bf16[1024,768]{1,0:T(8,128)(2,1)S(1)}, bf16[16,768]{1,0:T(8,128)(2,1)S(1)}) custom-call(f32[8,768]{1,0:T(8,128)S(1)} %stack.23.params_ref, bf16[1024,768]{1,0:T(8,128)(2,1)S(1)} %get-tuple-element.94.xh_ref, bf16[768,1280]{1,0:T(8,128)(2,1)S(1)} %get-tuple-element.104.w_ref, ...), custom_call_target="tpu_custom_call" | custom-call | flops 4000000000 | bytes 1 | tf_op jit(solution)/shard_map/pallas_call | solution.py:347
  65.8 1.2 %collective-permute-start.13 = (bf16[16,768]{1,0:T(8,128)(2,1)S(1)}, bf16[16,768]{1,0:T(8,128)(2,1)S(1)}, u32[]{:S(2)}, u32[]{:S(2)}) collective-permute-start(bf16[16,768]{1,0:T(8,128)(2,1)S(1)} %get-tuple-element.117.refs_0_), channel_id=1, source_target_pairs={{0,8},{2,10},{4,12},{6,14},{8,0},{10,2},{12,4},{14,6},{16,24},{18,... | collective-permute-start | bytes 73736 | tf_op jit(solution)/shard_map/ppermute | solution.py:393
  66.9 1.1 %collective-permute-start.14 = (bf16[16,768]{1,0:T(8,128)(2,1)S(1)}, bf16[16,768]{1,0:T(8,128)(2,1)S(1)}, u32[]{:S(2)}, u32[]{:S(2)}) collective-permute-start(bf16[16,768]{1,0:T(8,128)(2,1)S(1)} %get-tuple-element.117.refs_0_), channel_id=1, source_target_pairs={{0,16},{2,18},{4,20},{6,22},{8,24},{10,26},{12,28},{14,30},{16,0},... | collective-permute-start | bytes 73736 | tf_op jit(solution)/shard_map/ppermute | solution.py:393
  68.1 2.1 %collective-permute-start.15 = (bf16[16,768]{1,0:T(8,128)(2,1)S(1)}, bf16[16,768]{1,0:T(8,128)(2,1)S(1)}, u32[]{:S(2)}, u32[]{:S(2)}) collective-permute-start(bf16[16,768]{1,0:T(8,128)(2,1)S(1)} %get-tuple-element.117.refs_0_), channel_id=1, source_target_pairs={{0,24},{2,26},{4,28},{6,30},{8,16},{10,18},{12,20},{14,22},{16,8},... | collective-permute-start | bytes 73736 | tf_op jit(solution)/shard_map/ppermute | solution.py:393
  70.2 2.0 %collective-permute-done.11.passed_ref = bf16[192,1280]{1,0:T(8,128)(2,1)S(1)} collective-permute-done((bf16[192,1280]{1,0:T(8,128)(2,1)S(1)}, bf16[192,1280]{1,0:T(8,128)(2,1)S(1)}, u32[]{:S(2)}, u32[]{:S(2)}) %collective-permute-start.11) | collective-permute-done | bytes 491552 | tf_op jit(solution)/shard_map/ppermute | solution.py:402
  72.2 0.2 shard_map.287
  72.4 1.2 %collective-permute-done.12.peer_ref = bf16[1024,768]{1,0:T(8,128)(2,1)S(1)} collective-permute-done((bf16[1024,768]{1,0:T(8,128)(2,1)S(1)}, bf16[1024,768]{1,0:T(8,128)(2,1)S(1)}, u32[]{:S(2)}, u32[]{:S(2)}) %collective-permute-start.12) | collective-permute-done | bytes 1572896 | tf_op jit(solution)/shard_map/ppermute | solution.py:396
  73.6 0.2 collective-permute-start.19
  73.8 1.5 %collective-permute-start.20 = (bf16[192,1280]{1,0:T(8,128)(2,1)S(1)}, bf16[192,1280]{1,0:T(8,128)(2,1)S(1)}, u32[]{:S(2)}, u32[]{:S(2)}) collective-permute-start(bf16[192,1280]{1,0:T(8,128)(2,1)S(1)} %shard_map.287), channel_id=1, source_target_pairs={{0,24},{2,26},{4,28},{6,30},{8,16},{10,18},{12,20},{14,22},{16,8},... | collective-permute-start | bytes 1474568 | tf_op jit(solution)/shard_map/ppermute | solution.py:393
  75.4 0.4 shard_map.288
  75.8 1.0 collective-permute-start.16
  76.8 1.5 %collective-permute-start.17 = (bf16[272,768]{1,0:T(8,128)(2,1)S(1)}, bf16[272,768]{1,0:T(8,128)(2,1)S(1)}, u32[]{:S(2)}, u32[]{:S(2)}) collective-permute-start(bf16[272,768]{1,0:T(8,128)(2,1)S(1)} %get-tuple-element.120), channel_id=1, source_target_pairs={{0,4},{2,6},{4,0},{6,2},{8,12},{10,14},{12,8},{14,10},{16,20},{18,... | collective-permute-start | bytes 1253384 | tf_op jit(solution)/shard_map/ppermute | solution.py:390
  78.3 1.1 collective-permute-start.18
  79.4 9.0 %collective-permute-done.16.refs_1_ = bf16[272,768]{1,0:T(8,128)(2,1)S(1)} collective-permute-done((bf16[272,768]{1,0:T(8,128)(2,1)S(1)}, bf16[272,768]{1,0:T(8,128)(2,1)S(1)}, u32[]{:S(2)}, u32[]{:S(2)}) %collective-permute-start.16) | collective-permute-done | bytes 417824 | tf_op jit(solution)/shard_map/ppermute | solution.py:390
  88.4 8.2 %collective-permute-done.17.refs_2_ = bf16[272,768]{1,0:T(8,128)(2,1)S(1)} collective-permute-done((bf16[272,768]{1,0:T(8,128)(2,1)S(1)}, bf16[272,768]{1,0:T(8,128)(2,1)S(1)}, u32[]{:S(2)}, u32[]{:S(2)}) %collective-permute-start.17) | collective-permute-done | bytes 417824 | tf_op jit(solution)/shard_map/ppermute | solution.py:390
  96.6 0.9 collective-permute-done.20.far_ref
  97.5 0.3 shard_map.290
  97.7 1.2 %collective-permute-start.21 = (bf16[48,1280]{1,0:T(8,128)(2,1)S(1)}, bf16[48,1280]{1,0:T(8,128)(2,1)S(1)}, u32[]{:S(2)}, u32[]{:S(2)}) collective-permute-start(bf16[48,1280]{1,0:T(8,128)(2,1)S(1)} %get-tuple-element.134), channel_id=1, source_target_pairs={{0,2},{2,0},{4,6},{6,4},{8,10},{10,8},{12,14},{14,12},{16,18},{18,... | collective-permute-start | bytes 368648 | tf_op jit(solution)/shard_map/ppermute | solution.py:390
  98.9 1.2 %collective-permute-start.22 = (bf16[48,1280]{1,0:T(8,128)(2,1)S(1)}, bf16[48,1280]{1,0:T(8,128)(2,1)S(1)}, u32[]{:S(2)}, u32[]{:S(2)}) collective-permute-start(bf16[48,1280]{1,0:T(8,128)(2,1)S(1)} %get-tuple-element.135), channel_id=1, source_target_pairs={{0,4},{2,6},{4,0},{6,2},{8,12},{10,14},{12,8},{14,10},{16,20},{18,... | collective-permute-start | bytes 368648 | tf_op jit(solution)/shard_map/ppermute | solution.py:390
  100.1 1.1 %collective-permute-start.23 = (bf16[48,1280]{1,0:T(8,128)(2,1)S(1)}, bf16[48,1280]{1,0:T(8,128)(2,1)S(1)}, u32[]{:S(2)}, u32[]{:S(2)}) collective-permute-start(bf16[48,1280]{1,0:T(8,128)(2,1)S(1)} %get-tuple-element.136), channel_id=1, source_target_pairs={{0,6},{2,4},{4,2},{6,0},{8,14},{10,12},{12,10},{14,8},{16,22},{18,... | collective-permute-start | bytes 368648 | tf_op jit(solution)/shard_map/ppermute | solution.py:390
  101.3 1.2 %shard_map.289 = (bf16[128,768]{1,0:T(8,128)(2,1)}, f32[128,768]{1,0:T(8,128)}, f32[16,768]{1,0:T(8,128)S(1)}) custom-call(bf16[128,768]{1,0:T(8,128)(2,1)S(1)} %copy-done.1, bf16[128,768]{1,0:T(8,128)(2,1)S(1)} %get-tuple-element.93.g_ref, f32[1,768]{1,0:T(1,128)S(1)} %reshape.66.b_out_ref, f32[1,768]{1,0:T(1,128)S(1)} %reshape.67.b_down_ref, ...), custom_call_target="tpu_custom_call" | custom-call | flops 1000000000 | bytes 1 | tf_op jit(solution)/shard_map/pallas_call | solution.py:347
  102.5 1.2 %collective-permute-done.24.refs_5_ = f32[16,768]{1,0:T(8,128)S(1)} collective-permute-done((f32[16,768]{1,0:T(8,128)S(1)}, f32[16,768]{1,0:T(8,128)S(1)}, u32[]{:S(2)}, u32[]{:S(2)}) %collective-permute-start.24) | collective-permute-done | bytes 49184 | tf_op jit(solution)/shard_map/ppermute | solution.py:396
  103.7 0.1 collective-permute-done.21.refs_1_
  103.9 2.3 %collective-permute-done.22.refs_2_ = bf16[48,1280]{1,0:T(8,128)(2,1)S(1)} collective-permute-done((bf16[48,1280]{1,0:T(8,128)(2,1)S(1)}, bf16[48,1280]{1,0:T(8,128)(2,1)S(1)}, u32[]{:S(2)}, u32[]{:S(2)}) %collective-permute-start.22) | collective-permute-done | bytes 122912 | tf_op jit(solution)/shard_map/ppermute | solution.py:390
  106.2 1.0 shard_map.291
  (61 shorter events, 0.5 us)
Async XLA Ops:
  0.6 38.9 %copy-start = (f32[3,384]{1,0:T(4,128)S(1)}, f32[3,384]{1,0:T(4,128)}, u32[]{:S(2)}) copy-start(f32[3,384]{1,0:T(4,128)} %param.26) | copy-start | bytes 13828
  0.7 10.6 %copy-start.13 = (s32[1,4]{1,0:T(1,128)S(1)}, s32[1,4]{1,0:T(1,128)}, u32[]{:S(2)}) copy-start(s32[1,4]{1,0:T(1,128)} %param.20) | copy-start | bytes 52
  0.7 11.9 %copy-start.6 = (bf16[128,768]{1,0:T(8,128)(2,1)S(1)}, bf16[128,768]{1,0:T(8,128)(2,1)}, u32[]{:S(2)}) copy-start(bf16[128,768]{1,0:T(8,128)(2,1)} %param.19) | copy-start | bytes 589828
  0.7 12.0 %copy-start.1 = (bf16[128,768]{1,0:T(8,128)(2,1)S(1)}, bf16[128,768]{1,0:T(8,128)(2,1)}, u32[]{:S(2)}) copy-start(bf16[128,768]{1,0:T(8,128)(2,1)} %residual_ref.1) | copy-start | bytes 589828
  2.7 10.0 %collective-permute-start = (bf16[48,1280]{1,0:T(8,128)(2,1)}, bf16[48,1280]{1,0:T(8,128)(2,1)S(1)}, u32[]{:S(2)}, u32[]{:S(2)}) collective-permute-start(bf16[48,1280]{1,0:T(8,128)(2,1)} %get-tuple-element.83), channel_id=1, source_target_pairs={{0,2},{2,0},{4,6},{6,4},{8,10},{10,8},{12,14},{14,12},{16,18},{18,... | collective-permute-start | bytes 368648 | tf_op jit(solution)/shard_map/ppermute | solution.py:390
  5.7 7.7 %collective-permute-start.1 = (bf16[48,1280]{1,0:T(8,128)(2,1)}, bf16[48,1280]{1,0:T(8,128)(2,1)S(1)}, u32[]{:S(2)}, u32[]{:S(2)}) collective-permute-start(bf16[48,1280]{1,0:T(8,128)(2,1)} %get-tuple-element.84), channel_id=1, source_target_pairs={{0,4},{2,6},{4,0},{6,2},{8,12},{10,14},{12,8},{14,10},{16,20},{18,... | collective-permute-start | bytes 368648 | tf_op jit(solution)/shard_map/ppermute | solution.py:390
  7.2 6.2 %collective-permute-start.2 = (bf16[48,1280]{1,0:T(8,128)(2,1)}, bf16[48,1280]{1,0:T(8,128)(2,1)S(1)}, u32[]{:S(2)}, u32[]{:S(2)}) collective-permute-start(bf16[48,1280]{1,0:T(8,128)(2,1)} %get-tuple-element.85), channel_id=1, source_target_pairs={{0,6},{2,4},{4,2},{6,0},{8,14},{10,12},{12,10},{14,8},{16,22},{18,... | collective-permute-start | bytes 368648 | tf_op jit(solution)/shard_map/ppermute | solution.py:390
  7.2 7.2 %collective-permute-start.3 = (bf16[48,1280]{1,0:T(8,128)(2,1)}, bf16[48,1280]{1,0:T(8,128)(2,1)S(1)}, u32[]{:S(2)}, u32[]{:S(2)}) collective-permute-start(bf16[48,1280]{1,0:T(8,128)(2,1)} %get-tuple-element.82.refs_0_.own_ref), channel_id=1, source_target_pairs={{0,24},{2,26},{4,28},{6,30},{8,16},{10,18},{12,20},{14,22},{16,8},... | collective-permute-start | bytes 368648 | tf_op jit(solution)/shard_map/ppermute | solution.py:393
  13.4 0.9 copy-start.2
  14.4 12.1 %collective-permute-start.4 = (bf16[256,768]{1,0:T(8,128)(2,1)S(1)}, bf16[256,768]{1,0:T(8,128)(2,1)S(1)}, u32[]{:S(2)}, u32[]{:S(2)}) collective-permute-start(bf16[256,768]{1,0:T(8,128)(2,1)S(1)} %pad_maximum_fusion), channel_id=1, source_target_pairs={{0,2},{2,0},{4,6},{6,4},{8,10},{10,8},{12,14},{14,12},{16,18},{18,... | collective-permute-start | bytes 1179656 | tf_op jit(solution)/shard_map/ppermute | solution.py:390
  16.2 17.5 %collective-permute-start.5 = (bf16[256,768]{1,0:T(8,128)(2,1)S(1)}, bf16[256,768]{1,0:T(8,128)(2,1)S(1)}, u32[]{:S(2)}, u32[]{:S(2)}) collective-permute-start(bf16[256,768]{1,0:T(8,128)(2,1)S(1)} %pad_maximum_fusion), channel_id=1, source_target_pairs={{0,4},{2,6},{4,0},{6,2},{8,12},{10,14},{12,8},{14,10},{16,20},{18,... | collective-permute-start | bytes 1179656 | tf_op jit(solution)/shard_map/ppermute | solution.py:390
  17.7 16.1 %collective-permute-start.6 = (bf16[256,768]{1,0:T(8,128)(2,1)S(1)}, bf16[256,768]{1,0:T(8,128)(2,1)S(1)}, u32[]{:S(2)}, u32[]{:S(2)}) collective-permute-start(bf16[256,768]{1,0:T(8,128)(2,1)S(1)} %pad_maximum_fusion), channel_id=1, source_target_pairs={{0,6},{2,4},{4,2},{6,0},{8,14},{10,12},{12,10},{14,8},{16,22},{18,... | collective-permute-start | bytes 1179656 | tf_op jit(solution)/shard_map/ppermute | solution.py:390
  17.9 20.6 %collective-permute-start.8 = (bf16[192,1280]{1,0:T(8,128)(2,1)S(1)}, bf16[192,1280]{1,0:T(8,128)(2,1)S(1)}, u32[]{:S(2)}, u32[]{:S(2)}) collective-permute-start(bf16[192,1280]{1,0:T(8,128)(2,1)S(1)} %get-tuple-element.99.refs_9_), channel_id=1, source_target_pairs={{0,8},{2,10},{4,12},{6,14},{8,0},{10,2},{12,4},{14,6},{16,24},{18,... | collective-permute-start | bytes 1474568 | tf_op jit(solution)/shard_map/ppermute | solution.py:393
  19.8 18.8 %collective-permute-start.9 = (bf16[144,1280]{1,0:T(8,128)(2,1)S(1)}, bf16[144,1280]{1,0:T(8,128)(2,1)S(1)}, u32[]{:S(2)}, u32[]{:S(2)}) collective-permute-start(bf16[144,1280]{1,0:T(8,128)(2,1)S(1)} %get-tuple-element.100.others_ref), channel_id=1, source_target_pairs={{0,24},{2,26},{4,28},{6,30},{8,16},{10,18},{12,20},{14,22},{16,8},... | collective-permute-start | bytes 1105928 | tf_op jit(solution)/shard_map/ppermute | solution.py:393
  33.8 5.7 %copy-start.7 = (f32[768]{0:T(1024)S(1)}, f32[768]{0:T(1024)}, u32[]{:S(2)}) copy-start(f32[768]{0:T(1024)} %param.21) | copy-start | bytes 9220
  33.8 5.7 %copy-start.8 = (f32[768]{0:T(1024)S(1)}, f32[768]{0:T(1024)}, u32[]{:S(2)}) copy-start(f32[768]{0:T(1024)} %param.22) | copy-start | bytes 9220
  33.8 5.7 %copy-start.9 = (f32[768]{0:T(1024)S(1)}, f32[768]{0:T(1024)}, u32[]{:S(2)}) copy-start(f32[768]{0:T(1024)} %param.23) | copy-start | bytes 9220
  33.8 5.7 %copy-start.10 = (f32[768]{0:T(1024)S(1)}, f32[768]{0:T(1024)}, u32[]{:S(2)}) copy-start(f32[768]{0:T(1024)} %param.24) | copy-start | bytes 9220
  33.8 6.7 %collective-permute-start.7 = (bf16[1024,768]{1,0:T(8,128)(2,1)S(1)}, bf16[1024,768]{1,0:T(8,128)(2,1)}, u32[]{:S(2)}, u32[]{:S(2)}) collective-permute-start(bf16[1024,768]{1,0:T(8,128)(2,1)S(1)} %constant_dynamic-update-slice_fusion.own_ref), channel_id=1, source_target_pairs={{0,1},{1,0},{2,3},{3,2},{4,5},{5,4},{6,7},{7,6},{8,9},{9,8},{10,11... | collective-permute-start | bytes 4718600 | tf_op jit(solution)/shard_map/ppermute | solution.py:396
  39.5 9.9 %collective-permute-start.10 = (bf16[192,1280]{1,0:T(8,128)(2,1)}, bf16[192,1280]{1,0:T(8,128)(2,1)}, u32[]{:S(2)}, u32[]{:S(2)}) collective-permute-start(bf16[192,1280]{1,0:T(8,128)(2,1)} %shard_map.284), channel_id=1, source_target_pairs={{0,16},{2,18},{4,20},{6,22},{24,8},{26,10},{28,12},{30,14},{8,0},{... | collective-permute-start | bytes 1474568 | tf_op jit(solution)/shard_map/ppermute | solution.py:402
  40.4 9.0 %copy-start.3 = (f32[256,128]{1,0:T(8,128)S(1)}, f32[256,128]{1,0:T(8,128)}, u32[]{:S(2)}) copy-start(f32[256,128]{1,0:T(8,128)} %constant.40.clone.refs_6_) | copy-start | bytes 393220
  40.5 8.9 %copy-start.4 = (f32[256,128]{1,0:T(8,128)S(1)}, f32[256,128]{1,0:T(8,128)}, u32[]{:S(2)}) copy-start(f32[256,128]{1,0:T(8,128)} %constant.41.clone.refs_7_) | copy-start | bytes 393220
  40.5 8.9 %copy-start.5 = (f32[256,128]{1,0:T(8,128)S(1)}, f32[256,128]{1,0:T(8,128)}, u32[]{:S(2)}) copy-start(f32[256,128]{1,0:T(8,128)} %constant.42.clone.refs_8_) | copy-start | bytes 393220
  59.1 13.1 %collective-permute-start.11 = (bf16[192,1280]{1,0:T(8,128)(2,1)S(1)}, bf16[192,1280]{1,0:T(8,128)(2,1)S(1)}, u32[]{:S(2)}, u32[]{:S(2)}) collective-permute-start(bf16[192,1280]{1,0:T(8,128)(2,1)S(1)} %get-tuple-element.112), channel_id=1, source_target_pairs={{16,0},{18,2},{20,4},{22,6},{8,24},{10,26},{12,28},{14,30},{0,8},{... | collective-permute-start | bytes 1474568 | tf_op jit(solution)/shard_map/ppermute | solution.py:402
  65.8 9.6 %collective-permute-start.13 = (bf16[16,768]{1,0:T(8,128)(2,1)S(1)}, bf16[16,768]{1,0:T(8,128)(2,1)S(1)}, u32[]{:S(2)}, u32[]{:S(2)}) collective-permute-start(bf16[16,768]{1,0:T(8,128)(2,1)S(1)} %get-tuple-element.117.refs_0_), channel_id=1, source_target_pairs={{0,8},{2,10},{4,12},{6,14},{8,0},{10,2},{12,4},{14,6},{16,24},{18,... | collective-permute-start | bytes 73736 | tf_op jit(solution)/shard_map/ppermute | solution.py:393
  66.9 8.4 %collective-permute-start.14 = (bf16[16,768]{1,0:T(8,128)(2,1)S(1)}, bf16[16,768]{1,0:T(8,128)(2,1)S(1)}, u32[]{:S(2)}, u32[]{:S(2)}) collective-permute-start(bf16[16,768]{1,0:T(8,128)(2,1)S(1)} %get-tuple-element.117.refs_0_), channel_id=1, source_target_pairs={{0,16},{2,18},{4,20},{6,22},{8,24},{10,26},{12,28},{14,30},{16,0},... | collective-permute-start | bytes 73736 | tf_op jit(solution)/shard_map/ppermute | solution.py:393
  68.1 7.3 %collective-permute-start.15 = (bf16[16,768]{1,0:T(8,128)(2,1)S(1)}, bf16[16,768]{1,0:T(8,128)(2,1)S(1)}, u32[]{:S(2)}, u32[]{:S(2)}) collective-permute-start(bf16[16,768]{1,0:T(8,128)(2,1)S(1)} %get-tuple-element.117.refs_0_), channel_id=1, source_target_pairs={{0,24},{2,26},{4,28},{6,30},{8,16},{10,18},{12,20},{14,22},{16,8},... | collective-permute-start | bytes 73736 | tf_op jit(solution)/shard_map/ppermute | solution.py:393
  70.2 3.4 %collective-permute-start.12 = (bf16[1024,768]{1,0:T(8,128)(2,1)S(1)}, bf16[1024,768]{1,0:T(8,128)(2,1)S(1)}, u32[]{:S(2)}, u32[]{:S(2)}) collective-permute-start(bf16[1024,768]{1,0:T(8,128)(2,1)S(1)} %get-tuple-element.113), channel_id=1, source_target_pairs={{0,1},{1,0},{2,3},{3,2},{4,5},{5,4},{6,7},{7,6},{8,9},{9,8},{10,11... | collective-permute-start | bytes 4718600 | tf_op jit(solution)/shard_map/ppermute | solution.py:396
  73.6 22.9 %collective-permute-start.19 = (bf16[192,1280]{1,0:T(8,128)(2,1)S(1)}, bf16[192,1280]{1,0:T(8,128)(2,1)S(1)}, u32[]{:S(2)}, u32[]{:S(2)}) collective-permute-start(bf16[192,1280]{1,0:T(8,128)(2,1)S(1)} %get-tuple-element.122), channel_id=1, source_target_pairs={{0,8},{2,10},{4,12},{6,14},{8,0},{10,2},{12,4},{14,6},{16,24},{18,... | collective-permute-start | bytes 1474568 | tf_op jit(solution)/shard_map/ppermute | solution.py:393
  73.8 23.6 %collective-permute-start.20 = (bf16[192,1280]{1,0:T(8,128)(2,1)S(1)}, bf16[192,1280]{1,0:T(8,128)(2,1)S(1)}, u32[]{:S(2)}, u32[]{:S(2)}) collective-permute-start(bf16[192,1280]{1,0:T(8,128)(2,1)S(1)} %shard_map.287), channel_id=1, source_target_pairs={{0,24},{2,26},{4,28},{6,30},{8,16},{10,18},{12,20},{14,22},{16,8},... | collective-permute-start | bytes 1474568 | tf_op jit(solution)/shard_map/ppermute | solution.py:393
  75.3 4.0 %copy-start.11 = (f32[768]{0:T(1024)S(1)}, f32[768]{0:T(1024)}, u32[]{:S(2)}) copy-start(f32[768]{0:T(1024)} %param.28) | copy-start | bytes 9220
  75.4 4.0 %copy-start.12 = (f32[768]{0:T(1024)S(1)}, f32[768]{0:T(1024)}, u32[]{:S(2)}) copy-start(f32[768]{0:T(1024)} %param.32) | copy-start | bytes 9220
  75.8 12.6 %collective-permute-start.16 = (bf16[272,768]{1,0:T(8,128)(2,1)S(1)}, bf16[272,768]{1,0:T(8,128)(2,1)S(1)}, u32[]{:S(2)}, u32[]{:S(2)}) collective-permute-start(bf16[272,768]{1,0:T(8,128)(2,1)S(1)} %get-tuple-element.119), channel_id=1, source_target_pairs={{0,2},{2,0},{4,6},{6,4},{8,10},{10,8},{12,14},{14,12},{16,18},{18,... | collective-permute-start | bytes 1253384 | tf_op jit(solution)/shard_map/ppermute | solution.py:390
  76.8 19.8 %collective-permute-start.17 = (bf16[272,768]{1,0:T(8,128)(2,1)S(1)}, bf16[272,768]{1,0:T(8,128)(2,1)S(1)}, u32[]{:S(2)}, u32[]{:S(2)}) collective-permute-start(bf16[272,768]{1,0:T(8,128)(2,1)S(1)} %get-tuple-element.120), channel_id=1, source_target_pairs={{0,4},{2,6},{4,0},{6,2},{8,12},{10,14},{12,8},{14,10},{16,20},{18,... | collective-permute-start | bytes 1253384 | tf_op jit(solution)/shard_map/ppermute | solution.py:390
  78.3 18.3 %collective-permute-start.18 = (bf16[272,768]{1,0:T(8,128)(2,1)S(1)}, bf16[272,768]{1,0:T(8,128)(2,1)S(1)}, u32[]{:S(2)}, u32[]{:S(2)}) collective-permute-start(bf16[272,768]{1,0:T(8,128)(2,1)S(1)} %get-tuple-element.121), channel_id=1, source_target_pairs={{0,6},{2,4},{4,2},{6,0},{8,14},{10,12},{12,10},{14,8},{16,22},{18,... | collective-permute-start | bytes 1253384 | tf_op jit(solution)/shard_map/ppermute | solution.py:390
  97.7 6.1 %collective-permute-start.21 = (bf16[48,1280]{1,0:T(8,128)(2,1)S(1)}, bf16[48,1280]{1,0:T(8,128)(2,1)S(1)}, u32[]{:S(2)}, u32[]{:S(2)}) collective-permute-start(bf16[48,1280]{1,0:T(8,128)(2,1)S(1)} %get-tuple-element.134), channel_id=1, source_target_pairs={{0,2},{2,0},{4,6},{6,4},{8,10},{10,8},{12,14},{14,12},{16,18},{18,... | collective-permute-start | bytes 368648 | tf_op jit(solution)/shard_map/ppermute | solution.py:390
  98.9 7.3 %collective-permute-start.22 = (bf16[48,1280]{1,0:T(8,128)(2,1)S(1)}, bf16[48,1280]{1,0:T(8,128)(2,1)S(1)}, u32[]{:S(2)}, u32[]{:S(2)}) collective-permute-start(bf16[48,1280]{1,0:T(8,128)(2,1)S(1)} %get-tuple-element.135), channel_id=1, source_target_pairs={{0,4},{2,6},{4,0},{6,2},{8,12},{10,14},{12,8},{14,10},{16,20},{18,... | collective-permute-start | bytes 368648 | tf_op jit(solution)/shard_map/ppermute | solution.py:390
  100.1 6.1 %collective-permute-start.23 = (bf16[48,1280]{1,0:T(8,128)(2,1)S(1)}, bf16[48,1280]{1,0:T(8,128)(2,1)S(1)}, u32[]{:S(2)}, u32[]{:S(2)}) collective-permute-start(bf16[48,1280]{1,0:T(8,128)(2,1)S(1)} %get-tuple-element.136), channel_id=1, source_target_pairs={{0,6},{2,4},{4,2},{6,0},{8,14},{10,12},{12,10},{14,8},{16,22},{18,... | collective-permute-start | bytes 368648 | tf_op jit(solution)/shard_map/ppermute | solution.py:390
  102.5 1.2 %collective-permute-start.24 = (f32[16,768]{1,0:T(8,128)S(1)}, f32[16,768]{1,0:T(8,128)S(1)}, u32[]{:S(2)}, u32[]{:S(2)}) collective-permute-start(f32[16,768]{1,0:T(8,128)S(1)} %get-tuple-element.137.refs_4_), channel_id=1, source_target_pairs={{0,1},{1,0},{2,3},{3,2},{4,5},{5,4},{6,7},{7,6},{8,9},{9,8},{10,11... | collective-permute-start | bytes 147464 | tf_op jit(solution)/shard_map/ppermute | solution.py:396

commit v7 on v6

--- a/solution.py
+++ b/solution.py
@@ -479,11 +479,12 @@
     )
     from_peer = to_peer(send)
     if direct:
-        notes = [notes] + [to_level(notes, m) for m in range(1, levels)]
+        notes = (notes.astype(F32) + to_level(notes, 1).astype(F32)).astype(BF16)
+        notes = [notes, to_level(notes, 2)]
         relayed = kernel_call(
             relay_kernel, [shape((PLANE * owned, columns), BF16)], (messages[3], passed), micros=20
         )[0]
-        relayed, from_peer, messages = lax.optimization_barrier((relayed, from_peer, messages))
+        relayed, keep, messages = lax.optimization_barrier((relayed, keep, messages))
     else:
         notes = lax.all_gather(notes, "dp", axis=0, axis_index_groups=level_groups)
         notes = [jnp.sum(notes.astype(F32), axis=0)]

time: 108 us -> 107 us (level)
    ppermute x8 -> x7, waiting for transfers between devices: 5.61 us -> 27.1 us  [to_level(): return lax.ppermute(x, 'dp', [(j, j ^ m * PLANE) for j in range(places)])]
    ppermute x12, waiting for transfers between devices: 31.1 us -> 12.6 us  [to_plane(): return lax.ppermute(x, 'dp', [(j, j ^ k) for j in range(places)])]
    ppermute x2, waiting for transfers between devices: 7.48 us -> 5.45 us  [to_pass(): lax.ppermute(x, 'dp', [(a * PLANE + j, b * PLANE + j) for a, b in pairs f...]
    ppermute x3, waiting for transfers between devices: 2.43 us -> 1.23 us  [to_peer(): return lax.ppermute(x, 'tensor', [(0, 1), (1, 0)])]
    ppermute x8 -> x7, starting transfers between devices: 15.2 us -> 14.7 us  [to_level(): return lax.ppermute(x, 'dp', [(j, j ^ m * PLANE) for j in range(places)])]
  transfers between devices with their start and end apart: 25 -> 24, of which waited for: 13 -> 11; matrix products, arithmetic and copies ran while one was open for 2% -> 2% of each run, Pallas kernels for 9% -> 9%
where the time goes in v7:
time: 107 us
  waiting for transfers between devices  46.3 us (43%)
  starting transfers between devices  32.8 us (31%)
  Pallas kernels  22.9 us (21%)
  local copies, waits for them, and re-layouts  1.95 us (2%)
  other arithmetic  1.41 us (1%)
  between operations  1.18 us (1%)
    ppermute x7, waiting for transfers between devices, to_level(): return lax.ppermute(x, 'dp', [(j, j ^ m * PLANE) for j in range(places)])  27.1 us
    pallas_call x11, Pallas kernels, kernel_call(): pl.pallas_call(body, out_shape=out_shapes, in_specs=[taken] * len(operand...  22.9 us
    ppermute x12, starting transfers between devices, to_plane(): return lax.ppermute(x, 'dp', [(j, j ^ k) for j in range(places)])  15.2 us
    ppermute x7, starting transfers between devices, to_level(): return lax.ppermute(x, 'dp', [(j, j ^ m * PLANE) for j in range(places)])  14.7 us
    ppermute x12, waiting for transfers between devices, to_plane(): return lax.ppermute(x, 'dp', [(j, j ^ k) for j in range(places)])  12.6 us
    ppermute x2, waiting for transfers between devices, to_pass(): lax.ppermute(x, 'dp', [(a * PLANE + j, b * PLANE + j) for a, b in pairs f...  5.45 us
    ppermute x2, starting transfers between devices, to_pass(): lax.ppermute(x, 'dp', [(a * PLANE + j, b * PLANE + j) for a, b in pairs f...  2.87 us
  transfers between devices with their start and end apart: 24, of which 11 were waited for; matrix products, arithmetic and copies ran while one was open for 2% of the time, Pallas kernels for 9%

profile of v7, /device:TPU:0, one launch (start us, length us, event | category | flops | bytes accessed | tf_op | source)
XLA Modules:
  0.0 106.6 jit_solution(12084060452642596012)
XLA Ops:
  0.7 2.0 %shard_map.281 = (bf16[48,1280]{1,0:T(8,128)(2,1)}, bf16[48,1280]{1,0:T(8,128)(2,1)}, bf16[48,1280]{1,0:T(8,128)(2,1)}, bf16[48,1280]{1,0:T(8,128)(2,1)}) custom-call(bf16[3,48,384]{2,1,0:T(8,128)(2,1)} %refs_0_.1, bf16[48,384]{1,0:T(8,128)(2,1)} %bitcast.19, bf16[48,1536]{1,0:T(8,128)(2,1)} %refs_2_.1, bf16[48,1536]{1,0:T(8,128)(2,1)} %bitcast.18), custom_call_target="tpu_custom_call" | custom-call | flops 1000000000 | bytes 1 | tf_op jit(solution)/shard_map/pallas_call | solution.py:347
  2.7 3.0 %collective-permute-start = (bf16[48,1280]{1,0:T(8,128)(2,1)}, bf16[48,1280]{1,0:T(8,128)(2,1)S(1)}, u32[]{:S(2)}, u32[]{:S(2)}) collective-permute-start(bf16[48,1280]{1,0:T(8,128)(2,1)} %get-tuple-element.83), channel_id=1, source_target_pairs={{0,2},{2,0},{4,6},{6,4},{8,10},{10,8},{12,14},{14,12},{16,18},{18,... | collective-permute-start | bytes 368648 | tf_op jit(solution)/shard_map/ppermute | solution.py:390
  5.7 1.5 %collective-permute-start.1 = (bf16[48,1280]{1,0:T(8,128)(2,1)}, bf16[48,1280]{1,0:T(8,128)(2,1)S(1)}, u32[]{:S(2)}, u32[]{:S(2)}) collective-permute-start(bf16[48,1280]{1,0:T(8,128)(2,1)} %get-tuple-element.84), channel_id=1, source_target_pairs={{0,4},{2,6},{4,0},{6,2},{8,12},{10,14},{12,8},{14,10},{16,20},{18,... | collective-permute-start | bytes 368648 | tf_op jit(solution)/shard_map/ppermute | solution.py:390
  7.2 4.1 %collective-permute-start.3 = (bf16[48,1280]{1,0:T(8,128)(2,1)}, bf16[48,1280]{1,0:T(8,128)(2,1)S(1)}, u32[]{:S(2)}, u32[]{:S(2)}) collective-permute-start(bf16[48,1280]{1,0:T(8,128)(2,1)} %get-tuple-element.82.refs_0_.own_ref), channel_id=1, source_target_pairs={{0,24},{2,26},{4,28},{6,30},{8,16},{10,18},{12,20},{14,22},{16,8},... | collective-permute-start | bytes 368648 | tf_op jit(solution)/shard_map/ppermute | solution.py:393
  11.3 0.6 reduce_sum.9
  11.9 0.7 add_compare_fusion
  12.6 0.1 broadcast_select_fusion
  12.7 0.7 collective-permute-done.1.refs_2_
  13.4 0.9 copy-done.2
  14.3 0.1 shard_map.282
  14.4 0.0 collective-permute-done.3.own_far_ref.refs_12_
  14.4 1.8 %collective-permute-start.4 = (bf16[256,768]{1,0:T(8,128)(2,1)S(1)}, bf16[256,768]{1,0:T(8,128)(2,1)S(1)}, u32[]{:S(2)}, u32[]{:S(2)}) collective-permute-start(bf16[256,768]{1,0:T(8,128)(2,1)S(1)} %pad_maximum_fusion), channel_id=1, source_target_pairs={{0,2},{2,0},{4,6},{6,4},{8,10},{10,8},{12,14},{14,12},{16,18},{18,... | collective-permute-start | bytes 1179656 | tf_op jit(solution)/shard_map/ppermute | solution.py:390
  16.2 1.5 %collective-permute-start.5 = (bf16[256,768]{1,0:T(8,128)(2,1)S(1)}, bf16[256,768]{1,0:T(8,128)(2,1)S(1)}, u32[]{:S(2)}, u32[]{:S(2)}) collective-permute-start(bf16[256,768]{1,0:T(8,128)(2,1)S(1)} %pad_maximum_fusion), channel_id=1, source_target_pairs={{0,4},{2,6},{4,0},{6,2},{8,12},{10,14},{12,8},{14,10},{16,20},{18,... | collective-permute-start | bytes 1179656 | tf_op jit(solution)/shard_map/ppermute | solution.py:390
  17.7 0.2 collective-permute-start.6
  17.9 1.9 %collective-permute-start.8 = (bf16[192,1280]{1,0:T(8,128)(2,1)S(1)}, bf16[192,1280]{1,0:T(8,128)(2,1)S(1)}, u32[]{:S(2)}, u32[]{:S(2)}) collective-permute-start(bf16[192,1280]{1,0:T(8,128)(2,1)S(1)} %get-tuple-element.98.refs_9_), channel_id=1, source_target_pairs={{0,8},{2,10},{4,12},{6,14},{8,0},{10,2},{12,4},{14,6},{16,24},{18,... | collective-permute-start | bytes 1474568 | tf_op jit(solution)/shard_map/ppermute | solution.py:393
  19.8 3.1 %collective-permute-start.9 = (bf16[144,1280]{1,0:T(8,128)(2,1)S(1)}, bf16[144,1280]{1,0:T(8,128)(2,1)S(1)}, u32[]{:S(2)}, u32[]{:S(2)}) collective-permute-start(bf16[144,1280]{1,0:T(8,128)(2,1)S(1)} %get-tuple-element.99.others_ref), channel_id=1, source_target_pairs={{0,24},{2,26},{4,28},{6,30},{8,16},{10,18},{12,20},{14,22},{16,8},... | collective-permute-start | bytes 1105928 | tf_op jit(solution)/shard_map/ppermute | solution.py:393
  22.9 3.6 %collective-permute-done.4 = bf16[256,768]{1,0:T(8,128)(2,1)S(1)} collective-permute-done((bf16[256,768]{1,0:T(8,128)(2,1)S(1)}, bf16[256,768]{1,0:T(8,128)(2,1)S(1)}, u32[]{:S(2)}, u32[]{:S(2)}) %collective-permute-start.4) | collective-permute-done | bytes 393248 | tf_op jit(solution)/shard_map/ppermute | solution.py:390
  26.5 7.2 %collective-permute-done.5 = bf16[256,768]{1,0:T(8,128)(2,1)S(1)} collective-permute-done((bf16[256,768]{1,0:T(8,128)(2,1)S(1)}, bf16[256,768]{1,0:T(8,128)(2,1)S(1)}, u32[]{:S(2)}, u32[]{:S(2)}) %collective-permute-start.5) | collective-permute-done | bytes 393248 | tf_op jit(solution)/shard_map/ppermute | solution.py:390
  33.8 0.1 collective-permute-start.7
  33.9 4.7 %collective-permute-done.9.far_ref.refs_13_ = bf16[144,1280]{1,0:T(8,128)(2,1)S(1)} collective-permute-done((bf16[144,1280]{1,0:T(8,128)(2,1)S(1)}, bf16[144,1280]{1,0:T(8,128)(2,1)S(1)}, u32[]{:S(2)}, u32[]{:S(2)}) %collective-permute-start.9) | collective-permute-done | bytes 368672 | tf_op jit(solution)/shard_map/ppermute | solution.py:393
  38.6 0.9 shard_map.284
  39.6 0.8 dynamic_slice.7
  40.5 3.5 %shard_map.283 = (bf16[1024,768]{1,0:T(8,128)(2,1)S(1)}, bf16[1024,768]{1,0:T(8,128)(2,1)S(1)}, bf16[1024,768]{1,0:T(8,128)(2,1)S(1)}, bf16[1024,768]{1,0:T(8,12...) custom-call(f32[8,768]{1,0:T(8,128)S(1)} %stack.23.params_ref, ...), custom_call_target="tpu_custom_call" | custom-call | flops 1000000000 | bytes 1 | tf_op jit(solution)/shard_map/pallas_call | solution.py:347
  44.0 5.4 %collective-permute-done.10.refs_11_ = bf16[192,1280]{1,0:T(8,128)(2,1)} collective-permute-done((bf16[192,1280]{1,0:T(8,128)(2,1)}, bf16[192,1280]{1,0:T(8,128)(2,1)}, u32[]{:S(2)}, u32[]{:S(2)}) %collective-permute-start.10) | collective-permute-done | bytes 491552 | tf_op jit(solution)/shard_map/ppermute | solution.py:402
  49.4 9.7 %shard_map.285 = (bf16[1024,512]{1,0:T(8,128)(2,1)S(1)}, bf16[1024,384]{1,0:T(8,128)(2,1)S(1)}, bf16[1024,384]{1,0:T(8,128)(2,1)S(1)}, bf16[768,1280]{1,0:T(8,12...) custom-call(f32[8,128]{1,0:T(8,128)S(1)} %get-tuple-element.94.refs_, ...), custom_call_target="tpu_custom_call" | custom-call | flops 12000000000 | bytes 1 | tf_op jit(solution)/shard_map/pallas_call | solution.py:347
  59.1 2.9 %collective-permute-start.11 = (bf16[192,1280]{1,0:T(8,128)(2,1)S(1)}, bf16[192,1280]{1,0:T(8,128)(2,1)S(1)}, u32[]{:S(2)}, u32[]{:S(2)}) collective-permute-start(bf16[192,1280]{1,0:T(8,128)(2,1)S(1)} %get-tuple-element.104), channel_id=1, source_target_pairs={{16,0},{18,2},{20,4},{22,6},{8,24},{10,26},{12,28},{14,30},{0,8},{... | collective-permute-start | bytes 1474568 | tf_op jit(solution)/shard_map/ppermute | solution.py:402
  62.0 3.8 %shard_map.287 = (bf16[1024,768]{1,0:T(8,128)(2,1)S(1)}, bf16[1024,768]{1,0:T(8,128)(2,1)S(1)}, bf16[16,768]{1,0:T(8,128)(2,1)S(1)}) custom-call(f32[8,768]{1,0:T(8,128)S(1)} %stack.23.params_ref, bf16[1024,768]{1,0:T(8,128)(2,1)S(1)} %get-tuple-element.105.xh_ref, bf16[768,1280]{1,0:T(8,128)(2,1)S(1)} %get-tuple-element.106.w_ref, ...), custom_call_target="tpu_custom_call" | custom-call | flops 4000000000 | bytes 1 | tf_op jit(solution)/shard_map/pallas_call | solution.py:347
  65.8 1.2 %collective-permute-start.13 = (bf16[16,768]{1,0:T(8,128)(2,1)S(1)}, bf16[16,768]{1,0:T(8,128)(2,1)S(1)}, u32[]{:S(2)}, u32[]{:S(2)}) collective-permute-start(bf16[16,768]{1,0:T(8,128)(2,1)S(1)} %get-tuple-element.117), channel_id=1, source_target_pairs={{0,8},{2,10},{4,12},{6,14},{8,0},{10,2},{12,4},{14,6},{16,24},{18,... | collective-permute-start | bytes 73736 | tf_op jit(solution)/shard_map/ppermute | solution.py:393
  67.0 4.7 %collective-permute-done.13 = bf16[16,768]{1,0:T(8,128)(2,1)S(1)} collective-permute-done((bf16[16,768]{1,0:T(8,128)(2,1)S(1)}, bf16[16,768]{1,0:T(8,128)(2,1)S(1)}, u32[]{:S(2)}, u32[]{:S(2)}) %collective-permute-start.13) | collective-permute-done | bytes 24608 | tf_op jit(solution)/shard_map/ppermute | solution.py:393
  71.6 1.8 %collective-permute-start.14 = (bf16[16,768]{1,0:T(8,128)(2,1)S(1)}, bf16[16,768]{1,0:T(8,128)(2,1)S(1)}, u32[]{:S(2)}, u32[]{:S(2)}) collective-permute-start(bf16[16,768]{1,0:T(8,128)(2,1)S(1)} %add_convert_fusion.refs_0_), channel_id=1, source_target_pairs={{0,16},{2,18},{4,20},{6,22},{8,24},{10,26},{12,28},{14,30},{16,0},... | collective-permute-start | bytes 73736 | tf_op jit(solution)/shard_map/ppermute | solution.py:393
  73.4 0.2 shard_map.286
  73.6 0.9 collective-permute-start.18
  74.5 1.9 %collective-permute-start.19 = (bf16[192,1280]{1,0:T(8,128)(2,1)S(1)}, bf16[192,1280]{1,0:T(8,128)(2,1)S(1)}, u32[]{:S(2)}, u32[]{:S(2)}) collective-permute-start(bf16[192,1280]{1,0:T(8,128)(2,1)S(1)} %shard_map.286), channel_id=1, source_target_pairs={{0,24},{2,26},{4,28},{6,30},{8,16},{10,18},{12,20},{14,22},{16,8},... | collective-permute-start | bytes 1474568 | tf_op jit(solution)/shard_map/ppermute | solution.py:393
  76.3 0.2 collective-permute-done.14.refs_1_
  76.5 0.4 shard_map.288
  76.9 0.2 collective-permute-start.15
  77.1 0.9 collective-permute-start.16
  78.0 2.5 %collective-permute-start.17 = (bf16[272,768]{1,0:T(8,128)(2,1)S(1)}, bf16[272,768]{1,0:T(8,128)(2,1)S(1)}, u32[]{:S(2)}, u32[]{:S(2)}) collective-permute-start(bf16[272,768]{1,0:T(8,128)(2,1)S(1)} %get-tuple-element.121), channel_id=1, source_target_pairs={{0,6},{2,4},{4,2},{6,0},{8,14},{10,12},{12,10},{14,8},{16,22},{18,... | collective-permute-start | bytes 1253384 | tf_op jit(solution)/shard_map/ppermute | solution.py:390
  80.5 5.7 %collective-permute-done.18.near_ref = bf16[192,1280]{1,0:T(8,128)(2,1)S(1)} collective-permute-done((bf16[192,1280]{1,0:T(8,128)(2,1)S(1)}, bf16[192,1280]{1,0:T(8,128)(2,1)S(1)}, u32[]{:S(2)}, u32[]{:S(2)}) %collective-permute-start.18) | collective-permute-done | bytes 491552 | tf_op jit(solution)/shard_map/ppermute | solution.py:393
  86.1 11.8 %collective-permute-done.19.far_ref = bf16[192,1280]{1,0:T(8,128)(2,1)S(1)} collective-permute-done((bf16[192,1280]{1,0:T(8,128)(2,1)S(1)}, bf16[192,1280]{1,0:T(8,128)(2,1)S(1)}, u32[]{:S(2)}, u32[]{:S(2)}) %collective-permute-start.19) | collective-permute-done | bytes 491552 | tf_op jit(solution)/shard_map/ppermute | solution.py:393
  98.0 0.3 shard_map.290
  98.3 0.3 collective-permute-start.20
  98.6 1.0 collective-permute-start.21
  99.6 2.3 %collective-permute-start.22 = (bf16[48,1280]{1,0:T(8,128)(2,1)S(1)}, bf16[48,1280]{1,0:T(8,128)(2,1)S(1)}, u32[]{:S(2)}, u32[]{:S(2)}) collective-permute-start(bf16[48,1280]{1,0:T(8,128)(2,1)S(1)} %get-tuple-element.136), channel_id=1, source_target_pairs={{0,6},{2,4},{4,2},{6,0},{8,14},{10,12},{12,10},{14,8},{16,22},{18,... | collective-permute-start | bytes 368648 | tf_op jit(solution)/shard_map/ppermute | solution.py:390
  101.8 1.2 %shard_map.289 = (bf16[128,768]{1,0:T(8,128)(2,1)}, f32[128,768]{1,0:T(8,128)}, f32[16,768]{1,0:T(8,128)S(1)}) custom-call(bf16[128,768]{1,0:T(8,128)(2,1)S(1)} %copy-done.1, bf16[128,768]{1,0:T(8,128)(2,1)S(1)} %get-tuple-element.93.g_ref, f32[1,768]{1,0:T(1,128)S(1)} %reshape.66.b_out_ref, f32[1,768]{1,0:T(1,128)S(1)} %reshape.67.b_down_ref, ...), custom_call_target="tpu_custom_call" | custom-call | flops 1000000000 | bytes 1 | tf_op jit(solution)/shard_map/pallas_call | solution.py:347
  103.0 1.2 %collective-permute-done.23.refs_5_ = f32[16,768]{1,0:T(8,128)S(1)} collective-permute-done((f32[16,768]{1,0:T(8,128)S(1)}, f32[16,768]{1,0:T(8,128)S(1)}, u32[]{:S(2)}, u32[]{:S(2)}) %collective-permute-start.23) | collective-permute-done | bytes 49184 | tf_op jit(solution)/shard_map/ppermute | solution.py:396
  104.3 1.1 %collective-permute-done.22.refs_3_ = bf16[48,1280]{1,0:T(8,128)(2,1)S(1)} collective-permute-done((bf16[48,1280]{1,0:T(8,128)(2,1)S(1)}, bf16[48,1280]{1,0:T(8,128)(2,1)S(1)}, u32[]{:S(2)}, u32[]{:S(2)}) %collective-permute-start.22) | collective-permute-done | bytes 122912 | tf_op jit(solution)/shard_map/ppermute | solution.py:390
  105.4 1.0 shard_map.291
  (60 shorter events, 0.4 us)
Async XLA Ops:
  0.6 38.9 %copy-start = (f32[3,384]{1,0:T(4,128)S(1)}, f32[3,384]{1,0:T(4,128)}, u32[]{:S(2)}) copy-start(f32[3,384]{1,0:T(4,128)} %param.26) | copy-start | bytes 13828
  0.7 10.6 %copy-start.13 = (s32[1,4]{1,0:T(1,128)S(1)}, s32[1,4]{1,0:T(1,128)}, u32[]{:S(2)}) copy-start(s32[1,4]{1,0:T(1,128)} %param.20) | copy-start | bytes 52
  0.7 11.9 %copy-start.6 = (bf16[128,768]{1,0:T(8,128)(2,1)S(1)}, bf16[128,768]{1,0:T(8,128)(2,1)}, u32[]{:S(2)}) copy-start(bf16[128,768]{1,0:T(8,128)(2,1)} %param.19) | copy-start | bytes 589828
  0.7 12.0 %copy-start.1 = (bf16[128,768]{1,0:T(8,128)(2,1)S(1)}, bf16[128,768]{1,0:T(8,128)(2,1)}, u32[]{:S(2)}) copy-start(bf16[128,768]{1,0:T(8,128)(2,1)} %residual_ref.1) | copy-start | bytes 589828
  2.7 10.0 %collective-permute-start = (bf16[48,1280]{1,0:T(8,128)(2,1)}, bf16[48,1280]{1,0:T(8,128)(2,1)S(1)}, u32[]{:S(2)}, u32[]{:S(2)}) collective-permute-start(bf16[48,1280]{1,0:T(8,128)(2,1)} %get-tuple-element.83), channel_id=1, source_target_pairs={{0,2},{2,0},{4,6},{6,4},{8,10},{10,8},{12,14},{14,12},{16,18},{18,... | collective-permute-start | bytes 368648 | tf_op jit(solution)/shard_map/ppermute | solution.py:390
  5.7 7.7 %collective-permute-start.1 = (bf16[48,1280]{1,0:T(8,128)(2,1)}, bf16[48,1280]{1,0:T(8,128)(2,1)S(1)}, u32[]{:S(2)}, u32[]{:S(2)}) collective-permute-start(bf16[48,1280]{1,0:T(8,128)(2,1)} %get-tuple-element.84), channel_id=1, source_target_pairs={{0,4},{2,6},{4,0},{6,2},{8,12},{10,14},{12,8},{14,10},{16,20},{18,... | collective-permute-start | bytes 368648 | tf_op jit(solution)/shard_map/ppermute | solution.py:390
  7.2 6.2 %collective-permute-start.2 = (bf16[48,1280]{1,0:T(8,128)(2,1)}, bf16[48,1280]{1,0:T(8,128)(2,1)S(1)}, u32[]{:S(2)}, u32[]{:S(2)}) collective-permute-start(bf16[48,1280]{1,0:T(8,128)(2,1)} %get-tuple-element.85), channel_id=1, source_target_pairs={{0,6},{2,4},{4,2},{6,0},{8,14},{10,12},{12,10},{14,8},{16,22},{18,... | collective-permute-start | bytes 368648 | tf_op jit(solution)/shard_map/ppermute | solution.py:390
  7.2 7.2 %collective-permute-start.3 = (bf16[48,1280]{1,0:T(8,128)(2,1)}, bf16[48,1280]{1,0:T(8,128)(2,1)S(1)}, u32[]{:S(2)}, u32[]{:S(2)}) collective-permute-start(bf16[48,1280]{1,0:T(8,128)(2,1)} %get-tuple-element.82.refs_0_.own_ref), channel_id=1, source_target_pairs={{0,24},{2,26},{4,28},{6,30},{8,16},{10,18},{12,20},{14,22},{16,8},... | collective-permute-start | bytes 368648 | tf_op jit(solution)/shard_map/ppermute | solution.py:393
  13.4 0.9 copy-start.2
  14.4 12.1 %collective-permute-start.4 = (bf16[256,768]{1,0:T(8,128)(2,1)S(1)}, bf16[256,768]{1,0:T(8,128)(2,1)S(1)}, u32[]{:S(2)}, u32[]{:S(2)}) collective-permute-start(bf16[256,768]{1,0:T(8,128)(2,1)S(1)} %pad_maximum_fusion), channel_id=1, source_target_pairs={{0,2},{2,0},{4,6},{6,4},{8,10},{10,8},{12,14},{14,12},{16,18},{18,... | collective-permute-start | bytes 1179656 | tf_op jit(solution)/shard_map/ppermute | solution.py:390
  16.2 17.5 %collective-permute-start.5 = (bf16[256,768]{1,0:T(8,128)(2,1)S(1)}, bf16[256,768]{1,0:T(8,128)(2,1)S(1)}, u32[]{:S(2)}, u32[]{:S(2)}) collective-permute-start(bf16[256,768]{1,0:T(8,128)(2,1)S(1)} %pad_maximum_fusion), channel_id=1, source_target_pairs={{0,4},{2,6},{4,0},{6,2},{8,12},{10,14},{12,8},{14,10},{16,20},{18,... | collective-permute-start | bytes 1179656 | tf_op jit(solution)/shard_map/ppermute | solution.py:390
  17.7 16.1 %collective-permute-start.6 = (bf16[256,768]{1,0:T(8,128)(2,1)S(1)}, bf16[256,768]{1,0:T(8,128)(2,1)S(1)}, u32[]{:S(2)}, u32[]{:S(2)}) collective-permute-start(bf16[256,768]{1,0:T(8,128)(2,1)S(1)} %pad_maximum_fusion), channel_id=1, source_target_pairs={{0,6},{2,4},{4,2},{6,0},{8,14},{10,12},{12,10},{14,8},{16,22},{18,... | collective-permute-start | bytes 1179656 | tf_op jit(solution)/shard_map/ppermute | solution.py:390
  17.9 20.6 %collective-permute-start.8 = (bf16[192,1280]{1,0:T(8,128)(2,1)S(1)}, bf16[192,1280]{1,0:T(8,128)(2,1)S(1)}, u32[]{:S(2)}, u32[]{:S(2)}) collective-permute-start(bf16[192,1280]{1,0:T(8,128)(2,1)S(1)} %get-tuple-element.98.refs_9_), channel_id=1, source_target_pairs={{0,8},{2,10},{4,12},{6,14},{8,0},{10,2},{12,4},{14,6},{16,24},{18,... | collective-permute-start | bytes 1474568 | tf_op jit(solution)/shard_map/ppermute | solution.py:393
  19.8 18.8 %collective-permute-start.9 = (bf16[144,1280]{1,0:T(8,128)(2,1)S(1)}, bf16[144,1280]{1,0:T(8,128)(2,1)S(1)}, u32[]{:S(2)}, u32[]{:S(2)}) collective-permute-start(bf16[144,1280]{1,0:T(8,128)(2,1)S(1)} %get-tuple-element.99.others_ref), channel_id=1, source_target_pairs={{0,24},{2,26},{4,28},{6,30},{8,16},{10,18},{12,20},{14,22},{16,8},... | collective-permute-start | bytes 1105928 | tf_op jit(solution)/shard_map/ppermute | solution.py:393
  33.8 5.7 %copy-start.7 = (f32[768]{0:T(1024)S(1)}, f32[768]{0:T(1024)}, u32[]{:S(2)}) copy-start(f32[768]{0:T(1024)} %param.21) | copy-start | bytes 9220
  33.8 5.7 %copy-start.8 = (f32[768]{0:T(1024)S(1)}, f32[768]{0:T(1024)}, u32[]{:S(2)}) copy-start(f32[768]{0:T(1024)} %param.22) | copy-start | bytes 9220
  33.8 5.7 %copy-start.9 = (f32[768]{0:T(1024)S(1)}, f32[768]{0:T(1024)}, u32[]{:S(2)}) copy-start(f32[768]{0:T(1024)} %param.23) | copy-start | bytes 9220
  33.8 5.7 %copy-start.10 = (f32[768]{0:T(1024)S(1)}, f32[768]{0:T(1024)}, u32[]{:S(2)}) copy-start(f32[768]{0:T(1024)} %param.24) | copy-start | bytes 9220
  33.8 6.7 %collective-permute-start.7 = (bf16[1024,768]{1,0:T(8,128)(2,1)S(1)}, bf16[1024,768]{1,0:T(8,128)(2,1)}, u32[]{:S(2)}, u32[]{:S(2)}) collective-permute-start(bf16[1024,768]{1,0:T(8,128)(2,1)S(1)} %constant_dynamic-update-slice_fusion.own_ref), channel_id=1, source_target_pairs={{0,1},{1,0},{2,3},{3,2},{4,5},{5,4},{6,7},{7,6},{8,9},{9,8},{10,11... | collective-permute-start | bytes 4718600 | tf_op jit(solution)/shard_map/ppermute | solution.py:396
  39.5 9.9 %collective-permute-start.10 = (bf16[192,1280]{1,0:T(8,128)(2,1)}, bf16[192,1280]{1,0:T(8,128)(2,1)}, u32[]{:S(2)}, u32[]{:S(2)}) collective-permute-start(bf16[192,1280]{1,0:T(8,128)(2,1)} %shard_map.284), channel_id=1, source_target_pairs={{0,16},{2,18},{4,20},{6,22},{24,8},{26,10},{28,12},{30,14},{8,0},{... | collective-permute-start | bytes 1474568 | tf_op jit(solution)/shard_map/ppermute | solution.py:402
  40.4 9.0 %copy-start.3 = (f32[256,128]{1,0:T(8,128)S(1)}, f32[256,128]{1,0:T(8,128)}, u32[]{:S(2)}) copy-start(f32[256,128]{1,0:T(8,128)} %constant.40.clone.refs_6_) | copy-start | bytes 393220
  40.5 8.9 %copy-start.4 = (f32[256,128]{1,0:T(8,128)S(1)}, f32[256,128]{1,0:T(8,128)}, u32[]{:S(2)}) copy-start(f32[256,128]{1,0:T(8,128)} %constant.41.clone.refs_7_) | copy-start | bytes 393220
  40.5 8.9 %copy-start.5 = (f32[256,128]{1,0:T(8,128)S(1)}, f32[256,128]{1,0:T(8,128)}, u32[]{:S(2)}) copy-start(f32[256,128]{1,0:T(8,128)} %constant.42.clone.refs_8_) | copy-start | bytes 393220
  59.1 14.3 %collective-permute-start.11 = (bf16[192,1280]{1,0:T(8,128)(2,1)S(1)}, bf16[192,1280]{1,0:T(8,128)(2,1)S(1)}, u32[]{:S(2)}, u32[]{:S(2)}) collective-permute-start(bf16[192,1280]{1,0:T(8,128)(2,1)S(1)} %get-tuple-element.104), channel_id=1, source_target_pairs={{16,0},{18,2},{20,4},{22,6},{8,24},{10,26},{12,28},{14,30},{0,8},{... | collective-permute-start | bytes 1474568 | tf_op jit(solution)/shard_map/ppermute | solution.py:402
  65.8 5.9 %collective-permute-start.13 = (bf16[16,768]{1,0:T(8,128)(2,1)S(1)}, bf16[16,768]{1,0:T(8,128)(2,1)S(1)}, u32[]{:S(2)}, u32[]{:S(2)}) collective-permute-start(bf16[16,768]{1,0:T(8,128)(2,1)S(1)} %get-tuple-element.117), channel_id=1, source_target_pairs={{0,8},{2,10},{4,12},{6,14},{8,0},{10,2},{12,4},{14,6},{16,24},{18,... | collective-permute-start | bytes 73736 | tf_op jit(solution)/shard_map/ppermute | solution.py:393
  66.9 9.6 %collective-permute-start.12 = (bf16[1024,768]{1,0:T(8,128)(2,1)S(1)}, bf16[1024,768]{1,0:T(8,128)(2,1)S(1)}, u32[]{:S(2)}, u32[]{:S(2)}) collective-permute-start(bf16[1024,768]{1,0:T(8,128)(2,1)S(1)} %get-tuple-element.116), channel_id=1, source_target_pairs={{0,1},{1,0},{2,3},{3,2},{4,5},{5,4},{6,7},{7,6},{8,9},{9,8},{10,11... | collective-permute-start | bytes 4718600 | tf_op jit(solution)/shard_map/ppermute | solution.py:396
  71.6 4.9 %collective-permute-start.14 = (bf16[16,768]{1,0:T(8,128)(2,1)S(1)}, bf16[16,768]{1,0:T(8,128)(2,1)S(1)}, u32[]{:S(2)}, u32[]{:S(2)}) collective-permute-start(bf16[16,768]{1,0:T(8,128)(2,1)S(1)} %add_convert_fusion.refs_0_), channel_id=1, source_target_pairs={{0,16},{2,18},{4,20},{6,22},{8,24},{10,26},{12,28},{14,30},{16,0},... | collective-permute-start | bytes 73736 | tf_op jit(solution)/shard_map/ppermute | solution.py:393
  73.6 6.9 %copy-start.11 = (f32[768]{0:T(1024)S(1)}, f32[768]{0:T(1024)}, u32[]{:S(2)}) copy-start(f32[768]{0:T(1024)} %param.28) | copy-start | bytes 9220
  73.6 6.8 %copy-start.12 = (f32[768]{0:T(1024)S(1)}, f32[768]{0:T(1024)}, u32[]{:S(2)}) copy-start(f32[768]{0:T(1024)} %param.32) | copy-start | bytes 9220
  73.6 12.5 %collective-permute-start.18 = (bf16[192,1280]{1,0:T(8,128)(2,1)S(1)}, bf16[192,1280]{1,0:T(8,128)(2,1)S(1)}, u32[]{:S(2)}, u32[]{:S(2)}) collective-permute-start(bf16[192,1280]{1,0:T(8,128)(2,1)S(1)} %get-tuple-element.122), channel_id=1, source_target_pairs={{0,8},{2,10},{4,12},{6,14},{8,0},{10,2},{12,4},{14,6},{16,24},{18,... | collective-permute-start | bytes 1474568 | tf_op jit(solution)/shard_map/ppermute | solution.py:393
  74.5 23.5 %collective-permute-start.19 = (bf16[192,1280]{1,0:T(8,128)(2,1)S(1)}, bf16[192,1280]{1,0:T(8,128)(2,1)S(1)}, u32[]{:S(2)}, u32[]{:S(2)}) collective-permute-start(bf16[192,1280]{1,0:T(8,128)(2,1)S(1)} %shard_map.286), channel_id=1, source_target_pairs={{0,24},{2,26},{4,28},{6,30},{8,16},{10,18},{12,20},{14,22},{16,8},... | collective-permute-start | bytes 1474568 | tf_op jit(solution)/shard_map/ppermute | solution.py:393
  76.9 21.1 %collective-permute-start.15 = (bf16[272,768]{1,0:T(8,128)(2,1)S(1)}, bf16[272,768]{1,0:T(8,128)(2,1)S(1)}, u32[]{:S(2)}, u32[]{:S(2)}) collective-permute-start(bf16[272,768]{1,0:T(8,128)(2,1)S(1)} %get-tuple-element.119), channel_id=1, source_target_pairs={{0,2},{2,0},{4,6},{6,4},{8,10},{10,8},{12,14},{14,12},{16,18},{18,... | collective-permute-start | bytes 1253384 | tf_op jit(solution)/shard_map/ppermute | solution.py:390
  77.1 20.9 %collective-permute-start.16 = (bf16[272,768]{1,0:T(8,128)(2,1)S(1)}, bf16[272,768]{1,0:T(8,128)(2,1)S(1)}, u32[]{:S(2)}, u32[]{:S(2)}) collective-permute-start(bf16[272,768]{1,0:T(8,128)(2,1)S(1)} %get-tuple-element.120), channel_id=1, source_target_pairs={{0,4},{2,6},{4,0},{6,2},{8,12},{10,14},{12,8},{14,10},{16,20},{18,... | collective-permute-start | bytes 1253384 | tf_op jit(solution)/shard_map/ppermute | solution.py:390
  78.0 20.0 %collective-permute-start.17 = (bf16[272,768]{1,0:T(8,128)(2,1)S(1)}, bf16[272,768]{1,0:T(8,128)(2,1)S(1)}, u32[]{:S(2)}, u32[]{:S(2)}) collective-permute-start(bf16[272,768]{1,0:T(8,128)(2,1)S(1)} %get-tuple-element.121), channel_id=1, source_target_pairs={{0,6},{2,4},{4,2},{6,0},{8,14},{10,12},{12,10},{14,8},{16,22},{18,... | collective-permute-start | bytes 1253384 | tf_op jit(solution)/shard_map/ppermute | solution.py:390
  98.3 6.0 %collective-permute-start.20 = (bf16[48,1280]{1,0:T(8,128)(2,1)S(1)}, bf16[48,1280]{1,0:T(8,128)(2,1)S(1)}, u32[]{:S(2)}, u32[]{:S(2)}) collective-permute-start(bf16[48,1280]{1,0:T(8,128)(2,1)S(1)} %get-tuple-element.134), channel_id=1, source_target_pairs={{0,2},{2,0},{4,6},{6,4},{8,10},{10,8},{12,14},{14,12},{16,18},{18,... | collective-permute-start | bytes 368648 | tf_op jit(solution)/shard_map/ppermute | solution.py:390
  98.6 5.7 %collective-permute-start.21 = (bf16[48,1280]{1,0:T(8,128)(2,1)S(1)}, bf16[48,1280]{1,0:T(8,128)(2,1)S(1)}, u32[]{:S(2)}, u32[]{:S(2)}) collective-permute-start(bf16[48,1280]{1,0:T(8,128)(2,1)S(1)} %get-tuple-element.135), channel_id=1, source_target_pairs={{0,4},{2,6},{4,0},{6,2},{8,12},{10,14},{12,8},{14,10},{16,20},{18,... | collective-permute-start | bytes 368648 | tf_op jit(solution)/shard_map/ppermute | solution.py:390
  99.6 5.9 %collective-permute-start.22 = (bf16[48,1280]{1,0:T(8,128)(2,1)S(1)}, bf16[48,1280]{1,0:T(8,128)(2,1)S(1)}, u32[]{:S(2)}, u32[]{:S(2)}) collective-permute-start(bf16[48,1280]{1,0:T(8,128)(2,1)S(1)} %get-tuple-element.136), channel_id=1, source_target_pairs={{0,6},{2,4},{4,2},{6,0},{8,14},{10,12},{12,10},{14,8},{16,22},{18,... | collective-permute-start | bytes 368648 | tf_op jit(solution)/shard_map/ppermute | solution.py:390
  103.0 1.2 %collective-permute-start.23 = (f32[16,768]{1,0:T(8,128)S(1)}, f32[16,768]{1,0:T(8,128)S(1)}, u32[]{:S(2)}, u32[]{:S(2)}) collective-permute-start(f32[16,768]{1,0:T(8,128)S(1)} %get-tuple-element.137.refs_4_), channel_id=1, source_target_pairs={{0,1},{1,0},{2,3},{3,2},{4,5},{5,4},{6,7},{7,6},{8,9},{9,8},{10,11... | collective-permute-start | bytes 147464 | tf_op jit(solution)/shard_map/ppermute | solution.py:396
